TPU v7x, 32 devices: a whole 2x2x4 slice. The times are simulated.
32 devices in a mesh: pipe: 2 (over x), dp: 16 (over z, y, core).
Axes of the slice: x: 2, y: 2, z: 4, core: 2. Of those that a mesh axis runs over, the one named last changes fastest.
Arguments:
- samples: bfloat16 [80, 3, 32, 640], P('dp'), may hold values from -6 to 6
- timesteps: int32 [80], P('dp'), may hold values from 0 to 999
- cotangent: bfloat16 [80, 3, 32, 640], P('dp'), may hold values from -0.059814453 to 0.059814453
- spatial_weight: bfloat16 [2, 5760, 640], P('pipe', 'dp'), may hold values from -0.078125 to 0.078125
- temporal_weight: bfloat16 [2, 1920, 640], P('pipe', 'dp'), may hold values from -0.125 to 0.125
Outputs:
- spatial_grad: float32 [2, 5760, 640], P('pipe', 'dp')
- temporal_grad: float32 [2, 1920, 640], P('pipe', 'dp')
All inputs are finite; a program needn't handle non-finite values.
Results may differ from a plain program's by a relative error of at most 0.034.
Values may be sent and summed in bfloat16 or wider, within the bound.
No kernel may reach another device: no remote copies, remote signals or barrier semaphores. Data moves between devices by JAX's collectives and lax.ppermute only.
A program may use at most 128 MiB of HBM per device.

v0:
```python
import functools
import math

import jax
import jax.numpy as jnp
from jax import lax
from jax.experimental import pallas as pl
from jax.experimental.pallas import tpu as pltpu
from jax.sharding import PartitionSpec as P

HEIGHT = 8
WIDTH = 4
F32 = jnp.float32
BF16 = jnp.bfloat16
GRID = (4, 2, 2)
LANES = 128


def passed_along(value, axis, steps):
    count = lax.axis_size(axis)
    first, last = (max(0, -steps), min(count, count - steps))
    return lax.ppermute(value, axis, [(source, source + steps) for source in range(first, last)])


def embedding_of(step, channels):
    half_width = channels // 2
    frequency = jnp.exp(-math.log(10000.0) * jnp.arange(half_width, dtype=jnp.float32) / half_width)
    phases = step.astype(jnp.float32) * frequency
    return jnp.concatenate([jnp.sin(phases), jnp.cos(phases)])


def normalize(summed):
    return summed * lax.rsqrt(jnp.mean(summed * summed, axis=-1, keepdims=True) + 1e-06)


def spatial_columns(normed):
    frames, pixels, channels = normed.shape
    grid = normed.reshape(frames, HEIGHT, WIDTH, channels)
    padded = jnp.pad(grid, ((0, 0), (1, 1), (1, 1), (0, 0)))
    pieces = [
        padded[:, row : row + HEIGHT, col : col + WIDTH, :] for row in range(3) for col in range(3)
    ]
    return jnp.concatenate(pieces, axis=-1).reshape(frames * pixels, 9 * channels)


def spatial_fold(grads, frames, channels):
    parts = grads.reshape(frames, HEIGHT, WIDTH, 9, channels)
    padded = jnp.zeros((frames, HEIGHT + 2, WIDTH + 2, channels), jnp.float32)
    for row in range(3):
        for col in range(3):
            padded = padded.at[:, row : row + HEIGHT, col : col + WIDTH, :].add(
                parts[:, :, :, row * 3 + col, :]
            )
    return padded[:, 1 : HEIGHT + 1, 1 : WIDTH + 1, :].reshape(frames, HEIGHT * WIDTH, channels)


def temporal_columns(activated):
    frames, pixels, channels = activated.shape
    padded = jnp.pad(activated, ((1, 1), (0, 0), (0, 0)))
    pieces = [padded[tap : tap + frames] for tap in range(3)]
    return jnp.concatenate(pieces, axis=-1).reshape(frames * pixels, 3 * channels)


def temporal_fold(grads, frames, pixels, channels):
    parts = grads.reshape(frames, pixels, 3, channels)
    padded = jnp.zeros((frames + 2, pixels, channels), jnp.float32)
    for tap in range(3):
        padded = padded.at[tap : tap + frames].add(parts[:, :, tap, :])
    return padded[1 : frames + 1]


def section_forward(block_in, embedding, spatial, temporal):
    frames, pixels, channels = block_in.shape
    summed = block_in.astype(jnp.float32) + embedding
    normed = normalize(summed).astype(jnp.bfloat16)
    preact = jnp.dot(spatial_columns(normed), spatial, preferred_element_type=jnp.float32)
    activated = jax.nn.silu(preact).astype(jnp.bfloat16).reshape(frames, pixels, channels)
    mixed = jnp.dot(temporal_columns(activated), temporal, preferred_element_type=jnp.float32)
    return (block_in.astype(jnp.float32) + mixed.reshape(frames, pixels, channels)).astype(
        jnp.bfloat16
    )


def backward_first(block_in, embedding, spatial, temporal, upstream):
    frames, pixels, channels = block_in.shape
    summed = block_in.astype(jnp.float32) + embedding
    normed = normalize(summed).astype(jnp.bfloat16)
    columns = spatial_columns(normed)
    preact = jnp.dot(columns, spatial, preferred_element_type=jnp.float32)
    activated = jax.nn.silu(preact).astype(jnp.bfloat16).reshape(frames, pixels, channels)
    tcolumns = temporal_columns(activated)
    upstream_flat = upstream.reshape(frames * pixels, channels)
    temporal_term = jnp.dot(tcolumns.T, upstream_flat, preferred_element_type=jnp.float32)
    act_grad = temporal_fold(
        jnp.dot(upstream_flat, temporal.T, preferred_element_type=jnp.float32),
        frames,
        pixels,
        channels,
    )
    logistic = jax.nn.sigmoid(preact)
    slope = logistic * (1.0 + preact * (1.0 - logistic))
    pre_grad = (act_grad.reshape(frames * pixels, channels) * slope).astype(jnp.bfloat16)
    return (temporal_term, pre_grad, columns)


def backward_second(block_in, embedding, spatial, upstream, pre_grad, columns):
    frames, pixels, channels = block_in.shape
    summed = block_in.astype(jnp.float32) + embedding
    spatial_term = jnp.dot(columns.T, pre_grad, preferred_element_type=jnp.float32)
    norm_grad = spatial_fold(
        jnp.dot(pre_grad, spatial.T, preferred_element_type=jnp.float32), frames, channels
    )
    _, pullback = jax.vjp(normalize, summed)
    back_input = (upstream.astype(jnp.float32) + pullback(norm_grad)[0]).astype(jnp.bfloat16)
    return (back_input, spatial_term)


def section_backward(block_in, embedding, spatial, temporal, upstream):
    temporal_term, pre_grad, columns = backward_first(
        block_in, embedding, spatial, temporal, upstream
    )
    back_input, spatial_term = backward_second(
        block_in, embedding, spatial, upstream, pre_grad, columns
    )
    return (back_input, spatial_term, temporal_term)


def per_device(samples, timesteps, cotangent, spatial_weight, temporal_weight):
    sections = lax.axis_size("pipe")
    section_index = lax.axis_index("pipe")
    micro_count = samples.shape[0]
    frames, pixels, channels = (samples.shape[1], samples.shape[2], samples.shape[3])
    moments = jnp.arange(micro_count + sections - 1, dtype=jnp.int32)
    blank = jnp.zeros((frames, pixels, channels), jnp.bfloat16)
    full_spatial, full_temporal = (
        lax.all_gather(spatial_weight[0], "dp", axis=0, tiled=True),
        lax.all_gather(temporal_weight[0], "dp", axis=0, tiled=True),
    )

    def forward_step(carry, moment):
        incoming, stash = carry
        position = moment - section_index
        active = (position >= 0) & (position < micro_count)
        picked = jnp.clip(position, 0, micro_count - 1)
        own = lax.dynamic_index_in_dim(samples, picked, 0, keepdims=False)
        embedding = embedding_of(
            lax.dynamic_index_in_dim(timesteps, picked, 0, keepdims=False), channels
        )
        block_in = jnp.where(section_index == 0, own, incoming)
        result = lax.cond(
            active & (section_index < sections - 1),
            lambda: section_forward(block_in, embedding, full_spatial, full_temporal),
            lambda: blank,
        )
        stash = jnp.where(
            active, lax.dynamic_update_index_in_dim(stash, block_in, picked, 0), stash
        )
        passed = passed_along(result, "pipe", 1)
        return ((passed, stash), None)

    (_, stash), _ = lax.scan(forward_step, (blank, jnp.zeros_like(samples)), moments)
    back_spatial, back_temporal = (full_spatial, full_temporal)

    def inputs_at(moment, incoming):
        position = moment - (sections - 1 - section_index)
        active = (position >= 0) & (position < micro_count)
        picked = jnp.clip(position, 0, micro_count - 1)
        block_in = lax.dynamic_index_in_dim(stash, picked, 0, keepdims=False)
        embedding = embedding_of(
            lax.dynamic_index_in_dim(timesteps, picked, 0, keepdims=False), channels
        )
        given = lax.dynamic_index_in_dim(cotangent, picked, 0, keepdims=False)
        upstream = jnp.where(section_index == sections - 1, given, incoming)
        return (active, block_in, embedding, upstream)

    def backward_step(carry, moment):
        incoming, grad_spatial, grad_temporal = carry
        active, block_in, embedding, upstream = inputs_at(moment, incoming)

        def working():
            back_input, spatial_term, temporal_term = section_backward(
                block_in, embedding, back_spatial, back_temporal, upstream
            )
            return (back_input, grad_spatial + spatial_term, grad_temporal + temporal_term)

        def waiting():
            return (blank, grad_spatial, grad_temporal)

        back_input, grad_spatial, grad_temporal = lax.cond(active, working, waiting)
        passed = passed_along(back_input, "pipe", -1)
        return ((passed, grad_spatial, grad_temporal), None)

    start = (
        blank,
        jnp.zeros(back_spatial.shape, jnp.float32),
        jnp.zeros(back_temporal.shape, jnp.float32),
    )
    (_, grad_spatial, grad_temporal), _ = lax.scan(backward_step, start, moments)
    share_spatial, share_temporal = (
        lax.psum_scatter(
            grad_spatial.astype(jnp.bfloat16).astype(jnp.float32).astype(jnp.bfloat16),
            "dp",
            scatter_dimension=0,
            tiled=True,
        ).astype(jnp.float32),
        lax.psum_scatter(
            grad_temporal.astype(jnp.bfloat16).astype(jnp.float32).astype(jnp.bfloat16),
            "dp",
            scatter_dimension=0,
            tiled=True,
        ).astype(jnp.float32),
    )
    return (share_spatial[None], share_temporal[None])


SPAN = 40
CUTS = (24, 16)
PIECE = 64


def coordinates():
    index = lax.axis_index("dp")
    return index // (GRID[1] * GRID[2]), (index // GRID[2]) % GRID[1], index % GRID[2]


def shifted(value, dz=0, dy=0, dc=0):
    pairs = []
    for z in range(GRID[0]):
        for y in range(GRID[1]):
            for c in range(GRID[2]):
                place = ((z + dz) % GRID[0], (y + dy) % GRID[1], (c + dc) % GRID[2])
                pairs.append(
                    (
                        (z * GRID[1] + y) * GRID[2] + c,
                        (place[0] * GRID[1] + place[1]) * GRID[2] + place[2],
                    )
                )
    return lax.ppermute(value, "dp", pairs)


def swapped(value):
    return lax.ppermute(value, "pipe", [(0, 1), (1, 0)])


def part_of(value, index, axis):
    return lax.dynamic_index_in_dim(value, index, axis, keepdims=False)


def vmem_call(body, outs, scratch=(), flops=0, moved=0):
    return pl.pallas_call(
        body,
        out_shape=outs,
        scratch_shapes=list(scratch),
        compiler_params=pltpu.CompilerParams(vmem_limit_bytes=24 * 2**20),
        cost_estimate=pl.CostEstimate(
            flops=5 * flops // 2, bytes_accessed=moved, transcendentals=0
        ),
    )


def after(value, earlier):
    return value if earlier is None else lax.optimization_barrier((value, earlier))[0]


def in_order(swap, own, other, axis):
    return jnp.where(
        swap, jnp.concatenate([other, own], axis), jnp.concatenate([own, other], axis)
    )


def over_z(value, pairs):
    moves = []
    for source, target in pairs:
        for rest in range(GRID[1] * GRID[2]):
            moves.append(tuple(z * GRID[1] * GRID[2] + rest for z in (source, target)))
    return lax.ppermute(value, "dp", moves)


def sent_over_z(value):
    return [shifted(value, dz=step) for step in range(1, GRID[0])]


def sent_on_chip(value):
    return shifted(value, dc=1)


def places_of(channels, main):
    channel = jnp.arange(channels)
    span, inside = channel // SPAN, channel % SPAN
    odd = span % 2
    cut = jnp.where(odd == 0, CUTS[0], CUTS[1])
    second = (inside >= cut).astype(jnp.int32)
    before = span // 2 * SPAN + odd * jnp.where(second == 0, CUTS[0], CUTS[1])
    rank = before + inside - second * cut
    tail = channels // 2 - main
    return jnp.where(
        rank < main, second * main + rank, (1 + second) * main + second * (tail - main) + rank
    )


def spans_of(rows, odd):
    sets = ([], [])
    for index, start in enumerate(range(0, rows, SPAN)):
        cut = start + CUTS[(index + odd) % 2]
        sets[0].append((start, cut))
        sets[1].append((cut, start + SPAN))
    return sets


def sets_of(value):
    _, _, c = coordinates()
    results = []
    for which in range(2):
        by_core = []
        for odd in range(2):
            spans = spans_of(value.shape[0], odd)[which]
            taken = jnp.concatenate([value[start:end] for start, end in spans])
            by_core.append(jnp.pad(taken, ((0, PIECE - taken.shape[0]), (0, 0))))
        results.append(jnp.where(c == 0, by_core[0], by_core[1]))
    return results


def shard_of(own, given, rows):
    _, _, c = coordinates()
    by_core = []
    for odd in range(2):
        taken, pieces = [0, 0], []
        for spans in zip(*spans_of(rows, odd)):
            for which, (start, end) in enumerate(spans):
                source = (own, given)[which]
                pieces.append(source[taken[which] : taken[which] + end - start])
                taken[which] += end - start
        by_core.append(jnp.concatenate(pieces))
    return jnp.where(c == 0, by_core[0], by_core[1])


def compact(pieces, own):
    short = 3 * SPAN - PIECE
    low, high = pieces[:, 0], pieces[:, 1]
    both = jnp.where(
        own,
        jnp.concatenate([low, high[:, :short]], 1),
        jnp.concatenate([low[:, :short], high], 1),
    )
    return both.reshape(-1, pieces.shape[3])


def spread(rows, chips, own):
    rows = rows.reshape(chips, -1, rows.shape[1])
    short = rows.shape[1] - PIECE
    pad = ((0, 0), (0, PIECE - short), (0, 0))
    return jnp.where(
        own,
        jnp.stack([rows[:, :PIECE], jnp.pad(rows[:, PIECE:], pad)], 1),
        jnp.stack([jnp.pad(rows[:, :short], pad), rows[:, short:]], 1),
    )


def gathered_over_z(value, earlier=None):
    z, _, _ = coordinates()
    value = after(value, earlier)
    sent = sent_over_z(value)
    return (
        jnp.stack([lax.select_n((z - place) % GRID[0], value, *sent) for place in range(GRID[0])]),
        sent,
    )


def gathered_over_y(line):
    _, y, _ = coordinates()
    return in_order(y == 1, line[:, None], shifted(line, dy=1)[:, None], 1)


def gathered_on_chip(plane, earlier=None):
    _, _, c = coordinates()
    plane = after(plane, earlier)
    whole = in_order(c == 1, plane[:, :, None], sent_on_chip(plane)[:, :, None], 2)
    return whole.reshape(-1, plane.shape[3])


def added(*terms):
    return sum(term.astype(F32) for term in terms)


def summed_on_chip(value):
    _, _, c = coordinates()
    sent = sent_on_chip(part_of(value, 1 - c, 2))
    return added(part_of(value, c, 2), sent).astype(BF16)


def summed_over_y(value, earlier):
    _, y, _ = coordinates()
    sent = shifted(after(part_of(value, 1 - y, 1), earlier), dy=1)
    return added(part_of(value, y, 1), sent).astype(BF16), sent


def summed_over_z(line, earlier=None):
    z, _, _ = coordinates()
    line = after(line, earlier)
    sent = [
        shifted(part_of(line, (z + step) % GRID[0], 0), dz=step) for step in range(1, GRID[0])
    ]
    return added(part_of(line, z, 0), *sent), sent


def pixel_masks(rows):
    row = lax.broadcasted_iota(jnp.int32, (rows, 1), 0)
    high, wide = (row // WIDTH) % HEIGHT, row % WIDTH
    masks = []
    for dr in (-1, 0, 1):
        for dc in (-1, 0, 1):
            inside = (high + dr >= 0) & (high + dr < HEIGHT) & (wide + dc >= 0) & (wide + dc < WIDTH)
            masks.append((dr * WIDTH + dc, inside))
    return masks


def frame_masks(rows, frames):
    pixels = HEIGHT * WIDTH
    row = lax.broadcasted_iota(jnp.int32, (rows, 1), 0)
    frame = (row // pixels) % frames
    return [
        (step * pixels, (frame + step >= 0) & (frame + step < frames)) for step in (-1, 0, 1)
    ]


def moved_rows(value, move):
    shift, inside = move
    if shift:
        value = pltpu.roll(value, (-shift) % value.shape[0], 0)
    return jnp.where(inside, value, 0.0)


def dot(left, right, dims=((1,), (0,))):
    return lax.dot_general(left, right, (dims, ((), ())), preferred_element_type=F32)


def with_embedding(hidden, embedding_ref, samples):
    per = hidden.shape[0] // samples
    return jnp.concatenate(
        [hidden[s * per : (s + 1) * per] + embedding_ref[s : s + 1, :] for s in range(samples)]
    )


def scale_of(summed):
    return lax.rsqrt(jnp.mean(summed * summed, axis=-1, keepdims=True) + 1e-06)


def silu_parts(preact):
    logistic = 1.0 / (1.0 + jnp.exp(-preact))
    return logistic, preact * logistic


def tap_weight(weight_refs, tap, channels):
    return jnp.concatenate(
        [ref[tap * channels : (tap + 1) * channels, :] for ref in weight_refs], 1
    )


def convolved(normed, weight_refs, masks):
    rows, channels = normed.shape
    normed = normed.astype(F32)
    total = None
    for tap in range(9):
        term = dot(
            moved_rows(normed, masks[tap]).astype(BF16),
            tap_weight(weight_refs, tap, channels),
        )
        total = term if total is None else total + term
    return total


def tap_rows(temporal_ref, tap, width):
    tail = PIECE
    start = tap * (width - tail)
    rows = temporal_ref[start : start + width - tail, :]
    return jnp.concatenate([rows, rows[width - 2 * tail :]], 0)


def first_forward(frames, hidden_ref, embedding_ref, keep_ref, temporal_ref, *refs):
    *spatial_refs, normed_ref, preact_ref, mixed_ref = refs
    rows = hidden_ref.shape[0]
    width = keep_ref.shape[1]
    summed = with_embedding(hidden_ref[...].astype(F32), embedding_ref, embedding_ref.shape[0])
    normed = (summed * scale_of(summed)).astype(BF16)
    normed_ref[...] = normed
    preact = convolved(normed, spatial_refs, pixel_masks(rows))
    preact_ref[...] = preact
    activated = silu_parts(preact)[1].astype(BF16).astype(F32) * keep_ref[...]
    mixed = None
    for tap, move in enumerate(frame_masks(rows, frames)):
        term = dot(
            moved_rows(activated, move).astype(BF16),
            tap_rows(temporal_ref, tap, width),
        )
        mixed = term if mixed is None else mixed + term
    mixed_ref[...] = mixed.astype(BF16)


def slope_of(preact):
    logistic, _ = silu_parts(preact)
    return logistic * (1.0 + preact * (1.0 - logistic))


def act_grad_of(upstream, temporal_ref, width, frames):
    upstream = upstream.astype(F32)
    moves = frame_masks(upstream.shape[0], frames)
    total = None
    for tap in range(3):
        term = dot(
            moved_rows(upstream, moves[2 - tap]).astype(BF16),
            tap_rows(temporal_ref, tap, width),
            ((1,), (1,)),
        )
        total = term if total is None else total + term
    return total


def store_temporal_terms(activated, upstream, frames, out_ref):
    width = activated.shape[1]
    tail = PIECE
    upstream = upstream.astype(F32)
    moves = frame_masks(upstream.shape[0], frames)
    for tap in range(3):
        term = dot(activated, moved_rows(upstream, moves[2 - tap]).astype(BF16), ((0,), (0,)))
        start = tap * (width - tail)
        out_ref[start : start + width - 2 * tail, :] = term[: width - 2 * tail].astype(BF16)
        out_ref[start + width - 2 * tail : start + width - tail, :] = (
            term[width - 2 * tail : width - tail] + term[width - tail :]
        ).astype(BF16)


def store_spatial_terms(normed, pre_grad, out_refs):
    channels = normed.shape[1]
    pre_grad = pre_grad.astype(F32)
    masks = pixel_masks(pre_grad.shape[0])
    for tap in range(9):
        term = dot(
            normed, moved_rows(pre_grad, masks[8 - tap]).astype(BF16), ((0,), (0,))
        ).astype(BF16)
        start = 0
        for out_ref in out_refs:
            end = start + out_ref.shape[1]
            out_ref[tap * channels : (tap + 1) * channels, :] = term[:, start:end]
            start = end


def second_forward(
    frames, hidden_ref, own_ref, sent_ref, embedding_ref, keep_ref, upstream_ref, temporal_ref, *refs
):
    *spatial_refs, next_ref, normed_ref, activated_ref, pre_grad_ref, back_ref = refs
    rows, channels = hidden_ref.shape
    width = keep_ref.shape[1]
    masks = pixel_masks(rows)
    mixed = own_ref[...].astype(F32) + sent_ref[...].astype(F32)
    hidden = (hidden_ref[...].astype(F32) + mixed).astype(BF16)
    next_ref[...] = hidden
    summed = with_embedding(hidden.astype(F32), embedding_ref, embedding_ref.shape[0])
    normed = (summed * scale_of(summed)).astype(BF16)
    normed_ref[...] = normed
    preact = convolved(normed, spatial_refs, masks)
    activated_ref[...] = (silu_parts(preact)[1] * keep_ref[...]).astype(BF16)
    act_grad = act_grad_of(upstream_ref[...], temporal_ref, width, frames)
    pre_grad = (act_grad * slope_of(preact) * keep_ref[...]).astype(BF16)
    pre_grad_ref[...] = pre_grad
    pre_grad = pre_grad.astype(F32)
    back = None
    for tap in range(9):
        term = dot(
            moved_rows(pre_grad, masks[8 - tap]).astype(BF16),
            tap_weight(spatial_refs, tap, channels),
            ((1,), (1,)),
        )
        back = term if back is None else back + term
    back_ref[...] = back.astype(BF16)


def second_terms(frames, normed_ref, pre_grad_ref, activated_ref, upstream_ref, *outs):
    *spatial_refs, temporal_ref = outs
    store_spatial_terms(normed_ref[...], pre_grad_ref[...], spatial_refs)
    store_temporal_terms(activated_ref[...], upstream_ref[...], frames, temporal_ref)


def first_terms(
    frames, hidden_ref, embedding_ref, upstream_ref, own_ref, sent_ref, normed_ref, preact_ref,
    keep_ref, temporal_ref, *outs
):
    *spatial_outs, temporal_out = outs
    width = keep_ref.shape[1]
    channels = hidden_ref.shape[1]
    summed = with_embedding(hidden_ref[...].astype(F32), embedding_ref, embedding_ref.shape[0])
    scale = scale_of(summed)
    grad = own_ref[...].astype(F32) + sent_ref[...].astype(F32)
    inner = jnp.sum(grad * summed, axis=-1, keepdims=True)
    back = grad * scale - summed * (scale * scale * scale) * (inner / channels)
    upstream = (upstream_ref[...].astype(F32) + back).astype(BF16)
    preact = preact_ref[...]
    activated = (silu_parts(preact)[1] * keep_ref[...]).astype(BF16)
    act_grad = act_grad_of(upstream, temporal_ref, width, frames)
    pre_grad = (act_grad * slope_of(preact) * keep_ref[...]).astype(BF16)
    store_spatial_terms(normed_ref[...], pre_grad, spatial_outs)
    store_temporal_terms(activated, upstream, frames, temporal_out)


def paired_device(samples, timesteps, cotangent, spatial_weight, temporal_weight):
    me = lax.axis_index("pipe")
    first = me == 0
    _, y, _ = coordinates()
    count, frames, pixels, channels = samples.shape
    rows = count * frames * pixels
    main = 2 * LANES
    width = main + LANES
    hidden = samples.reshape(rows, channels)
    upstream = cotangent.reshape(rows, channels)
    embedding = jax.vmap(lambda step: embedding_of(step, channels))(timesteps)
    lane = jnp.arange(LANES)
    keep_own = jnp.concatenate([jnp.ones(main), lane < LANES // 2]).astype(F32)[None]
    keep_other = jnp.concatenate([jnp.ones(main), lane >= LANES // 2]).astype(F32)[None]
    keep_first = jnp.where(first, keep_own, keep_other)
    keep_second = jnp.where(first, keep_other, keep_own)
    tail = lane[None] < LANES // 2

    places = places_of(channels, main)
    order = (places[:, None] == jnp.arange(channels)).astype(BF16)
    temporal_own, temporal_sent = sets_of(temporal_weight[0])
    temporal_given = swapped(temporal_sent)
    line, sent = gathered_over_z(in_order(me == 1, temporal_own, temporal_given, 0))
    plane_temporal = gathered_over_y(line)
    spatial_own = dot(spatial_weight[0], order).astype(BF16)
    given = swapped(spatial_own[:, main:])
    main_own, main_given = spatial_own[:, :main], given[:, :main]
    tails = jnp.where(tail, spatial_own[:, 2 * main :], given[:, main:])
    line, sent = gathered_over_z(jnp.where(first, main_own, main_given), sent)
    plane_first = gathered_over_y(line)
    line, sent = gathered_over_z(tails, sent)
    plane_tails = gathered_over_y(line)
    line_second, _ = gathered_over_z(jnp.where(first, main_given, main_own), sent)
    side_second = shifted(line_second, dy=1)

    chips = GRID[0] * GRID[1]
    temporal = gathered_on_chip(plane_temporal).reshape(chips, GRID[2], 2, PIECE, channels)
    temporal_first = compact(temporal[:, :, 0], first)
    temporal_second = compact(temporal[:, :, 1], me == 1)
    tails = gathered_on_chip(plane_tails)
    spatial_first = [gathered_on_chip(plane_first), tails]

    def shape(extent, dtype=BF16):
        return jax.ShapeDtypeStruct(extent, dtype)

    spatial_flops = 2 * rows * 9 * channels * width
    temporal_flops = 2 * rows * 3 * channels * width
    spatial_bytes = 2 * 9 * channels * width
    temporal_bytes = 2 * 3 * channels * width
    normed_first, preact_first, mixed = vmem_call(
        functools.partial(first_forward, frames),
        (shape((rows, channels)), shape((rows, width), F32), shape((rows, channels))),
        flops=spatial_flops + temporal_flops,
        moved=spatial_bytes + temporal_bytes,
    )(hidden, embedding, keep_first, temporal_first, *spatial_first)
    mixed_given = swapped(mixed)
    side_second = after(side_second, mixed)
    plane_second = in_order(y == 1, line_second[:, None], side_second[:, None], 1)
    spatial_second = [gathered_on_chip(plane_second), tails]
    hidden_second, normed_second, activated_second, pre_grad_second, back = vmem_call(
        functools.partial(second_forward, frames),
        (
            shape((rows, channels)),
            shape((rows, channels)),
            shape((rows, width)),
            shape((rows, width)),
            shape((rows, channels)),
        ),
        flops=2 * spatial_flops + temporal_flops,
        moved=spatial_bytes + temporal_bytes,
    )(
        hidden, mixed, mixed_given, embedding, keep_second, upstream, temporal_second,
        *spatial_second,
    )

    def terms_shape():
        return (
            shape((9 * channels, main)),
            shape((9 * channels, width - main)),
            shape((3 * (width - PIECE), channels)),
        )

    def on_chip(terms):
        return summed_on_chip(terms.reshape(*GRID, -1, terms.shape[1]))

    back_given = swapped(back)
    main_terms_second, tail_terms_second, temporal_terms_second = vmem_call(
        functools.partial(second_terms, frames),
        terms_shape(),
        flops=spatial_flops + temporal_flops,
        moved=spatial_bytes + temporal_bytes,
    )(normed_second, pre_grad_second, activated_second, upstream)
    chip_second = on_chip(main_terms_second)
    back_given = after(back_given, chip_second)
    line, side = summed_over_y(chip_second, None)
    share_second, sent_second = summed_over_z(line)
    main_terms_first, tail_terms_first, temporal_terms_first = vmem_call(
        functools.partial(first_terms, frames),
        terms_shape(),
        flops=spatial_flops + 2 * temporal_flops,
        moved=spatial_bytes + 2 * temporal_bytes,
    )(
        hidden_second, embedding, upstream, back, back_given, normed_first, preact_first,
        keep_first, temporal_first,
    )
    chip_tails = on_chip(after(tail_terms_first + tail_terms_second, side))
    chip_first = on_chip(after(main_terms_first, side))
    terms = jnp.concatenate(
        [
            spread(temporal_terms_first, chips, first),
            spread(temporal_terms_second, chips, me == 1),
        ],
        2,
    )
    chip_temporal = summed_on_chip(terms.reshape(*GRID, -1, channels))

    line, side = summed_over_y(chip_tails, side)
    line_low, side = summed_over_y(chip_first[..., :LANES], side)
    share_tails, sent_tails = summed_over_z(line, (side, sent_second))
    line_high, side = summed_over_y(chip_first[..., LANES:], side)
    share_first, sent_first = summed_over_z(
        jnp.concatenate([line_low, line_high], 2), sent_tails
    )
    line, side = summed_over_y(chip_temporal, side)
    share_temporal, _ = summed_over_z(line, sent_first)

    kept = jnp.where(first, share_first, share_second)
    passed = jnp.where(first, share_second, share_first)
    given = jnp.concatenate([passed, share_tails], 1).astype(BF16)
    given = swapped(after(given, side)).astype(F32)
    share_spatial = jnp.concatenate(
        [kept, given[:, :main], jnp.where(tail, share_tails, given[:, main:])], 1
    )
    share_spatial = lax.dot_general(
        share_spatial, order.astype(F32), (((1,), (1,)), ((), ())), precision=lax.Precision.HIGH
    )
    low, high = share_temporal[:PIECE], share_temporal[PIECE:]
    given = swapped(jnp.where(first, high, low).astype(BF16)).astype(F32)
    share_temporal = shard_of(jnp.where(first, low, high), given, temporal_weight.shape[1])
    return (share_spatial[None], share_temporal[None])


def solution(mesh):
    paired = mesh.shape["pipe"] == 2 and mesh.shape["dp"] == math.prod(GRID)
    return jax.shard_map(
        paired_device if paired else per_device,
        mesh=mesh,
        in_specs=(
            P("dp", None, None, None),
            P("dp"),
            P("dp", None, None, None),
            P("pipe", "dp", None),
            P("pipe", "dp", None),
        ),
        out_specs=(P("pipe", "dp", None), P("pipe", "dp", None)),
        check_vma=False,
    )
```

profile of v0, /device:TPU:0, one launch (start us, length us, event | category | flops | bytes accessed | tf_op | source)
XLA Modules:
  0.0 256.1 jit_solution(16018330056737972366)
XLA Ops:
  2.5 3.0 %collective-permute-start = (bf16[64,640]{1,0:T(8,128)(2,1)S(1)}, bf16[64,640]{1,0:T(8,128)(2,1)S(1)}, u32[]{:S(2)}, u32[]{:S(2)}) collective-permute-start(bf16[64,640]{1,0:T(8,128)(2,1)S(1)} %fusion.42), channel_id=1, source_target_pairs={{0,16},{16,0},{1,17},{17,1},{2,18},{18,2},{3,19},{19,3},{4,20},{20... | collective-permute-start | bytes 245768 | tf_op jit(solution)/shard_map/ppermute | solution.py:242
  6.6 1.7 collective-permute-done
  8.3 2.8 %collective-permute-start.2 = (bf16[128,640]{1,0:T(8,128)(2,1)S(1)}, bf16[128,640]{1,0:T(8,128)(2,1)S(1)}, u32[]{:S(2)}, u32[]{:S(2)}) collective-permute-start(bf16[128,640]{1,0:T(8,128)(2,1)S(1)} %maximum_select_fusion.15), channel_id=1, source_target_pairs={{0,8},{1,9},{2,10},{3,11},{4,12},{5,13},{6,14},{7,15},{8,0},{9,1},... | collective-permute-start | bytes 491528 | tf_op jit(solution)/shard_map/ppermute | solution.py:238
  11.1 1.3 collective-permute-start.3
  13.3 7.4 %collective-permute-done.2 = bf16[128,640]{1,0:T(8,128)(2,1)S(1)} collective-permute-done((bf16[128,640]{1,0:T(8,128)(2,1)S(1)}, bf16[128,640]{1,0:T(8,128)(2,1)S(1)}, u32[]{:S(2)}, u32[]{:S(2)}) %collective-permute-start.2) | collective-permute-done | bytes 163872 | tf_op jit(solution)/shard_map/ppermute | solution.py:238
  20.7 1.8 collective-permute-done.1
  23.3 4.9 %collective-permute-start.8 = (bf16[360,256]{1,0:T(8,128)(2,1)S(1)}, bf16[360,256]{1,0:T(8,128)(2,1)S(1)}, u32[]{:S(2)}, u32[]{:S(2)}) collective-permute-start(bf16[360,256]{1,0:T(8,128)(2,1)S(1)} %get-tuple-element.31), channel_id=1, source_target_pairs={{0,8},{1,9},{2,10},{3,11},{4,12},{5,13},{6,14},{7,15},{8,0},{9,1},... | collective-permute-start | bytes 552968 | tf_op jit(solution)/shard_map/ppermute | solution.py:238
  28.6 1.6 collective-permute-start.7
  30.2 8.0 %collective-permute-done.8 = bf16[360,256]{1,0:T(8,128)(2,1)S(1)} collective-permute-done((bf16[360,256]{1,0:T(8,128)(2,1)S(1)}, bf16[360,256]{1,0:T(8,128)(2,1)S(1)}, u32[]{:S(2)}, u32[]{:S(2)}) %collective-permute-start.8) | collective-permute-done | bytes 184352 | tf_op jit(solution)/shard_map/ppermute | solution.py:238
  38.2 3.9 %collective-permute-done.9 = bf16[360,256]{1,0:T(8,128)(2,1)S(1)} collective-permute-done((bf16[360,256]{1,0:T(8,128)(2,1)S(1)}, bf16[360,256]{1,0:T(8,128)(2,1)S(1)}, u32[]{:S(2)}, u32[]{:S(2)}) %collective-permute-start.9) | collective-permute-done | bytes 184352 | tf_op jit(solution)/shard_map/ppermute | solution.py:238
  42.1 2.3 collective-permute-start.13
  44.4 3.4 %collective-permute-start.14 = (bf16[360,128]{1,0:T(8,128)(2,1)S(1)}, bf16[360,128]{1,0:T(8,128)(2,1)S(1)}, u32[]{:S(2)}, u32[]{:S(2)}) collective-permute-start(bf16[360,128]{1,0:T(8,128)(2,1)S(1)} %slice_select_fusion.2), channel_id=1, source_target_pairs={{0,12},{1,13},{2,14},{3,15},{4,0},{5,1},{6,2},{7,3},{8,4},{9,5},{1... | collective-permute-start | bytes 276488 | tf_op jit(solution)/shard_map/ppermute | solution.py:238
  48.0 1.6 collective-permute-start.4
  50.5 3.7 %collective-permute-done.12 = bf16[360,128]{1,0:T(8,128)(2,1)S(1)} collective-permute-done((bf16[360,128]{1,0:T(8,128)(2,1)S(1)}, bf16[360,128]{1,0:T(8,128)(2,1)S(1)}, u32[]{:S(2)}, u32[]{:S(2)}) %collective-permute-start.12) | collective-permute-done | bytes 92192 | tf_op jit(solution)/shard_map/ppermute | solution.py:238
  55.1 1.5 collective-permute-start.15
  58.3 1.4 collective-permute-start.19
  60.4 5.3 %collective-permute-done.4 = bf16[4,128,640]{2,1,0:T(8,128)(2,1)S(1)} collective-permute-done((bf16[4,128,640]{2,1,0:T(8,128)(2,1)S(1)}, bf16[4,128,640]{2,1,0:T(8,128)(2,1)S(1)}, u32[]{:S(2)}, u32[]{:S(2)}) %collective-permute-start.4) | collective-permute-done | bytes 655392 | tf_op jit(solution)/shard_map/ppermute | solution.py:238
  65.9 1.3 maximum_select_fusion.7
  67.1 6.6 %collective-permute-done.15 = bf16[4,360,128]{2,1,0:T(8,128)(2,1)} collective-permute-done((bf16[4,360,128]{2,1,0:T(8,128)(2,1)S(1)}, bf16[4,360,128]{2,1,0:T(8,128)(2,1)}, u32[]{:S(2)}, u32[]{:S(2)}) %collective-permute-start.15) | collective-permute-done | bytes 368672 | tf_op jit(solution)/shard_map/ppermute | solution.py:238
  73.7 1.4 maximum_select_fusion.13
  75.8 1.3 select_bitcast_fusion.3
  78.1 1.5 collective-permute-start.21
  80.0 9.4 %collective-permute-done.10 = bf16[4,360,256]{2,1,0:T(8,128)(2,1)S(1)} collective-permute-done((bf16[4,360,256]{2,1,0:T(8,128)(2,1)}, bf16[4,360,256]{2,1,0:T(8,128)(2,1)S(1)}, u32[]{:S(2)}, u32[]{:S(2)}) %collective-permute-start.10) | collective-permute-done | bytes 737312 | tf_op jit(solution)/shard_map/ppermute | solution.py:238
  89.7 1.2 maximum_select_fusion.14
  91.6 2.2 maximum_select_fusion.2
  94.0 1.1 slice_bitcast_fusion.3
  97.2 7.0 %shard_map.68 = (bf16[480,640]{1,0:T(8,128)(2,1)S(1)}, f32[480,384]{1,0:T(8,128)S(1)}, bf16[480,640]{1,0:T(8,128)(2,1)}) custom-call(bf16[480,640]{1,0:T(8,128)(2,1)S(1)} %bitcast.291, f32[5,640]{1,0:T(8,128)S(1)} %pad_maximum_fusion.6.embedding_ref, f32[1,384]{1,0:T(1,128)S(1)} %select_n.851.keep_ref, bf16[960,640]{1,0:T(8,128)(2,1)S(1)} %bitcast.288, ...), custom_call_target="tpu_custom_call" | custom-call | flops 7077888000 | bytes 5898240 | tf_op jit(solution)/shard_map/pallas_call | solution.py:653
  104.3 1.6 maximum_select_fusion.6
  106.5 1.5 collective-permute-start.17
  108.1 1.1 slice.269
  109.3 1.5 maximum_select_fusion.12
  111.1 2.5 maximum_select_fusion.1
  113.8 8.9 %collective-permute-done.17.sent_ref = bf16[480,640]{1,0:T(8,128)(2,1)} collective-permute-done((bf16[480,640]{1,0:T(8,128)(2,1)}, bf16[480,640]{1,0:T(8,128)(2,1)}, u32[]{:S(2)}, u32[]{:S(2)}) %collective-permute-start.17) | collective-permute-done | bytes 614432 | tf_op jit(solution)/shard_map/ppermute | solution.py:242
  122.6 10.6 %shard_map.69 = (bf16[480,640]{1,0:T(8,128)(2,1)S(1)}, bf16[480,640]{1,0:T(8,128)(2,1)S(1)}, bf16[480,384]{1,0:T(8,128)(2,1)S(1)}, bf16[480,384]{1,0:T(8,128)(2,1)S(1)}, bf16[480,640]{1,0:T(8,128)(2,1)}) custom-call(bf16[480,640]{1,0:T(8,128)(2,1)S(1)} %bitcast.292, bf16[480,640]{1,0:T(8,128)(2,1)} %get-tuple-element.33.own_ref, ...), custom_call_target="tpu_custom_call" | custom-call | flops 12386304000 | bytes 5898240 | tf_op jit(solution)/shard_map/pallas_call | solution.py:663
  133.2 4.4 %shard_map.70 = (bf16[5760,256]{1,0:T(8,128)(2,1)S(1)}, bf16[5760,128]{1,0:T(8,128)(2,1)S(1)}, bf16[960,640]{1,0:T(8,128)(2,1)S(1)}) custom-call(bf16[480,640]{1,0:T(8,128)(2,1)S(1)} %get-tuple-element.38.normed_ref, bf16[480,384]{1,0:T(8,128)(2,1)S(1)} %get-tuple-element.39.pre_grad_ref, bf16[480,384]{1,0:T(8,128)(2,1)S(1)} %get-tuple-element.40.activated_ref, ...), custom_call_target="tpu_custom_call" | custom-call | flops 7077888000 | bytes 5898240 | tf_op jit(solution)/shard_map/pallas_call | solution.py:690
  137.6 1.7 constant_dynamic-slice_fusion.5
  139.3 1.3 copy.46
  140.6 1.5 collective-permute-start.23
  142.3 1.9 collective-permute-done.24
  144.2 2.0 fusion.1
  146.2 11.0 %collective-permute-done.23.sent_ref = bf16[480,640]{1,0:T(8,128)(2,1)} collective-permute-done((bf16[480,640]{1,0:T(8,128)(2,1)}, bf16[480,640]{1,0:T(8,128)(2,1)}, u32[]{:S(2)}, u32[]{:S(2)}) %collective-permute-start.23) | collective-permute-done | bytes 614432 | tf_op jit(solution)/shard_map/ppermute | solution.py:242
  157.2 1.6 collective-permute-start.25
  158.8 7.6 %shard_map.71 = (bf16[5760,256]{1,0:T(8,128)(2,1)S(1)}, bf16[5760,128]{1,0:T(8,128)(2,1)S(1)}, bf16[960,640]{1,0:T(8,128)(2,1)S(1)}) custom-call(bf16[480,640]{1,0:T(8,128)(2,1)S(1)} %copy-done.11, f32[5,640]{1,0:T(8,128)S(1)} %pad_maximum_fusion.6.embedding_ref, bf16[480,640]{1,0:T(8,128)(2,1)S(1)} %bitcast.295, ...), custom_call_target="tpu_custom_call" | custom-call | flops 8847360000 | bytes 7372800 | tf_op jit(solution)/shard_map/pallas_call | solution.py:700
  166.5 9.0 %collective-permute-done.25 = bf16[4,360,256]{2,1,0:T(8,128)(2,1)S(1)} collective-permute-done((bf16[4,360,256]{2,1,0:T(8,128)(2,1)S(1)}, bf16[4,360,256]{2,1,0:T(8,128)(2,1)S(1)}, u32[]{:S(2)}, u32[]{:S(2)}) %collective-permute-start.25) | collective-permute-done | bytes 737312 | tf_op jit(solution)/shard_map/ppermute | solution.py:238
  179.0 4.4 %collective-permute-start.32 = (bf16[360,256]{1,0:T(8,128)(2,1)S(1)}, bf16[360,256]{1,0:T(8,128)(2,1)S(1)}, u32[]{:S(2)}, u32[]{:S(2)}) collective-permute-start(bf16[360,256]{1,0:T(8,128)(2,1)S(1)} %get-tuple-element.86), channel_id=1, source_target_pairs={{0,8},{1,9},{2,10},{3,11},{4,12},{5,13},{6,14},{7,15},{8,0},{9,1},... | collective-permute-start | bytes 552968 | tf_op jit(solution)/shard_map/ppermute | solution.py:238
  184.2 1.6 collective-permute-start.28
  186.5 8.1 %collective-permute-done.28 = bf16[4,360,128]{2,1,0:T(8,128)(2,1)S(1)} collective-permute-done((bf16[4,360,128]{2,1,0:T(8,128)(2,1)S(1)}, bf16[4,360,128]{2,1,0:T(8,128)(2,1)S(1)}, u32[]{:S(2)}, u32[]{:S(2)}) %collective-permute-start.28) | collective-permute-done | bytes 368672 | tf_op jit(solution)/shard_map/ppermute | solution.py:238
  194.6 1.5 collective-permute-start.29
  196.6 7.5 %collective-permute-done.29 = bf16[4,360,128]{2,1,0:T(8,128)(2,1)S(1)} collective-permute-done((bf16[4,360,128]{2,1,0:T(8,128)(2,1)S(1)}, bf16[4,360,128]{2,1,0:T(8,128)(2,1)S(1)}, u32[]{:S(2)}, u32[]{:S(2)}) %collective-permute-start.29) | collective-permute-done | bytes 368672 | tf_op jit(solution)/shard_map/ppermute | solution.py:238
  204.1 1.5 collective-permute-start.30
  205.9 1.5 collective-permute-start.35
  208.3 4.6 %collective-permute-done.30 = bf16[4,360,128]{2,1,0:T(8,128)(2,1)S(1)} collective-permute-done((bf16[4,360,128]{2,1,0:T(8,128)(2,1)S(1)}, bf16[4,360,128]{2,1,0:T(8,128)(2,1)S(1)}, u32[]{:S(2)}, u32[]{:S(2)}) %collective-permute-start.30) | collective-permute-done | bytes 368672 | tf_op jit(solution)/shard_map/ppermute | solution.py:238
  212.9 1.5 collective-permute-start.41
  214.7 1.3 collective-permute-start.39
  216.3 1.4 collective-permute-start.37
  217.7 9.0 %collective-permute-done.41 = bf16[4,128,640]{2,1,0:T(8,128)(2,1)S(1)} collective-permute-done((bf16[4,128,640]{2,1,0:T(8,128)(2,1)S(1)}, bf16[4,128,640]{2,1,0:T(8,128)(2,1)S(1)}, u32[]{:S(2)}, u32[]{:S(2)}) %collective-permute-start.41) | collective-permute-done | bytes 655392 | tf_op jit(solution)/shard_map/ppermute | solution.py:238
  226.9 4.1 %collective-permute-done.38 = bf16[360,256]{1,0:T(8,128)(2,1)S(1)} collective-permute-done((bf16[360,256]{1,0:T(8,128)(2,1)S(1)}, bf16[360,256]{1,0:T(8,128)(2,1)S(1)}, u32[]{:S(2)}, u32[]{:S(2)}) %collective-permute-start.38) | collective-permute-done | bytes 184352 | tf_op jit(solution)/shard_map/ppermute | solution.py:238
  231.1 2.1 collective-permute-start.44
  233.3 1.9 collective-permute-start.43
  235.5 1.6 collective-permute-start.42
  237.1 11.0 %collective-permute-done.44 = bf16[128,640]{1,0:T(8,128)(2,1)S(1)} collective-permute-done((bf16[128,640]{1,0:T(8,128)(2,1)S(1)}, bf16[128,640]{1,0:T(8,128)(2,1)S(1)}, u32[]{:S(2)}, u32[]{:S(2)}) %collective-permute-start.44) | collective-permute-done | bytes 163872 | tf_op jit(solution)/shard_map/ppermute | solution.py:238
  248.2 1.6 collective-permute-start.46
  249.8 2.9 %collective-permute-done.46 = bf16[64,640]{1,0:T(8,128)(2,1)S(1)} collective-permute-done((bf16[64,640]{1,0:T(8,128)(2,1)S(1)}, bf16[64,640]{1,0:T(8,128)(2,1)S(1)}, u32[]{:S(2)}, u32[]{:S(2)}) %collective-permute-start.46) | collective-permute-done | bytes 81952 | tf_op jit(solution)/shard_map/ppermute | solution.py:242
  253.8 2.1 fusion.7
  (180 shorter events, 24.8 us)
Async XLA Ops:
  0.6 4.9 %copy-start = (bf16[1,360,640]{2,1,0:T(8,128)(2,1)S(1)}, bf16[1,360,640]{2,1,0:T(8,128)(2,1)}, u32[]{:S(2)}) copy-start(bf16[1,360,640]{2,1,0:T(8,128)(2,1)} %param.8) | copy-start | bytes 1382404
  1.5 4.8 %copy-start.19 = (s32[5]{0:T(128)S(1)}, s32[5]{0:T(128)}, u32[]{:S(2)}) copy-start(s32[5]{0:T(128)} %param.6) | copy-start | bytes 64
  2.5 5.8 %collective-permute-start = (bf16[64,640]{1,0:T(8,128)(2,1)S(1)}, bf16[64,640]{1,0:T(8,128)(2,1)S(1)}, u32[]{:S(2)}, u32[]{:S(2)}) collective-permute-start(bf16[64,640]{1,0:T(8,128)(2,1)S(1)} %fusion.42), channel_id=1, source_target_pairs={{0,16},{16,0},{1,17},{17,1},{2,18},{18,2},{3,19},{19,3},{4,20},{20... | collective-permute-start | bytes 245768 | tf_op jit(solution)/shard_map/ppermute | solution.py:242
  6.3 16.3 %collective-permute-start.6 = (bf16[360,384]{1,0:T(8,128)(2,1)S(1)}, bf16[360,384]{1,0:T(8,128)(2,1)S(1)}, u32[]{:S(2)}, u32[]{:S(2)}) collective-permute-start(bf16[360,384]{1,0:T(8,128)(2,1)S(1)} %slice.262), channel_id=1, source_target_pairs={{0,16},{16,0},{1,17},{17,1},{2,18},{18,2},{3,19},{19,3},{4,20},{20... | collective-permute-start | bytes 829448 | tf_op jit(solution)/shard_map/ppermute | solution.py:242
  8.3 12.3 %collective-permute-start.2 = (bf16[128,640]{1,0:T(8,128)(2,1)S(1)}, bf16[128,640]{1,0:T(8,128)(2,1)S(1)}, u32[]{:S(2)}, u32[]{:S(2)}) collective-permute-start(bf16[128,640]{1,0:T(8,128)(2,1)S(1)} %maximum_select_fusion.15), channel_id=1, source_target_pairs={{0,8},{1,9},{2,10},{3,11},{4,12},{5,13},{6,14},{7,15},{8,0},{9,1},... | collective-permute-start | bytes 491528 | tf_op jit(solution)/shard_map/ppermute | solution.py:238
  11.1 9.6 %collective-permute-start.3 = (bf16[128,640]{1,0:T(8,128)(2,1)S(1)}, bf16[128,640]{1,0:T(8,128)(2,1)S(1)}, u32[]{:S(2)}, u32[]{:S(2)}) collective-permute-start(bf16[128,640]{1,0:T(8,128)(2,1)S(1)} %maximum_select_fusion.15), channel_id=1, source_target_pairs={{0,12},{1,13},{2,14},{3,15},{4,0},{5,1},{6,2},{7,3},{8,4},{9,5},{1... | collective-permute-start | bytes 491528 | tf_op jit(solution)/shard_map/ppermute | solution.py:238
  12.4 10.0 %collective-permute-start.1 = (bf16[128,640]{1,0:T(8,128)(2,1)S(1)}, bf16[128,640]{1,0:T(8,128)(2,1)S(1)}, u32[]{:S(2)}, u32[]{:S(2)}) collective-permute-start(bf16[128,640]{1,0:T(8,128)(2,1)S(1)} %maximum_select_fusion.15), channel_id=1, source_target_pairs={{0,4},{1,5},{2,6},{3,7},{4,8},{5,9},{6,10},{7,11},{8,12},{9,13},{1... | collective-permute-start | bytes 491528 | tf_op jit(solution)/shard_map/ppermute | solution.py:238
  23.3 14.9 %collective-permute-start.8 = (bf16[360,256]{1,0:T(8,128)(2,1)S(1)}, bf16[360,256]{1,0:T(8,128)(2,1)S(1)}, u32[]{:S(2)}, u32[]{:S(2)}) collective-permute-start(bf16[360,256]{1,0:T(8,128)(2,1)S(1)} %get-tuple-element.31), channel_id=1, source_target_pairs={{0,8},{1,9},{2,10},{3,11},{4,12},{5,13},{6,14},{7,15},{8,0},{9,1},... | collective-permute-start | bytes 552968 | tf_op jit(solution)/shard_map/ppermute | solution.py:238
  28.2 13.9 %collective-permute-start.9 = (bf16[360,256]{1,0:T(8,128)(2,1)S(1)}, bf16[360,256]{1,0:T(8,128)(2,1)S(1)}, u32[]{:S(2)}, u32[]{:S(2)}) collective-permute-start(bf16[360,256]{1,0:T(8,128)(2,1)S(1)} %get-tuple-element.31), channel_id=1, source_target_pairs={{0,12},{1,13},{2,14},{3,15},{4,0},{5,1},{6,2},{7,3},{8,4},{9,5},{1... | collective-permute-start | bytes 552968 | tf_op jit(solution)/shard_map/ppermute | solution.py:238
  28.6 13.5 %collective-permute-start.7 = (bf16[360,256]{1,0:T(8,128)(2,1)S(1)}, bf16[360,256]{1,0:T(8,128)(2,1)S(1)}, u32[]{:S(2)}, u32[]{:S(2)}) collective-permute-start(bf16[360,256]{1,0:T(8,128)(2,1)S(1)} %get-tuple-element.31), channel_id=1, source_target_pairs={{0,4},{1,5},{2,6},{3,7},{4,8},{5,9},{6,10},{7,11},{8,12},{9,13},{1... | collective-permute-start | bytes 552968 | tf_op jit(solution)/shard_map/ppermute | solution.py:238
  42.1 7.5 %collective-permute-start.13 = (bf16[360,128]{1,0:T(8,128)(2,1)S(1)}, bf16[360,128]{1,0:T(8,128)(2,1)S(1)}, u32[]{:S(2)}, u32[]{:S(2)}) collective-permute-start(bf16[360,128]{1,0:T(8,128)(2,1)S(1)} %slice_select_fusion.2), channel_id=1, source_target_pairs={{0,8},{1,9},{2,10},{3,11},{4,12},{5,13},{6,14},{7,15},{8,0},{9,1},... | collective-permute-start | bytes 276488 | tf_op jit(solution)/shard_map/ppermute | solution.py:238
  44.4 6.1 %collective-permute-start.14 = (bf16[360,128]{1,0:T(8,128)(2,1)S(1)}, bf16[360,128]{1,0:T(8,128)(2,1)S(1)}, u32[]{:S(2)}, u32[]{:S(2)}) collective-permute-start(bf16[360,128]{1,0:T(8,128)(2,1)S(1)} %slice_select_fusion.2), channel_id=1, source_target_pairs={{0,12},{1,13},{2,14},{3,15},{4,0},{5,1},{6,2},{7,3},{8,4},{9,5},{1... | collective-permute-start | bytes 276488 | tf_op jit(solution)/shard_map/ppermute | solution.py:238
  47.8 6.4 %collective-permute-start.12 = (bf16[360,128]{1,0:T(8,128)(2,1)S(1)}, bf16[360,128]{1,0:T(8,128)(2,1)S(1)}, u32[]{:S(2)}, u32[]{:S(2)}) collective-permute-start(bf16[360,128]{1,0:T(8,128)(2,1)S(1)} %slice_select_fusion.2), channel_id=1, source_target_pairs={{0,4},{1,5},{2,6},{3,7},{4,8},{5,9},{6,10},{7,11},{8,12},{9,13},{1... | collective-permute-start | bytes 276488 | tf_op jit(solution)/shard_map/ppermute | solution.py:238
  48.0 17.7 %collective-permute-start.4 = (bf16[4,128,640]{2,1,0:T(8,128)(2,1)S(1)}, bf16[4,128,640]{2,1,0:T(8,128)(2,1)S(1)}, u32[]{:S(2)}, u32[]{:S(2)}) collective-permute-start(bf16[4,128,640]{2,1,0:T(8,128)(2,1)S(1)} %get-tuple-element.109), channel_id=1, source_target_pairs={{0,2},{1,3},{2,0},{3,1},{4,6},{5,7},{6,4},{7,5},{8,10},{9,11},{10,... | collective-permute-start | bytes 1966088 | tf_op jit(solution)/shard_map/ppermute | solution.py:238
  55.1 18.6 %collective-permute-start.15 = (bf16[4,360,128]{2,1,0:T(8,128)(2,1)S(1)}, bf16[4,360,128]{2,1,0:T(8,128)(2,1)}, u32[]{:S(2)}, u32[]{:S(2)}) collective-permute-start(bf16[4,360,128]{2,1,0:T(8,128)(2,1)S(1)} %get-tuple-element.119), channel_id=1, source_target_pairs={{0,2},{1,3},{2,0},{3,1},{4,6},{5,7},{6,4},{7,5},{8,10},{9,11},{10,... | collective-permute-start | bytes 1105928 | tf_op jit(solution)/shard_map/ppermute | solution.py:238
  57.8 31.6 %collective-permute-start.10 = (bf16[4,360,256]{2,1,0:T(8,128)(2,1)}, bf16[4,360,256]{2,1,0:T(8,128)(2,1)S(1)}, u32[]{:S(2)}, u32[]{:S(2)}) collective-permute-start(bf16[4,360,256]{2,1,0:T(8,128)(2,1)} %get-tuple-element.99), channel_id=1, source_target_pairs={{0,2},{1,3},{2,0},{3,1},{4,6},{5,7},{6,4},{7,5},{8,10},{9,11},{10,... | collective-permute-start | bytes 2211848 | tf_op jit(solution)/shard_map/ppermute | solution.py:238
  58.3 16.9 %collective-permute-start.19 = (bf16[360,256]{1,0:T(8,128)(2,1)}, bf16[360,256]{1,0:T(8,128)(2,1)}, u32[]{:S(2)}, u32[]{:S(2)}) collective-permute-start(bf16[360,256]{1,0:T(8,128)(2,1)} %get-tuple-element.34), channel_id=1, source_target_pairs={{0,8},{1,9},{2,10},{3,11},{4,12},{5,13},{6,14},{7,15},{8,0},{9,1},... | collective-permute-start | bytes 552968 | tf_op jit(solution)/shard_map/ppermute | solution.py:238
  59.6 16.1 %collective-permute-start.20 = (bf16[360,256]{1,0:T(8,128)(2,1)}, bf16[360,256]{1,0:T(8,128)(2,1)}, u32[]{:S(2)}, u32[]{:S(2)}) collective-permute-start(bf16[360,256]{1,0:T(8,128)(2,1)} %get-tuple-element.34), channel_id=1, source_target_pairs={{0,12},{1,13},{2,14},{3,15},{4,0},{5,1},{6,2},{7,3},{8,4},{9,5},{1... | collective-permute-start | bytes 552968 | tf_op jit(solution)/shard_map/ppermute | solution.py:238
  65.7 1.4 copy-start.16
  65.7 10.1 %collective-permute-start.18 = (bf16[360,256]{1,0:T(8,128)(2,1)}, bf16[360,256]{1,0:T(8,128)(2,1)}, u32[]{:S(2)}, u32[]{:S(2)}) collective-permute-start(bf16[360,256]{1,0:T(8,128)(2,1)} %get-tuple-element.34), channel_id=1, source_target_pairs={{0,4},{1,5},{2,6},{3,7},{4,8},{5,9},{6,10},{7,11},{8,12},{9,13},{1... | collective-permute-start | bytes 552968 | tf_op jit(solution)/shard_map/ppermute | solution.py:238
  73.7 17.9 %collective-permute-start.5 = (bf16[4,2,128,640]{3,2,1,0:T(8,128)(2,1)}, bf16[4,2,128,640]{3,2,1,0:T(8,128)(2,1)}, u32[]{:S(2)}, u32[]{:S(2)}) collective-permute-start(bf16[4,2,128,640]{3,2,1,0:T(8,128)(2,1)} %maximum_select_fusion.7), channel_id=1, source_target_pairs={{0,1},{1,0},{2,3},{3,2},{4,5},{5,4},{6,7},{7,6},{8,9},{9,8},{10,11... | collective-permute-start | bytes 3932168 | tf_op jit(solution)/shard_map/ppermute | solution.py:238
  75.2 16.0 %collective-permute-start.16 = (bf16[4,2,360,128]{3,2,0,1:T(8,128)(2,1)S(1)}, bf16[4,2,360,128]{3,2,0,1:T(8,128)(2,1)S(1)}, u32[]{:S(2)}, u32[]{:S(2)}) collective-permute-start(bf16[4,2,360,128]{3,2,0,1:T(8,128)(2,1)S(1)} %maximum_select_fusion.13), channel_id=1, source_target_pairs={{0,1},{1,0},{2,3},{3,2},{4,5},{5,4},{6,7},{7,6},{8,9},{9,8},{10,11... | collective-permute-start | bytes 2211848 | tf_op jit(solution)/shard_map/ppermute | solution.py:238
  77.0 2.6 %copy-start.17 = (bf16[4,128,640]{2,1,0:T(8,128)(2,1)S(1)}, bf16[4,128,640]{2,1,0:T(8,128)(2,1)}, u32[]{:S(2)}) copy-start(bf16[4,128,640]{2,1,0:T(8,128)(2,1)} %copy-done.16) | copy-start | bytes 1966084
  78.1 26.2 %collective-permute-start.21 = (bf16[4,360,256]{2,1,0:T(8,128)(2,1)S(1)}, bf16[4,360,256]{2,1,0:T(8,128)(2,1)S(1)}, u32[]{:S(2)}, u32[]{:S(2)}) collective-permute-start(bf16[4,360,256]{2,1,0:T(8,128)(2,1)S(1)} %get-tuple-element.90), channel_id=1, source_target_pairs={{0,2},{1,3},{2,0},{3,1},{4,6},{5,7},{6,4},{7,5},{8,10},{9,11},{10,... | collective-permute-start | bytes 2211848 | tf_op jit(solution)/shard_map/ppermute | solution.py:238
  89.6 5.9 %collective-permute-start.11 = (bf16[4,2,360,256]{3,2,0,1:T(8,128)(2,1)S(1)}, bf16[4,2,360,256]{3,2,0,1:T(8,128)(2,1)S(1)}, u32[]{:S(2)}, u32[]{:S(2)}) collective-permute-start(bf16[4,2,360,256]{3,2,0,1:T(8,128)(2,1)S(1)} %maximum_select_fusion.3), channel_id=1, source_target_pairs={{0,1},{1,0},{2,3},{3,2},{4,5},{5,4},{6,7},{7,6},{8,9},{9,8},{10,11... | collective-permute-start | bytes 4423688 | tf_op jit(solution)/shard_map/ppermute | solution.py:238
  104.2 1.6 copy-start.6
  104.2 1.6 copy-start.8
  104.3 1.8 copy-start.14
  106.0 5.0 %collective-permute-start.22 = (bf16[4,2,360,256]{3,2,0,1:T(8,128)(2,1)}, bf16[4,2,360,256]{3,2,0,1:T(8,128)(2,1)}, u32[]{:S(2)}, u32[]{:S(2)}) collective-permute-start(bf16[4,2,360,256]{3,2,0,1:T(8,128)(2,1)} %maximum_select_fusion.6), channel_id=1, source_target_pairs={{0,1},{1,0},{2,3},{3,2},{4,5},{5,4},{6,7},{7,6},{8,9},{9,8},{10,11... | collective-permute-start | bytes 4423688 | tf_op jit(solution)/shard_map/ppermute | solution.py:238
  106.5 16.1 %collective-permute-start.17 = (bf16[480,640]{1,0:T(8,128)(2,1)}, bf16[480,640]{1,0:T(8,128)(2,1)}, u32[]{:S(2)}, u32[]{:S(2)}) collective-permute-start(bf16[480,640]{1,0:T(8,128)(2,1)} %get-tuple-element.33.own_ref), channel_id=1, source_target_pairs={{0,16},{16,0},{1,17},{17,1},{2,18},{18,2},{3,19},{19,3},{4,20},{20... | collective-permute-start | bytes 1843208 | tf_op jit(solution)/shard_map/ppermute | solution.py:242
  109.2 1.5 copy-start.13
  109.3 1.5 copy-start.15
  113.5 9.1 %copy-start.5 = (bf16[5,3,32,640]{3,2,1,0:T(8,128)(2,1)S(1)}, bf16[5,3,32,640]{3,2,1,0:T(8,128)(2,1)}, u32[]{:S(2)}) copy-start(bf16[5,3,32,640]{3,2,1,0:T(8,128)(2,1)} %param.7) | copy-start | bytes 1843204
  133.2 4.4 %copy-start.10 = (bf16[480,640]{1,0:T(8,128)(2,1)}, bf16[480,640]{1,0:T(8,128)(2,1)S(1)}, u32[]{:S(2)}) copy-start(bf16[480,640]{1,0:T(8,128)(2,1)S(1)} %get-tuple-element.36.hidden_ref) | copy-start | bytes 1843204
  140.6 3.6 %collective-permute-start.24 = (bf16[4,2,360,256]{3,2,0,1:T(8,128)(2,1)}, bf16[4,2,360,256]{3,2,0,1:T(8,128)(2,1)}, u32[]{:S(2)}, u32[]{:S(2)}) collective-permute-start(bf16[4,2,360,256]{3,2,0,1:T(8,128)(2,1)} %bitcast.276), channel_id=1, source_target_pairs={{0,1},{1,0},{2,3},{3,2},{4,5},{5,4},{6,7},{7,6},{8,9},{9,8},{10,11... | collective-permute-start | bytes 4423688 | tf_op jit(solution)/shard_map/ppermute | solution.py:238
  140.6 16.6 %collective-permute-start.23 = (bf16[480,640]{1,0:T(8,128)(2,1)}, bf16[480,640]{1,0:T(8,128)(2,1)}, u32[]{:S(2)}, u32[]{:S(2)}) collective-permute-start(bf16[480,640]{1,0:T(8,128)(2,1)} %get-tuple-element.37.own_ref), channel_id=1, source_target_pairs={{0,16},{16,0},{1,17},{17,1},{2,18},{18,2},{3,19},{19,3},{4,20},{20... | collective-permute-start | bytes 1843208 | tf_op jit(solution)/shard_map/ppermute | solution.py:242
  142.1 2.1 copy-start.12
  144.2 14.6 %copy-start.7 = (f32[480,384]{1,0:T(8,128)S(1)}, f32[480,384]{1,0:T(8,128)}, u32[]{:S(2)}) copy-start(f32[480,384]{1,0:T(8,128)} %copy-done.6) | copy-start | bytes 2211844
  144.2 14.6 %copy-start.9 = (bf16[480,640]{1,0:T(8,128)(2,1)S(1)}, bf16[480,640]{1,0:T(8,128)(2,1)}, u32[]{:S(2)}) copy-start(bf16[480,640]{1,0:T(8,128)(2,1)} %copy-done.8) | copy-start | bytes 1843204
  144.2 14.6 %copy-start.11 = (bf16[480,640]{1,0:T(8,128)(2,1)S(1)}, bf16[480,640]{1,0:T(8,128)(2,1)}, u32[]{:S(2)}) copy-start(bf16[480,640]{1,0:T(8,128)(2,1)} %copy-done.10) | copy-start | bytes 1843204
  146.2 12.6 %copy-start.3 = (bf16[8,120,640]{2,1,0:T(8,128)(2,1)S(1)}, bf16[8,120,640]{2,1,0:T(8,128)(2,1)}, u32[]{:S(2)}) copy-start(bf16[8,120,640]{2,1,0:T(8,128)(2,1)} %copy-done.2) | copy-start | bytes 3686404
  157.2 18.2 %collective-permute-start.25 = (bf16[4,360,256]{2,1,0:T(8,128)(2,1)S(1)}, bf16[4,360,256]{2,1,0:T(8,128)(2,1)S(1)}, u32[]{:S(2)}, u32[]{:S(2)}) collective-permute-start(bf16[4,360,256]{2,1,0:T(8,128)(2,1)S(1)} %dynamic-slice_bitcast_fusion), channel_id=1, source_target_pairs={{0,2},{1,3},{2,0},{3,1},{4,6},{5,7},{6,4},{7,5},{8,10},{9,11},{10,... | collective-permute-start | bytes 2211848 | tf_op jit(solution)/shard_map/ppermute | solution.py:238
  175.7 8.5 %collective-permute-start.26 = (bf16[4,2,360,256]{3,2,0,1:T(8,128)(2,1)S(1)}, bf16[4,2,360,256]{3,2,0,1:T(8,128)(2,1)S(1)}, u32[]{:S(2)}, u32[]{:S(2)}) collective-permute-start(bf16[4,2,360,256]{3,2,0,1:T(8,128)(2,1)S(1)} %bitcast.312), channel_id=1, source_target_pairs={{0,1},{1,0},{2,3},{3,2},{4,5},{5,4},{6,7},{7,6},{8,9},{9,8},{10,11... | collective-permute-start | bytes 4423688 | tf_op jit(solution)/shard_map/ppermute | solution.py:238
  177.4 6.0 %collective-permute-start.27 = (bf16[4,2,360,128]{3,2,0,1:T(8,128)(2,1)S(1)}, bf16[4,2,360,128]{3,2,0,1:T(8,128)(2,1)S(1)}, u32[]{:S(2)}, u32[]{:S(2)}) collective-permute-start(bf16[4,2,360,128]{3,2,0,1:T(8,128)(2,1)S(1)} %bitcast.315), channel_id=1, source_target_pairs={{0,1},{1,0},{2,3},{3,2},{4,5},{5,4},{6,7},{7,6},{8,9},{9,8},{10,11... | collective-permute-start | bytes 2211848 | tf_op jit(solution)/shard_map/ppermute | solution.py:238
  178.1 18.0 %collective-permute-start.40 = (bf16[4,2,128,640]{3,2,1,0:T(8,128)(2,1)S(1)}, bf16[4,2,128,640]{3,2,1,0:T(8,128)(2,1)S(1)}, u32[]{:S(2)}, u32[]{:S(2)}) collective-permute-start(bf16[4,2,128,640]{3,2,1,0:T(8,128)(2,1)S(1)} %fusion.9), channel_id=1, source_target_pairs={{0,1},{1,0},{2,3},{3,2},{4,5},{5,4},{6,7},{7,6},{8,9},{9,8},{10,11... | collective-permute-start | bytes 3932168 | tf_op jit(solution)/shard_map/ppermute | solution.py:238
  178.9 26.8 %collective-permute-start.31 = (bf16[360,256]{1,0:T(8,128)(2,1)S(1)}, bf16[360,256]{1,0:T(8,128)(2,1)S(1)}, u32[]{:S(2)}, u32[]{:S(2)}) collective-permute-start(bf16[360,256]{1,0:T(8,128)(2,1)S(1)} %get-tuple-element.87), channel_id=1, source_target_pairs={{0,4},{1,5},{2,6},{3,7},{4,8},{5,9},{6,10},{7,11},{8,12},{9,13},{1... | collective-permute-start | bytes 552968 | tf_op jit(solution)/shard_map/ppermute | solution.py:238
  179.0 26.8 %collective-permute-start.32 = (bf16[360,256]{1,0:T(8,128)(2,1)S(1)}, bf16[360,256]{1,0:T(8,128)(2,1)S(1)}, u32[]{:S(2)}, u32[]{:S(2)}) collective-permute-start(bf16[360,256]{1,0:T(8,128)(2,1)S(1)} %get-tuple-element.86), channel_id=1, source_target_pairs={{0,8},{1,9},{2,10},{3,11},{4,12},{5,13},{6,14},{7,15},{8,0},{9,1},... | collective-permute-start | bytes 552968 | tf_op jit(solution)/shard_map/ppermute | solution.py:238
  183.4 22.4 %collective-permute-start.33 = (bf16[360,256]{1,0:T(8,128)(2,1)S(1)}, bf16[360,256]{1,0:T(8,128)(2,1)S(1)}, u32[]{:S(2)}, u32[]{:S(2)}) collective-permute-start(bf16[360,256]{1,0:T(8,128)(2,1)S(1)} %get-tuple-element.85), channel_id=1, source_target_pairs={{0,12},{1,13},{2,14},{3,15},{4,0},{5,1},{6,2},{7,3},{8,4},{9,5},{1... | collective-permute-start | bytes 552968 | tf_op jit(solution)/shard_map/ppermute | solution.py:238
  184.2 10.4 %collective-permute-start.28 = (bf16[4,360,128]{2,1,0:T(8,128)(2,1)S(1)}, bf16[4,360,128]{2,1,0:T(8,128)(2,1)S(1)}, u32[]{:S(2)}, u32[]{:S(2)}) collective-permute-start(bf16[4,360,128]{2,1,0:T(8,128)(2,1)S(1)} %dynamic-slice_bitcast_fusion.3), channel_id=1, source_target_pairs={{0,2},{1,3},{2,0},{3,1},{4,6},{5,7},{6,4},{7,5},{8,10},{9,11},{10,... | collective-permute-start | bytes 1105928 | tf_op jit(solution)/shard_map/ppermute | solution.py:238
  194.6 9.5 %collective-permute-start.29 = (bf16[4,360,128]{2,1,0:T(8,128)(2,1)S(1)}, bf16[4,360,128]{2,1,0:T(8,128)(2,1)S(1)}, u32[]{:S(2)}, u32[]{:S(2)}) collective-permute-start(bf16[4,360,128]{2,1,0:T(8,128)(2,1)S(1)} %dynamic-slice_bitcast_fusion.4), channel_id=1, source_target_pairs={{0,2},{1,3},{2,0},{3,1},{4,6},{5,7},{6,4},{7,5},{8,10},{9,11},{10,... | collective-permute-start | bytes 1105928 | tf_op jit(solution)/shard_map/ppermute | solution.py:238
  204.1 8.8 %collective-permute-start.30 = (bf16[4,360,128]{2,1,0:T(8,128)(2,1)S(1)}, bf16[4,360,128]{2,1,0:T(8,128)(2,1)S(1)}, u32[]{:S(2)}, u32[]{:S(2)}) collective-permute-start(bf16[4,360,128]{2,1,0:T(8,128)(2,1)S(1)} %dynamic-slice_bitcast_fusion.2), channel_id=1, source_target_pairs={{0,2},{1,3},{2,0},{3,1},{4,6},{5,7},{6,4},{7,5},{8,10},{9,11},{10,... | collective-permute-start | bytes 1105928 | tf_op jit(solution)/shard_map/ppermute | solution.py:238
  205.8 8.6 %collective-permute-start.36 = (bf16[360,128]{1,0:T(8,128)(2,1)S(1)}, bf16[360,128]{1,0:T(8,128)(2,1)S(1)}, u32[]{:S(2)}, u32[]{:S(2)}) collective-permute-start(bf16[360,128]{1,0:T(8,128)(2,1)S(1)} %get-tuple-element.115), channel_id=1, source_target_pairs={{0,12},{1,13},{2,14},{3,15},{4,0},{5,1},{6,2},{7,3},{8,4},{9,5},{1... | collective-permute-start | bytes 276488 | tf_op jit(solution)/shard_map/ppermute | solution.py:238
  205.9 8.5 %collective-permute-start.35 = (bf16[360,128]{1,0:T(8,128)(2,1)S(1)}, bf16[360,128]{1,0:T(8,128)(2,1)S(1)}, u32[]{:S(2)}, u32[]{:S(2)}) collective-permute-start(bf16[360,128]{1,0:T(8,128)(2,1)S(1)} %get-tuple-element.116), channel_id=1, source_target_pairs={{0,8},{1,9},{2,10},{3,11},{4,12},{5,13},{6,14},{7,15},{8,0},{9,1},... | collective-permute-start | bytes 276488 | tf_op jit(solution)/shard_map/ppermute | solution.py:238
  207.4 7.0 %collective-permute-start.34 = (bf16[360,128]{1,0:T(8,128)(2,1)S(1)}, bf16[360,128]{1,0:T(8,128)(2,1)S(1)}, u32[]{:S(2)}, u32[]{:S(2)}) collective-permute-start(bf16[360,128]{1,0:T(8,128)(2,1)S(1)} %get-tuple-element.114), channel_id=1, source_target_pairs={{0,4},{1,5},{2,6},{3,7},{4,8},{5,9},{6,10},{7,11},{8,12},{9,13},{1... | collective-permute-start | bytes 276488 | tf_op jit(solution)/shard_map/ppermute | solution.py:238
  212.9 13.9 %collective-permute-start.41 = (bf16[4,128,640]{2,1,0:T(8,128)(2,1)S(1)}, bf16[4,128,640]{2,1,0:T(8,128)(2,1)S(1)}, u32[]{:S(2)}, u32[]{:S(2)}) collective-permute-start(bf16[4,128,640]{2,1,0:T(8,128)(2,1)S(1)} %dynamic-slice_bitcast_fusion.1), channel_id=1, source_target_pairs={{0,2},{1,3},{2,0},{3,1},{4,6},{5,7},{6,4},{7,5},{8,10},{9,11},{10,... | collective-permute-start | bytes 1966088 | tf_op jit(solution)/shard_map/ppermute | solution.py:238
  214.7 12.2 %collective-permute-start.39 = (bf16[360,256]{1,0:T(8,128)(2,1)S(1)}, bf16[360,256]{1,0:T(8,128)(2,1)S(1)}, u32[]{:S(2)}, u32[]{:S(2)}) collective-permute-start(bf16[360,256]{1,0:T(8,128)(2,1)S(1)} %get-tuple-element.83), channel_id=1, source_target_pairs={{0,12},{1,13},{2,14},{3,15},{4,0},{5,1},{6,2},{7,3},{8,4},{9,5},{1... | collective-permute-start | bytes 552968 | tf_op jit(solution)/shard_map/ppermute | solution.py:238
  216.1 14.9 %collective-permute-start.38 = (bf16[360,256]{1,0:T(8,128)(2,1)S(1)}, bf16[360,256]{1,0:T(8,128)(2,1)S(1)}, u32[]{:S(2)}, u32[]{:S(2)}) collective-permute-start(bf16[360,256]{1,0:T(8,128)(2,1)S(1)} %get-tuple-element.84), channel_id=1, source_target_pairs={{0,8},{1,9},{2,10},{3,11},{4,12},{5,13},{6,14},{7,15},{8,0},{9,1},... | collective-permute-start | bytes 552968 | tf_op jit(solution)/shard_map/ppermute | solution.py:238
  216.3 14.7 %collective-permute-start.37 = (bf16[360,256]{1,0:T(8,128)(2,1)S(1)}, bf16[360,256]{1,0:T(8,128)(2,1)S(1)}, u32[]{:S(2)}, u32[]{:S(2)}) collective-permute-start(bf16[360,256]{1,0:T(8,128)(2,1)S(1)} %get-tuple-element.82), channel_id=1, source_target_pairs={{0,4},{1,5},{2,6},{3,7},{4,8},{5,9},{6,10},{7,11},{8,12},{9,13},{1... | collective-permute-start | bytes 552968 | tf_op jit(solution)/shard_map/ppermute | solution.py:238
  231.1 6.0 %collective-permute-start.45 = (bf16[128,640]{1,0:T(8,128)(2,1)S(1)}, bf16[128,640]{1,0:T(8,128)(2,1)S(1)}, u32[]{:S(2)}, u32[]{:S(2)}) collective-permute-start(bf16[128,640]{1,0:T(8,128)(2,1)S(1)} %get-tuple-element.105), channel_id=1, source_target_pairs={{0,12},{1,13},{2,14},{3,15},{4,0},{5,1},{6,2},{7,3},{8,4},{9,5},{1... | collective-permute-start | bytes 491528 | tf_op jit(solution)/shard_map/ppermute | solution.py:238
  231.1 17.0 %collective-permute-start.44 = (bf16[128,640]{1,0:T(8,128)(2,1)S(1)}, bf16[128,640]{1,0:T(8,128)(2,1)S(1)}, u32[]{:S(2)}, u32[]{:S(2)}) collective-permute-start(bf16[128,640]{1,0:T(8,128)(2,1)S(1)} %get-tuple-element.106), channel_id=1, source_target_pairs={{0,8},{1,9},{2,10},{3,11},{4,12},{5,13},{6,14},{7,15},{8,0},{9,1},... | collective-permute-start | bytes 491528 | tf_op jit(solution)/shard_map/ppermute | solution.py:238
  233.3 14.8 %collective-permute-start.43 = (bf16[128,640]{1,0:T(8,128)(2,1)S(1)}, bf16[128,640]{1,0:T(8,128)(2,1)S(1)}, u32[]{:S(2)}, u32[]{:S(2)}) collective-permute-start(bf16[128,640]{1,0:T(8,128)(2,1)S(1)} %get-tuple-element.104), channel_id=1, source_target_pairs={{0,4},{1,5},{2,6},{3,7},{4,8},{5,9},{6,10},{7,11},{8,12},{9,13},{1... | collective-permute-start | bytes 491528 | tf_op jit(solution)/shard_map/ppermute | solution.py:238
  235.5 18.2 %collective-permute-start.42 = (bf16[360,384]{1,0:T(8,128)(2,1)S(1)}, bf16[360,384]{1,0:T(8,128)(2,1)S(1)}, u32[]{:S(2)}, u32[]{:S(2)}) collective-permute-start(bf16[360,384]{1,0:T(8,128)(2,1)S(1)} %pad_maximum_fusion.5), channel_id=1, source_target_pairs={{0,16},{16,0},{1,17},{17,1},{2,18},{18,2},{3,19},{19,3},{4,20},{20... | collective-permute-start | bytes 829448 | tf_op jit(solution)/shard_map/ppermute | solution.py:242
  248.2 4.5 %collective-permute-start.46 = (bf16[64,640]{1,0:T(8,128)(2,1)S(1)}, bf16[64,640]{1,0:T(8,128)(2,1)S(1)}, u32[]{:S(2)}, u32[]{:S(2)}) collective-permute-start(bf16[64,640]{1,0:T(8,128)(2,1)S(1)} %select_convert_fusion.1), channel_id=1, source_target_pairs={{0,16},{16,0},{1,17},{17,1},{2,18},{18,2},{3,19},{19,3},{4,20},{20... | collective-permute-start | bytes 245768 | tf_op jit(solution)/shard_map/ppermute | solution.py:242
  253.7 2.2 copy-start.1
  (3 other events, 2.8 us)
where the time goes:
time: 260 us; the launch traced here: 256 us
  waiting for transfers between devices  127 us (49%)
  starting transfers between devices  58.3 us (22%)
  Pallas kernels  29.6 us (11%)
  other arithmetic  25.8 us (10%)
  local copies, waits for them, and re-layouts  11.1 us (4%)
  matrix products  2.84 us (1%)
    ppermute x41, waiting for transfers between devices, shifted(): return lax.ppermute(value, 'dp', pairs)  102 us
    ppermute x41, starting transfers between devices, shifted(): return lax.ppermute(value, 'dp', pairs)  49 us
    ppermute x6, waiting for transfers between devices, swapped(): return lax.ppermute(value, 'pipe', [(0, 1), (1, 0)])  24.4 us
    select_n x13, other arithmetic, in_order(): jnp.where(swap, jnp.concatenate([other, own], axis), jnp.concatenate([own...  11.9 us
    pallas_call x1, Pallas kernels, paired_device(): vmem_call(functools.partial(second_forward, frames), (shape((rows, channe...  10.6 us
    ppermute x6, starting transfers between devices, swapped(): return lax.ppermute(value, 'pipe', [(0, 1), (1, 0)])  9.34 us
    pallas_call x1, Pallas kernels, paired_device(): vmem_call(functools.partial(first_terms, frames), terms_shape(), flops=sp...  7.63 us
    pallas_call x1, Pallas kernels, paired_device(): vmem_call(functools.partial(first_forward, frames), (shape((rows, channel...  7.05 us
  transfers between devices with their start and end apart: 47, of which 21 were waited for; matrix products, arithmetic and copies ran while one was open for 11% of the time, Pallas kernels for 6%

commit v1 on v0

--- a/solution.py
+++ b/solution.py
@@ -280,8 +280,8 @@
     return [shifted(value, dz=step) for step in range(1, GRID[0])]
 
 
-def sent_on_chip(value):
-    return shifted(value, dc=1)
+def sent_on_chip(value, pieces=1):
+    return jnp.concatenate([shifted(piece, dc=1) for piece in jnp.split(value, pieces)])
 
 
 def places_of(channels, main):
@@ -368,7 +368,8 @@
 
 def gathered_over_y(line):
     _, y, _ = coordinates()
-    return in_order(y == 1, line[:, None], shifted(line, dy=1)[:, None], 1)
+    sent = shifted(line, dy=1)
+    return in_order(y == 1, line[:, None], sent[:, None], 1), sent
 
 
 def gathered_on_chip(plane, earlier=None):
@@ -382,9 +383,9 @@
     return sum(term.astype(F32) for term in terms)
 
 
-def summed_on_chip(value):
+def summed_on_chip(value, pieces=1):
     _, _, c = coordinates()
-    sent = sent_on_chip(part_of(value, 1 - c, 2))
+    sent = sent_on_chip(part_of(value, 1 - c, 2), pieces)
     return added(part_of(value, c, 2), sent).astype(BF16)
 
 
@@ -450,22 +451,31 @@
     return logistic, preact * logistic
 
 
-def tap_weight(weight_refs, tap, channels):
-    return jnp.concatenate(
-        [ref[tap * channels : (tap + 1) * channels, :] for ref in weight_refs], 1
-    )
-
-
 def convolved(normed, weight_refs, masks):
     rows, channels = normed.shape
     normed = normed.astype(F32)
+    totals = [None] * len(weight_refs)
+    for tap in range(9):
+        moved = moved_rows(normed, masks[tap]).astype(BF16)
+        for index, ref in enumerate(weight_refs):
+            term = dot(moved, ref[tap * channels : (tap + 1) * channels, :])
+            totals[index] = term if totals[index] is None else totals[index] + term
+    return jnp.concatenate(totals, 1)
+
+
+def back_through(pre_grad, weight_refs, masks, channels):
+    pre_grad = pre_grad.astype(F32)
     total = None
     for tap in range(9):
-        term = dot(
-            moved_rows(normed, masks[tap]).astype(BF16),
-            tap_weight(weight_refs, tap, channels),
-        )
-        total = term if total is None else total + term
+        moved = moved_rows(pre_grad, masks[8 - tap]).astype(BF16)
+        start = 0
+        for ref in weight_refs:
+            end = start + ref.shape[1]
+            term = dot(
+                moved[:, start:end], ref[tap * channels : (tap + 1) * channels, :], ((1,), (1,))
+            )
+            total = term if total is None else total + term
+            start = end
     return total
 
 
@@ -562,15 +572,7 @@
     act_grad = act_grad_of(upstream_ref[...], temporal_ref, width, frames)
     pre_grad = (act_grad * slope_of(preact) * keep_ref[...]).astype(BF16)
     pre_grad_ref[...] = pre_grad
-    pre_grad = pre_grad.astype(F32)
-    back = None
-    for tap in range(9):
-        term = dot(
-            moved_rows(pre_grad, masks[8 - tap]).astype(BF16),
-            tap_weight(spatial_refs, tap, channels),
-            ((1,), (1,)),
-        )
-        back = term if back is None else back + term
+    back = back_through(pre_grad, spatial_refs, masks, channels)
     back_ref[...] = back.astype(BF16)
 
 
@@ -624,16 +626,16 @@
     temporal_own, temporal_sent = sets_of(temporal_weight[0])
     temporal_given = swapped(temporal_sent)
     line, sent = gathered_over_z(in_order(me == 1, temporal_own, temporal_given, 0))
-    plane_temporal = gathered_over_y(line)
+    plane_temporal, side = gathered_over_y(line)
     spatial_own = dot(spatial_weight[0], order).astype(BF16)
     given = swapped(spatial_own[:, main:])
     main_own, main_given = spatial_own[:, :main], given[:, :main]
     tails = jnp.where(tail, spatial_own[:, 2 * main :], given[:, main:])
     line, sent = gathered_over_z(jnp.where(first, main_own, main_given), sent)
-    plane_first = gathered_over_y(line)
-    line, sent = gathered_over_z(tails, sent)
-    plane_tails = gathered_over_y(line)
-    line_second, _ = gathered_over_z(jnp.where(first, main_given, main_own), sent)
+    line_tails, sent = gathered_over_z(tails, (sent, side))
+    plane_first, side = gathered_over_y(line)
+    plane_tails, _ = gathered_over_y(line_tails)
+    line_second, _ = gathered_over_z(jnp.where(first, main_given, main_own), (sent, side))
     side_second = shifted(line_second, dy=1)
 
     chips = GRID[0] * GRID[1]
@@ -683,8 +685,8 @@
             shape((3 * (width - PIECE), channels)),
         )
 
-    def on_chip(terms):
-        return summed_on_chip(terms.reshape(*GRID, -1, terms.shape[1]))
+    def on_chip(terms, pieces=1):
+        return summed_on_chip(terms.reshape(*GRID, -1, terms.shape[1]), pieces)
 
     back_given = swapped(back)
     main_terms_second, tail_terms_second, temporal_terms_second = vmem_call(
@@ -693,7 +695,7 @@
         flops=spatial_flops + temporal_flops,
         moved=spatial_bytes + temporal_bytes,
     )(normed_second, pre_grad_second, activated_second, upstream)
-    chip_second = on_chip(main_terms_second)
+    chip_second = on_chip(main_terms_second, GRID[0])
     back_given = after(back_given, chip_second)
     line, side = summed_over_y(chip_second, None)
     share_second, sent_second = summed_over_z(line)
@@ -706,7 +708,7 @@
         hidden_second, embedding, upstream, back, back_given, normed_first, preact_first,
         keep_first, temporal_first,
     )
-    chip_tails = on_chip(after(tail_terms_first + tail_terms_second, side))
+    chip_tails = on_chip(tail_terms_first + tail_terms_second)
     chip_first = on_chip(after(main_terms_first, side))
     terms = jnp.concatenate(
         [

time: 260 us -> 244 us (0.938)
  other arithmetic: 25.8 us -> 17.1 us
  starting transfers between devices: 58.3 us -> 52.6 us
  waiting for transfers between devices: 127 us -> 122 us
    ppermute x41 -> x44, starting transfers between devices: 49 us -> 43.1 us  [shifted(): return lax.ppermute(value, 'dp', pairs)]
    select_n x13, other arithmetic: 11.9 us -> 6.6 us  [in_order(): jnp.where(swap, jnp.concatenate([other, own], axis), jnp.concatenate([own...]
    ppermute x41 -> x44, waiting for transfers between devices: 102 us -> 98.4 us  [shifted(): return lax.ppermute(value, 'dp', pairs)]
    dynamic_slice x6 -> x4, local copies, waits for them, and re-layouts: 3.53 us -> 0.55 us  [part_of(): return lax.dynamic_index_in_dim(value, index, axis, keepdims=False)]
  transfers between devices with their start and end apart: 47 -> 50, of which waited for: 21 -> 21; matrix products, arithmetic and copies ran while one was open for 11% -> 10% of each run, Pallas kernels for 6% -> 6%
where the time goes in v1:
time: 244 us; the launch traced here: 240 us
  waiting for transfers between devices  122 us (50%)
  starting transfers between devices  52.6 us (22%)
  Pallas kernels  31.7 us (13%)
  other arithmetic  17.1 us (7%)
  local copies, waits for them, and re-layouts  12.3 us (5%)
  matrix products  2.84 us (1%)
    ppermute x44, waiting for transfers between devices, shifted(): return lax.ppermute(value, 'dp', pairs)  98.4 us
    ppermute x44, starting transfers between devices, shifted(): return lax.ppermute(value, 'dp', pairs)  43.1 us
    ppermute x6, waiting for transfers between devices, swapped(): return lax.ppermute(value, 'pipe', [(0, 1), (1, 0)])  23.2 us
    pallas_call x1, Pallas kernels, paired_device(): vmem_call(functools.partial(second_forward, frames), (shape((rows, channe...  12.9 us
    ppermute x6, starting transfers between devices, swapped(): return lax.ppermute(value, 'pipe', [(0, 1), (1, 0)])  9.41 us
    pallas_call x1, Pallas kernels, paired_device(): vmem_call(functools.partial(first_terms, frames), terms_shape(), flops=sp...  7.77 us
    select_n x13, other arithmetic, in_order(): jnp.where(swap, jnp.concatenate([other, own], axis), jnp.concatenate([own...  6.6 us
    pallas_call x1, Pallas kernels, paired_device(): vmem_call(functools.partial(first_forward, frames), (shape((rows, channel...  6.25 us
  transfers between devices with their start and end apart: 50, of which 21 were waited for; matrix products, arithmetic and copies ran while one was open for 10% of the time, Pallas kernels for 6%

profile of v1, /device:TPU:0, one launch (start us, length us, event | category | flops | bytes accessed | tf_op | source)
XLA Modules:
  0.0 240.2 jit_solution(7723686389846162487)
XLA Ops:
  0.6 0.9 slice_bitcast_fusion.27
  1.5 0.9 slice_bitcast_fusion.22
  2.5 3.0 %collective-permute-start = (bf16[64,640]{1,0:T(8,128)(2,1)S(1)}, bf16[64,640]{1,0:T(8,128)(2,1)S(1)}, u32[]{:S(2)}, u32[]{:S(2)}) collective-permute-start(bf16[64,640]{1,0:T(8,128)(2,1)S(1)} %fusion.42), channel_id=1, source_target_pairs={{0,16},{16,0},{1,17},{17,1},{2,18},{18,2},{3,19},{19,3},{4,20},{20... | collective-permute-start | bytes 245768 | tf_op jit(solution)/shard_map/ppermute | solution.py:242
  5.5 0.7 fusion.14
  6.6 1.7 collective-permute-done
  8.3 2.8 %collective-permute-start.2 = (bf16[128,640]{1,0:T(8,128)(2,1)S(1)}, bf16[128,640]{1,0:T(8,128)(2,1)S(1)}, u32[]{:S(2)}, u32[]{:S(2)}) collective-permute-start(bf16[128,640]{1,0:T(8,128)(2,1)S(1)} %maximum_select_fusion.15), channel_id=1, source_target_pairs={{0,8},{1,9},{2,10},{3,11},{4,12},{5,13},{6,14},{7,15},{8,0},{9,1},... | collective-permute-start | bytes 491528 | tf_op jit(solution)/shard_map/ppermute | solution.py:238
  11.1 1.3 collective-permute-start.3
  12.4 0.7 collective-permute-start.1
  13.3 7.4 %collective-permute-done.2 = bf16[128,640]{1,0:T(8,128)(2,1)S(1)} collective-permute-done((bf16[128,640]{1,0:T(8,128)(2,1)S(1)}, bf16[128,640]{1,0:T(8,128)(2,1)S(1)}, u32[]{:S(2)}, u32[]{:S(2)}) %collective-permute-start.2) | collective-permute-done | bytes 163872 | tf_op jit(solution)/shard_map/ppermute | solution.py:238
  20.7 1.8 collective-permute-done.1
  22.7 1.6 collective-permute-start.4
  24.3 5.0 %collective-permute-start.8 = (bf16[360,256]{1,0:T(8,128)(2,1)S(1)}, bf16[360,256]{1,0:T(8,128)(2,1)S(1)}, u32[]{:S(2)}, u32[]{:S(2)}) collective-permute-start(bf16[360,256]{1,0:T(8,128)(2,1)S(1)} %get-tuple-element.30), channel_id=1, source_target_pairs={{0,8},{1,9},{2,10},{3,11},{4,12},{5,13},{6,14},{7,15},{8,0},{9,1},... | collective-permute-start | bytes 552968 | tf_op jit(solution)/shard_map/ppermute | solution.py:238
  29.8 1.6 collective-permute-start.7
  31.4 8.0 %collective-permute-done.8 = bf16[360,256]{1,0:T(8,128)(2,1)S(1)} collective-permute-done((bf16[360,256]{1,0:T(8,128)(2,1)S(1)}, bf16[360,256]{1,0:T(8,128)(2,1)S(1)}, u32[]{:S(2)}, u32[]{:S(2)}) %collective-permute-start.8) | collective-permute-done | bytes 184352 | tf_op jit(solution)/shard_map/ppermute | solution.py:238
  39.3 3.6 %collective-permute-done.9 = bf16[360,256]{1,0:T(8,128)(2,1)S(1)} collective-permute-done((bf16[360,256]{1,0:T(8,128)(2,1)S(1)}, bf16[360,256]{1,0:T(8,128)(2,1)S(1)}, u32[]{:S(2)}, u32[]{:S(2)}) %collective-permute-start.9) | collective-permute-done | bytes 184352 | tf_op jit(solution)/shard_map/ppermute | solution.py:238
  43.1 2.4 collective-permute-start.13
  45.5 3.4 %collective-permute-start.14 = (bf16[360,128]{1,0:T(8,128)(2,1)S(1)}, bf16[360,128]{1,0:T(8,128)(2,1)S(1)}, u32[]{:S(2)}, u32[]{:S(2)}) collective-permute-start(bf16[360,128]{1,0:T(8,128)(2,1)S(1)} %slice_select_fusion.2), channel_id=1, source_target_pairs={{0,12},{1,13},{2,14},{3,15},{4,0},{5,1},{6,2},{7,3},{8,4},{9,5},{1... | collective-permute-start | bytes 276488 | tf_op jit(solution)/shard_map/ppermute | solution.py:238
  49.6 2.0 collective-permute-done.14
  51.6 3.7 %collective-permute-done.12 = bf16[360,128]{1,0:T(8,128)(2,1)S(1)} collective-permute-done((bf16[360,128]{1,0:T(8,128)(2,1)S(1)}, bf16[360,128]{1,0:T(8,128)(2,1)S(1)}, u32[]{:S(2)}, u32[]{:S(2)}) %collective-permute-start.12) | collective-permute-done | bytes 92192 | tf_op jit(solution)/shard_map/ppermute | solution.py:238
  56.8 11.7 %collective-permute-done.10 = bf16[4,360,256]{2,1,0:T(8,128)(2,1)S(1)} collective-permute-done((bf16[4,360,256]{2,1,0:T(8,128)(2,1)S(1)}, bf16[4,360,256]{2,1,0:T(8,128)(2,1)S(1)}, u32[]{:S(2)}, u32[]{:S(2)}) %collective-permute-start.10) | collective-permute-done | bytes 737312 | tf_op jit(solution)/shard_map/ppermute | solution.py:238
  69.1 3.3 %collective-permute-start.20 = (bf16[360,256]{1,0:T(8,128)(2,1)S(1)}, bf16[360,256]{1,0:T(8,128)(2,1)S(1)}, u32[]{:S(2)}, u32[]{:S(2)}) collective-permute-start(bf16[360,256]{1,0:T(8,128)(2,1)S(1)} %get-tuple-element.33), channel_id=1, source_target_pairs={{0,12},{1,13},{2,14},{3,15},{4,0},{5,1},{6,2},{7,3},{8,4},{9,5},{1... | collective-permute-start | bytes 552968 | tf_op jit(solution)/shard_map/ppermute | solution.py:238
  72.3 0.7 collective-permute-start.18
  73.0 1.6 collective-permute-done.15
  75.5 7.0 %collective-permute-done.19 = bf16[360,256]{1,0:T(8,128)(2,1)S(1)} collective-permute-done((bf16[360,256]{1,0:T(8,128)(2,1)S(1)}, bf16[360,256]{1,0:T(8,128)(2,1)S(1)}, u32[]{:S(2)}, u32[]{:S(2)}) %collective-permute-start.19) | collective-permute-done | bytes 184352 | tf_op jit(solution)/shard_map/ppermute | solution.py:238
  82.6 1.0 fusion.82
  85.3 1.3 slice_bitcast_fusion.3
  88.7 6.3 %shard_map.68 = (bf16[480,640]{1,0:T(8,128)(2,1)S(1)}, f32[480,384]{1,0:T(8,128)S(1)}, bf16[480,640]{1,0:T(8,128)(2,1)S(1)}) custom-call(bf16[480,640]{1,0:T(8,128)(2,1)S(1)} %bitcast.309, f32[5,640]{1,0:T(8,128)S(1)} %pad_maximum_fusion.6.embedding_ref, f32[1,384]{1,0:T(1,128)S(1)} %select_n.851.keep_ref, bf16[960,640]{1,0:T(8,128)(2,1)S(1)} %bitcast.306, ...), custom_call_target="tpu_custom_call" | custom-call | flops 7077888000 | bytes 5898240 | tf_op jit(solution)/shard_map/pallas_call | solution.py:655
  95.0 7.6 %collective-permute-done.21 = bf16[4,360,256]{2,1,0:T(8,128)(2,1)S(1)} collective-permute-done((bf16[4,360,256]{2,1,0:T(8,128)(2,1)S(1)}, bf16[4,360,256]{2,1,0:T(8,128)(2,1)S(1)}, u32[]{:S(2)}, u32[]{:S(2)}) %collective-permute-start.21) | collective-permute-done | bytes 737312 | tf_op jit(solution)/shard_map/ppermute | solution.py:238
  102.5 1.4 maximum_select_fusion.6
  104.0 1.6 collective-permute-start.17
  105.6 1.1 slice.273
  106.7 1.1 slice.274
  107.9 1.7 maximum_select_fusion.12
  109.9 2.5 %maximum_select_fusion.1 = bf16[4,2,2,360,256]{4,3,0,2,1:T(8,128)(2,1)S(1)} fusion(bf16[4,2,1,360,256]{4,3,0,2,1:T(8,128)(2,1)S(1)} %bitcast_select_fusion, bf16[4,2,1,360,256]{4,3,0,2,1:T(8,128)(2,1)} %bitcast.60, pred[]{:T(512)S(6)} %eq.114), kind=kLoop, calls=%fused_computation.5 | loop fusion | flops 4423680 | bytes 5898241 | tf_op jit(solution)/shard_map/jit(_where)/select_n | solution.py:266
  112.6 7.8 %collective-permute-done.17.sent_ref = bf16[480,640]{1,0:T(8,128)(2,1)} collective-permute-done((bf16[480,640]{1,0:T(8,128)(2,1)S(1)}, bf16[480,640]{1,0:T(8,128)(2,1)}, u32[]{:S(2)}, u32[]{:S(2)}) %collective-permute-start.17) | collective-permute-done | bytes 614432 | tf_op jit(solution)/shard_map/ppermute | solution.py:242
  120.4 12.9 %shard_map.69 = (bf16[480,640]{1,0:T(8,128)(2,1)S(1)}, bf16[480,640]{1,0:T(8,128)(2,1)S(1)}, bf16[480,384]{1,0:T(8,128)(2,1)S(1)}, bf16[480,384]{1,0:T(8,128)(2,1)S(1)}, bf16[480,640]{1,0:T(8,128)(2,1)}) custom-call(bf16[480,640]{1,0:T(8,128)(2,1)S(1)} %bitcast.310, bf16[480,640]{1,0:T(8,128)(2,1)S(1)} %get-tuple-element.32.own_ref, ...), custom_call_target="tpu_custom_call" | custom-call | flops 12386304000 | bytes 5898240 | tf_op jit(solution)/shard_map/pallas_call | solution.py:665
  133.3 4.8 %shard_map.70 = (bf16[5760,256]{1,0:T(8,128)(2,1)S(1)}, bf16[5760,128]{1,0:T(8,128)(2,1)S(1)}, bf16[960,640]{1,0:T(8,128)(2,1)S(1)}) custom-call(bf16[480,640]{1,0:T(8,128)(2,1)S(1)} %get-tuple-element.37.normed_ref, bf16[480,384]{1,0:T(8,128)(2,1)S(1)} %get-tuple-element.38.pre_grad_ref, bf16[480,384]{1,0:T(8,128)(2,1)S(1)} %get-tuple-element.39.activated_ref, ...), custom_call_target="tpu_custom_call" | custom-call | flops 7077888000 | bytes 5898240 | tf_op jit(solution)/shard_map/pallas_call | solution.py:692
  138.1 1.2 dynamic-slice_bitcast_fusion.5
  141.1 1.5 collective-permute-start.23
  142.6 1.1 slice.281
  143.9 1.9 fusion.1
  146.4 10.8 %collective-permute-done.23.sent_ref = bf16[480,640]{1,0:T(8,128)(2,1)} collective-permute-done((bf16[480,640]{1,0:T(8,128)(2,1)}, bf16[480,640]{1,0:T(8,128)(2,1)}, u32[]{:S(2)}, u32[]{:S(2)}) %collective-permute-start.23) | collective-permute-done | bytes 614432 | tf_op jit(solution)/shard_map/ppermute | solution.py:242
  157.2 7.8 %shard_map.71 = (bf16[5760,256]{1,0:T(8,128)(2,1)S(1)}, bf16[5760,128]{1,0:T(8,128)(2,1)S(1)}, bf16[960,640]{1,0:T(8,128)(2,1)S(1)}) custom-call(bf16[480,640]{1,0:T(8,128)(2,1)S(1)} %copy-done.16, f32[5,640]{1,0:T(8,128)S(1)} %pad_maximum_fusion.6.embedding_ref, bf16[480,640]{1,0:T(8,128)(2,1)S(1)} %bitcast.313, ...), custom_call_target="tpu_custom_call" | custom-call | flops 8847360000 | bytes 7372800 | tf_op jit(solution)/shard_map/pallas_call | solution.py:702
  166.6 0.6 copy-done.3
  170.0 1.7 collective-permute-start.35
  171.7 8.0 %collective-permute-done.31 = bf16[4,360,128]{2,1,0:T(8,128)(2,1)S(1)} collective-permute-done((bf16[4,360,128]{2,1,0:T(8,128)(2,1)S(1)}, bf16[4,360,128]{2,1,0:T(8,128)(2,1)S(1)}, u32[]{:S(2)}, u32[]{:S(2)}) %collective-permute-start.31) | collective-permute-done | bytes 368672 | tf_op jit(solution)/shard_map/ppermute | solution.py:238
  179.7 1.3 collective-permute-start.36
  182.8 8.5 %collective-permute-done.32 = bf16[4,360,128]{2,1,0:T(8,128)(2,1)S(1)} collective-permute-done((bf16[4,360,128]{2,1,0:T(8,128)(2,1)S(1)}, bf16[4,360,128]{2,1,0:T(8,128)(2,1)S(1)}, u32[]{:S(2)}, u32[]{:S(2)}) %collective-permute-start.32) | collective-permute-done | bytes 368672 | tf_op jit(solution)/shard_map/ppermute | solution.py:238
  191.9 0.9 collective-permute-start.39
  192.8 1.5 collective-permute-start.38
  194.4 5.6 %collective-permute-done.33 = bf16[4,360,128]{2,1,0:T(8,128)(2,1)S(1)} collective-permute-done((bf16[4,360,128]{2,1,0:T(8,128)(2,1)S(1)}, bf16[4,360,128]{2,1,0:T(8,128)(2,1)S(1)}, u32[]{:S(2)}, u32[]{:S(2)}) %collective-permute-start.33) | collective-permute-done | bytes 368672 | tf_op jit(solution)/shard_map/ppermute | solution.py:238
  201.2 0.7 collective-permute-start.42
  201.9 1.4 collective-permute-start.41
  203.3 0.7 collective-permute-start.40
  204.0 9.8 %collective-permute-done.44 = bf16[4,128,640]{2,1,0:T(8,128)(2,1)S(1)} collective-permute-done((bf16[4,128,640]{2,1,0:T(8,128)(2,1)S(1)}, bf16[4,128,640]{2,1,0:T(8,128)(2,1)S(1)}, u32[]{:S(2)}, u32[]{:S(2)}) %collective-permute-start.44) | collective-permute-done | bytes 655392 | tf_op jit(solution)/shard_map/ppermute | solution.py:238
  214.0 3.2 %collective-permute-done.41 = bf16[360,256]{1,0:T(8,128)(2,1)S(1)} collective-permute-done((bf16[360,256]{1,0:T(8,128)(2,1)S(1)}, bf16[360,256]{1,0:T(8,128)(2,1)S(1)}, u32[]{:S(2)}, u32[]{:S(2)}) %collective-permute-start.41) | collective-permute-done | bytes 184352 | tf_op jit(solution)/shard_map/ppermute | solution.py:238
  217.3 2.5 %collective-permute-start.47 = (bf16[128,640]{1,0:T(8,128)(2,1)S(1)}, bf16[128,640]{1,0:T(8,128)(2,1)S(1)}, u32[]{:S(2)}, u32[]{:S(2)}) collective-permute-start(bf16[128,640]{1,0:T(8,128)(2,1)S(1)} %get-tuple-element.106), channel_id=1, source_target_pairs={{0,8},{1,9},{2,10},{3,11},{4,12},{5,13},{6,14},{7,15},{8,0},{9,1},... | collective-permute-start | bytes 491528 | tf_op jit(solution)/shard_map/ppermute | solution.py:238
  219.8 1.9 collective-permute-start.46
  222.0 1.6 collective-permute-start.45
  223.6 8.6 %collective-permute-done.47 = bf16[128,640]{1,0:T(8,128)(2,1)S(1)} collective-permute-done((bf16[128,640]{1,0:T(8,128)(2,1)S(1)}, bf16[128,640]{1,0:T(8,128)(2,1)S(1)}, u32[]{:S(2)}, u32[]{:S(2)}) %collective-permute-start.47) | collective-permute-done | bytes 163872 | tf_op jit(solution)/shard_map/ppermute | solution.py:238
  232.3 1.6 collective-permute-start.49
  233.9 2.9 %collective-permute-done.49 = bf16[64,640]{1,0:T(8,128)(2,1)S(1)} collective-permute-done((bf16[64,640]{1,0:T(8,128)(2,1)S(1)}, bf16[64,640]{1,0:T(8,128)(2,1)S(1)}, u32[]{:S(2)}, u32[]{:S(2)}) %collective-permute-start.49) | collective-permute-done | bytes 81952 | tf_op jit(solution)/shard_map/ppermute | solution.py:242
  236.9 0.8 broadcast_select_fusion.5
  237.9 2.1 fusion.7
  (189 shorter events, 20.6 us)
Async XLA Ops:
  0.6 4.9 %copy-start = (bf16[1,360,640]{2,1,0:T(8,128)(2,1)S(1)}, bf16[1,360,640]{2,1,0:T(8,128)(2,1)}, u32[]{:S(2)}) copy-start(bf16[1,360,640]{2,1,0:T(8,128)(2,1)} %param.8) | copy-start | bytes 1382404
  1.5 5.0 %copy-start.21 = (s32[5]{0:T(128)S(1)}, s32[5]{0:T(128)}, u32[]{:S(2)}) copy-start(s32[5]{0:T(128)} %param.6) | copy-start | bytes 64
  2.5 5.8 %collective-permute-start = (bf16[64,640]{1,0:T(8,128)(2,1)S(1)}, bf16[64,640]{1,0:T(8,128)(2,1)S(1)}, u32[]{:S(2)}, u32[]{:S(2)}) collective-permute-start(bf16[64,640]{1,0:T(8,128)(2,1)S(1)} %fusion.42), channel_id=1, source_target_pairs={{0,16},{16,0},{1,17},{17,1},{2,18},{18,2},{3,19},{19,3},{4,20},{20... | collective-permute-start | bytes 245768 | tf_op jit(solution)/shard_map/ppermute | solution.py:242
  6.3 18.0 %collective-permute-start.6 = (bf16[360,384]{1,0:T(8,128)(2,1)S(1)}, bf16[360,384]{1,0:T(8,128)(2,1)S(1)}, u32[]{:S(2)}, u32[]{:S(2)}) collective-permute-start(bf16[360,384]{1,0:T(8,128)(2,1)S(1)} %slice.266), channel_id=1, source_target_pairs={{0,16},{16,0},{1,17},{17,1},{2,18},{18,2},{3,19},{19,3},{4,20},{20... | collective-permute-start | bytes 829448 | tf_op jit(solution)/shard_map/ppermute | solution.py:242
  8.3 12.3 %collective-permute-start.2 = (bf16[128,640]{1,0:T(8,128)(2,1)S(1)}, bf16[128,640]{1,0:T(8,128)(2,1)S(1)}, u32[]{:S(2)}, u32[]{:S(2)}) collective-permute-start(bf16[128,640]{1,0:T(8,128)(2,1)S(1)} %maximum_select_fusion.15), channel_id=1, source_target_pairs={{0,8},{1,9},{2,10},{3,11},{4,12},{5,13},{6,14},{7,15},{8,0},{9,1},... | collective-permute-start | bytes 491528 | tf_op jit(solution)/shard_map/ppermute | solution.py:238
  11.1 9.6 %collective-permute-start.3 = (bf16[128,640]{1,0:T(8,128)(2,1)S(1)}, bf16[128,640]{1,0:T(8,128)(2,1)S(1)}, u32[]{:S(2)}, u32[]{:S(2)}) collective-permute-start(bf16[128,640]{1,0:T(8,128)(2,1)S(1)} %maximum_select_fusion.15), channel_id=1, source_target_pairs={{0,12},{1,13},{2,14},{3,15},{4,0},{5,1},{6,2},{7,3},{8,4},{9,5},{1... | collective-permute-start | bytes 491528 | tf_op jit(solution)/shard_map/ppermute | solution.py:238
  12.4 10.0 %collective-permute-start.1 = (bf16[128,640]{1,0:T(8,128)(2,1)S(1)}, bf16[128,640]{1,0:T(8,128)(2,1)S(1)}, u32[]{:S(2)}, u32[]{:S(2)}) collective-permute-start(bf16[128,640]{1,0:T(8,128)(2,1)S(1)} %maximum_select_fusion.15), channel_id=1, source_target_pairs={{0,4},{1,5},{2,6},{3,7},{4,8},{5,9},{6,10},{7,11},{8,12},{9,13},{1... | collective-permute-start | bytes 491528 | tf_op jit(solution)/shard_map/ppermute | solution.py:238
  22.7 20.3 %collective-permute-start.4 = (bf16[4,128,640]{2,1,0:T(8,128)(2,1)S(1)}, bf16[4,128,640]{2,1,0:T(8,128)(2,1)S(1)}, u32[]{:S(2)}, u32[]{:S(2)}) collective-permute-start(bf16[4,128,640]{2,1,0:T(8,128)(2,1)S(1)} %get-tuple-element.109), channel_id=1, source_target_pairs={{0,2},{1,3},{2,0},{3,1},{4,6},{5,7},{6,4},{7,5},{8,10},{9,11},{10,... | collective-permute-start | bytes 1966088 | tf_op jit(solution)/shard_map/ppermute | solution.py:238
  24.3 15.0 %collective-permute-start.8 = (bf16[360,256]{1,0:T(8,128)(2,1)S(1)}, bf16[360,256]{1,0:T(8,128)(2,1)S(1)}, u32[]{:S(2)}, u32[]{:S(2)}) collective-permute-start(bf16[360,256]{1,0:T(8,128)(2,1)S(1)} %get-tuple-element.30), channel_id=1, source_target_pairs={{0,8},{1,9},{2,10},{3,11},{4,12},{5,13},{6,14},{7,15},{8,0},{9,1},... | collective-permute-start | bytes 552968 | tf_op jit(solution)/shard_map/ppermute | solution.py:238
  29.3 13.6 %collective-permute-start.9 = (bf16[360,256]{1,0:T(8,128)(2,1)S(1)}, bf16[360,256]{1,0:T(8,128)(2,1)S(1)}, u32[]{:S(2)}, u32[]{:S(2)}) collective-permute-start(bf16[360,256]{1,0:T(8,128)(2,1)S(1)} %get-tuple-element.30), channel_id=1, source_target_pairs={{0,12},{1,13},{2,14},{3,15},{4,0},{5,1},{6,2},{7,3},{8,4},{9,5},{1... | collective-permute-start | bytes 552968 | tf_op jit(solution)/shard_map/ppermute | solution.py:238
  29.8 13.2 %collective-permute-start.7 = (bf16[360,256]{1,0:T(8,128)(2,1)S(1)}, bf16[360,256]{1,0:T(8,128)(2,1)S(1)}, u32[]{:S(2)}, u32[]{:S(2)}) collective-permute-start(bf16[360,256]{1,0:T(8,128)(2,1)S(1)} %get-tuple-element.30), channel_id=1, source_target_pairs={{0,4},{1,5},{2,6},{3,7},{4,8},{5,9},{6,10},{7,11},{8,12},{9,13},{1... | collective-permute-start | bytes 552968 | tf_op jit(solution)/shard_map/ppermute | solution.py:238
  43.1 6.5 %collective-permute-start.13 = (bf16[360,128]{1,0:T(8,128)(2,1)S(1)}, bf16[360,128]{1,0:T(8,128)(2,1)S(1)}, u32[]{:S(2)}, u32[]{:S(2)}) collective-permute-start(bf16[360,128]{1,0:T(8,128)(2,1)S(1)} %slice_select_fusion.2), channel_id=1, source_target_pairs={{0,8},{1,9},{2,10},{3,11},{4,12},{5,13},{6,14},{7,15},{8,0},{9,1},... | collective-permute-start | bytes 276488 | tf_op jit(solution)/shard_map/ppermute | solution.py:238
  45.5 6.1 %collective-permute-start.14 = (bf16[360,128]{1,0:T(8,128)(2,1)S(1)}, bf16[360,128]{1,0:T(8,128)(2,1)S(1)}, u32[]{:S(2)}, u32[]{:S(2)}) collective-permute-start(bf16[360,128]{1,0:T(8,128)(2,1)S(1)} %slice_select_fusion.2), channel_id=1, source_target_pairs={{0,12},{1,13},{2,14},{3,15},{4,0},{5,1},{6,2},{7,3},{8,4},{9,5},{1... | collective-permute-start | bytes 276488 | tf_op jit(solution)/shard_map/ppermute | solution.py:238
  48.9 6.4 %collective-permute-start.12 = (bf16[360,128]{1,0:T(8,128)(2,1)S(1)}, bf16[360,128]{1,0:T(8,128)(2,1)S(1)}, u32[]{:S(2)}, u32[]{:S(2)}) collective-permute-start(bf16[360,128]{1,0:T(8,128)(2,1)S(1)} %slice_select_fusion.2), channel_id=1, source_target_pairs={{0,4},{1,5},{2,6},{3,7},{4,8},{5,9},{6,10},{7,11},{8,12},{9,13},{1... | collective-permute-start | bytes 276488 | tf_op jit(solution)/shard_map/ppermute | solution.py:238
  49.0 19.5 %collective-permute-start.10 = (bf16[4,360,256]{2,1,0:T(8,128)(2,1)S(1)}, bf16[4,360,256]{2,1,0:T(8,128)(2,1)S(1)}, u32[]{:S(2)}, u32[]{:S(2)}) collective-permute-start(bf16[4,360,256]{2,1,0:T(8,128)(2,1)S(1)} %get-tuple-element.99), channel_id=1, source_target_pairs={{0,2},{1,3},{2,0},{3,1},{4,6},{5,7},{6,4},{7,5},{8,10},{9,11},{10,... | collective-permute-start | bytes 2211848 | tf_op jit(solution)/shard_map/ppermute | solution.py:238
  55.5 19.2 %collective-permute-start.15 = (bf16[4,360,128]{2,1,0:T(8,128)(2,1)S(1)}, bf16[4,360,128]{2,1,0:T(8,128)(2,1)S(1)}, u32[]{:S(2)}, u32[]{:S(2)}) collective-permute-start(bf16[4,360,128]{2,1,0:T(8,128)(2,1)S(1)} %get-tuple-element.119), channel_id=1, source_target_pairs={{0,2},{1,3},{2,0},{3,1},{4,6},{5,7},{6,4},{7,5},{8,10},{9,11},{10,... | collective-permute-start | bytes 1105928 | tf_op jit(solution)/shard_map/ppermute | solution.py:238
  56.3 28.3 %collective-permute-start.5 = (bf16[4,2,128,640]{3,2,1,0:T(8,128)(2,1)S(1)}, bf16[4,2,128,640]{3,2,1,0:T(8,128)(2,1)S(1)}, u32[]{:S(2)}, u32[]{:S(2)}) collective-permute-start(bf16[4,2,128,640]{3,2,1,0:T(8,128)(2,1)S(1)} %maximum_select_fusion.7), channel_id=1, source_target_pairs={{0,1},{1,0},{2,3},{3,2},{4,5},{5,4},{6,7},{7,6},{8,9},{9,8},{10,11... | collective-permute-start | bytes 3932168 | tf_op jit(solution)/shard_map/ppermute | solution.py:238
  68.5 14.0 %collective-permute-start.19 = (bf16[360,256]{1,0:T(8,128)(2,1)S(1)}, bf16[360,256]{1,0:T(8,128)(2,1)S(1)}, u32[]{:S(2)}, u32[]{:S(2)}) collective-permute-start(bf16[360,256]{1,0:T(8,128)(2,1)S(1)} %get-tuple-element.33), channel_id=1, source_target_pairs={{0,8},{1,9},{2,10},{3,11},{4,12},{5,13},{6,14},{7,15},{8,0},{9,1},... | collective-permute-start | bytes 552968 | tf_op jit(solution)/shard_map/ppermute | solution.py:238
  69.1 13.4 %collective-permute-start.20 = (bf16[360,256]{1,0:T(8,128)(2,1)S(1)}, bf16[360,256]{1,0:T(8,128)(2,1)S(1)}, u32[]{:S(2)}, u32[]{:S(2)}) collective-permute-start(bf16[360,256]{1,0:T(8,128)(2,1)S(1)} %get-tuple-element.33), channel_id=1, source_target_pairs={{0,12},{1,13},{2,14},{3,15},{4,0},{5,1},{6,2},{7,3},{8,4},{9,5},{1... | collective-permute-start | bytes 552968 | tf_op jit(solution)/shard_map/ppermute | solution.py:238
  72.3 10.2 %collective-permute-start.18 = (bf16[360,256]{1,0:T(8,128)(2,1)S(1)}, bf16[360,256]{1,0:T(8,128)(2,1)S(1)}, u32[]{:S(2)}, u32[]{:S(2)}) collective-permute-start(bf16[360,256]{1,0:T(8,128)(2,1)S(1)} %get-tuple-element.33), channel_id=1, source_target_pairs={{0,4},{1,5},{2,6},{3,7},{4,8},{5,9},{6,10},{7,11},{8,12},{9,13},{1... | collective-permute-start | bytes 552968 | tf_op jit(solution)/shard_map/ppermute | solution.py:238
  74.8 9.4 %collective-permute-start.16 = (bf16[4,2,360,128]{3,2,0,1:T(8,128)(2,1)S(1)}, bf16[4,2,360,128]{3,2,0,1:T(8,128)(2,1)S(1)}, u32[]{:S(2)}, u32[]{:S(2)}) collective-permute-start(bf16[4,2,360,128]{3,2,0,1:T(8,128)(2,1)S(1)} %maximum_select_fusion.13), channel_id=1, source_target_pairs={{0,1},{1,0},{2,3},{3,2},{4,5},{5,4},{6,7},{7,6},{8,9},{9,8},{10,11... | collective-permute-start | bytes 2211848 | tf_op jit(solution)/shard_map/ppermute | solution.py:238
  82.5 4.6 %collective-permute-start.11 = (bf16[4,2,360,256]{3,2,0,1:T(8,128)(2,1)S(1)}, bf16[4,2,360,256]{3,2,0,1:T(8,128)(2,1)S(1)}, u32[]{:S(2)}, u32[]{:S(2)}) collective-permute-start(bf16[4,2,360,256]{3,2,0,1:T(8,128)(2,1)S(1)} %maximum_select_fusion.3), channel_id=1, source_target_pairs={{0,1},{1,0},{2,3},{3,2},{4,5},{5,4},{6,7},{7,6},{8,9},{9,8},{10,11... | collective-permute-start | bytes 4423688 | tf_op jit(solution)/shard_map/ppermute | solution.py:238
  83.7 18.9 %collective-permute-start.21 = (bf16[4,360,256]{2,1,0:T(8,128)(2,1)S(1)}, bf16[4,360,256]{2,1,0:T(8,128)(2,1)S(1)}, u32[]{:S(2)}, u32[]{:S(2)}) collective-permute-start(bf16[4,360,256]{2,1,0:T(8,128)(2,1)S(1)} %get-tuple-element.90), channel_id=1, source_target_pairs={{0,2},{1,3},{2,0},{3,1},{4,6},{5,7},{6,4},{7,5},{8,10},{9,11},{10,... | collective-permute-start | bytes 2211848 | tf_op jit(solution)/shard_map/ppermute | solution.py:238
  94.9 9.0 %copy-start.11 = (f32[480,384]{1,0:T(8,128)}, f32[480,384]{1,0:T(8,128)S(1)}, u32[]{:S(2)}) copy-start(f32[480,384]{1,0:T(8,128)S(1)} %get-tuple-element.43.preact_ref) | copy-start | bytes 2211844
  95.0 9.0 %copy-start.13 = (bf16[480,640]{1,0:T(8,128)(2,1)}, bf16[480,640]{1,0:T(8,128)(2,1)S(1)}, u32[]{:S(2)}) copy-start(bf16[480,640]{1,0:T(8,128)(2,1)S(1)} %get-tuple-element.42.normed_ref) | copy-start | bytes 1843204
  103.9 5.9 %collective-permute-start.22 = (bf16[4,2,360,256]{3,2,0,1:T(8,128)(2,1)}, bf16[4,2,360,256]{3,2,0,1:T(8,128)(2,1)}, u32[]{:S(2)}, u32[]{:S(2)}) collective-permute-start(bf16[4,2,360,256]{3,2,0,1:T(8,128)(2,1)} %maximum_select_fusion.6), channel_id=1, source_target_pairs={{0,1},{1,0},{2,3},{3,2},{4,5},{5,4},{6,7},{7,6},{8,9},{9,8},{10,11... | collective-permute-start | bytes 4423688 | tf_op jit(solution)/shard_map/ppermute | solution.py:238
  104.0 16.4 %collective-permute-start.17 = (bf16[480,640]{1,0:T(8,128)(2,1)S(1)}, bf16[480,640]{1,0:T(8,128)(2,1)}, u32[]{:S(2)}, u32[]{:S(2)}) collective-permute-start(bf16[480,640]{1,0:T(8,128)(2,1)S(1)} %get-tuple-element.32.own_ref), channel_id=1, source_target_pairs={{0,16},{16,0},{1,17},{17,1},{2,18},{18,2},{3,19},{19,3},{4,20},{20... | collective-permute-start | bytes 1843208 | tf_op jit(solution)/shard_map/ppermute | solution.py:242
  112.3 8.1 %copy-start.9 = (bf16[5,3,32,640]{3,2,1,0:T(8,128)(2,1)S(1)}, bf16[5,3,32,640]{3,2,1,0:T(8,128)(2,1)}, u32[]{:S(2)}) copy-start(bf16[5,3,32,640]{3,2,1,0:T(8,128)(2,1)} %param.7) | copy-start | bytes 1843204
  133.3 4.8 %copy-start.15 = (bf16[480,640]{1,0:T(8,128)(2,1)}, bf16[480,640]{1,0:T(8,128)(2,1)S(1)}, u32[]{:S(2)}) copy-start(bf16[480,640]{1,0:T(8,128)(2,1)S(1)} %get-tuple-element.35.hidden_ref) | copy-start | bytes 1843204
  138.1 1.9 copy-start.4
  140.0 3.7 %collective-permute-start.27 = (bf16[1,2,360,256]{3,2,0,1:T(8,128)(2,1)}, bf16[1,2,360,256]{3,2,0,1:T(8,128)(2,1)}, u32[]{:S(2)}, u32[]{:S(2)}) collective-permute-start(bf16[1,2,360,256]{3,2,0,1:T(8,128)(2,1)} %get-tuple-element.63), channel_id=1, source_target_pairs={{0,1},{1,0},{2,3},{3,2},{4,5},{5,4},{6,7},{7,6},{8,9},{9,8},{10,11... | collective-permute-start | bytes 1105928 | tf_op jit(solution)/shard_map/ppermute | solution.py:238
  140.0 3.7 %collective-permute-start.26 = (bf16[1,2,360,256]{3,2,1,0:T(8,128)(2,1)}, bf16[1,2,360,256]{3,2,1,0:T(8,128)(2,1)}, u32[]{:S(2)}, u32[]{:S(2)}) collective-permute-start(bf16[1,2,360,256]{3,2,1,0:T(8,128)(2,1)} %get-tuple-element.61), channel_id=1, source_target_pairs={{0,1},{1,0},{2,3},{3,2},{4,5},{5,4},{6,7},{7,6},{8,9},{9,8},{10,11... | collective-permute-start | bytes 1105928 | tf_op jit(solution)/shard_map/ppermute | solution.py:238
  140.6 3.2 %collective-permute-start.25 = (bf16[1,2,360,256]{3,2,1,0:T(8,128)(2,1)}, bf16[1,2,360,256]{3,2,1,0:T(8,128)(2,1)}, u32[]{:S(2)}, u32[]{:S(2)}) collective-permute-start(bf16[1,2,360,256]{3,2,1,0:T(8,128)(2,1)} %get-tuple-element.62), channel_id=1, source_target_pairs={{0,1},{1,0},{2,3},{3,2},{4,5},{5,4},{6,7},{7,6},{8,9},{9,8},{10,11... | collective-permute-start | bytes 1105928 | tf_op jit(solution)/shard_map/ppermute | solution.py:238
  140.6 3.3 %collective-permute-start.24 = (bf16[1,2,360,256]{3,2,1,0:T(8,128)(2,1)S(1)}, bf16[1,2,360,256]{3,2,1,0:T(8,128)(2,1)}, u32[]{:S(2)}, u32[]{:S(2)}) collective-permute-start(bf16[1,2,360,256]{3,2,1,0:T(8,128)(2,1)S(1)} %get-tuple-element.60), channel_id=1, source_target_pairs={{0,1},{1,0},{2,3},{3,2},{4,5},{5,4},{6,7},{7,6},{8,9},{9,8},{10,11... | collective-permute-start | bytes 1105928 | tf_op jit(solution)/shard_map/ppermute | solution.py:238
  141.1 16.1 %collective-permute-start.23 = (bf16[480,640]{1,0:T(8,128)(2,1)}, bf16[480,640]{1,0:T(8,128)(2,1)}, u32[]{:S(2)}, u32[]{:S(2)}) collective-permute-start(bf16[480,640]{1,0:T(8,128)(2,1)} %get-tuple-element.36.own_ref), channel_id=1, source_target_pairs={{0,16},{16,0},{1,17},{17,1},{2,18},{18,2},{3,19},{19,3},{4,20},{20... | collective-permute-start | bytes 1843208 | tf_op jit(solution)/shard_map/ppermute | solution.py:242
  143.8 13.3 %copy-start.10 = (bf16[5,3,32,640]{3,2,1,0:T(8,128)(2,1)S(1)}, bf16[5,3,32,640]{3,2,1,0:T(8,128)(2,1)}, u32[]{:S(2)}) copy-start(bf16[5,3,32,640]{3,2,1,0:T(8,128)(2,1)} %param.7) | copy-start | bytes 1843204
  143.8 13.3 %copy-start.12 = (f32[480,384]{1,0:T(8,128)S(1)}, f32[480,384]{1,0:T(8,128)}, u32[]{:S(2)}) copy-start(f32[480,384]{1,0:T(8,128)} %copy-done.11) | copy-start | bytes 2211844
  143.8 13.3 %copy-start.14 = (bf16[480,640]{1,0:T(8,128)(2,1)S(1)}, bf16[480,640]{1,0:T(8,128)(2,1)}, u32[]{:S(2)}) copy-start(bf16[480,640]{1,0:T(8,128)(2,1)} %copy-done.13) | copy-start | bytes 1843204
  143.8 13.3 %copy-start.16 = (bf16[480,640]{1,0:T(8,128)(2,1)S(1)}, bf16[480,640]{1,0:T(8,128)(2,1)}, u32[]{:S(2)}) copy-start(bf16[480,640]{1,0:T(8,128)(2,1)} %copy-done.15) | copy-start | bytes 1843204
  145.7 11.4 %copy-start.7 = (bf16[8,120,640]{2,1,0:T(8,128)(2,1)S(1)}, bf16[8,120,640]{2,1,0:T(8,128)(2,1)}, u32[]{:S(2)}) copy-start(bf16[8,120,640]{2,1,0:T(8,128)(2,1)} %copy-done.6) | copy-start | bytes 3686404
  145.8 19.9 %collective-permute-start.28 = (bf16[4,360,256]{2,1,0:T(8,128)(2,1)S(1)}, bf16[4,360,256]{2,1,0:T(8,128)(2,1)S(1)}, u32[]{:S(2)}, u32[]{:S(2)}) collective-permute-start(bf16[4,360,256]{2,1,0:T(8,128)(2,1)S(1)} %dynamic-slice_bitcast_fusion), channel_id=1, source_target_pairs={{0,2},{1,3},{2,0},{3,1},{4,6},{5,7},{6,4},{7,5},{8,10},{9,11},{10,... | collective-permute-start | bytes 2211848 | tf_op jit(solution)/shard_map/ppermute | solution.py:238
  157.2 7.8 %copy-start.5 = (bf16[5760,128]{1,0:T(8,128)(2,1)S(1)}, bf16[5760,128]{1,0:T(8,128)(2,1)}, u32[]{:S(2)}) copy-start(bf16[5760,128]{1,0:T(8,128)(2,1)} %copy-done.4) | copy-start | bytes 4423684
  165.6 3.2 %collective-permute-start.30 = (bf16[4,2,360,128]{3,2,0,1:T(8,128)(2,1)S(1)}, bf16[4,2,360,128]{3,2,0,1:T(8,128)(2,1)S(1)}, u32[]{:S(2)}, u32[]{:S(2)}) collective-permute-start(bf16[4,2,360,128]{3,2,0,1:T(8,128)(2,1)S(1)} %bitcast.336), channel_id=1, source_target_pairs={{0,1},{1,0},{2,3},{3,2},{4,5},{5,4},{6,7},{7,6},{8,9},{9,8},{10,11... | collective-permute-start | bytes 2211848 | tf_op jit(solution)/shard_map/ppermute | solution.py:238
  166.0 15.0 %collective-permute-start.29 = (bf16[4,2,360,256]{3,2,0,1:T(8,128)(2,1)S(1)}, bf16[4,2,360,256]{3,2,0,1:T(8,128)(2,1)S(1)}, u32[]{:S(2)}, u32[]{:S(2)}) collective-permute-start(bf16[4,2,360,256]{3,2,0,1:T(8,128)(2,1)S(1)} %bitcast.331), channel_id=1, source_target_pairs={{0,1},{1,0},{2,3},{3,2},{4,5},{5,4},{6,7},{7,6},{8,9},{9,8},{10,11... | collective-permute-start | bytes 4423688 | tf_op jit(solution)/shard_map/ppermute | solution.py:238
  168.3 14.1 %collective-permute-start.43 = (bf16[4,2,128,640]{3,2,1,0:T(8,128)(2,1)S(1)}, bf16[4,2,128,640]{3,2,1,0:T(8,128)(2,1)S(1)}, u32[]{:S(2)}, u32[]{:S(2)}) collective-permute-start(bf16[4,2,128,640]{3,2,1,0:T(8,128)(2,1)S(1)} %fusion.9), channel_id=1, source_target_pairs={{0,1},{1,0},{2,3},{3,2},{4,5},{5,4},{6,7},{7,6},{8,9},{9,8},{10,11... | collective-permute-start | bytes 3932168 | tf_op jit(solution)/shard_map/ppermute | solution.py:238
  169.1 10.6 %collective-permute-start.31 = (bf16[4,360,128]{2,1,0:T(8,128)(2,1)S(1)}, bf16[4,360,128]{2,1,0:T(8,128)(2,1)S(1)}, u32[]{:S(2)}, u32[]{:S(2)}) collective-permute-start(bf16[4,360,128]{2,1,0:T(8,128)(2,1)S(1)} %dynamic-slice_bitcast_fusion.7), channel_id=1, source_target_pairs={{0,2},{1,3},{2,0},{3,1},{4,6},{5,7},{6,4},{7,5},{8,10},{9,11},{10,... | collective-permute-start | bytes 1105928 | tf_op jit(solution)/shard_map/ppermute | solution.py:238
  169.9 21.9 %collective-permute-start.34 = (bf16[360,256]{1,0:T(8,128)(2,1)S(1)}, bf16[360,256]{1,0:T(8,128)(2,1)S(1)}, u32[]{:S(2)}, u32[]{:S(2)}) collective-permute-start(bf16[360,256]{1,0:T(8,128)(2,1)S(1)} %get-tuple-element.87), channel_id=1, source_target_pairs={{0,4},{1,5},{2,6},{3,7},{4,8},{5,9},{6,10},{7,11},{8,12},{9,13},{1... | collective-permute-start | bytes 552968 | tf_op jit(solution)/shard_map/ppermute | solution.py:238
  170.0 21.8 %collective-permute-start.35 = (bf16[360,256]{1,0:T(8,128)(2,1)S(1)}, bf16[360,256]{1,0:T(8,128)(2,1)S(1)}, u32[]{:S(2)}, u32[]{:S(2)}) collective-permute-start(bf16[360,256]{1,0:T(8,128)(2,1)S(1)} %get-tuple-element.86), channel_id=1, source_target_pairs={{0,8},{1,9},{2,10},{3,11},{4,12},{5,13},{6,14},{7,15},{8,0},{9,1},... | collective-permute-start | bytes 552968 | tf_op jit(solution)/shard_map/ppermute | solution.py:238
  179.7 12.2 %collective-permute-start.36 = (bf16[360,256]{1,0:T(8,128)(2,1)S(1)}, bf16[360,256]{1,0:T(8,128)(2,1)S(1)}, u32[]{:S(2)}, u32[]{:S(2)}) collective-permute-start(bf16[360,256]{1,0:T(8,128)(2,1)S(1)} %get-tuple-element.85), channel_id=1, source_target_pairs={{0,12},{1,13},{2,14},{3,15},{4,0},{5,1},{6,2},{7,3},{8,4},{9,5},{1... | collective-permute-start | bytes 552968 | tf_op jit(solution)/shard_map/ppermute | solution.py:238
  181.8 9.5 %collective-permute-start.32 = (bf16[4,360,128]{2,1,0:T(8,128)(2,1)S(1)}, bf16[4,360,128]{2,1,0:T(8,128)(2,1)S(1)}, u32[]{:S(2)}, u32[]{:S(2)}) collective-permute-start(bf16[4,360,128]{2,1,0:T(8,128)(2,1)S(1)} %dynamic-slice_bitcast_fusion.8), channel_id=1, source_target_pairs={{0,2},{1,3},{2,0},{3,1},{4,6},{5,7},{6,4},{7,5},{8,10},{9,11},{10,... | collective-permute-start | bytes 1105928 | tf_op jit(solution)/shard_map/ppermute | solution.py:238
  191.3 8.8 %collective-permute-start.33 = (bf16[4,360,128]{2,1,0:T(8,128)(2,1)S(1)}, bf16[4,360,128]{2,1,0:T(8,128)(2,1)S(1)}, u32[]{:S(2)}, u32[]{:S(2)}) collective-permute-start(bf16[4,360,128]{2,1,0:T(8,128)(2,1)S(1)} %dynamic-slice_bitcast_fusion.6), channel_id=1, source_target_pairs={{0,2},{1,3},{2,0},{3,1},{4,6},{5,7},{6,4},{7,5},{8,10},{9,11},{10,... | collective-permute-start | bytes 1105928 | tf_op jit(solution)/shard_map/ppermute | solution.py:238
  191.9 8.6 %collective-permute-start.39 = (bf16[360,128]{1,0:T(8,128)(2,1)S(1)}, bf16[360,128]{1,0:T(8,128)(2,1)S(1)}, u32[]{:S(2)}, u32[]{:S(2)}) collective-permute-start(bf16[360,128]{1,0:T(8,128)(2,1)S(1)} %get-tuple-element.115), channel_id=1, source_target_pairs={{0,12},{1,13},{2,14},{3,15},{4,0},{5,1},{6,2},{7,3},{8,4},{9,5},{1... | collective-permute-start | bytes 276488 | tf_op jit(solution)/shard_map/ppermute | solution.py:238
  192.8 8.1 %collective-permute-start.38 = (bf16[360,128]{1,0:T(8,128)(2,1)S(1)}, bf16[360,128]{1,0:T(8,128)(2,1)S(1)}, u32[]{:S(2)}, u32[]{:S(2)}) collective-permute-start(bf16[360,128]{1,0:T(8,128)(2,1)S(1)} %get-tuple-element.116), channel_id=1, source_target_pairs={{0,8},{1,9},{2,10},{3,11},{4,12},{5,13},{6,14},{7,15},{8,0},{9,1},... | collective-permute-start | bytes 276488 | tf_op jit(solution)/shard_map/ppermute | solution.py:238
  194.3 6.6 %collective-permute-start.37 = (bf16[360,128]{1,0:T(8,128)(2,1)S(1)}, bf16[360,128]{1,0:T(8,128)(2,1)S(1)}, u32[]{:S(2)}, u32[]{:S(2)}) collective-permute-start(bf16[360,128]{1,0:T(8,128)(2,1)S(1)} %get-tuple-element.114), channel_id=1, source_target_pairs={{0,4},{1,5},{2,6},{3,7},{4,8},{5,9},{6,10},{7,11},{8,12},{9,13},{1... | collective-permute-start | bytes 276488 | tf_op jit(solution)/shard_map/ppermute | solution.py:238
  200.0 13.8 %collective-permute-start.44 = (bf16[4,128,640]{2,1,0:T(8,128)(2,1)S(1)}, bf16[4,128,640]{2,1,0:T(8,128)(2,1)S(1)}, u32[]{:S(2)}, u32[]{:S(2)}) collective-permute-start(bf16[4,128,640]{2,1,0:T(8,128)(2,1)S(1)} %dynamic-slice_bitcast_fusion.1), channel_id=1, source_target_pairs={{0,2},{1,3},{2,0},{3,1},{4,6},{5,7},{6,4},{7,5},{8,10},{9,11},{10,... | collective-permute-start | bytes 1966088 | tf_op jit(solution)/shard_map/ppermute | solution.py:238
  201.2 12.7 %collective-permute-start.42 = (bf16[360,256]{1,0:T(8,128)(2,1)S(1)}, bf16[360,256]{1,0:T(8,128)(2,1)S(1)}, u32[]{:S(2)}, u32[]{:S(2)}) collective-permute-start(bf16[360,256]{1,0:T(8,128)(2,1)S(1)} %get-tuple-element.83), channel_id=1, source_target_pairs={{0,12},{1,13},{2,14},{3,15},{4,0},{5,1},{6,2},{7,3},{8,4},{9,5},{1... | collective-permute-start | bytes 552968 | tf_op jit(solution)/shard_map/ppermute | solution.py:238
  201.9 15.3 %collective-permute-start.41 = (bf16[360,256]{1,0:T(8,128)(2,1)S(1)}, bf16[360,256]{1,0:T(8,128)(2,1)S(1)}, u32[]{:S(2)}, u32[]{:S(2)}) collective-permute-start(bf16[360,256]{1,0:T(8,128)(2,1)S(1)} %get-tuple-element.84), channel_id=1, source_target_pairs={{0,8},{1,9},{2,10},{3,11},{4,12},{5,13},{6,14},{7,15},{8,0},{9,1},... | collective-permute-start | bytes 552968 | tf_op jit(solution)/shard_map/ppermute | solution.py:238
  203.3 13.9 %collective-permute-start.40 = (bf16[360,256]{1,0:T(8,128)(2,1)S(1)}, bf16[360,256]{1,0:T(8,128)(2,1)S(1)}, u32[]{:S(2)}, u32[]{:S(2)}) collective-permute-start(bf16[360,256]{1,0:T(8,128)(2,1)S(1)} %get-tuple-element.82), channel_id=1, source_target_pairs={{0,4},{1,5},{2,6},{3,7},{4,8},{5,9},{6,10},{7,11},{8,12},{9,13},{1... | collective-permute-start | bytes 552968 | tf_op jit(solution)/shard_map/ppermute | solution.py:238
  217.2 6.3 %collective-permute-start.48 = (bf16[128,640]{1,0:T(8,128)(2,1)S(1)}, bf16[128,640]{1,0:T(8,128)(2,1)S(1)}, u32[]{:S(2)}, u32[]{:S(2)}) collective-permute-start(bf16[128,640]{1,0:T(8,128)(2,1)S(1)} %get-tuple-element.105), channel_id=1, source_target_pairs={{0,12},{1,13},{2,14},{3,15},{4,0},{5,1},{6,2},{7,3},{8,4},{9,5},{1... | collective-permute-start | bytes 491528 | tf_op jit(solution)/shard_map/ppermute | solution.py:238
  217.3 14.9 %collective-permute-start.47 = (bf16[128,640]{1,0:T(8,128)(2,1)S(1)}, bf16[128,640]{1,0:T(8,128)(2,1)S(1)}, u32[]{:S(2)}, u32[]{:S(2)}) collective-permute-start(bf16[128,640]{1,0:T(8,128)(2,1)S(1)} %get-tuple-element.106), channel_id=1, source_target_pairs={{0,8},{1,9},{2,10},{3,11},{4,12},{5,13},{6,14},{7,15},{8,0},{9,1},... | collective-permute-start | bytes 491528 | tf_op jit(solution)/shard_map/ppermute | solution.py:238
  219.8 12.4 %collective-permute-start.46 = (bf16[128,640]{1,0:T(8,128)(2,1)S(1)}, bf16[128,640]{1,0:T(8,128)(2,1)S(1)}, u32[]{:S(2)}, u32[]{:S(2)}) collective-permute-start(bf16[128,640]{1,0:T(8,128)(2,1)S(1)} %get-tuple-element.104), channel_id=1, source_target_pairs={{0,4},{1,5},{2,6},{3,7},{4,8},{5,9},{6,10},{7,11},{8,12},{9,13},{1... | collective-permute-start | bytes 491528 | tf_op jit(solution)/shard_map/ppermute | solution.py:238
  222.0 15.7 %collective-permute-start.45 = (bf16[360,384]{1,0:T(8,128)(2,1)S(1)}, bf16[360,384]{1,0:T(8,128)(2,1)S(1)}, u32[]{:S(2)}, u32[]{:S(2)}) collective-permute-start(bf16[360,384]{1,0:T(8,128)(2,1)S(1)} %pad_maximum_fusion.5), channel_id=1, source_target_pairs={{0,16},{16,0},{1,17},{17,1},{2,18},{18,2},{3,19},{19,3},{4,20},{20... | collective-permute-start | bytes 829448 | tf_op jit(solution)/shard_map/ppermute | solution.py:242
  232.3 4.5 %collective-permute-start.49 = (bf16[64,640]{1,0:T(8,128)(2,1)S(1)}, bf16[64,640]{1,0:T(8,128)(2,1)S(1)}, u32[]{:S(2)}, u32[]{:S(2)}) collective-permute-start(bf16[64,640]{1,0:T(8,128)(2,1)S(1)} %select_convert_fusion.1), channel_id=1, source_target_pairs={{0,16},{16,0},{1,17},{17,1},{2,18},{18,2},{3,19},{19,3},{4,20},{20... | collective-permute-start | bytes 245768 | tf_op jit(solution)/shard_map/ppermute | solution.py:242
  237.7 2.2 copy-start.1
  (8 other events, 11.1 us)

commit v2 on v1

--- a/solution.py
+++ b/solution.py
@@ -281,7 +281,11 @@
 
 
 def sent_on_chip(value, pieces=1):
-    return jnp.concatenate([shifted(piece, dc=1) for piece in jnp.split(value, pieces)])
+    if pieces == 1:
+        return shifted(value, dc=1)
+    flat = value.reshape(-1, *value.shape[-2:])
+    sent = [shifted(piece, dc=1) for piece in jnp.split(flat, pieces)]
+    return jnp.concatenate(sent).reshape(value.shape)
 
 
 def places_of(channels, main):
@@ -366,8 +370,9 @@
     )
 
 
-def gathered_over_y(line):
+def gathered_over_y(line, earlier=None):
     _, y, _ = coordinates()
+    line = after(line, earlier)
     sent = shifted(line, dy=1)
     return in_order(y == 1, line[:, None], sent[:, None], 1), sent
 
@@ -395,12 +400,17 @@
     return added(part_of(value, y, 1), sent).astype(BF16), sent
 
 
+def sent_for_sums(line, earlier=None):
+    z, _, _ = coordinates()
+    line = after(line, earlier)
+    return [
+        shifted(part_of(line, (z + step) % GRID[0], 0), dz=step) for step in range(1, GRID[0])
+    ]
+
+
 def summed_over_z(line, earlier=None):
     z, _, _ = coordinates()
-    line = after(line, earlier)
-    sent = [
-        shifted(part_of(line, (z + step) % GRID[0], 0), dz=step) for step in range(1, GRID[0])
-    ]
+    sent = sent_for_sums(line, earlier)
     return added(part_of(line, z, 0), *sent), sent
 
 
@@ -467,15 +477,13 @@
     pre_grad = pre_grad.astype(F32)
     total = None
     for tap in range(9):
-        moved = moved_rows(pre_grad, masks[8 - tap]).astype(BF16)
-        start = 0
-        for ref in weight_refs:
-            end = start + ref.shape[1]
-            term = dot(
-                moved[:, start:end], ref[tap * channels : (tap + 1) * channels, :], ((1,), (1,))
-            )
-            total = term if total is None else total + term
-            start = end
+        weights = [ref[tap * channels : (tap + 1) * channels, :] for ref in weight_refs]
+        term = dot(
+            moved_rows(pre_grad, masks[8 - tap]).astype(BF16),
+            jnp.concatenate(weights, 1),
+            ((1,), (1,)),
+        )
+        total = term if total is None else total + term
     return total
 
 
@@ -633,7 +641,8 @@
     tails = jnp.where(tail, spatial_own[:, 2 * main :], given[:, main:])
     line, sent = gathered_over_z(jnp.where(first, main_own, main_given), sent)
     line_tails, sent = gathered_over_z(tails, (sent, side))
-    plane_first, side = gathered_over_y(line)
+    plane_low, side = gathered_over_y(line[..., :LANES])
+    plane_high, _ = gathered_over_y(line[..., LANES:], side)
     plane_tails, _ = gathered_over_y(line_tails)
     line_second, _ = gathered_over_z(jnp.where(first, main_given, main_own), (sent, side))
     side_second = shifted(line_second, dy=1)
@@ -643,7 +652,7 @@
     temporal_first = compact(temporal[:, :, 0], first)
     temporal_second = compact(temporal[:, :, 1], me == 1)
     tails = gathered_on_chip(plane_tails)
-    spatial_first = [gathered_on_chip(plane_first), tails]
+    spatial_first = [gathered_on_chip(jnp.concatenate([plane_low, plane_high], 3)), tails]
 
     def shape(extent, dtype=BF16):
         return jax.ShapeDtypeStruct(extent, dtype)
@@ -719,28 +728,42 @@
     )
     chip_temporal = summed_on_chip(terms.reshape(*GRID, -1, channels))
 
-    line, side = summed_over_y(chip_tails, side)
+    line_tails, side = summed_over_y(chip_tails, side)
+    line_temporal, side = summed_over_y(chip_temporal, side)
+    share_tails, sent_tails = summed_over_z(line_tails, sent_second)
     line_low, side = summed_over_y(chip_first[..., :LANES], side)
-    share_tails, sent_tails = summed_over_z(line, (side, sent_second))
-    line_high, side = summed_over_y(chip_first[..., LANES:], side)
-    share_first, sent_first = summed_over_z(
-        jnp.concatenate([line_low, line_high], 2), sent_tails
-    )
-    line, side = summed_over_y(chip_temporal, side)
-    share_temporal, _ = summed_over_z(line, sent_first)
-
-    kept = jnp.where(first, share_first, share_second)
-    passed = jnp.where(first, share_second, share_first)
-    given = jnp.concatenate([passed, share_tails], 1).astype(BF16)
-    given = swapped(after(given, side)).astype(F32)
+    share_temporal, sent_temporal = summed_over_z(line_temporal, sent_tails)
+    line_high, side = summed_over_y(chip_first[..., LANES:], (side, sent_temporal))
+    share_low, sent_low = summed_over_z(line_low)
+    share_high, sent_high = summed_over_z(line_high, sent_low)
+
+    def exchanged(own, earlier=None):
+        return swapped(after(own.astype(BF16), earlier)).astype(F32)
+
+    low, high = (
+        (jnp.where(first, ours, theirs), jnp.where(first, theirs, ours))
+        for ours, theirs in (
+            (share_low, share_second[:, :LANES]),
+            (share_high, share_second[:, LANES:]),
+        )
+    )
+    given = exchanged(jnp.concatenate([low[1], share_tails], 1), sent_high)
+    given_high = exchanged(high[1])
     share_spatial = jnp.concatenate(
-        [kept, given[:, :main], jnp.where(tail, share_tails, given[:, main:])], 1
+        [
+            low[0],
+            high[0],
+            given[:, :LANES],
+            given_high,
+            jnp.where(tail, share_tails, given[:, LANES:]),
+        ],
+        1,
     )
     share_spatial = lax.dot_general(
         share_spatial, order.astype(F32), (((1,), (1,)), ((), ())), precision=lax.Precision.HIGH
     )
     low, high = share_temporal[:PIECE], share_temporal[PIECE:]
-    given = swapped(jnp.where(first, high, low).astype(BF16)).astype(F32)
+    given = exchanged(jnp.where(first, high, low), sent_low)
     share_temporal = shard_of(jnp.where(first, low, high), given, temporal_weight.shape[1])
     return (share_spatial[None], share_temporal[None])
 

time: 244 us -> 253 us (1.037)
  waiting for transfers between devices: 122 us -> 99.9 us
  starting transfers between devices: 52.6 us -> 71.8 us
  other arithmetic: 17.1 us -> 24.9 us
  local copies, waits for them, and re-layouts: 12.3 us -> 18.1 us
  Pallas kernels: 31.7 us -> 28.8 us
    ppermute x44 -> x48, waiting for transfers between devices: 98.4 us -> 73.7 us  [shifted(): return lax.ppermute(value, 'dp', pairs)]
    ppermute x44 -> x48, starting transfers between devices: 43.1 us -> 62.1 us  [shifted(): return lax.ppermute(value, 'dp', pairs)]
    ppermute x6 -> x7, waiting for transfers between devices: 23.2 us -> 26.3 us  [swapped(): return lax.ppermute(value, 'pipe', [(0, 1), (1, 0)])]
    ppermute x6 -> x7, starting transfers between devices: 9.41 us -> 9.7 us  [swapped(): return lax.ppermute(value, 'pipe', [(0, 1), (1, 0)])]
  transfers between devices with their start and end apart: 50 -> 55, of which waited for: 21 -> 29; matrix products, arithmetic and copies ran while one was open for 10% -> 14% of each run, Pallas kernels for 6% -> 6%
where the time goes in v2:
time: 253 us; the launch traced here: 249 us
  waiting for transfers between devices  99.9 us (39%)
  starting transfers between devices  71.8 us (28%)
  Pallas kernels  28.8 us (11%)
  other arithmetic  24.9 us (10%)
  local copies, waits for them, and re-layouts  18.1 us (7%)
  matrix products  2.84 us (1%)
    ppermute x48, waiting for transfers between devices, shifted(): return lax.ppermute(value, 'dp', pairs)  73.7 us
    ppermute x48, starting transfers between devices, shifted(): return lax.ppermute(value, 'dp', pairs)  62.1 us
    ppermute x7, waiting for transfers between devices, swapped(): return lax.ppermute(value, 'pipe', [(0, 1), (1, 0)])  26.3 us
    pallas_call x1, Pallas kernels, paired_device(): vmem_call(functools.partial(second_forward, frames), (shape((rows, channe...  10.5 us
    ppermute x7, starting transfers between devices, swapped(): return lax.ppermute(value, 'pipe', [(0, 1), (1, 0)])  9.7 us
    pallas_call x1, Pallas kernels, paired_device(): vmem_call(functools.partial(first_terms, frames), terms_shape(), flops=sp...  7.74 us
    select_n x13, other arithmetic, in_order(): jnp.where(swap, jnp.concatenate([other, own], axis), jnp.concatenate([own...  7.3 us
    pallas_call x1, Pallas kernels, paired_device(): vmem_call(functools.partial(first_forward, frames), (shape((rows, channel...  6.25 us
  transfers between devices with their start and end apart: 55, of which 29 were waited for; matrix products, arithmetic and copies ran while one was open for 14% of the time, Pallas kernels for 6%

profile of v2, /device:TPU:0, one launch (start us, length us, event | category | flops | bytes accessed | tf_op | source)
XLA Modules:
  0.0 248.7 jit_solution(3513961084830505211)
XLA Ops:
  2.5 3.0 %collective-permute-start = (bf16[64,640]{1,0:T(8,128)(2,1)S(1)}, bf16[64,640]{1,0:T(8,128)(2,1)S(1)}, u32[]{:S(2)}, u32[]{:S(2)}) collective-permute-start(bf16[64,640]{1,0:T(8,128)(2,1)S(1)} %fusion.40), channel_id=1, source_target_pairs={{0,16},{16,0},{1,17},{17,1},{2,18},{18,2},{3,19},{19,3},{4,20},{20... | collective-permute-start | bytes 245768 | tf_op jit(solution)/shard_map/ppermute | solution.py:242
  6.7 1.6 collective-permute-done
  8.3 1.7 collective-permute-start.1
  10.1 2.6 %collective-permute-start.2 = (bf16[128,640]{1,0:T(8,128)(2,1)S(1)}, bf16[128,640]{1,0:T(8,128)(2,1)S(1)}, u32[]{:S(2)}, u32[]{:S(2)}) collective-permute-start(bf16[128,640]{1,0:T(8,128)(2,1)S(1)} %maximum_select_fusion.16), channel_id=1, source_target_pairs={{0,8},{1,9},{2,10},{3,11},{4,12},{5,13},{6,14},{7,15},{8,0},{9,1},... | collective-permute-start | bytes 491528 | tf_op jit(solution)/shard_map/ppermute | solution.py:238
  14.4 2.9 %collective-permute-done.1 = bf16[128,640]{1,0:T(8,128)(2,1)S(1)} collective-permute-done((bf16[128,640]{1,0:T(8,128)(2,1)S(1)}, bf16[128,640]{1,0:T(8,128)(2,1)S(1)}, u32[]{:S(2)}, u32[]{:S(2)}) %collective-permute-start.1) | collective-permute-done | bytes 163872 | tf_op jit(solution)/shard_map/ppermute | solution.py:238
  17.4 4.9 %collective-permute-done.2 = bf16[128,640]{1,0:T(8,128)(2,1)S(1)} collective-permute-done((bf16[128,640]{1,0:T(8,128)(2,1)S(1)}, bf16[128,640]{1,0:T(8,128)(2,1)S(1)}, u32[]{:S(2)}, u32[]{:S(2)}) %collective-permute-start.2) | collective-permute-done | bytes 163872 | tf_op jit(solution)/shard_map/ppermute | solution.py:238
  22.3 4.0 %collective-permute-start.7 = (bf16[360,256]{1,0:T(8,128)(2,1)S(1)}, bf16[360,256]{1,0:T(8,128)(2,1)S(1)}, u32[]{:S(2)}, u32[]{:S(2)}) collective-permute-start(bf16[360,256]{1,0:T(8,128)(2,1)S(1)} %get-tuple-element.32), channel_id=1, source_target_pairs={{0,4},{1,5},{2,6},{3,7},{4,8},{5,9},{6,10},{7,11},{8,12},{9,13},{1... | collective-permute-start | bytes 552968 | tf_op jit(solution)/shard_map/ppermute | solution.py:238
  26.3 1.6 collective-permute-start.8
  29.8 1.5 collective-permute-start.4
  32.6 6.2 %collective-permute-done.8 = bf16[360,256]{1,0:T(8,128)(2,1)S(1)} collective-permute-done((bf16[360,256]{1,0:T(8,128)(2,1)S(1)}, bf16[360,256]{1,0:T(8,128)(2,1)S(1)}, u32[]{:S(2)}, u32[]{:S(2)}) %collective-permute-start.8) | collective-permute-done | bytes 184352 | tf_op jit(solution)/shard_map/ppermute | solution.py:238
  40.0 1.5 collective-permute-start.10
  42.4 5.2 %collective-permute-done.4 = bf16[4,128,640]{2,1,0:T(8,128)(2,1)S(1)} collective-permute-done((bf16[4,128,640]{2,1,0:T(8,128)(2,1)}, bf16[4,128,640]{2,1,0:T(8,128)(2,1)S(1)}, u32[]{:S(2)}, u32[]{:S(2)}) %collective-permute-start.4) | collective-permute-done | bytes 655392 | tf_op jit(solution)/shard_map/ppermute | solution.py:238
  47.7 1.8 collective-permute-start.14
  49.5 2.0 collective-permute-start.15
  51.6 2.5 %collective-permute-done.10 = bf16[4,360,128]{2,1,0:T(8,128)(2,1)} collective-permute-done((bf16[4,360,128]{2,1,0:T(8,128)(2,1)}, bf16[4,360,128]{2,1,0:T(8,128)(2,1)}, u32[]{:S(2)}, u32[]{:S(2)}) %collective-permute-start.10) | collective-permute-done | bytes 368672 | tf_op jit(solution)/shard_map/ppermute | solution.py:238
  54.1 1.5 collective-permute-start.11
  56.1 1.4 collective-permute-start.16
  59.4 1.6 collective-permute-start.19
  61.0 1.7 collective-permute-start.20
  62.7 8.3 %collective-permute-done.16 = bf16[4,360,128]{2,1,0:T(8,128)(2,1)S(1)} collective-permute-done((bf16[4,360,128]{2,1,0:T(8,128)(2,1)S(1)}, bf16[4,360,128]{2,1,0:T(8,128)(2,1)S(1)}, u32[]{:S(2)}, u32[]{:S(2)}) %collective-permute-start.16) | collective-permute-done | bytes 368672 | tf_op jit(solution)/shard_map/ppermute | solution.py:238
  71.0 2.8 %collective-permute-start.21 = (bf16[360,256]{1,0:T(8,128)(2,1)S(1)}, bf16[360,256]{1,0:T(8,128)(2,1)S(1)}, u32[]{:S(2)}, u32[]{:S(2)}) collective-permute-start(bf16[360,256]{1,0:T(8,128)(2,1)S(1)} %get-tuple-element.36), channel_id=1, source_target_pairs={{0,12},{1,13},{2,14},{3,15},{4,0},{5,1},{6,2},{7,3},{8,4},{9,5},{1... | collective-permute-start | bytes 552968 | tf_op jit(solution)/shard_map/ppermute | solution.py:238
  76.3 3.5 %collective-permute-done.21 = bf16[360,256]{1,0:T(8,128)(2,1)S(1)} collective-permute-done((bf16[360,256]{1,0:T(8,128)(2,1)S(1)}, bf16[360,256]{1,0:T(8,128)(2,1)S(1)}, u32[]{:S(2)}, u32[]{:S(2)}) %collective-permute-start.21) | collective-permute-done | bytes 184352 | tf_op jit(solution)/shard_map/ppermute | solution.py:238
  83.3 1.4 slice_bitcast_fusion.3
  86.7 6.2 %shard_map.68 = (bf16[480,640]{1,0:T(8,128)(2,1)S(1)}, f32[480,384]{1,0:T(8,128)S(1)}, bf16[480,640]{1,0:T(8,128)(2,1)S(1)}) custom-call(bf16[480,640]{1,0:T(8,128)(2,1)S(1)} %bitcast.317, f32[5,640]{1,0:T(8,128)S(1)} %pad_maximum_fusion.7.embedding_ref, f32[1,384]{1,0:T(1,128)S(1)} %select_n.875.keep_ref, bf16[960,640]{1,0:T(8,128)(2,1)S(1)} %bitcast.314, ...), custom_call_target="tpu_custom_call" | custom-call | flops 7077888000 | bytes 5898240 | tf_op jit(solution)/shard_map/pallas_call | solution.py:664
  93.0 6.0 %collective-permute-done.22 = bf16[4,360,256]{2,1,0:T(8,128)(2,1)S(1)} collective-permute-done((bf16[4,360,256]{2,1,0:T(8,128)(2,1)S(1)}, bf16[4,360,256]{2,1,0:T(8,128)(2,1)S(1)}, u32[]{:S(2)}, u32[]{:S(2)}) %collective-permute-start.22) | collective-permute-done | bytes 737312 | tf_op jit(solution)/shard_map/ppermute | solution.py:238
  100.4 1.6 collective-permute-start.18
  104.2 1.7 maximum_select_fusion.11
  106.2 2.4 maximum_select_fusion.1
  108.8 7.9 %collective-permute-done.18.sent_ref = bf16[480,640]{1,0:T(8,128)(2,1)} collective-permute-done((bf16[480,640]{1,0:T(8,128)(2,1)S(1)}, bf16[480,640]{1,0:T(8,128)(2,1)}, u32[]{:S(2)}, u32[]{:S(2)}) %collective-permute-start.18) | collective-permute-done | bytes 614432 | tf_op jit(solution)/shard_map/ppermute | solution.py:242
  116.7 10.5 %shard_map.69 = (bf16[480,640]{1,0:T(8,128)(2,1)S(1)}, bf16[480,640]{1,0:T(8,128)(2,1)S(1)}, bf16[480,384]{1,0:T(8,128)(2,1)S(1)}, bf16[480,384]{1,0:T(8,128)(2,1)S(1)}, bf16[480,640]{1,0:T(8,128)(2,1)}) custom-call(bf16[480,640]{1,0:T(8,128)(2,1)S(1)} %bitcast.318, bf16[480,640]{1,0:T(8,128)(2,1)S(1)} %get-tuple-element.35.own_ref, ...), custom_call_target="tpu_custom_call" | custom-call | flops 12386304000 | bytes 5898240 | tf_op jit(solution)/shard_map/pallas_call | solution.py:674
  127.2 4.4 %shard_map.70 = (bf16[5760,256]{1,0:T(8,128)(2,1)S(1)}, bf16[5760,128]{1,0:T(8,128)(2,1)S(1)}, bf16[960,640]{1,0:T(8,128)(2,1)S(1)}) custom-call(bf16[480,640]{1,0:T(8,128)(2,1)S(1)} %get-tuple-element.40.normed_ref, bf16[480,384]{1,0:T(8,128)(2,1)S(1)} %get-tuple-element.41.pre_grad_ref, bf16[480,384]{1,0:T(8,128)(2,1)S(1)} %get-tuple-element.42.activated_ref, ...), custom_call_target="tpu_custom_call" | custom-call | flops 7077888000 | bytes 5898240 | tf_op jit(solution)/shard_map/pallas_call | solution.py:701
  134.9 1.5 collective-permute-start.24
  137.6 1.5 pad_maximum_fusion.1
  140.6 1.4 collective-permute-start.29
  142.0 9.0 %collective-permute-done.24.sent_ref = bf16[480,640]{1,0:T(8,128)(2,1)} collective-permute-done((bf16[480,640]{1,0:T(8,128)(2,1)}, bf16[480,640]{1,0:T(8,128)(2,1)}, u32[]{:S(2)}, u32[]{:S(2)}) %collective-permute-start.24) | collective-permute-done | bytes 614432 | tf_op jit(solution)/shard_map/ppermute | solution.py:242
  151.1 7.7 %shard_map.71 = (bf16[5760,256]{1,0:T(8,128)(2,1)S(1)}, bf16[5760,128]{1,0:T(8,128)(2,1)S(1)}, bf16[960,640]{1,0:T(8,128)(2,1)S(1)}) custom-call(bf16[480,640]{1,0:T(8,128)(2,1)S(1)} %copy-done.16, f32[5,640]{1,0:T(8,128)S(1)} %pad_maximum_fusion.7.embedding_ref, bf16[480,640]{1,0:T(8,128)(2,1)S(1)} %bitcast.321, ...), custom_call_target="tpu_custom_call" | custom-call | flops 8847360000 | bytes 7372800 | tf_op jit(solution)/shard_map/pallas_call | solution.py:711
  165.4 1.5 fusion.5
  167.0 1.4 collective-permute-start.39
  168.5 2.4 collective-permute-start.41
  172.2 1.5 fusion.6
  173.7 1.5 collective-permute-start.33
  175.2 1.6 fusion.2
  177.0 7.3 %collective-permute-done.33 = bf16[4,360,128]{2,1,0:T(8,128)(2,1)S(1)} collective-permute-done((bf16[4,360,128]{2,1,0:T(8,128)(2,1)S(1)}, bf16[4,360,128]{2,1,0:T(8,128)(2,1)S(1)}, u32[]{:S(2)}, u32[]{:S(2)}) %collective-permute-start.33) | collective-permute-done | bytes 368672 | tf_op jit(solution)/shard_map/ppermute | solution.py:238
  184.2 1.4 collective-permute-start.34
  185.9 2.6 %collective-permute-start.42 = (bf16[360,128]{1,0:T(8,128)(2,1)S(1)}, bf16[360,128]{1,0:T(8,128)(2,1)S(1)}, u32[]{:S(2)}, u32[]{:S(2)}) collective-permute-start(bf16[360,128]{1,0:T(8,128)(2,1)S(1)} %get-tuple-element.122), channel_id=1, source_target_pairs={{0,4},{1,5},{2,6},{3,7},{4,8},{5,9},{6,10},{7,11},{8,12},{9,13},{1... | collective-permute-start | bytes 276488 | tf_op jit(solution)/shard_map/ppermute | solution.py:238
  188.6 2.3 collective-permute-start.44
  191.0 2.1 collective-permute-done.42
  193.1 3.2 %collective-permute-done.43 = bf16[360,128]{1,0:T(8,128)(2,1)S(1)} collective-permute-done((bf16[360,128]{1,0:T(8,128)(2,1)S(1)}, bf16[360,128]{1,0:T(8,128)(2,1)S(1)}, u32[]{:S(2)}, u32[]{:S(2)}) %collective-permute-start.43) | collective-permute-done | bytes 92192 | tf_op jit(solution)/shard_map/ppermute | solution.py:238
  196.4 3.6 %collective-permute-done.34 = bf16[4,128,640]{2,1,0:T(8,128)(2,1)S(1)} collective-permute-done((bf16[4,128,640]{2,1,0:T(8,128)(2,1)S(1)}, bf16[4,128,640]{2,1,0:T(8,128)(2,1)S(1)}, u32[]{:S(2)}, u32[]{:S(2)}) %collective-permute-start.34) | collective-permute-done | bytes 655392 | tf_op jit(solution)/shard_map/ppermute | solution.py:238
  202.2 2.6 %collective-permute-start.47 = (bf16[128,640]{1,0:T(8,128)(2,1)S(1)}, bf16[128,640]{1,0:T(8,128)(2,1)S(1)}, u32[]{:S(2)}, u32[]{:S(2)}) collective-permute-start(bf16[128,640]{1,0:T(8,128)(2,1)S(1)} %get-tuple-element.105), channel_id=1, source_target_pairs={{0,12},{1,13},{2,14},{3,15},{4,0},{5,1},{6,2},{7,3},{8,4},{9,5},{1... | collective-permute-start | bytes 491528 | tf_op jit(solution)/shard_map/ppermute | solution.py:238
  205.5 1.5 collective-permute-start.35
  207.1 2.2 collective-permute-done.45
  209.3 4.3 %collective-permute-done.46 = bf16[128,640]{1,0:T(8,128)(2,1)S(1)} collective-permute-done((bf16[128,640]{1,0:T(8,128)(2,1)S(1)}, bf16[128,640]{1,0:T(8,128)(2,1)S(1)}, u32[]{:S(2)}, u32[]{:S(2)}) %collective-permute-start.46) | collective-permute-done | bytes 163872 | tf_op jit(solution)/shard_map/ppermute | solution.py:238
  213.9 3.4 %collective-permute-start.36 = (bf16[360,128]{1,0:T(8,128)(2,1)S(1)}, bf16[360,128]{1,0:T(8,128)(2,1)S(1)}, u32[]{:S(2)}, u32[]{:S(2)}) collective-permute-start(bf16[360,128]{1,0:T(8,128)(2,1)S(1)} %get-tuple-element.123), channel_id=1, source_target_pairs={{0,4},{1,5},{2,6},{3,7},{4,8},{5,9},{6,10},{7,11},{8,12},{9,13},{1... | collective-permute-start | bytes 276488 | tf_op jit(solution)/shard_map/ppermute | solution.py:238
  221.2 3.3 %collective-permute-done.37 = bf16[360,128]{1,0:T(8,128)(2,1)S(1)} collective-permute-done((bf16[360,128]{1,0:T(8,128)(2,1)S(1)}, bf16[360,128]{1,0:T(8,128)(2,1)S(1)}, u32[]{:S(2)}, u32[]{:S(2)}) %collective-permute-start.37) | collective-permute-done | bytes 92192 | tf_op jit(solution)/shard_map/ppermute | solution.py:238
  224.7 1.5 collective-permute-start.54
  226.3 2.9 %collective-permute-done.54 = bf16[64,640]{1,0:T(8,128)(2,1)S(1)} collective-permute-done((bf16[64,640]{1,0:T(8,128)(2,1)S(1)}, bf16[64,640]{1,0:T(8,128)(2,1)S(1)}, u32[]{:S(2)}, u32[]{:S(2)}) %collective-permute-start.54) | collective-permute-done | bytes 81952 | tf_op jit(solution)/shard_map/ppermute | solution.py:242
  229.5 2.3 collective-permute-start.49
  231.7 1.5 collective-permute-start.50
  234.9 1.9 collective-permute-done.49
  236.8 2.7 %collective-permute-done.50 = bf16[360,128]{1,0:T(8,128)(2,1)S(1)} collective-permute-done((bf16[360,128]{1,0:T(8,128)(2,1)S(1)}, bf16[360,128]{1,0:T(8,128)(2,1)S(1)}, u32[]{:S(2)}, u32[]{:S(2)}) %collective-permute-start.50) | collective-permute-done | bytes 92192 | tf_op jit(solution)/shard_map/ppermute | solution.py:238
  239.7 1.5 collective-permute-start.52
  241.8 3.5 %collective-permute-done.52 = bf16[360,256]{1,0:T(8,128)(2,1)S(1)} collective-permute-done((bf16[360,256]{1,0:T(8,128)(2,1)S(1)}, bf16[360,256]{1,0:T(8,128)(2,1)S(1)}, u32[]{:S(2)}, u32[]{:S(2)}) %collective-permute-start.52) | collective-permute-done | bytes 184352 | tf_op jit(solution)/shard_map/ppermute | solution.py:242
  246.4 2.1 fusion.7
  (220 shorter events, 49.3 us)
Async XLA Ops:
  2.5 5.8 %collective-permute-start = (bf16[64,640]{1,0:T(8,128)(2,1)S(1)}, bf16[64,640]{1,0:T(8,128)(2,1)S(1)}, u32[]{:S(2)}, u32[]{:S(2)}) collective-permute-start(bf16[64,640]{1,0:T(8,128)(2,1)S(1)} %fusion.40), channel_id=1, source_target_pairs={{0,16},{16,0},{1,17},{17,1},{2,18},{18,2},{3,19},{19,3},{4,20},{20... | collective-permute-start | bytes 245768 | tf_op jit(solution)/shard_map/ppermute | solution.py:242
  6.3 8.1 %collective-permute-start.6 = (bf16[360,384]{1,0:T(8,128)(2,1)S(1)}, bf16[360,384]{1,0:T(8,128)(2,1)S(1)}, u32[]{:S(2)}, u32[]{:S(2)}) collective-permute-start(bf16[360,384]{1,0:T(8,128)(2,1)S(1)} %slice.282), channel_id=1, source_target_pairs={{0,16},{16,0},{1,17},{17,1},{2,18},{18,2},{3,19},{19,3},{4,20},{20... | collective-permute-start | bytes 829448 | tf_op jit(solution)/shard_map/ppermute | solution.py:242
  8.3 9.1 %collective-permute-start.1 = (bf16[128,640]{1,0:T(8,128)(2,1)S(1)}, bf16[128,640]{1,0:T(8,128)(2,1)S(1)}, u32[]{:S(2)}, u32[]{:S(2)}) collective-permute-start(bf16[128,640]{1,0:T(8,128)(2,1)S(1)} %maximum_select_fusion.16), channel_id=1, source_target_pairs={{0,4},{1,5},{2,6},{3,7},{4,8},{5,9},{6,10},{7,11},{8,12},{9,13},{1... | collective-permute-start | bytes 491528 | tf_op jit(solution)/shard_map/ppermute | solution.py:238
  10.1 12.2 %collective-permute-start.2 = (bf16[128,640]{1,0:T(8,128)(2,1)S(1)}, bf16[128,640]{1,0:T(8,128)(2,1)S(1)}, u32[]{:S(2)}, u32[]{:S(2)}) collective-permute-start(bf16[128,640]{1,0:T(8,128)(2,1)S(1)} %maximum_select_fusion.16), channel_id=1, source_target_pairs={{0,8},{1,9},{2,10},{3,11},{4,12},{5,13},{6,14},{7,15},{8,0},{9,1},... | collective-permute-start | bytes 491528 | tf_op jit(solution)/shard_map/ppermute | solution.py:238
  12.7 9.6 %collective-permute-start.3 = (bf16[128,640]{1,0:T(8,128)(2,1)S(1)}, bf16[128,640]{1,0:T(8,128)(2,1)S(1)}, u32[]{:S(2)}, u32[]{:S(2)}) collective-permute-start(bf16[128,640]{1,0:T(8,128)(2,1)S(1)} %maximum_select_fusion.16), channel_id=1, source_target_pairs={{0,12},{1,13},{2,14},{3,15},{4,0},{5,1},{6,2},{7,3},{8,4},{9,5},{1... | collective-permute-start | bytes 491528 | tf_op jit(solution)/shard_map/ppermute | solution.py:238
  14.4 15.4 %copy-start.26 = (bf16[360,384]{1,0:T(8,128)(2,1)}, bf16[360,384]{1,0:T(8,128)(2,1)S(1)}, u32[]{:S(2)}) copy-start(bf16[360,384]{1,0:T(8,128)(2,1)S(1)} %collective-permute-done.6) | copy-start | bytes 829444
  22.3 10.3 %collective-permute-start.7 = (bf16[360,256]{1,0:T(8,128)(2,1)S(1)}, bf16[360,256]{1,0:T(8,128)(2,1)S(1)}, u32[]{:S(2)}, u32[]{:S(2)}) collective-permute-start(bf16[360,256]{1,0:T(8,128)(2,1)S(1)} %get-tuple-element.32), channel_id=1, source_target_pairs={{0,4},{1,5},{2,6},{3,7},{4,8},{5,9},{6,10},{7,11},{8,12},{9,13},{1... | collective-permute-start | bytes 552968 | tf_op jit(solution)/shard_map/ppermute | solution.py:238
  26.3 12.5 %collective-permute-start.8 = (bf16[360,256]{1,0:T(8,128)(2,1)S(1)}, bf16[360,256]{1,0:T(8,128)(2,1)S(1)}, u32[]{:S(2)}, u32[]{:S(2)}) collective-permute-start(bf16[360,256]{1,0:T(8,128)(2,1)S(1)} %get-tuple-element.32), channel_id=1, source_target_pairs={{0,8},{1,9},{2,10},{3,11},{4,12},{5,13},{6,14},{7,15},{8,0},{9,1},... | collective-permute-start | bytes 552968 | tf_op jit(solution)/shard_map/ppermute | solution.py:238
  27.9 10.9 %collective-permute-start.9 = (bf16[360,256]{1,0:T(8,128)(2,1)S(1)}, bf16[360,256]{1,0:T(8,128)(2,1)S(1)}, u32[]{:S(2)}, u32[]{:S(2)}) collective-permute-start(bf16[360,256]{1,0:T(8,128)(2,1)S(1)} %get-tuple-element.32), channel_id=1, source_target_pairs={{0,12},{1,13},{2,14},{3,15},{4,0},{5,1},{6,2},{7,3},{8,4},{9,5},{1... | collective-permute-start | bytes 552968 | tf_op jit(solution)/shard_map/ppermute | solution.py:238
  29.8 17.9 %collective-permute-start.4 = (bf16[4,128,640]{2,1,0:T(8,128)(2,1)}, bf16[4,128,640]{2,1,0:T(8,128)(2,1)S(1)}, u32[]{:S(2)}, u32[]{:S(2)}) collective-permute-start(bf16[4,128,640]{2,1,0:T(8,128)(2,1)} %get-tuple-element.110), channel_id=1, source_target_pairs={{0,2},{1,3},{2,0},{3,1},{4,6},{5,7},{6,4},{7,5},{8,10},{9,11},{10,... | collective-permute-start | bytes 1966088 | tf_op jit(solution)/shard_map/ppermute | solution.py:238
  40.0 14.1 %collective-permute-start.10 = (bf16[4,360,128]{2,1,0:T(8,128)(2,1)}, bf16[4,360,128]{2,1,0:T(8,128)(2,1)}, u32[]{:S(2)}, u32[]{:S(2)}) collective-permute-start(bf16[4,360,128]{2,1,0:T(8,128)(2,1)} %get-tuple-element.100), channel_id=1, source_target_pairs={{0,2},{1,3},{2,0},{3,1},{4,6},{5,7},{6,4},{7,5},{8,10},{9,11},{10,... | collective-permute-start | bytes 1105928 | tf_op jit(solution)/shard_map/ppermute | solution.py:238
  47.7 7.9 %collective-permute-start.13 = (bf16[360,128]{1,0:T(8,128)(2,1)S(1)}, bf16[360,128]{1,0:T(8,128)(2,1)S(1)}, u32[]{:S(2)}, u32[]{:S(2)}) collective-permute-start(bf16[360,128]{1,0:T(8,128)(2,1)S(1)} %slice_select_fusion.2), channel_id=1, source_target_pairs={{0,4},{1,5},{2,6},{3,7},{4,8},{5,9},{6,10},{7,11},{8,12},{9,13},{1... | collective-permute-start | bytes 276488 | tf_op jit(solution)/shard_map/ppermute | solution.py:238
  47.7 8.3 %collective-permute-start.14 = (bf16[360,128]{1,0:T(8,128)(2,1)S(1)}, bf16[360,128]{1,0:T(8,128)(2,1)S(1)}, u32[]{:S(2)}, u32[]{:S(2)}) collective-permute-start(bf16[360,128]{1,0:T(8,128)(2,1)S(1)} %slice_select_fusion.2), channel_id=1, source_target_pairs={{0,8},{1,9},{2,10},{3,11},{4,12},{5,13},{6,14},{7,15},{8,0},{9,1},... | collective-permute-start | bytes 276488 | tf_op jit(solution)/shard_map/ppermute | solution.py:238
  49.5 6.4 %collective-permute-start.15 = (bf16[360,128]{1,0:T(8,128)(2,1)S(1)}, bf16[360,128]{1,0:T(8,128)(2,1)S(1)}, u32[]{:S(2)}, u32[]{:S(2)}) collective-permute-start(bf16[360,128]{1,0:T(8,128)(2,1)S(1)} %slice_select_fusion.2), channel_id=1, source_target_pairs={{0,12},{1,13},{2,14},{3,15},{4,0},{5,1},{6,2},{7,3},{8,4},{9,5},{1... | collective-permute-start | bytes 276488 | tf_op jit(solution)/shard_map/ppermute | solution.py:238
  54.1 19.9 %collective-permute-start.11 = (bf16[4,360,128]{2,1,0:T(8,128)(2,1)S(1)}, bf16[4,360,128]{2,1,0:T(8,128)(2,1)S(1)}, u32[]{:S(2)}, u32[]{:S(2)}) collective-permute-start(bf16[4,360,128]{2,1,0:T(8,128)(2,1)S(1)} %get-tuple-element.33), channel_id=1, source_target_pairs={{0,2},{1,3},{2,0},{3,1},{4,6},{5,7},{6,4},{7,5},{8,10},{9,11},{10,... | collective-permute-start | bytes 1105928 | tf_op jit(solution)/shard_map/ppermute | solution.py:238
  56.1 14.9 %collective-permute-start.16 = (bf16[4,360,128]{2,1,0:T(8,128)(2,1)S(1)}, bf16[4,360,128]{2,1,0:T(8,128)(2,1)S(1)}, u32[]{:S(2)}, u32[]{:S(2)}) collective-permute-start(bf16[4,360,128]{2,1,0:T(8,128)(2,1)S(1)} %get-tuple-element.128), channel_id=1, source_target_pairs={{0,2},{1,3},{2,0},{3,1},{4,6},{5,7},{6,4},{7,5},{8,10},{9,11},{10,... | collective-permute-start | bytes 1105928 | tf_op jit(solution)/shard_map/ppermute | solution.py:238
  57.7 24.7 %collective-permute-start.5 = (bf16[4,2,128,640]{3,2,1,0:T(8,128)(2,1)S(1)}, bf16[4,2,128,640]{3,2,1,0:T(8,128)(2,1)S(1)}, u32[]{:S(2)}, u32[]{:S(2)}) collective-permute-start(bf16[4,2,128,640]{3,2,1,0:T(8,128)(2,1)S(1)} %maximum_select_fusion.6), channel_id=1, source_target_pairs={{0,1},{1,0},{2,3},{3,2},{4,5},{5,4},{6,7},{7,6},{8,9},{9,8},{10,11... | collective-permute-start | bytes 3932168 | tf_op jit(solution)/shard_map/ppermute | solution.py:238
  59.4 15.0 %collective-permute-start.19 = (bf16[360,256]{1,0:T(8,128)(2,1)S(1)}, bf16[360,256]{1,0:T(8,128)(2,1)S(1)}, u32[]{:S(2)}, u32[]{:S(2)}) collective-permute-start(bf16[360,256]{1,0:T(8,128)(2,1)S(1)} %get-tuple-element.36), channel_id=1, source_target_pairs={{0,4},{1,5},{2,6},{3,7},{4,8},{5,9},{6,10},{7,11},{8,12},{9,13},{1... | collective-permute-start | bytes 552968 | tf_op jit(solution)/shard_map/ppermute | solution.py:238
  61.0 15.3 %collective-permute-start.20 = (bf16[360,256]{1,0:T(8,128)(2,1)S(1)}, bf16[360,256]{1,0:T(8,128)(2,1)S(1)}, u32[]{:S(2)}, u32[]{:S(2)}) collective-permute-start(bf16[360,256]{1,0:T(8,128)(2,1)S(1)} %get-tuple-element.36), channel_id=1, source_target_pairs={{0,8},{1,9},{2,10},{3,11},{4,12},{5,13},{6,14},{7,15},{8,0},{9,1},... | collective-permute-start | bytes 552968 | tf_op jit(solution)/shard_map/ppermute | solution.py:238
  71.0 8.8 %collective-permute-start.21 = (bf16[360,256]{1,0:T(8,128)(2,1)S(1)}, bf16[360,256]{1,0:T(8,128)(2,1)S(1)}, u32[]{:S(2)}, u32[]{:S(2)}) collective-permute-start(bf16[360,256]{1,0:T(8,128)(2,1)S(1)} %get-tuple-element.36), channel_id=1, source_target_pairs={{0,12},{1,13},{2,14},{3,15},{4,0},{5,1},{6,2},{7,3},{8,4},{9,5},{1... | collective-permute-start | bytes 552968 | tf_op jit(solution)/shard_map/ppermute | solution.py:238
  74.0 8.1 %collective-permute-start.17 = (bf16[4,2,360,128]{3,2,0,1:T(8,128)(2,1)S(1)}, bf16[4,2,360,128]{3,2,0,1:T(8,128)(2,1)S(1)}, u32[]{:S(2)}, u32[]{:S(2)}) collective-permute-start(bf16[4,2,360,128]{3,2,0,1:T(8,128)(2,1)S(1)} %maximum_select_fusion.14), channel_id=1, source_target_pairs={{0,1},{1,0},{2,3},{3,2},{4,5},{5,4},{6,7},{7,6},{8,9},{9,8},{10,11... | collective-permute-start | bytes 2211848 | tf_op jit(solution)/shard_map/ppermute | solution.py:238
  74.4 10.7 %collective-permute-start.12 = (bf16[4,2,360,256]{3,2,0,1:T(8,128)(2,1)S(1)}, bf16[4,2,360,256]{3,2,0,1:T(8,128)(2,1)S(1)}, u32[]{:S(2)}, u32[]{:S(2)}) collective-permute-start(bf16[4,2,360,256]{3,2,0,1:T(8,128)(2,1)S(1)} %get-tuple-element.74), channel_id=1, source_target_pairs={{0,1},{1,0},{2,3},{3,2},{4,5},{5,4},{6,7},{7,6},{8,9},{9,8},{10,11... | collective-permute-start | bytes 4423688 | tf_op jit(solution)/shard_map/ppermute | solution.py:238
  80.9 18.0 %collective-permute-start.22 = (bf16[4,360,256]{2,1,0:T(8,128)(2,1)S(1)}, bf16[4,360,256]{2,1,0:T(8,128)(2,1)S(1)}, u32[]{:S(2)}, u32[]{:S(2)}) collective-permute-start(bf16[4,360,256]{2,1,0:T(8,128)(2,1)S(1)} %get-tuple-element.91), channel_id=1, source_target_pairs={{0,2},{1,3},{2,0},{3,1},{4,6},{5,7},{6,4},{7,5},{8,10},{9,11},{10,... | collective-permute-start | bytes 2211848 | tf_op jit(solution)/shard_map/ppermute | solution.py:238
  100.3 5.9 %collective-permute-start.23 = (bf16[4,2,360,256]{3,2,0,1:T(8,128)(2,1)}, bf16[4,2,360,256]{3,2,0,1:T(8,128)(2,1)}, u32[]{:S(2)}, u32[]{:S(2)}) collective-permute-start(bf16[4,2,360,256]{3,2,0,1:T(8,128)(2,1)} %maximum_select_fusion.4), channel_id=1, source_target_pairs={{0,1},{1,0},{2,3},{3,2},{4,5},{5,4},{6,7},{7,6},{8,9},{9,8},{10,11... | collective-permute-start | bytes 4423688 | tf_op jit(solution)/shard_map/ppermute | solution.py:238
  100.4 16.4 %collective-permute-start.18 = (bf16[480,640]{1,0:T(8,128)(2,1)S(1)}, bf16[480,640]{1,0:T(8,128)(2,1)}, u32[]{:S(2)}, u32[]{:S(2)}) collective-permute-start(bf16[480,640]{1,0:T(8,128)(2,1)S(1)} %get-tuple-element.35.own_ref), channel_id=1, source_target_pairs={{0,16},{16,0},{1,17},{17,1},{2,18},{18,2},{3,19},{19,3},{4,20},{20... | collective-permute-start | bytes 1843208 | tf_op jit(solution)/shard_map/ppermute | solution.py:242
  108.6 8.2 %copy-start.9 = (bf16[5,3,32,640]{3,2,1,0:T(8,128)(2,1)S(1)}, bf16[5,3,32,640]{3,2,1,0:T(8,128)(2,1)}, u32[]{:S(2)}) copy-start(bf16[5,3,32,640]{3,2,1,0:T(8,128)(2,1)} %param.7) | copy-start | bytes 1843204
  133.8 3.8 %collective-permute-start.25 = (bf16[2,360,256]{2,1,0:T(8,128)(2,1)}, bf16[2,360,256]{2,1,0:T(8,128)(2,1)}, u32[]{:S(2)}, u32[]{:S(2)}) collective-permute-start(bf16[2,360,256]{2,1,0:T(8,128)(2,1)} %get-tuple-element.64), channel_id=1, source_target_pairs={{0,1},{1,0},{2,3},{3,2},{4,5},{5,4},{6,7},{7,6},{8,9},{9,8},{10,11... | collective-permute-start | bytes 1105928 | tf_op jit(solution)/shard_map/ppermute | solution.py:238
  133.9 3.7 %collective-permute-start.26 = (bf16[2,360,256]{2,1,0:T(8,128)(2,1)}, bf16[2,360,256]{2,1,0:T(8,128)(2,1)}, u32[]{:S(2)}, u32[]{:S(2)}) collective-permute-start(bf16[2,360,256]{2,1,0:T(8,128)(2,1)} %get-tuple-element.66), channel_id=1, source_target_pairs={{0,1},{1,0},{2,3},{3,2},{4,5},{5,4},{6,7},{7,6},{8,9},{9,8},{10,11... | collective-permute-start | bytes 1105928 | tf_op jit(solution)/shard_map/ppermute | solution.py:238
  134.4 3.2 %collective-permute-start.27 = (bf16[2,360,256]{2,1,0:T(8,128)(2,1)}, bf16[2,360,256]{2,1,0:T(8,128)(2,1)}, u32[]{:S(2)}, u32[]{:S(2)}) collective-permute-start(bf16[2,360,256]{2,1,0:T(8,128)(2,1)} %get-tuple-element.65), channel_id=1, source_target_pairs={{0,1},{1,0},{2,3},{3,2},{4,5},{5,4},{6,7},{7,6},{8,9},{9,8},{10,11... | collective-permute-start | bytes 1105928 | tf_op jit(solution)/shard_map/ppermute | solution.py:238
  134.5 3.1 %collective-permute-start.28 = (bf16[2,360,256]{2,1,0:T(8,128)(2,1)S(1)}, bf16[2,360,256]{2,1,0:T(8,128)(2,1)}, u32[]{:S(2)}, u32[]{:S(2)}) collective-permute-start(bf16[2,360,256]{2,1,0:T(8,128)(2,1)S(1)} %get-tuple-element.67), channel_id=1, source_target_pairs={{0,1},{1,0},{2,3},{3,2},{4,5},{5,4},{6,7},{7,6},{8,9},{9,8},{10,11... | collective-permute-start | bytes 1105928 | tf_op jit(solution)/shard_map/ppermute | solution.py:238
  134.9 16.2 %collective-permute-start.24 = (bf16[480,640]{1,0:T(8,128)(2,1)}, bf16[480,640]{1,0:T(8,128)(2,1)}, u32[]{:S(2)}, u32[]{:S(2)}) collective-permute-start(bf16[480,640]{1,0:T(8,128)(2,1)} %get-tuple-element.39.own_ref), channel_id=1, source_target_pairs={{0,16},{16,0},{1,17},{17,1},{2,18},{18,2},{3,19},{19,3},{4,20},{20... | collective-permute-start | bytes 1843208 | tf_op jit(solution)/shard_map/ppermute | solution.py:242
  139.2 11.9 %copy-start.10 = (bf16[5,3,32,640]{3,2,1,0:T(8,128)(2,1)S(1)}, bf16[5,3,32,640]{3,2,1,0:T(8,128)(2,1)}, u32[]{:S(2)}) copy-start(bf16[5,3,32,640]{3,2,1,0:T(8,128)(2,1)} %param.7) | copy-start | bytes 1843204
  139.2 11.9 %copy-start.12 = (f32[480,384]{1,0:T(8,128)S(1)}, f32[480,384]{1,0:T(8,128)}, u32[]{:S(2)}) copy-start(f32[480,384]{1,0:T(8,128)} %copy-done.11) | copy-start | bytes 2211844
  139.2 11.9 %copy-start.14 = (bf16[480,640]{1,0:T(8,128)(2,1)S(1)}, bf16[480,640]{1,0:T(8,128)(2,1)}, u32[]{:S(2)}) copy-start(bf16[480,640]{1,0:T(8,128)(2,1)} %copy-done.13) | copy-start | bytes 1843204
  139.2 11.9 %copy-start.16 = (bf16[480,640]{1,0:T(8,128)(2,1)S(1)}, bf16[480,640]{1,0:T(8,128)(2,1)}, u32[]{:S(2)}) copy-start(bf16[480,640]{1,0:T(8,128)(2,1)} %copy-done.15) | copy-start | bytes 1843204
  139.7 11.4 %copy-start.21 = (bf16[4,2,360,256]{3,2,0,1:T(8,128)(2,1)}, bf16[4,2,360,256]{3,2,0,1:T(8,128)(2,1)S(1)}, u32[]{:S(2)}) copy-start(bf16[4,2,360,256]{3,2,0,1:T(8,128)(2,1)S(1)} %fusion.1) | copy-start | bytes 4423684
  139.7 11.4 %copy-start.7 = (bf16[8,120,640]{2,1,0:T(8,128)(2,1)S(1)}, bf16[8,120,640]{2,1,0:T(8,128)(2,1)}, u32[]{:S(2)}) copy-start(bf16[8,120,640]{2,1,0:T(8,128)(2,1)} %copy-done.6) | copy-start | bytes 3686404
  140.6 24.8 %collective-permute-start.29 = (bf16[4,360,256]{2,1,0:T(8,128)(2,1)}, bf16[4,360,256]{2,1,0:T(8,128)(2,1)}, u32[]{:S(2)}, u32[]{:S(2)}) collective-permute-start(bf16[4,360,256]{2,1,0:T(8,128)(2,1)} %dynamic-slice_bitcast_fusion), channel_id=1, source_target_pairs={{0,2},{1,3},{2,0},{3,1},{4,6},{5,7},{6,4},{7,5},{8,10},{9,11},{10,... | collective-permute-start | bytes 2211848 | tf_op jit(solution)/shard_map/ppermute | solution.py:238
  151.1 7.8 %copy-start.3 = (bf16[960,640]{1,0:T(8,128)(2,1)S(1)}, bf16[960,640]{1,0:T(8,128)(2,1)}, u32[]{:S(2)}) copy-start(bf16[960,640]{1,0:T(8,128)(2,1)} %copy-done.2) | copy-start | bytes 3686404
  162.3 11.5 %collective-permute-start.31 = (bf16[4,2,128,640]{3,2,1,0:T(8,128)(2,1)}, bf16[4,2,128,640]{3,2,1,0:T(8,128)(2,1)}, u32[]{:S(2)}, u32[]{:S(2)}) collective-permute-start(bf16[4,2,128,640]{3,2,1,0:T(8,128)(2,1)} %fusion.9), channel_id=1, source_target_pairs={{0,1},{1,0},{2,3},{3,2},{4,5},{5,4},{6,7},{7,6},{8,9},{9,8},{10,11... | collective-permute-start | bytes 3932168 | tf_op jit(solution)/shard_map/ppermute | solution.py:238
  165.4 5.8 %collective-permute-start.32 = (bf16[4,2,360,128]{3,2,0,1:T(8,128)(2,1)}, bf16[4,2,360,128]{3,2,0,1:T(8,128)(2,1)}, u32[]{:S(2)}, u32[]{:S(2)}) collective-permute-start(bf16[4,2,360,128]{3,2,0,1:T(8,128)(2,1)} %bitcast.302), channel_id=1, source_target_pairs={{0,1},{1,0},{2,3},{3,2},{4,5},{5,4},{6,7},{7,6},{8,9},{9,8},{10,11... | collective-permute-start | bytes 2211848 | tf_op jit(solution)/shard_map/ppermute | solution.py:238
  167.0 18.8 %collective-permute-start.39 = (bf16[360,256]{1,0:T(8,128)(2,1)S(1)}, bf16[360,256]{1,0:T(8,128)(2,1)S(1)}, u32[]{:S(2)}, u32[]{:S(2)}) collective-permute-start(bf16[360,256]{1,0:T(8,128)(2,1)S(1)} %get-tuple-element.86), channel_id=1, source_target_pairs={{0,4},{1,5},{2,6},{3,7},{4,8},{5,9},{6,10},{7,11},{8,12},{9,13},{1... | collective-permute-start | bytes 552968 | tf_op jit(solution)/shard_map/ppermute | solution.py:238
  168.4 17.4 %collective-permute-start.40 = (bf16[360,256]{1,0:T(8,128)(2,1)S(1)}, bf16[360,256]{1,0:T(8,128)(2,1)S(1)}, u32[]{:S(2)}, u32[]{:S(2)}) collective-permute-start(bf16[360,256]{1,0:T(8,128)(2,1)S(1)} %get-tuple-element.88), channel_id=1, source_target_pairs={{0,8},{1,9},{2,10},{3,11},{4,12},{5,13},{6,14},{7,15},{8,0},{9,1},... | collective-permute-start | bytes 552968 | tf_op jit(solution)/shard_map/ppermute | solution.py:238
  168.5 17.4 %collective-permute-start.41 = (bf16[360,256]{1,0:T(8,128)(2,1)S(1)}, bf16[360,256]{1,0:T(8,128)(2,1)S(1)}, u32[]{:S(2)}, u32[]{:S(2)}) collective-permute-start(bf16[360,256]{1,0:T(8,128)(2,1)S(1)} %get-tuple-element.87), channel_id=1, source_target_pairs={{0,12},{1,13},{2,14},{3,15},{4,0},{5,1},{6,2},{7,3},{8,4},{9,5},{1... | collective-permute-start | bytes 552968 | tf_op jit(solution)/shard_map/ppermute | solution.py:238
  171.2 33.6 %collective-permute-start.30 = (bf16[4,2,360,256]{3,2,0,1:T(8,128)(2,1)S(1)}, bf16[4,2,360,256]{3,2,0,1:T(8,128)(2,1)S(1)}, u32[]{:S(2)}, u32[]{:S(2)}) collective-permute-start(bf16[4,2,360,256]{3,2,0,1:T(8,128)(2,1)S(1)} %bitcast.338), channel_id=1, source_target_pairs={{0,1},{1,0},{2,3},{3,2},{4,5},{5,4},{6,7},{7,6},{8,9},{9,8},{10,11... | collective-permute-start | bytes 4423688 | tf_op jit(solution)/shard_map/ppermute | solution.py:238
  173.7 10.5 %collective-permute-start.33 = (bf16[4,360,128]{2,1,0:T(8,128)(2,1)S(1)}, bf16[4,360,128]{2,1,0:T(8,128)(2,1)S(1)}, u32[]{:S(2)}, u32[]{:S(2)}) collective-permute-start(bf16[4,360,128]{2,1,0:T(8,128)(2,1)S(1)} %dynamic-slice_bitcast_fusion.7), channel_id=1, source_target_pairs={{0,2},{1,3},{2,0},{3,1},{4,6},{5,7},{6,4},{7,5},{8,10},{9,11},{10,... | collective-permute-start | bytes 1105928 | tf_op jit(solution)/shard_map/ppermute | solution.py:238
  184.2 15.7 %collective-permute-start.34 = (bf16[4,128,640]{2,1,0:T(8,128)(2,1)S(1)}, bf16[4,128,640]{2,1,0:T(8,128)(2,1)S(1)}, u32[]{:S(2)}, u32[]{:S(2)}) collective-permute-start(bf16[4,128,640]{2,1,0:T(8,128)(2,1)S(1)} %dynamic-slice_bitcast_fusion.1), channel_id=1, source_target_pairs={{0,2},{1,3},{2,0},{3,1},{4,6},{5,7},{6,4},{7,5},{8,10},{9,11},{10,... | collective-permute-start | bytes 1966088 | tf_op jit(solution)/shard_map/ppermute | solution.py:238
  185.9 7.3 %collective-permute-start.42 = (bf16[360,128]{1,0:T(8,128)(2,1)S(1)}, bf16[360,128]{1,0:T(8,128)(2,1)S(1)}, u32[]{:S(2)}, u32[]{:S(2)}) collective-permute-start(bf16[360,128]{1,0:T(8,128)(2,1)S(1)} %get-tuple-element.122), channel_id=1, source_target_pairs={{0,4},{1,5},{2,6},{3,7},{4,8},{5,9},{6,10},{7,11},{8,12},{9,13},{1... | collective-permute-start | bytes 276488 | tf_op jit(solution)/shard_map/ppermute | solution.py:238
  188.4 7.9 %collective-permute-start.43 = (bf16[360,128]{1,0:T(8,128)(2,1)S(1)}, bf16[360,128]{1,0:T(8,128)(2,1)S(1)}, u32[]{:S(2)}, u32[]{:S(2)}) collective-permute-start(bf16[360,128]{1,0:T(8,128)(2,1)S(1)} %get-tuple-element.121), channel_id=1, source_target_pairs={{0,8},{1,9},{2,10},{3,11},{4,12},{5,13},{6,14},{7,15},{8,0},{9,1},... | collective-permute-start | bytes 276488 | tf_op jit(solution)/shard_map/ppermute | solution.py:238
  188.6 7.7 %collective-permute-start.44 = (bf16[360,128]{1,0:T(8,128)(2,1)S(1)}, bf16[360,128]{1,0:T(8,128)(2,1)S(1)}, u32[]{:S(2)}, u32[]{:S(2)}) collective-permute-start(bf16[360,128]{1,0:T(8,128)(2,1)S(1)} %get-tuple-element.120), channel_id=1, source_target_pairs={{0,12},{1,13},{2,14},{3,15},{4,0},{5,1},{6,2},{7,3},{8,4},{9,5},{1... | collective-permute-start | bytes 276488 | tf_op jit(solution)/shard_map/ppermute | solution.py:238
  200.2 9.0 %collective-permute-start.45 = (bf16[128,640]{1,0:T(8,128)(2,1)S(1)}, bf16[128,640]{1,0:T(8,128)(2,1)S(1)}, u32[]{:S(2)}, u32[]{:S(2)}) collective-permute-start(bf16[128,640]{1,0:T(8,128)(2,1)S(1)} %get-tuple-element.107), channel_id=1, source_target_pairs={{0,4},{1,5},{2,6},{3,7},{4,8},{5,9},{6,10},{7,11},{8,12},{9,13},{1... | collective-permute-start | bytes 491528 | tf_op jit(solution)/shard_map/ppermute | solution.py:238
  200.8 12.8 %collective-permute-start.46 = (bf16[128,640]{1,0:T(8,128)(2,1)S(1)}, bf16[128,640]{1,0:T(8,128)(2,1)S(1)}, u32[]{:S(2)}, u32[]{:S(2)}) collective-permute-start(bf16[128,640]{1,0:T(8,128)(2,1)S(1)} %get-tuple-element.106), channel_id=1, source_target_pairs={{0,8},{1,9},{2,10},{3,11},{4,12},{5,13},{6,14},{7,15},{8,0},{9,1},... | collective-permute-start | bytes 491528 | tf_op jit(solution)/shard_map/ppermute | solution.py:238
  202.2 11.4 %collective-permute-start.47 = (bf16[128,640]{1,0:T(8,128)(2,1)S(1)}, bf16[128,640]{1,0:T(8,128)(2,1)S(1)}, u32[]{:S(2)}, u32[]{:S(2)}) collective-permute-start(bf16[128,640]{1,0:T(8,128)(2,1)S(1)} %get-tuple-element.105), channel_id=1, source_target_pairs={{0,12},{1,13},{2,14},{3,15},{4,0},{5,1},{6,2},{7,3},{8,4},{9,5},{1... | collective-permute-start | bytes 491528 | tf_op jit(solution)/shard_map/ppermute | solution.py:238
  205.5 8.2 %collective-permute-start.35 = (bf16[4,360,128]{2,1,0:T(8,128)(2,1)S(1)}, bf16[4,360,128]{2,1,0:T(8,128)(2,1)S(1)}, u32[]{:S(2)}, u32[]{:S(2)}) collective-permute-start(bf16[4,360,128]{2,1,0:T(8,128)(2,1)S(1)} %dynamic-slice_bitcast_fusion.8), channel_id=1, source_target_pairs={{0,2},{1,3},{2,0},{3,1},{4,6},{5,7},{6,4},{7,5},{8,10},{9,11},{10,... | collective-permute-start | bytes 1105928 | tf_op jit(solution)/shard_map/ppermute | solution.py:238
  213.9 7.3 %collective-permute-start.36 = (bf16[360,128]{1,0:T(8,128)(2,1)S(1)}, bf16[360,128]{1,0:T(8,128)(2,1)S(1)}, u32[]{:S(2)}, u32[]{:S(2)}) collective-permute-start(bf16[360,128]{1,0:T(8,128)(2,1)S(1)} %get-tuple-element.123), channel_id=1, source_target_pairs={{0,4},{1,5},{2,6},{3,7},{4,8},{5,9},{6,10},{7,11},{8,12},{9,13},{1... | collective-permute-start | bytes 276488 | tf_op jit(solution)/shard_map/ppermute | solution.py:238
  217.4 7.2 %collective-permute-start.37 = (bf16[360,128]{1,0:T(8,128)(2,1)S(1)}, bf16[360,128]{1,0:T(8,128)(2,1)S(1)}, u32[]{:S(2)}, u32[]{:S(2)}) collective-permute-start(bf16[360,128]{1,0:T(8,128)(2,1)S(1)} %get-tuple-element.125), channel_id=1, source_target_pairs={{0,8},{1,9},{2,10},{3,11},{4,12},{5,13},{6,14},{7,15},{8,0},{9,1},... | collective-permute-start | bytes 276488 | tf_op jit(solution)/shard_map/ppermute | solution.py:238
  218.5 6.2 %collective-permute-start.38 = (bf16[360,128]{1,0:T(8,128)(2,1)S(1)}, bf16[360,128]{1,0:T(8,128)(2,1)S(1)}, u32[]{:S(2)}, u32[]{:S(2)}) collective-permute-start(bf16[360,128]{1,0:T(8,128)(2,1)S(1)} %get-tuple-element.124), channel_id=1, source_target_pairs={{0,12},{1,13},{2,14},{3,15},{4,0},{5,1},{6,2},{7,3},{8,4},{9,5},{1... | collective-permute-start | bytes 276488 | tf_op jit(solution)/shard_map/ppermute | solution.py:238
  219.8 9.5 %collective-permute-start.48 = (bf16[4,360,128]{2,1,0:T(8,128)(2,1)S(1)}, bf16[4,360,128]{2,1,0:T(8,128)(2,1)S(1)}, u32[]{:S(2)}, u32[]{:S(2)}) collective-permute-start(bf16[4,360,128]{2,1,0:T(8,128)(2,1)S(1)} %dynamic-slice_bitcast_fusion.6), channel_id=1, source_target_pairs={{0,2},{1,3},{2,0},{3,1},{4,6},{5,7},{6,4},{7,5},{8,10},{9,11},{10,... | collective-permute-start | bytes 1105928 | tf_op jit(solution)/shard_map/ppermute | solution.py:238
  224.7 4.4 %collective-permute-start.54 = (bf16[64,640]{1,0:T(8,128)(2,1)S(1)}, bf16[64,640]{1,0:T(8,128)(2,1)S(1)}, u32[]{:S(2)}, u32[]{:S(2)}) collective-permute-start(bf16[64,640]{1,0:T(8,128)(2,1)S(1)} %select_convert_fusion.2), channel_id=1, source_target_pairs={{0,16},{16,0},{1,17},{17,1},{2,18},{18,2},{3,19},{19,3},{4,20},{20... | collective-permute-start | bytes 245768 | tf_op jit(solution)/shard_map/ppermute | solution.py:242
  229.5 7.3 %collective-permute-start.49 = (bf16[360,128]{1,0:T(8,128)(2,1)S(1)}, bf16[360,128]{1,0:T(8,128)(2,1)S(1)}, u32[]{:S(2)}, u32[]{:S(2)}) collective-permute-start(bf16[360,128]{1,0:T(8,128)(2,1)S(1)} %get-tuple-element.117), channel_id=1, source_target_pairs={{0,4},{1,5},{2,6},{3,7},{4,8},{5,9},{6,10},{7,11},{8,12},{9,13},{1... | collective-permute-start | bytes 276488 | tf_op jit(solution)/shard_map/ppermute | solution.py:238
  231.7 7.8 %collective-permute-start.50 = (bf16[360,128]{1,0:T(8,128)(2,1)S(1)}, bf16[360,128]{1,0:T(8,128)(2,1)S(1)}, u32[]{:S(2)}, u32[]{:S(2)}) collective-permute-start(bf16[360,128]{1,0:T(8,128)(2,1)S(1)} %get-tuple-element.119), channel_id=1, source_target_pairs={{0,8},{1,9},{2,10},{3,11},{4,12},{5,13},{6,14},{7,15},{8,0},{9,1},... | collective-permute-start | bytes 276488 | tf_op jit(solution)/shard_map/ppermute | solution.py:238
  233.2 6.3 %collective-permute-start.51 = (bf16[360,128]{1,0:T(8,128)(2,1)S(1)}, bf16[360,128]{1,0:T(8,128)(2,1)S(1)}, u32[]{:S(2)}, u32[]{:S(2)}) collective-permute-start(bf16[360,128]{1,0:T(8,128)(2,1)S(1)} %get-tuple-element.118), channel_id=1, source_target_pairs={{0,12},{1,13},{2,14},{3,15},{4,0},{5,1},{6,2},{7,3},{8,4},{9,5},{1... | collective-permute-start | bytes 276488 | tf_op jit(solution)/shard_map/ppermute | solution.py:238
  239.7 5.6 %collective-permute-start.52 = (bf16[360,256]{1,0:T(8,128)(2,1)S(1)}, bf16[360,256]{1,0:T(8,128)(2,1)S(1)}, u32[]{:S(2)}, u32[]{:S(2)}) collective-permute-start(bf16[360,256]{1,0:T(8,128)(2,1)S(1)} %pad_maximum_fusion.6), channel_id=1, source_target_pairs={{0,16},{16,0},{1,17},{17,1},{2,18},{18,2},{3,19},{19,3},{4,20},{20... | collective-permute-start | bytes 552968 | tf_op jit(solution)/shard_map/ppermute | solution.py:242
  241.2 5.1 %collective-permute-start.53 = (bf16[360,128]{1,0:T(8,128)(2,1)S(1)}, bf16[360,128]{1,0:T(8,128)(2,1)S(1)}, u32[]{:S(2)}, u32[]{:S(2)}) collective-permute-start(bf16[360,128]{1,0:T(8,128)(2,1)S(1)} %get-tuple-element.115), channel_id=1, source_target_pairs={{0,16},{16,0},{1,17},{17,1},{2,18},{18,2},{3,19},{19,3},{4,20},{20... | collective-permute-start | bytes 276488 | tf_op jit(solution)/shard_map/ppermute | solution.py:242
  (20 other events, 62.1 us)

commit v3 on v1

--- a/solution.py
+++ b/solution.py
@@ -281,7 +281,11 @@
 
 
 def sent_on_chip(value, pieces=1):
-    return jnp.concatenate([shifted(piece, dc=1) for piece in jnp.split(value, pieces)])
+    if pieces == 1:
+        return shifted(value, dc=1)
+    flat = value.reshape(-1, *value.shape[-2:])
+    sent = [shifted(piece, dc=1) for piece in jnp.split(flat, pieces)]
+    return jnp.concatenate(sent).reshape(value.shape)
 
 
 def places_of(channels, main):
@@ -366,10 +370,13 @@
     )
 
 
-def gathered_over_y(line):
+def sent_over_y(line, earlier=None):
+    return shifted(after(line, earlier), dy=1)
+
+
+def joined_over_y(line, sent):
     _, y, _ = coordinates()
-    sent = shifted(line, dy=1)
-    return in_order(y == 1, line[:, None], sent[:, None], 1), sent
+    return in_order(y == 1, line[:, None], sent[:, None], 1)
 
 
 def gathered_on_chip(plane, earlier=None):
@@ -395,12 +402,17 @@
     return added(part_of(value, y, 1), sent).astype(BF16), sent
 
 
+def sent_for_sums(line, earlier=None):
+    z, _, _ = coordinates()
+    line = after(line, earlier)
+    return [
+        shifted(part_of(line, (z + step) % GRID[0], 0), dz=step) for step in range(1, GRID[0])
+    ]
+
+
 def summed_over_z(line, earlier=None):
     z, _, _ = coordinates()
-    line = after(line, earlier)
-    sent = [
-        shifted(part_of(line, (z + step) % GRID[0], 0), dz=step) for step in range(1, GRID[0])
-    ]
+    sent = sent_for_sums(line, earlier)
     return added(part_of(line, z, 0), *sent), sent
 
 
@@ -467,15 +479,13 @@
     pre_grad = pre_grad.astype(F32)
     total = None
     for tap in range(9):
-        moved = moved_rows(pre_grad, masks[8 - tap]).astype(BF16)
-        start = 0
-        for ref in weight_refs:
-            end = start + ref.shape[1]
-            term = dot(
-                moved[:, start:end], ref[tap * channels : (tap + 1) * channels, :], ((1,), (1,))
-            )
-            total = term if total is None else total + term
-            start = end
+        weights = [ref[tap * channels : (tap + 1) * channels, :] for ref in weight_refs]
+        term = dot(
+            moved_rows(pre_grad, masks[8 - tap]).astype(BF16),
+            jnp.concatenate(weights, 1),
+            ((1,), (1,)),
+        )
+        total = term if total is None else total + term
     return total
 
 
@@ -606,7 +616,6 @@
 def paired_device(samples, timesteps, cotangent, spatial_weight, temporal_weight):
     me = lax.axis_index("pipe")
     first = me == 0
-    _, y, _ = coordinates()
     count, frames, pixels, channels = samples.shape
     rows = count * frames * pixels
     main = 2 * LANES
@@ -625,18 +634,25 @@
     order = (places[:, None] == jnp.arange(channels)).astype(BF16)
     temporal_own, temporal_sent = sets_of(temporal_weight[0])
     temporal_given = swapped(temporal_sent)
-    line, sent = gathered_over_z(in_order(me == 1, temporal_own, temporal_given, 0))
-    plane_temporal, side = gathered_over_y(line)
+    line_temporal, sent = gathered_over_z(in_order(me == 1, temporal_own, temporal_given, 0))
+    side_temporal = sent_over_y(line_temporal)
     spatial_own = dot(spatial_weight[0], order).astype(BF16)
     given = swapped(spatial_own[:, main:])
     main_own, main_given = spatial_own[:, :main], given[:, :main]
     tails = jnp.where(tail, spatial_own[:, 2 * main :], given[:, main:])
     line, sent = gathered_over_z(jnp.where(first, main_own, main_given), sent)
-    line_tails, sent = gathered_over_z(tails, (sent, side))
-    plane_first, side = gathered_over_y(line)
-    plane_tails, _ = gathered_over_y(line_tails)
-    line_second, _ = gathered_over_z(jnp.where(first, main_given, main_own), (sent, side))
-    side_second = shifted(line_second, dy=1)
+    line_tails, sent = gathered_over_z(tails, (sent, side_temporal))
+    side_low = sent_over_y(line[..., :LANES])
+    side_high = sent_over_y(line[..., LANES:], side_low)
+    side_tails = sent_over_y(line_tails)
+    line_second, sent = gathered_over_z(
+        jnp.where(first, main_given, main_own), (sent, side_low)
+    )
+    side_first = jnp.concatenate([side_low, after(side_high, sent)], 2)
+    plane_first = joined_over_y(line, side_first)
+    plane_tails = joined_over_y(line_tails, after(side_tails, sent))
+    plane_temporal = joined_over_y(line_temporal, side_temporal)
+    side_second = sent_over_y(line_second)
 
     chips = GRID[0] * GRID[1]
     temporal = gathered_on_chip(plane_temporal).reshape(chips, GRID[2], 2, PIECE, channels)
@@ -659,8 +675,7 @@
         moved=spatial_bytes + temporal_bytes,
     )(hidden, embedding, keep_first, temporal_first, *spatial_first)
     mixed_given = swapped(mixed)
-    side_second = after(side_second, mixed)
-    plane_second = in_order(y == 1, line_second[:, None], side_second[:, None], 1)
+    plane_second = joined_over_y(line_second, after(side_second, mixed))
     spatial_second = [gathered_on_chip(plane_second), tails]
     hidden_second, normed_second, activated_second, pre_grad_second, back = vmem_call(
         functools.partial(second_forward, frames),
@@ -740,7 +755,7 @@
         share_spatial, order.astype(F32), (((1,), (1,)), ((), ())), precision=lax.Precision.HIGH
     )
     low, high = share_temporal[:PIECE], share_temporal[PIECE:]
-    given = swapped(jnp.where(first, high, low).astype(BF16)).astype(F32)
+    given = swapped(after(jnp.where(first, high, low).astype(BF16), share_spatial)).astype(F32)
     share_temporal = shard_of(jnp.where(first, low, high), given, temporal_weight.shape[1])
     return (share_spatial[None], share_temporal[None])
 

time: 244 us -> 238 us (0.975)
  waiting for transfers between devices: 122 us -> 99.7 us
  starting transfers between devices: 52.6 us -> 64.2 us
  other arithmetic: 17.1 us -> 21.6 us
  Pallas kernels: 31.7 us -> 28.8 us
    ppermute x44 -> x45, waiting for transfers between devices: 98.4 us -> 75.9 us  [shifted(): return lax.ppermute(value, 'dp', pairs)]
    ppermute x44 -> x45, starting transfers between devices: 43.1 us -> 54.8 us  [shifted(): return lax.ppermute(value, 'dp', pairs)]
    select_n x13, other arithmetic: 6.6 us -> 9.24 us  [in_order(): jnp.where(swap, jnp.concatenate([other, own], axis), jnp.concatenate([own...]
    pallas_call x1, Pallas kernels: 12.9 us -> 10.4 us  [paired_device(): vmem_call(functools.partial(second_forward, frames), (shape((rows, channe...]
  transfers between devices with their start and end apart: 50 -> 51, of which waited for: 21 -> 25; matrix products, arithmetic and copies ran while one was open for 10% -> 12% of each run, Pallas kernels for 6% -> 6%
where the time goes in v3:
time: 238 us; the launch traced here: 234 us
  waiting for transfers between devices  99.7 us (42%)
  starting transfers between devices  64.2 us (27%)
  Pallas kernels  28.8 us (12%)
  other arithmetic  21.6 us (9%)
  local copies, waits for them, and re-layouts  14.5 us (6%)
  matrix products  2.85 us (1%)
    ppermute x45, waiting for transfers between devices, shifted(): return lax.ppermute(value, 'dp', pairs)  75.9 us
    ppermute x45, starting transfers between devices, shifted(): return lax.ppermute(value, 'dp', pairs)  54.8 us
    ppermute x6, waiting for transfers between devices, swapped(): return lax.ppermute(value, 'pipe', [(0, 1), (1, 0)])  23.7 us
    pallas_call x1, Pallas kernels, paired_device(): vmem_call(functools.partial(second_forward, frames), (shape((rows, channe...  10.4 us
    ppermute x6, starting transfers between devices, swapped(): return lax.ppermute(value, 'pipe', [(0, 1), (1, 0)])  9.34 us
    select_n x13, other arithmetic, in_order(): jnp.where(swap, jnp.concatenate([other, own], axis), jnp.concatenate([own...  9.24 us
    pallas_call x1, Pallas kernels, paired_device(): vmem_call(functools.partial(first_terms, frames), terms_shape(), flops=sp...  7.77 us
    pallas_call x1, Pallas kernels, paired_device(): vmem_call(functools.partial(first_forward, frames), (shape((rows, channel...  6.25 us
  transfers between devices with their start and end apart: 51, of which 25 were waited for; matrix products, arithmetic and copies ran while one was open for 12% of the time, Pallas kernels for 6%

profile of v3, /device:TPU:0, one launch (start us, length us, event | category | flops | bytes accessed | tf_op | source)
XLA Modules:
  0.0 234.0 jit_solution(13321004517418335168)
XLA Ops:
  2.5 3.0 %collective-permute-start = (bf16[64,640]{1,0:T(8,128)(2,1)S(1)}, bf16[64,640]{1,0:T(8,128)(2,1)S(1)}, u32[]{:S(2)}, u32[]{:S(2)}) collective-permute-start(bf16[64,640]{1,0:T(8,128)(2,1)S(1)} %fusion.43), channel_id=1, source_target_pairs={{0,16},{16,0},{1,17},{17,1},{2,18},{18,2},{3,19},{19,3},{4,20},{20... | collective-permute-start | bytes 245768 | tf_op jit(solution)/shard_map/ppermute | solution.py:242
  6.7 1.6 collective-permute-done
  8.3 2.8 %collective-permute-start.2 = (bf16[128,640]{1,0:T(8,128)(2,1)S(1)}, bf16[128,640]{1,0:T(8,128)(2,1)S(1)}, u32[]{:S(2)}, u32[]{:S(2)}) collective-permute-start(bf16[128,640]{1,0:T(8,128)(2,1)S(1)} %maximum_select_fusion.15), channel_id=1, source_target_pairs={{0,8},{1,9},{2,10},{3,11},{4,12},{5,13},{6,14},{7,15},{8,0},{9,1},... | collective-permute-start | bytes 491528 | tf_op jit(solution)/shard_map/ppermute | solution.py:238
  11.1 1.3 collective-permute-start.3
  13.1 1.3 collective-permute-done.6
  14.4 6.2 %collective-permute-done.2 = bf16[128,640]{1,0:T(8,128)(2,1)S(1)} collective-permute-done((bf16[128,640]{1,0:T(8,128)(2,1)S(1)}, bf16[128,640]{1,0:T(8,128)(2,1)S(1)}, u32[]{:S(2)}, u32[]{:S(2)}) %collective-permute-start.2) | collective-permute-done | bytes 163872 | tf_op jit(solution)/shard_map/ppermute | solution.py:238
  20.7 1.8 collective-permute-done.1
  22.4 4.9 %collective-permute-start.8 = (bf16[360,256]{1,0:T(8,128)(2,1)S(1)}, bf16[360,256]{1,0:T(8,128)(2,1)S(1)}, u32[]{:S(2)}, u32[]{:S(2)}) collective-permute-start(bf16[360,256]{1,0:T(8,128)(2,1)S(1)} %get-tuple-element.34), channel_id=1, source_target_pairs={{0,8},{1,9},{2,10},{3,11},{4,12},{5,13},{6,14},{7,15},{8,0},{9,1},... | collective-permute-start | bytes 552968 | tf_op jit(solution)/shard_map/ppermute | solution.py:238
  27.8 1.6 collective-permute-start.7
  30.5 1.5 collective-permute-start.4
  32.0 5.3 %collective-permute-done.8 = bf16[360,256]{1,0:T(8,128)(2,1)S(1)} collective-permute-done((bf16[360,256]{1,0:T(8,128)(2,1)S(1)}, bf16[360,256]{1,0:T(8,128)(2,1)S(1)}, u32[]{:S(2)}, u32[]{:S(2)}) %collective-permute-start.8) | collective-permute-done | bytes 184352 | tf_op jit(solution)/shard_map/ppermute | solution.py:238
  37.3 3.9 %collective-permute-done.9 = bf16[360,256]{1,0:T(8,128)(2,1)S(1)} collective-permute-done((bf16[360,256]{1,0:T(8,128)(2,1)S(1)}, bf16[360,256]{1,0:T(8,128)(2,1)S(1)}, u32[]{:S(2)}, u32[]{:S(2)}) %collective-permute-start.9) | collective-permute-done | bytes 184352 | tf_op jit(solution)/shard_map/ppermute | solution.py:238
  42.5 1.5 collective-permute-start.10
  45.0 3.5 %collective-permute-done.4 = bf16[4,128,640]{2,1,0:T(8,128)(2,1)} collective-permute-done((bf16[4,128,640]{2,1,0:T(8,128)(2,1)}, bf16[4,128,640]{2,1,0:T(8,128)(2,1)}, u32[]{:S(2)}, u32[]{:S(2)}) %collective-permute-start.4) | collective-permute-done | bytes 655392 | tf_op jit(solution)/shard_map/ppermute | solution.py:238
  48.5 2.8 %collective-permute-start.13 = (bf16[360,128]{1,0:T(8,128)(2,1)S(1)}, bf16[360,128]{1,0:T(8,128)(2,1)S(1)}, u32[]{:S(2)}, u32[]{:S(2)}) collective-permute-start(bf16[360,128]{1,0:T(8,128)(2,1)S(1)} %slice_select_fusion.2), channel_id=1, source_target_pairs={{0,8},{1,9},{2,10},{3,11},{4,12},{5,13},{6,14},{7,15},{8,0},{9,1},... | collective-permute-start | bytes 276488 | tf_op jit(solution)/shard_map/ppermute | solution.py:238
  52.4 2.1 collective-permute-done.10
  54.9 2.0 collective-permute-done.13
  59.0 1.6 collective-permute-start.15
  60.6 2.4 %collective-permute-start.16 = (bf16[360,256]{1,0:T(8,128)(2,1)S(1)}, bf16[360,256]{1,0:T(8,128)(2,1)S(1)}, u32[]{:S(2)}, u32[]{:S(2)}) collective-permute-start(bf16[360,256]{1,0:T(8,128)(2,1)S(1)} %get-tuple-element.37), channel_id=1, source_target_pairs={{0,8},{1,9},{2,10},{3,11},{4,12},{5,13},{6,14},{7,15},{8,0},{9,1},... | collective-permute-start | bytes 552968 | tf_op jit(solution)/shard_map/ppermute | solution.py:238
  63.4 1.5 maximum_select_fusion.7
  65.0 1.6 maximum_select_fusion.8
  66.8 1.4 collective-permute-done.15
  68.2 1.6 collective-permute-start.11
  69.8 2.9 %collective-permute-done.16 = bf16[360,256]{1,0:T(8,128)(2,1)S(1)} collective-permute-done((bf16[360,256]{1,0:T(8,128)(2,1)S(1)}, bf16[360,256]{1,0:T(8,128)(2,1)S(1)}, u32[]{:S(2)}, u32[]{:S(2)}) %collective-permute-start.16) | collective-permute-done | bytes 184352 | tf_op jit(solution)/shard_map/ppermute | solution.py:238
  74.1 1.3 collective-permute-start.22
  75.4 4.2 %collective-permute-done.11 = bf16[4,360,128]{2,1,0:T(8,128)(2,1)S(1)} collective-permute-done((bf16[4,360,128]{2,1,0:T(8,128)(2,1)S(1)}, bf16[4,360,128]{2,1,0:T(8,128)(2,1)S(1)}, u32[]{:S(2)}, u32[]{:S(2)}) %collective-permute-start.11) | collective-permute-done | bytes 368672 | tf_op jit(solution)/shard_map/ppermute | solution.py:238
  81.6 1.3 slice_bitcast_fusion.3
  85.0 6.3 %shard_map.68 = (bf16[480,640]{1,0:T(8,128)(2,1)S(1)}, f32[480,384]{1,0:T(8,128)S(1)}, bf16[480,640]{1,0:T(8,128)(2,1)S(1)}) custom-call(bf16[480,640]{1,0:T(8,128)(2,1)S(1)} %bitcast.309, f32[5,640]{1,0:T(8,128)S(1)} %pad_maximum_fusion.7.embedding_ref, f32[1,384]{1,0:T(1,128)S(1)} %select_n.855.keep_ref, bf16[960,640]{1,0:T(8,128)(2,1)S(1)} %bitcast.306, ...), custom_call_target="tpu_custom_call" | custom-call | flops 7077888000 | bytes 5898240 | tf_op jit(solution)/shard_map/pallas_call | solution.py:671
  91.2 3.1 %collective-permute-done.22 = bf16[4,360,256]{2,1,0:T(8,128)(2,1)S(1)} collective-permute-done((bf16[4,360,256]{2,1,0:T(8,128)(2,1)S(1)}, bf16[4,360,256]{2,1,0:T(8,128)(2,1)S(1)}, u32[]{:S(2)}, u32[]{:S(2)}) %collective-permute-start.22) | collective-permute-done | bytes 737312 | tf_op jit(solution)/shard_map/ppermute | solution.py:238
  94.4 1.4 maximum_select_fusion.6
  95.9 1.6 collective-permute-start.21
  99.7 1.7 maximum_select_fusion.12
  101.7 2.4 %maximum_select_fusion.1 = bf16[4,2,2,360,256]{4,3,0,2,1:T(8,128)(2,1)S(1)} fusion(bf16[4,2,1,360,256]{4,3,0,2,1:T(8,128)(2,1)S(1)} %bitcast_select_fusion, bf16[4,2,1,360,256]{4,3,0,2,1:T(8,128)(2,1)} %bitcast.60, pred[]{:T(512)S(6)} %eq.114), kind=kLoop, calls=%fused_computation.5 | loop fusion | flops 4423680 | bytes 5898241 | tf_op jit(solution)/shard_map/jit(_where)/select_n | solution.py:266
  104.4 7.9 %collective-permute-done.21.sent_ref = bf16[480,640]{1,0:T(8,128)(2,1)} collective-permute-done((bf16[480,640]{1,0:T(8,128)(2,1)S(1)}, bf16[480,640]{1,0:T(8,128)(2,1)}, u32[]{:S(2)}, u32[]{:S(2)}) %collective-permute-start.21) | collective-permute-done | bytes 614432 | tf_op jit(solution)/shard_map/ppermute | solution.py:242
  112.2 10.4 %shard_map.69 = (bf16[480,640]{1,0:T(8,128)(2,1)S(1)}, bf16[480,640]{1,0:T(8,128)(2,1)S(1)}, bf16[480,384]{1,0:T(8,128)(2,1)S(1)}, bf16[480,384]{1,0:T(8,128)(2,1)S(1)}, bf16[480,640]{1,0:T(8,128)(2,1)}) custom-call(bf16[480,640]{1,0:T(8,128)(2,1)S(1)} %bitcast.310, bf16[480,640]{1,0:T(8,128)(2,1)S(1)} %get-tuple-element.40.own_ref, ...), custom_call_target="tpu_custom_call" | custom-call | flops 12386304000 | bytes 5898240 | tf_op jit(solution)/shard_map/pallas_call | solution.py:680
  122.7 4.4 %shard_map.70 = (bf16[5760,256]{1,0:T(8,128)(2,1)S(1)}, bf16[5760,128]{1,0:T(8,128)(2,1)S(1)}, bf16[960,640]{1,0:T(8,128)(2,1)S(1)}) custom-call(bf16[480,640]{1,0:T(8,128)(2,1)S(1)} %get-tuple-element.44.normed_ref, bf16[480,384]{1,0:T(8,128)(2,1)S(1)} %get-tuple-element.45.pre_grad_ref, bf16[480,384]{1,0:T(8,128)(2,1)S(1)} %get-tuple-element.46.activated_ref, ...), custom_call_target="tpu_custom_call" | custom-call | flops 7077888000 | bytes 5898240 | tf_op jit(solution)/shard_map/pallas_call | solution.py:707
  127.1 1.2 dynamic-slice_bitcast_fusion.5
  130.5 1.5 collective-permute-start.24
  133.3 1.5 pad_maximum_fusion
  135.4 1.2 collective-permute-start.29
  136.6 10.1 %collective-permute-done.24.sent_ref = bf16[480,640]{1,0:T(8,128)(2,1)} collective-permute-done((bf16[480,640]{1,0:T(8,128)(2,1)}, bf16[480,640]{1,0:T(8,128)(2,1)}, u32[]{:S(2)}, u32[]{:S(2)}) %collective-permute-start.24) | collective-permute-done | bytes 614432 | tf_op jit(solution)/shard_map/ppermute | solution.py:242
  146.7 7.8 %shard_map.71 = (bf16[5760,256]{1,0:T(8,128)(2,1)S(1)}, bf16[5760,128]{1,0:T(8,128)(2,1)S(1)}, bf16[960,640]{1,0:T(8,128)(2,1)S(1)}) custom-call(bf16[480,640]{1,0:T(8,128)(2,1)S(1)} %copy-done.16, f32[5,640]{1,0:T(8,128)S(1)} %pad_maximum_fusion.7.embedding_ref, bf16[480,640]{1,0:T(8,128)(2,1)S(1)} %bitcast.313, ...), custom_call_target="tpu_custom_call" | custom-call | flops 8847360000 | bytes 7372800 | tf_op jit(solution)/shard_map/pallas_call | solution.py:717
  158.6 1.2 collective-permute-start.32
  160.1 3.0 %collective-permute-start.35 = (bf16[360,256]{1,0:T(8,128)(2,1)S(1)}, bf16[360,256]{1,0:T(8,128)(2,1)S(1)}, u32[]{:S(2)}, u32[]{:S(2)}) collective-permute-start(bf16[360,256]{1,0:T(8,128)(2,1)S(1)} %get-tuple-element.95), channel_id=1, source_target_pairs={{0,4},{1,5},{2,6},{3,7},{4,8},{5,9},{6,10},{7,11},{8,12},{9,13},{1... | collective-permute-start | bytes 552968 | tf_op jit(solution)/shard_map/ppermute | solution.py:238
  163.2 2.1 collective-permute-start.36
  165.3 3.9 %collective-permute-done.32 = bf16[4,360,128]{2,1,0:T(8,128)(2,1)S(1)} collective-permute-done((bf16[4,360,128]{2,1,0:T(8,128)(2,1)S(1)}, bf16[4,360,128]{2,1,0:T(8,128)(2,1)S(1)}, u32[]{:S(2)}, u32[]{:S(2)}) %collective-permute-start.32) | collective-permute-done | bytes 368672 | tf_op jit(solution)/shard_map/ppermute | solution.py:238
  169.2 4.0 %collective-permute-start.37 = (bf16[360,256]{1,0:T(8,128)(2,1)S(1)}, bf16[360,256]{1,0:T(8,128)(2,1)S(1)}, u32[]{:S(2)}, u32[]{:S(2)}) collective-permute-start(bf16[360,256]{1,0:T(8,128)(2,1)S(1)} %get-tuple-element.93), channel_id=1, source_target_pairs={{0,12},{1,13},{2,14},{3,15},{4,0},{5,1},{6,2},{7,3},{8,4},{9,5},{1... | collective-permute-start | bytes 552968 | tf_op jit(solution)/shard_map/ppermute | solution.py:238
  174.1 1.8 collective-permute-start.33
  176.3 7.2 %collective-permute-done.33 = bf16[4,360,128]{2,1,0:T(8,128)(2,1)S(1)} collective-permute-done((bf16[4,360,128]{2,1,0:T(8,128)(2,1)S(1)}, bf16[4,360,128]{2,1,0:T(8,128)(2,1)S(1)}, u32[]{:S(2)}, u32[]{:S(2)}) %collective-permute-start.33) | collective-permute-done | bytes 368672 | tf_op jit(solution)/shard_map/ppermute | solution.py:238
  183.5 1.7 collective-permute-start.34
  185.4 1.6 collective-permute-start.40
  188.1 4.2 %collective-permute-done.34 = bf16[4,360,128]{2,1,0:T(8,128)(2,1)S(1)} collective-permute-done((bf16[4,360,128]{2,1,0:T(8,128)(2,1)S(1)}, bf16[4,360,128]{2,1,0:T(8,128)(2,1)S(1)}, u32[]{:S(2)}, u32[]{:S(2)}) %collective-permute-start.34) | collective-permute-done | bytes 368672 | tf_op jit(solution)/shard_map/ppermute | solution.py:238
  192.3 1.7 collective-permute-start.45
  194.7 1.3 collective-permute-start.43
  196.0 1.9 collective-permute-start.41
  197.9 8.2 %collective-permute-done.45 = bf16[4,128,640]{2,1,0:T(8,128)(2,1)S(1)} collective-permute-done((bf16[4,128,640]{2,1,0:T(8,128)(2,1)S(1)}, bf16[4,128,640]{2,1,0:T(8,128)(2,1)S(1)}, u32[]{:S(2)}, u32[]{:S(2)}) %collective-permute-start.45) | collective-permute-done | bytes 655392 | tf_op jit(solution)/shard_map/ppermute | solution.py:238
  206.2 4.7 %collective-permute-done.42 = bf16[360,256]{1,0:T(8,128)(2,1)S(1)} collective-permute-done((bf16[360,256]{1,0:T(8,128)(2,1)S(1)}, bf16[360,256]{1,0:T(8,128)(2,1)S(1)}, u32[]{:S(2)}, u32[]{:S(2)}) %collective-permute-start.42) | collective-permute-done | bytes 184352 | tf_op jit(solution)/shard_map/ppermute | solution.py:238
  212.0 1.9 collective-permute-start.47
  214.2 1.6 collective-permute-start.46
  215.8 1.3 collective-permute-done.49
  217.1 9.0 %collective-permute-done.48 = bf16[128,640]{1,0:T(8,128)(2,1)S(1)} collective-permute-done((bf16[128,640]{1,0:T(8,128)(2,1)S(1)}, bf16[128,640]{1,0:T(8,128)(2,1)S(1)}, u32[]{:S(2)}, u32[]{:S(2)}) %collective-permute-start.48) | collective-permute-done | bytes 163872 | tf_op jit(solution)/shard_map/ppermute | solution.py:238
  226.4 2.1 fusion.3
  228.5 1.5 collective-permute-start.50
  230.0 2.9 %collective-permute-done.50 = bf16[64,640]{1,0:T(8,128)(2,1)S(1)} collective-permute-done((bf16[64,640]{1,0:T(8,128)(2,1)S(1)}, bf16[64,640]{1,0:T(8,128)(2,1)S(1)}, u32[]{:S(2)}, u32[]{:S(2)}) %collective-permute-start.50) | collective-permute-done | bytes 81952 | tf_op jit(solution)/shard_map/ppermute | solution.py:242
  (199 shorter events, 32.8 us)
Async XLA Ops:
  0.6 4.9 %copy-start = (bf16[1,360,640]{2,1,0:T(8,128)(2,1)S(1)}, bf16[1,360,640]{2,1,0:T(8,128)(2,1)}, u32[]{:S(2)}) copy-start(bf16[1,360,640]{2,1,0:T(8,128)(2,1)} %param.8) | copy-start | bytes 1382404
  1.5 4.8 %copy-start.23 = (s32[5]{0:T(128)S(1)}, s32[5]{0:T(128)}, u32[]{:S(2)}) copy-start(s32[5]{0:T(128)} %param.6) | copy-start | bytes 64
  2.5 5.8 %collective-permute-start = (bf16[64,640]{1,0:T(8,128)(2,1)S(1)}, bf16[64,640]{1,0:T(8,128)(2,1)S(1)}, u32[]{:S(2)}, u32[]{:S(2)}) collective-permute-start(bf16[64,640]{1,0:T(8,128)(2,1)S(1)} %fusion.43), channel_id=1, source_target_pairs={{0,16},{16,0},{1,17},{17,1},{2,18},{18,2},{3,19},{19,3},{4,20},{20... | collective-permute-start | bytes 245768 | tf_op jit(solution)/shard_map/ppermute | solution.py:242
  6.2 23.2 %copy-start.20 = (bf16[360,640]{1,0:T(8,128)(2,1)}, bf16[360,640]{1,0:T(8,128)(2,1)S(1)}, u32[]{:S(2)}) copy-start(bf16[360,640]{1,0:T(8,128)(2,1)S(1)} %fusion.13) | copy-start | bytes 1382404
  6.3 8.1 %collective-permute-start.6 = (bf16[360,384]{1,0:T(8,128)(2,1)S(1)}, bf16[360,384]{1,0:T(8,128)(2,1)S(1)}, u32[]{:S(2)}, u32[]{:S(2)}) collective-permute-start(bf16[360,384]{1,0:T(8,128)(2,1)S(1)} %slice.274), channel_id=1, source_target_pairs={{0,16},{16,0},{1,17},{17,1},{2,18},{18,2},{3,19},{19,3},{4,20},{20... | collective-permute-start | bytes 829448 | tf_op jit(solution)/shard_map/ppermute | solution.py:242
  8.3 12.3 %collective-permute-start.2 = (bf16[128,640]{1,0:T(8,128)(2,1)S(1)}, bf16[128,640]{1,0:T(8,128)(2,1)S(1)}, u32[]{:S(2)}, u32[]{:S(2)}) collective-permute-start(bf16[128,640]{1,0:T(8,128)(2,1)S(1)} %maximum_select_fusion.15), channel_id=1, source_target_pairs={{0,8},{1,9},{2,10},{3,11},{4,12},{5,13},{6,14},{7,15},{8,0},{9,1},... | collective-permute-start | bytes 491528 | tf_op jit(solution)/shard_map/ppermute | solution.py:238
  11.1 9.6 %collective-permute-start.3 = (bf16[128,640]{1,0:T(8,128)(2,1)S(1)}, bf16[128,640]{1,0:T(8,128)(2,1)S(1)}, u32[]{:S(2)}, u32[]{:S(2)}) collective-permute-start(bf16[128,640]{1,0:T(8,128)(2,1)S(1)} %maximum_select_fusion.15), channel_id=1, source_target_pairs={{0,12},{1,13},{2,14},{3,15},{4,0},{5,1},{6,2},{7,3},{8,4},{9,5},{1... | collective-permute-start | bytes 491528 | tf_op jit(solution)/shard_map/ppermute | solution.py:238
  12.4 10.0 %collective-permute-start.1 = (bf16[128,640]{1,0:T(8,128)(2,1)S(1)}, bf16[128,640]{1,0:T(8,128)(2,1)S(1)}, u32[]{:S(2)}, u32[]{:S(2)}) collective-permute-start(bf16[128,640]{1,0:T(8,128)(2,1)S(1)} %maximum_select_fusion.15), channel_id=1, source_target_pairs={{0,4},{1,5},{2,6},{3,7},{4,8},{5,9},{6,10},{7,11},{8,12},{9,13},{1... | collective-permute-start | bytes 491528 | tf_op jit(solution)/shard_map/ppermute | solution.py:238
  22.4 14.9 %collective-permute-start.8 = (bf16[360,256]{1,0:T(8,128)(2,1)S(1)}, bf16[360,256]{1,0:T(8,128)(2,1)S(1)}, u32[]{:S(2)}, u32[]{:S(2)}) collective-permute-start(bf16[360,256]{1,0:T(8,128)(2,1)S(1)} %get-tuple-element.34), channel_id=1, source_target_pairs={{0,8},{1,9},{2,10},{3,11},{4,12},{5,13},{6,14},{7,15},{8,0},{9,1},... | collective-permute-start | bytes 552968 | tf_op jit(solution)/shard_map/ppermute | solution.py:238
  27.3 13.9 %collective-permute-start.9 = (bf16[360,256]{1,0:T(8,128)(2,1)S(1)}, bf16[360,256]{1,0:T(8,128)(2,1)S(1)}, u32[]{:S(2)}, u32[]{:S(2)}) collective-permute-start(bf16[360,256]{1,0:T(8,128)(2,1)S(1)} %get-tuple-element.34), channel_id=1, source_target_pairs={{0,12},{1,13},{2,14},{3,15},{4,0},{5,1},{6,2},{7,3},{8,4},{9,5},{1... | collective-permute-start | bytes 552968 | tf_op jit(solution)/shard_map/ppermute | solution.py:238
  27.8 13.5 %collective-permute-start.7 = (bf16[360,256]{1,0:T(8,128)(2,1)S(1)}, bf16[360,256]{1,0:T(8,128)(2,1)S(1)}, u32[]{:S(2)}, u32[]{:S(2)}) collective-permute-start(bf16[360,256]{1,0:T(8,128)(2,1)S(1)} %get-tuple-element.34), channel_id=1, source_target_pairs={{0,4},{1,5},{2,6},{3,7},{4,8},{5,9},{6,10},{7,11},{8,12},{9,13},{1... | collective-permute-start | bytes 552968 | tf_op jit(solution)/shard_map/ppermute | solution.py:238
  30.5 18.0 %collective-permute-start.4 = (bf16[4,128,640]{2,1,0:T(8,128)(2,1)}, bf16[4,128,640]{2,1,0:T(8,128)(2,1)}, u32[]{:S(2)}, u32[]{:S(2)}) collective-permute-start(bf16[4,128,640]{2,1,0:T(8,128)(2,1)} %get-tuple-element.119), channel_id=1, source_target_pairs={{0,2},{1,3},{2,0},{3,1},{4,6},{5,7},{6,4},{7,5},{8,10},{9,11},{10,... | collective-permute-start | bytes 1966088 | tf_op jit(solution)/shard_map/ppermute | solution.py:238
  42.5 12.0 %collective-permute-start.10 = (bf16[4,360,128]{2,1,0:T(8,128)(2,1)}, bf16[4,360,128]{2,1,0:T(8,128)(2,1)}, u32[]{:S(2)}, u32[]{:S(2)}) collective-permute-start(bf16[4,360,128]{2,1,0:T(8,128)(2,1)} %get-tuple-element.109), channel_id=1, source_target_pairs={{0,2},{1,3},{2,0},{3,1},{4,6},{5,7},{6,4},{7,5},{8,10},{9,11},{10,... | collective-permute-start | bytes 1105928 | tf_op jit(solution)/shard_map/ppermute | solution.py:238
  48.5 6.5 %collective-permute-start.12 = (bf16[360,128]{1,0:T(8,128)(2,1)S(1)}, bf16[360,128]{1,0:T(8,128)(2,1)S(1)}, u32[]{:S(2)}, u32[]{:S(2)}) collective-permute-start(bf16[360,128]{1,0:T(8,128)(2,1)S(1)} %slice_select_fusion.2), channel_id=1, source_target_pairs={{0,4},{1,5},{2,6},{3,7},{4,8},{5,9},{6,10},{7,11},{8,12},{9,13},{1... | collective-permute-start | bytes 276488 | tf_op jit(solution)/shard_map/ppermute | solution.py:238
  48.5 8.5 %collective-permute-start.13 = (bf16[360,128]{1,0:T(8,128)(2,1)S(1)}, bf16[360,128]{1,0:T(8,128)(2,1)S(1)}, u32[]{:S(2)}, u32[]{:S(2)}) collective-permute-start(bf16[360,128]{1,0:T(8,128)(2,1)S(1)} %slice_select_fusion.2), channel_id=1, source_target_pairs={{0,8},{1,9},{2,10},{3,11},{4,12},{5,13},{6,14},{7,15},{8,0},{9,1},... | collective-permute-start | bytes 276488 | tf_op jit(solution)/shard_map/ppermute | solution.py:238
  51.3 5.7 %collective-permute-start.14 = (bf16[360,128]{1,0:T(8,128)(2,1)S(1)}, bf16[360,128]{1,0:T(8,128)(2,1)S(1)}, u32[]{:S(2)}, u32[]{:S(2)}) collective-permute-start(bf16[360,128]{1,0:T(8,128)(2,1)S(1)} %slice_select_fusion.2), channel_id=1, source_target_pairs={{0,12},{1,13},{2,14},{3,15},{4,0},{5,1},{6,2},{7,3},{8,4},{9,5},{1... | collective-permute-start | bytes 276488 | tf_op jit(solution)/shard_map/ppermute | solution.py:238
  57.2 15.6 %collective-permute-start.19 = (bf16[4,360,128]{2,1,0:T(8,128)(2,1)S(1)}, bf16[4,360,128]{2,1,0:T(8,128)(2,1)S(1)}, u32[]{:S(2)}, u32[]{:S(2)}) collective-permute-start(bf16[4,360,128]{2,1,0:T(8,128)(2,1)S(1)} %get-tuple-element.129), channel_id=1, source_target_pairs={{0,2},{1,3},{2,0},{3,1},{4,6},{5,7},{6,4},{7,5},{8,10},{9,11},{10,... | collective-permute-start | bytes 1105928 | tf_op jit(solution)/shard_map/ppermute | solution.py:238
  59.0 9.1 %collective-permute-start.15 = (bf16[360,256]{1,0:T(8,128)(2,1)S(1)}, bf16[360,256]{1,0:T(8,128)(2,1)S(1)}, u32[]{:S(2)}, u32[]{:S(2)}) collective-permute-start(bf16[360,256]{1,0:T(8,128)(2,1)S(1)} %get-tuple-element.37), channel_id=1, source_target_pairs={{0,4},{1,5},{2,6},{3,7},{4,8},{5,9},{6,10},{7,11},{8,12},{9,13},{1... | collective-permute-start | bytes 552968 | tf_op jit(solution)/shard_map/ppermute | solution.py:238
  60.6 12.1 %collective-permute-start.16 = (bf16[360,256]{1,0:T(8,128)(2,1)S(1)}, bf16[360,256]{1,0:T(8,128)(2,1)S(1)}, u32[]{:S(2)}, u32[]{:S(2)}) collective-permute-start(bf16[360,256]{1,0:T(8,128)(2,1)S(1)} %get-tuple-element.37), channel_id=1, source_target_pairs={{0,8},{1,9},{2,10},{3,11},{4,12},{5,13},{6,14},{7,15},{8,0},{9,1},... | collective-permute-start | bytes 552968 | tf_op jit(solution)/shard_map/ppermute | solution.py:238
  63.1 9.7 %collective-permute-start.17 = (bf16[360,256]{1,0:T(8,128)(2,1)S(1)}, bf16[360,256]{1,0:T(8,128)(2,1)S(1)}, u32[]{:S(2)}, u32[]{:S(2)}) collective-permute-start(bf16[360,256]{1,0:T(8,128)(2,1)S(1)} %get-tuple-element.37), channel_id=1, source_target_pairs={{0,12},{1,13},{2,14},{3,15},{4,0},{5,1},{6,2},{7,3},{8,4},{9,5},{1... | collective-permute-start | bytes 552968 | tf_op jit(solution)/shard_map/ppermute | solution.py:238
  64.9 15.9 %collective-permute-start.5 = (bf16[4,2,128,640]{3,2,1,0:T(8,128)(2,1)S(1)}, bf16[4,2,128,640]{3,2,1,0:T(8,128)(2,1)S(1)}, u32[]{:S(2)}, u32[]{:S(2)}) collective-permute-start(bf16[4,2,128,640]{3,2,1,0:T(8,128)(2,1)S(1)} %maximum_select_fusion.7), channel_id=1, source_target_pairs={{0,1},{1,0},{2,3},{3,2},{4,5},{5,4},{6,7},{7,6},{8,9},{9,8},{10,11... | collective-permute-start | bytes 3932168 | tf_op jit(solution)/shard_map/ppermute | solution.py:238
  68.2 11.5 %collective-permute-start.11 = (bf16[4,360,128]{2,1,0:T(8,128)(2,1)S(1)}, bf16[4,360,128]{2,1,0:T(8,128)(2,1)S(1)}, u32[]{:S(2)}, u32[]{:S(2)}) collective-permute-start(bf16[4,360,128]{2,1,0:T(8,128)(2,1)S(1)} %copy-done.21), channel_id=1, source_target_pairs={{0,2},{1,3},{2,0},{3,1},{4,6},{5,7},{6,4},{7,5},{8,10},{9,11},{10,... | collective-permute-start | bytes 1105928 | tf_op jit(solution)/shard_map/ppermute | solution.py:238
  72.9 7.6 %collective-permute-start.20 = (bf16[4,2,360,128]{3,2,0,1:T(8,128)(2,1)S(1)}, bf16[4,2,360,128]{3,2,0,1:T(8,128)(2,1)S(1)}, u32[]{:S(2)}, u32[]{:S(2)}) collective-permute-start(bf16[4,2,360,128]{3,2,0,1:T(8,128)(2,1)S(1)} %maximum_select_fusion.13), channel_id=1, source_target_pairs={{0,1},{1,0},{2,3},{3,2},{4,5},{5,4},{6,7},{7,6},{8,9},{9,8},{10,11... | collective-permute-start | bytes 2211848 | tf_op jit(solution)/shard_map/ppermute | solution.py:238
  74.1 20.3 %collective-permute-start.22 = (bf16[4,360,256]{2,1,0:T(8,128)(2,1)S(1)}, bf16[4,360,256]{2,1,0:T(8,128)(2,1)S(1)}, u32[]{:S(2)}, u32[]{:S(2)}) collective-permute-start(bf16[4,360,256]{2,1,0:T(8,128)(2,1)S(1)} %get-tuple-element.98), channel_id=1, source_target_pairs={{0,2},{1,3},{2,0},{3,1},{4,6},{5,7},{6,4},{7,5},{8,10},{9,11},{10,... | collective-permute-start | bytes 2211848 | tf_op jit(solution)/shard_map/ppermute | solution.py:238
  80.0 3.4 %collective-permute-start.18 = (bf16[4,2,360,256]{3,2,0,1:T(8,128)(2,1)S(1)}, bf16[4,2,360,256]{3,2,0,1:T(8,128)(2,1)S(1)}, u32[]{:S(2)}, u32[]{:S(2)}) collective-permute-start(bf16[4,2,360,256]{3,2,0,1:T(8,128)(2,1)S(1)} %maximum_select_fusion.3), channel_id=1, source_target_pairs={{0,1},{1,0},{2,3},{3,2},{4,5},{5,4},{6,7},{7,6},{8,9},{9,8},{10,11... | collective-permute-start | bytes 4423688 | tf_op jit(solution)/shard_map/ppermute | solution.py:238
  91.2 4.6 %copy-start.11 = (f32[480,384]{1,0:T(8,128)}, f32[480,384]{1,0:T(8,128)S(1)}, u32[]{:S(2)}) copy-start(f32[480,384]{1,0:T(8,128)S(1)} %get-tuple-element.50.preact_ref) | copy-start | bytes 2211844
  91.2 4.6 %copy-start.13 = (bf16[480,640]{1,0:T(8,128)(2,1)}, bf16[480,640]{1,0:T(8,128)(2,1)S(1)}, u32[]{:S(2)}) copy-start(bf16[480,640]{1,0:T(8,128)(2,1)S(1)} %get-tuple-element.49.normed_ref) | copy-start | bytes 1843204
  95.8 5.9 %collective-permute-start.23 = (bf16[4,2,360,256]{3,2,0,1:T(8,128)(2,1)}, bf16[4,2,360,256]{3,2,0,1:T(8,128)(2,1)}, u32[]{:S(2)}, u32[]{:S(2)}) collective-permute-start(bf16[4,2,360,256]{3,2,0,1:T(8,128)(2,1)} %maximum_select_fusion.6), channel_id=1, source_target_pairs={{0,1},{1,0},{2,3},{3,2},{4,5},{5,4},{6,7},{7,6},{8,9},{9,8},{10,11... | collective-permute-start | bytes 4423688 | tf_op jit(solution)/shard_map/ppermute | solution.py:238
  95.9 16.4 %collective-permute-start.21 = (bf16[480,640]{1,0:T(8,128)(2,1)S(1)}, bf16[480,640]{1,0:T(8,128)(2,1)}, u32[]{:S(2)}, u32[]{:S(2)}) collective-permute-start(bf16[480,640]{1,0:T(8,128)(2,1)S(1)} %get-tuple-element.40.own_ref), channel_id=1, source_target_pairs={{0,16},{16,0},{1,17},{17,1},{2,18},{18,2},{3,19},{19,3},{4,20},{20... | collective-permute-start | bytes 1843208 | tf_op jit(solution)/shard_map/ppermute | solution.py:242
  104.2 8.1 %copy-start.9 = (bf16[5,3,32,640]{3,2,1,0:T(8,128)(2,1)S(1)}, bf16[5,3,32,640]{3,2,1,0:T(8,128)(2,1)}, u32[]{:S(2)}) copy-start(bf16[5,3,32,640]{3,2,1,0:T(8,128)(2,1)} %param.7) | copy-start | bytes 1843204
  129.4 3.8 %collective-permute-start.28 = (bf16[2,360,256]{2,1,0:T(8,128)(2,1)}, bf16[2,360,256]{2,1,0:T(8,128)(2,1)}, u32[]{:S(2)}, u32[]{:S(2)}) collective-permute-start(bf16[2,360,256]{2,1,0:T(8,128)(2,1)} %get-tuple-element.71), channel_id=1, source_target_pairs={{0,1},{1,0},{2,3},{3,2},{4,5},{5,4},{6,7},{7,6},{8,9},{9,8},{10,11... | collective-permute-start | bytes 1105928 | tf_op jit(solution)/shard_map/ppermute | solution.py:238
  129.5 3.7 %collective-permute-start.27 = (bf16[2,360,256]{2,1,0:T(8,128)(2,1)}, bf16[2,360,256]{2,1,0:T(8,128)(2,1)}, u32[]{:S(2)}, u32[]{:S(2)}) collective-permute-start(bf16[2,360,256]{2,1,0:T(8,128)(2,1)} %get-tuple-element.69), channel_id=1, source_target_pairs={{0,1},{1,0},{2,3},{3,2},{4,5},{5,4},{6,7},{7,6},{8,9},{9,8},{10,11... | collective-permute-start | bytes 1105928 | tf_op jit(solution)/shard_map/ppermute | solution.py:238
  130.0 3.3 %collective-permute-start.26 = (bf16[2,360,256]{2,1,0:T(8,128)(2,1)}, bf16[2,360,256]{2,1,0:T(8,128)(2,1)}, u32[]{:S(2)}, u32[]{:S(2)}) collective-permute-start(bf16[2,360,256]{2,1,0:T(8,128)(2,1)} %get-tuple-element.70), channel_id=1, source_target_pairs={{0,1},{1,0},{2,3},{3,2},{4,5},{5,4},{6,7},{7,6},{8,9},{9,8},{10,11... | collective-permute-start | bytes 1105928 | tf_op jit(solution)/shard_map/ppermute | solution.py:238
  130.1 3.2 %collective-permute-start.25 = (bf16[2,360,256]{2,1,0:T(8,128)(2,1)S(1)}, bf16[2,360,256]{2,1,0:T(8,128)(2,1)}, u32[]{:S(2)}, u32[]{:S(2)}) collective-permute-start(bf16[2,360,256]{2,1,0:T(8,128)(2,1)S(1)} %get-tuple-element.68), channel_id=1, source_target_pairs={{0,1},{1,0},{2,3},{3,2},{4,5},{5,4},{6,7},{7,6},{8,9},{9,8},{10,11... | collective-permute-start | bytes 1105928 | tf_op jit(solution)/shard_map/ppermute | solution.py:238
  130.5 16.2 %collective-permute-start.24 = (bf16[480,640]{1,0:T(8,128)(2,1)}, bf16[480,640]{1,0:T(8,128)(2,1)}, u32[]{:S(2)}, u32[]{:S(2)}) collective-permute-start(bf16[480,640]{1,0:T(8,128)(2,1)} %get-tuple-element.43.own_ref), channel_id=1, source_target_pairs={{0,16},{16,0},{1,17},{17,1},{2,18},{18,2},{3,19},{19,3},{4,20},{20... | collective-permute-start | bytes 1843208 | tf_op jit(solution)/shard_map/ppermute | solution.py:242
  134.8 11.9 %copy-start.10 = (bf16[5,3,32,640]{3,2,1,0:T(8,128)(2,1)S(1)}, bf16[5,3,32,640]{3,2,1,0:T(8,128)(2,1)}, u32[]{:S(2)}) copy-start(bf16[5,3,32,640]{3,2,1,0:T(8,128)(2,1)} %param.7) | copy-start | bytes 1843204
  134.8 11.9 %copy-start.12 = (f32[480,384]{1,0:T(8,128)S(1)}, f32[480,384]{1,0:T(8,128)}, u32[]{:S(2)}) copy-start(f32[480,384]{1,0:T(8,128)} %copy-done.11) | copy-start | bytes 2211844
  134.8 11.9 %copy-start.14 = (bf16[480,640]{1,0:T(8,128)(2,1)S(1)}, bf16[480,640]{1,0:T(8,128)(2,1)}, u32[]{:S(2)}) copy-start(bf16[480,640]{1,0:T(8,128)(2,1)} %copy-done.13) | copy-start | bytes 1843204
  134.8 11.9 %copy-start.16 = (bf16[480,640]{1,0:T(8,128)(2,1)S(1)}, bf16[480,640]{1,0:T(8,128)(2,1)}, u32[]{:S(2)}) copy-start(bf16[480,640]{1,0:T(8,128)(2,1)} %copy-done.15) | copy-start | bytes 1843204
  135.3 11.4 %copy-start.7 = (bf16[8,120,640]{2,1,0:T(8,128)(2,1)S(1)}, bf16[8,120,640]{2,1,0:T(8,128)(2,1)}, u32[]{:S(2)}) copy-start(bf16[8,120,640]{2,1,0:T(8,128)(2,1)} %copy-done.6) | copy-start | bytes 3686404
  135.4 19.8 %collective-permute-start.29 = (bf16[4,360,256]{2,1,0:T(8,128)(2,1)S(1)}, bf16[4,360,256]{2,1,0:T(8,128)(2,1)S(1)}, u32[]{:S(2)}, u32[]{:S(2)}) collective-permute-start(bf16[4,360,256]{2,1,0:T(8,128)(2,1)S(1)} %dynamic-slice_bitcast_fusion), channel_id=1, source_target_pairs={{0,2},{1,3},{2,0},{3,1},{4,6},{5,7},{6,4},{7,5},{8,10},{9,11},{10,... | collective-permute-start | bytes 2211848 | tf_op jit(solution)/shard_map/ppermute | solution.py:238
  146.7 7.8 %copy-start.5 = (bf16[5760,128]{1,0:T(8,128)(2,1)S(1)}, bf16[5760,128]{1,0:T(8,128)(2,1)}, u32[]{:S(2)}) copy-start(bf16[5760,128]{1,0:T(8,128)(2,1)} %copy-done.4) | copy-start | bytes 4423684
  155.1 3.2 %collective-permute-start.31 = (bf16[4,2,360,128]{3,2,0,1:T(8,128)(2,1)S(1)}, bf16[4,2,360,128]{3,2,0,1:T(8,128)(2,1)S(1)}, u32[]{:S(2)}, u32[]{:S(2)}) collective-permute-start(bf16[4,2,360,128]{3,2,0,1:T(8,128)(2,1)S(1)} %bitcast.335), channel_id=1, source_target_pairs={{0,1},{1,0},{2,3},{3,2},{4,5},{5,4},{6,7},{7,6},{8,9},{9,8},{10,11... | collective-permute-start | bytes 2211848 | tf_op jit(solution)/shard_map/ppermute | solution.py:238
  155.6 17.7 %collective-permute-start.30 = (bf16[4,2,360,256]{3,2,0,1:T(8,128)(2,1)S(1)}, bf16[4,2,360,256]{3,2,0,1:T(8,128)(2,1)S(1)}, u32[]{:S(2)}, u32[]{:S(2)}) collective-permute-start(bf16[4,2,360,256]{3,2,0,1:T(8,128)(2,1)S(1)} %bitcast.329), channel_id=1, source_target_pairs={{0,1},{1,0},{2,3},{3,2},{4,5},{5,4},{6,7},{7,6},{8,9},{9,8},{10,11... | collective-permute-start | bytes 4423688 | tf_op jit(solution)/shard_map/ppermute | solution.py:238
  157.8 18.0 %collective-permute-start.44 = (bf16[4,2,128,640]{3,2,1,0:T(8,128)(2,1)S(1)}, bf16[4,2,128,640]{3,2,1,0:T(8,128)(2,1)S(1)}, u32[]{:S(2)}, u32[]{:S(2)}) collective-permute-start(bf16[4,2,128,640]{3,2,1,0:T(8,128)(2,1)S(1)} %fusion.8), channel_id=1, source_target_pairs={{0,1},{1,0},{2,3},{3,2},{4,5},{5,4},{6,7},{7,6},{8,9},{9,8},{10,11... | collective-permute-start | bytes 3932168 | tf_op jit(solution)/shard_map/ppermute | solution.py:238
  158.6 10.6 %collective-permute-start.32 = (bf16[4,360,128]{2,1,0:T(8,128)(2,1)S(1)}, bf16[4,360,128]{2,1,0:T(8,128)(2,1)S(1)}, u32[]{:S(2)}, u32[]{:S(2)}) collective-permute-start(bf16[4,360,128]{2,1,0:T(8,128)(2,1)S(1)} %dynamic-slice_bitcast_fusion.7), channel_id=1, source_target_pairs={{0,2},{1,3},{2,0},{3,1},{4,6},{5,7},{6,4},{7,5},{8,10},{9,11},{10,... | collective-permute-start | bytes 1105928 | tf_op jit(solution)/shard_map/ppermute | solution.py:238
  160.1 25.2 %collective-permute-start.35 = (bf16[360,256]{1,0:T(8,128)(2,1)S(1)}, bf16[360,256]{1,0:T(8,128)(2,1)S(1)}, u32[]{:S(2)}, u32[]{:S(2)}) collective-permute-start(bf16[360,256]{1,0:T(8,128)(2,1)S(1)} %get-tuple-element.95), channel_id=1, source_target_pairs={{0,4},{1,5},{2,6},{3,7},{4,8},{5,9},{6,10},{7,11},{8,12},{9,13},{1... | collective-permute-start | bytes 552968 | tf_op jit(solution)/shard_map/ppermute | solution.py:238
  163.2 22.2 %collective-permute-start.36 = (bf16[360,256]{1,0:T(8,128)(2,1)S(1)}, bf16[360,256]{1,0:T(8,128)(2,1)S(1)}, u32[]{:S(2)}, u32[]{:S(2)}) collective-permute-start(bf16[360,256]{1,0:T(8,128)(2,1)S(1)} %get-tuple-element.94), channel_id=1, source_target_pairs={{0,8},{1,9},{2,10},{3,11},{4,12},{5,13},{6,14},{7,15},{8,0},{9,1},... | collective-permute-start | bytes 552968 | tf_op jit(solution)/shard_map/ppermute | solution.py:238
  169.2 16.1 %collective-permute-start.37 = (bf16[360,256]{1,0:T(8,128)(2,1)S(1)}, bf16[360,256]{1,0:T(8,128)(2,1)S(1)}, u32[]{:S(2)}, u32[]{:S(2)}) collective-permute-start(bf16[360,256]{1,0:T(8,128)(2,1)S(1)} %get-tuple-element.93), channel_id=1, source_target_pairs={{0,12},{1,13},{2,14},{3,15},{4,0},{5,1},{6,2},{7,3},{8,4},{9,5},{1... | collective-permute-start | bytes 552968 | tf_op jit(solution)/shard_map/ppermute | solution.py:238
  174.1 9.5 %collective-permute-start.33 = (bf16[4,360,128]{2,1,0:T(8,128)(2,1)S(1)}, bf16[4,360,128]{2,1,0:T(8,128)(2,1)S(1)}, u32[]{:S(2)}, u32[]{:S(2)}) collective-permute-start(bf16[4,360,128]{2,1,0:T(8,128)(2,1)S(1)} %dynamic-slice_bitcast_fusion.8), channel_id=1, source_target_pairs={{0,2},{1,3},{2,0},{3,1},{4,6},{5,7},{6,4},{7,5},{8,10},{9,11},{10,... | collective-permute-start | bytes 1105928 | tf_op jit(solution)/shard_map/ppermute | solution.py:238
  183.5 8.8 %collective-permute-start.34 = (bf16[4,360,128]{2,1,0:T(8,128)(2,1)S(1)}, bf16[4,360,128]{2,1,0:T(8,128)(2,1)S(1)}, u32[]{:S(2)}, u32[]{:S(2)}) collective-permute-start(bf16[4,360,128]{2,1,0:T(8,128)(2,1)S(1)} %dynamic-slice_bitcast_fusion.6), channel_id=1, source_target_pairs={{0,2},{1,3},{2,0},{3,1},{4,6},{5,7},{6,4},{7,5},{8,10},{9,11},{10,... | collective-permute-start | bytes 1105928 | tf_op jit(solution)/shard_map/ppermute | solution.py:238
  185.4 8.6 %collective-permute-start.40 = (bf16[360,128]{1,0:T(8,128)(2,1)S(1)}, bf16[360,128]{1,0:T(8,128)(2,1)S(1)}, u32[]{:S(2)}, u32[]{:S(2)}) collective-permute-start(bf16[360,128]{1,0:T(8,128)(2,1)S(1)} %get-tuple-element.125), channel_id=1, source_target_pairs={{0,12},{1,13},{2,14},{3,15},{4,0},{5,1},{6,2},{7,3},{8,4},{9,5},{1... | collective-permute-start | bytes 276488 | tf_op jit(solution)/shard_map/ppermute | solution.py:238
  187.0 7.3 %collective-permute-start.39 = (bf16[360,128]{1,0:T(8,128)(2,1)S(1)}, bf16[360,128]{1,0:T(8,128)(2,1)S(1)}, u32[]{:S(2)}, u32[]{:S(2)}) collective-permute-start(bf16[360,128]{1,0:T(8,128)(2,1)S(1)} %get-tuple-element.126), channel_id=1, source_target_pairs={{0,8},{1,9},{2,10},{3,11},{4,12},{5,13},{6,14},{7,15},{8,0},{9,1},... | collective-permute-start | bytes 276488 | tf_op jit(solution)/shard_map/ppermute | solution.py:238
  187.0 7.3 %collective-permute-start.38 = (bf16[360,128]{1,0:T(8,128)(2,1)S(1)}, bf16[360,128]{1,0:T(8,128)(2,1)S(1)}, u32[]{:S(2)}, u32[]{:S(2)}) collective-permute-start(bf16[360,128]{1,0:T(8,128)(2,1)S(1)} %get-tuple-element.124), channel_id=1, source_target_pairs={{0,4},{1,5},{2,6},{3,7},{4,8},{5,9},{6,10},{7,11},{8,12},{9,13},{1... | collective-permute-start | bytes 276488 | tf_op jit(solution)/shard_map/ppermute | solution.py:238
  192.3 13.8 %collective-permute-start.45 = (bf16[4,128,640]{2,1,0:T(8,128)(2,1)S(1)}, bf16[4,128,640]{2,1,0:T(8,128)(2,1)S(1)}, u32[]{:S(2)}, u32[]{:S(2)}) collective-permute-start(bf16[4,128,640]{2,1,0:T(8,128)(2,1)S(1)} %dynamic-slice_bitcast_fusion.1), channel_id=1, source_target_pairs={{0,2},{1,3},{2,0},{3,1},{4,6},{5,7},{6,4},{7,5},{8,10},{9,11},{10,... | collective-permute-start | bytes 1966088 | tf_op jit(solution)/shard_map/ppermute | solution.py:238
  194.7 11.5 %collective-permute-start.43 = (bf16[360,256]{1,0:T(8,128)(2,1)S(1)}, bf16[360,256]{1,0:T(8,128)(2,1)S(1)}, u32[]{:S(2)}, u32[]{:S(2)}) collective-permute-start(bf16[360,256]{1,0:T(8,128)(2,1)S(1)} %get-tuple-element.91), channel_id=1, source_target_pairs={{0,12},{1,13},{2,14},{3,15},{4,0},{5,1},{6,2},{7,3},{8,4},{9,5},{1... | collective-permute-start | bytes 552968 | tf_op jit(solution)/shard_map/ppermute | solution.py:238
  196.0 15.0 %collective-permute-start.42 = (bf16[360,256]{1,0:T(8,128)(2,1)S(1)}, bf16[360,256]{1,0:T(8,128)(2,1)S(1)}, u32[]{:S(2)}, u32[]{:S(2)}) collective-permute-start(bf16[360,256]{1,0:T(8,128)(2,1)S(1)} %get-tuple-element.92), channel_id=1, source_target_pairs={{0,8},{1,9},{2,10},{3,11},{4,12},{5,13},{6,14},{7,15},{8,0},{9,1},... | collective-permute-start | bytes 552968 | tf_op jit(solution)/shard_map/ppermute | solution.py:238
  196.0 15.0 %collective-permute-start.41 = (bf16[360,256]{1,0:T(8,128)(2,1)S(1)}, bf16[360,256]{1,0:T(8,128)(2,1)S(1)}, u32[]{:S(2)}, u32[]{:S(2)}) collective-permute-start(bf16[360,256]{1,0:T(8,128)(2,1)S(1)} %get-tuple-element.90), channel_id=1, source_target_pairs={{0,4},{1,5},{2,6},{3,7},{4,8},{5,9},{6,10},{7,11},{8,12},{9,13},{1... | collective-permute-start | bytes 552968 | tf_op jit(solution)/shard_map/ppermute | solution.py:238
  211.0 6.1 %collective-permute-start.49 = (bf16[128,640]{1,0:T(8,128)(2,1)S(1)}, bf16[128,640]{1,0:T(8,128)(2,1)S(1)}, u32[]{:S(2)}, u32[]{:S(2)}) collective-permute-start(bf16[128,640]{1,0:T(8,128)(2,1)S(1)} %get-tuple-element.115), channel_id=1, source_target_pairs={{0,12},{1,13},{2,14},{3,15},{4,0},{5,1},{6,2},{7,3},{8,4},{9,5},{1... | collective-permute-start | bytes 491528 | tf_op jit(solution)/shard_map/ppermute | solution.py:238
  211.1 15.0 %collective-permute-start.48 = (bf16[128,640]{1,0:T(8,128)(2,1)S(1)}, bf16[128,640]{1,0:T(8,128)(2,1)S(1)}, u32[]{:S(2)}, u32[]{:S(2)}) collective-permute-start(bf16[128,640]{1,0:T(8,128)(2,1)S(1)} %get-tuple-element.116), channel_id=1, source_target_pairs={{0,8},{1,9},{2,10},{3,11},{4,12},{5,13},{6,14},{7,15},{8,0},{9,1},... | collective-permute-start | bytes 491528 | tf_op jit(solution)/shard_map/ppermute | solution.py:238
  212.0 14.1 %collective-permute-start.47 = (bf16[128,640]{1,0:T(8,128)(2,1)S(1)}, bf16[128,640]{1,0:T(8,128)(2,1)S(1)}, u32[]{:S(2)}, u32[]{:S(2)}) collective-permute-start(bf16[128,640]{1,0:T(8,128)(2,1)S(1)} %get-tuple-element.114), channel_id=1, source_target_pairs={{0,4},{1,5},{2,6},{3,7},{4,8},{5,9},{6,10},{7,11},{8,12},{9,13},{1... | collective-permute-start | bytes 491528 | tf_op jit(solution)/shard_map/ppermute | solution.py:238
  214.2 12.0 %collective-permute-start.46 = (bf16[360,384]{1,0:T(8,128)(2,1)S(1)}, bf16[360,384]{1,0:T(8,128)(2,1)S(1)}, u32[]{:S(2)}, u32[]{:S(2)}) collective-permute-start(bf16[360,384]{1,0:T(8,128)(2,1)S(1)} %pad_maximum_fusion.6), channel_id=1, source_target_pairs={{0,16},{16,0},{1,17},{17,1},{2,18},{18,2},{3,19},{19,3},{4,20},{20... | collective-permute-start | bytes 829448 | tf_op jit(solution)/shard_map/ppermute | solution.py:242
  226.4 7.5 %copy-start.1 = (bf16[1,360,640]{2,1,0:T(8,128)(2,1)S(1)}, bf16[1,360,640]{2,1,0:T(8,128)(2,1)}, u32[]{:S(2)}) copy-start(bf16[1,360,640]{2,1,0:T(8,128)(2,1)} %param.8) | copy-start | bytes 1382404
  228.5 4.4 %collective-permute-start.50 = (bf16[64,640]{1,0:T(8,128)(2,1)S(1)}, bf16[64,640]{1,0:T(8,128)(2,1)S(1)}, u32[]{:S(2)}, u32[]{:S(2)}) collective-permute-start(bf16[64,640]{1,0:T(8,128)(2,1)S(1)} %select_convert_fusion.1), channel_id=1, source_target_pairs={{0,16},{16,0},{1,17},{17,1},{2,18},{18,2},{3,19},{19,3},{4,20},{20... | collective-permute-start | bytes 245768 | tf_op jit(solution)/shard_map/ppermute | solution.py:242
  (11 other events, 19.0 us)

commit v4 on v3

--- a/solution.py
+++ b/solution.py
@@ -360,10 +360,10 @@
     )
 
 
-def gathered_over_z(value, earlier=None):
+def gathered_over_z(value, earlier=None, beside=None):
     z, _, _ = coordinates()
     value = after(value, earlier)
-    sent = sent_over_z(value)
+    sent = after(sent_over_z(value), beside)
     return (
         jnp.stack([lax.select_n((z - place) % GRID[0], value, *sent) for place in range(GRID[0])]),
         sent,
@@ -640,8 +640,8 @@
     given = swapped(spatial_own[:, main:])
     main_own, main_given = spatial_own[:, :main], given[:, :main]
     tails = jnp.where(tail, spatial_own[:, 2 * main :], given[:, main:])
-    line, sent = gathered_over_z(jnp.where(first, main_own, main_given), sent)
-    line_tails, sent = gathered_over_z(tails, (sent, side_temporal))
+    line, sent = gathered_over_z(jnp.where(first, main_own, main_given), sent, side_temporal)
+    line_tails, sent = gathered_over_z(tails, sent)
     side_low = sent_over_y(line[..., :LANES])
     side_high = sent_over_y(line[..., LANES:], side_low)
     side_tails = sent_over_y(line_tails)
@@ -755,7 +755,8 @@
         share_spatial, order.astype(F32), (((1,), (1,)), ((), ())), precision=lax.Precision.HIGH
     )
     low, high = share_temporal[:PIECE], share_temporal[PIECE:]
-    given = swapped(after(jnp.where(first, high, low).astype(BF16), share_spatial)).astype(F32)
+    given = swapped(jnp.where(first, high, low).astype(BF16))
+    given = after(given, share_spatial).astype(F32)
     share_temporal = shard_of(jnp.where(first, low, high), given, temporal_weight.shape[1])
     return (share_spatial[None], share_temporal[None])
 

time: 238 us -> 236 us (level)
  other arithmetic: 21.6 us -> 19 us
    ppermute x45, waiting for transfers between devices: 75.9 us -> 80.5 us  [shifted(): return lax.ppermute(value, 'dp', pairs)]
    ppermute x6, waiting for transfers between devices: 23.7 us -> 20 us  [swapped(): return lax.ppermute(value, 'pipe', [(0, 1), (1, 0)])]
    select_n x13, other arithmetic: 9.24 us -> 6.5 us  [in_order(): jnp.where(swap, jnp.concatenate([other, own], axis), jnp.concatenate([own...]
  transfers between devices with their start and end apart: 51 -> 51, of which waited for: 25 -> 23; matrix products, arithmetic and copies ran while one was open for 12% -> 12% of each run, Pallas kernels for 6% -> 6%
where the time goes in v4:
time: 236 us; the launch traced here: 232 us
  waiting for transfers between devices  100 us (42%)
  starting transfers between devices  64.9 us (28%)
  Pallas kernels  28.8 us (12%)
  other arithmetic  19 us (8%)
  local copies, waits for them, and re-layouts  13.4 us (6%)
  matrix products  2.84 us (1%)
    ppermute x45, waiting for transfers between devices, shifted(): return lax.ppermute(value, 'dp', pairs)  80.5 us
    ppermute x45, starting transfers between devices, shifted(): return lax.ppermute(value, 'dp', pairs)  55.7 us
    ppermute x6, waiting for transfers between devices, swapped(): return lax.ppermute(value, 'pipe', [(0, 1), (1, 0)])  20 us
    pallas_call x1, Pallas kernels, paired_device(): vmem_call(functools.partial(second_forward, frames), (shape((rows, channe...  10.4 us
    ppermute x6, starting transfers between devices, swapped(): return lax.ppermute(value, 'pipe', [(0, 1), (1, 0)])  9.19 us
    pallas_call x1, Pallas kernels, paired_device(): vmem_call(functools.partial(first_terms, frames), terms_shape(), flops=sp...  7.76 us
    select_n x13, other arithmetic, in_order(): jnp.where(swap, jnp.concatenate([other, own], axis), jnp.concatenate([own...  6.5 us
    pallas_call x1, Pallas kernels, paired_device(): vmem_call(functools.partial(first_forward, frames), (shape((rows, channel...  6.25 us
  transfers between devices with their start and end apart: 51, of which 23 were waited for; matrix products, arithmetic and copies ran while one was open for 12% of the time, Pallas kernels for 6%

profile of v4, /device:TPU:0, one launch (start us, length us, event | category | flops | bytes accessed | tf_op | source)
XLA Modules:
  0.0 231.6 jit_solution(6965672684118417455)
XLA Ops:
  0.6 0.9 slice_bitcast_fusion.27
  2.5 3.0 %collective-permute-start = (bf16[64,640]{1,0:T(8,128)(2,1)S(1)}, bf16[64,640]{1,0:T(8,128)(2,1)S(1)}, u32[]{:S(2)}, u32[]{:S(2)}) collective-permute-start(bf16[64,640]{1,0:T(8,128)(2,1)S(1)} %fusion.43), channel_id=1, source_target_pairs={{0,16},{16,0},{1,17},{17,1},{2,18},{18,2},{3,19},{19,3},{4,20},{20... | collective-permute-start | bytes 245768 | tf_op jit(solution)/shard_map/ppermute | solution.py:242
  7.9 3.2 %collective-permute-start.2 = (bf16[128,640]{1,0:T(8,128)(2,1)S(1)}, bf16[128,640]{1,0:T(8,128)(2,1)S(1)}, u32[]{:S(2)}, u32[]{:S(2)}) collective-permute-start(bf16[128,640]{1,0:T(8,128)(2,1)S(1)} %maximum_select_fusion.15), channel_id=1, source_target_pairs={{0,8},{1,9},{2,10},{3,11},{4,12},{5,13},{6,14},{7,15},{8,0},{9,1},... | collective-permute-start | bytes 491528 | tf_op jit(solution)/shard_map/ppermute | solution.py:238
  11.1 1.3 collective-permute-start.3
  13.1 7.5 %collective-permute-done.2 = bf16[128,640]{1,0:T(8,128)(2,1)S(1)} collective-permute-done((bf16[128,640]{1,0:T(8,128)(2,1)S(1)}, bf16[128,640]{1,0:T(8,128)(2,1)S(1)}, u32[]{:S(2)}, u32[]{:S(2)}) %collective-permute-start.2) | collective-permute-done | bytes 163872 | tf_op jit(solution)/shard_map/ppermute | solution.py:238
  20.7 1.8 collective-permute-done.1
  22.7 1.6 collective-permute-start.4
  24.4 1.0 broadcast_select_fusion.3
  25.4 3.0 %collective-permute-start.7 = (bf16[360,256]{1,0:T(8,128)(2,1)S(1)}, bf16[360,256]{1,0:T(8,128)(2,1)S(1)}, u32[]{:S(2)}, u32[]{:S(2)}) collective-permute-start(bf16[360,256]{1,0:T(8,128)(2,1)S(1)} %get-tuple-element.37), channel_id=1, source_target_pairs={{0,4},{1,5},{2,6},{3,7},{4,8},{5,9},{6,10},{7,11},{8,12},{9,13},{1... | collective-permute-start | bytes 552968 | tf_op jit(solution)/shard_map/ppermute | solution.py:238
  28.4 2.0 collective-permute-start.8
  30.4 2.8 %collective-permute-start.9 = (bf16[360,256]{1,0:T(8,128)(2,1)S(1)}, bf16[360,256]{1,0:T(8,128)(2,1)S(1)}, u32[]{:S(2)}, u32[]{:S(2)}) collective-permute-start(bf16[360,256]{1,0:T(8,128)(2,1)S(1)} %get-tuple-element.37), channel_id=1, source_target_pairs={{0,12},{1,13},{2,14},{3,15},{4,0},{5,1},{6,2},{7,3},{8,4},{9,5},{1... | collective-permute-start | bytes 552968 | tf_op jit(solution)/shard_map/ppermute | solution.py:238
  33.2 0.9 slice_select_fusion.2
  34.2 6.6 %collective-permute-done.8 = bf16[360,256]{1,0:T(8,128)(2,1)S(1)} collective-permute-done((bf16[360,256]{1,0:T(8,128)(2,1)S(1)}, bf16[360,256]{1,0:T(8,128)(2,1)S(1)}, u32[]{:S(2)}, u32[]{:S(2)}) %collective-permute-start.8) | collective-permute-done | bytes 184352 | tf_op jit(solution)/shard_map/ppermute | solution.py:238
  40.9 6.3 %collective-permute-start.12 = (bf16[360,128]{1,0:T(8,128)(2,1)S(1)}, bf16[360,128]{1,0:T(8,128)(2,1)S(1)}, u32[]{:S(2)}, u32[]{:S(2)}) collective-permute-start(bf16[360,128]{1,0:T(8,128)(2,1)S(1)} %slice_select_fusion.2), channel_id=1, source_target_pairs={{0,4},{1,5},{2,6},{3,7},{4,8},{5,9},{6,10},{7,11},{8,12},{9,13},{1... | collective-permute-start | bytes 276488 | tf_op jit(solution)/shard_map/ppermute | solution.py:238
  47.2 3.4 %collective-permute-start.13 = (bf16[360,128]{1,0:T(8,128)(2,1)S(1)}, bf16[360,128]{1,0:T(8,128)(2,1)S(1)}, u32[]{:S(2)}, u32[]{:S(2)}) collective-permute-start(bf16[360,128]{1,0:T(8,128)(2,1)S(1)} %slice_select_fusion.2), channel_id=1, source_target_pairs={{0,8},{1,9},{2,10},{3,11},{4,12},{5,13},{6,14},{7,15},{8,0},{9,1},... | collective-permute-start | bytes 276488 | tf_op jit(solution)/shard_map/ppermute | solution.py:238
  51.5 1.8 collective-permute-done.12
  53.2 2.7 %collective-permute-done.13 = bf16[360,128]{1,0:T(8,128)(2,1)S(1)} collective-permute-done((bf16[360,128]{1,0:T(8,128)(2,1)S(1)}, bf16[360,128]{1,0:T(8,128)(2,1)S(1)}, u32[]{:S(2)}, u32[]{:S(2)}) %collective-permute-start.13) | collective-permute-done | bytes 92192 | tf_op jit(solution)/shard_map/ppermute | solution.py:238
  57.2 3.8 %collective-permute-done.10 = bf16[4,360,128]{2,1,0:T(8,128)(2,1)S(1)} collective-permute-done((bf16[4,360,128]{2,1,0:T(8,128)(2,1)S(1)}, bf16[4,360,128]{2,1,0:T(8,128)(2,1)S(1)}, u32[]{:S(2)}, u32[]{:S(2)}) %collective-permute-start.10) | collective-permute-done | bytes 368672 | tf_op jit(solution)/shard_map/ppermute | solution.py:238
  61.0 1.0 collective-permute-start.15
  61.9 1.6 collective-permute-start.16
  63.5 2.0 collective-permute-start.17
  66.1 1.1 collective-permute-done.19
  67.6 1.0 collective-permute-done.15
  68.6 5.7 %collective-permute-done.16 = bf16[360,256]{1,0:T(8,128)(2,1)S(1)} collective-permute-done((bf16[360,256]{1,0:T(8,128)(2,1)S(1)}, bf16[360,256]{1,0:T(8,128)(2,1)S(1)}, u32[]{:S(2)}, u32[]{:S(2)}) %collective-permute-start.16) | collective-permute-done | bytes 184352 | tf_op jit(solution)/shard_map/ppermute | solution.py:238
  74.6 1.0 fusion.83
  76.2 0.9 collective-permute-done.11
  79.1 1.3 slice_bitcast_fusion.3
  82.5 6.2 %shard_map.68 = (bf16[480,640]{1,0:T(8,128)(2,1)S(1)}, f32[480,384]{1,0:T(8,128)S(1)}, bf16[480,640]{1,0:T(8,128)(2,1)S(1)}) custom-call(bf16[480,640]{1,0:T(8,128)(2,1)S(1)} %bitcast.309, f32[5,640]{1,0:T(8,128)S(1)} %pad_maximum_fusion.7.embedding_ref, f32[1,384]{1,0:T(1,128)S(1)} %select_n.855.keep_ref, bf16[960,640]{1,0:T(8,128)(2,1)S(1)} %bitcast.306, ...), custom_call_target="tpu_custom_call" | custom-call | flops 7077888000 | bytes 5898240 | tf_op jit(solution)/shard_map/pallas_call | solution.py:671
  88.7 5.8 %collective-permute-done.22 = bf16[4,360,256]{2,1,0:T(8,128)(2,1)S(1)} collective-permute-done((bf16[4,360,256]{2,1,0:T(8,128)(2,1)S(1)}, bf16[4,360,256]{2,1,0:T(8,128)(2,1)S(1)}, u32[]{:S(2)}, u32[]{:S(2)}) %collective-permute-start.22) | collective-permute-done | bytes 737312 | tf_op jit(solution)/shard_map/ppermute | solution.py:238
  94.5 1.4 maximum_select_fusion.6
  96.0 1.6 collective-permute-start.21
  97.5 1.1 slice.283
  98.6 1.1 slice.284
  99.8 1.7 maximum_select_fusion.12
  101.8 2.4 %maximum_select_fusion.1 = bf16[4,2,2,360,256]{4,3,0,2,1:T(8,128)(2,1)S(1)} fusion(bf16[4,2,1,360,256]{4,3,0,2,1:T(8,128)(2,1)S(1)} %bitcast_select_fusion, bf16[4,2,1,360,256]{4,3,0,2,1:T(8,128)(2,1)} %bitcast.60, pred[]{:T(512)S(6)} %eq.114), kind=kLoop, calls=%fused_computation.5 | loop fusion | flops 4423680 | bytes 5898241 | tf_op jit(solution)/shard_map/jit(_where)/select_n | solution.py:266
  104.5 7.9 %collective-permute-done.21.sent_ref = bf16[480,640]{1,0:T(8,128)(2,1)} collective-permute-done((bf16[480,640]{1,0:T(8,128)(2,1)S(1)}, bf16[480,640]{1,0:T(8,128)(2,1)}, u32[]{:S(2)}, u32[]{:S(2)}) %collective-permute-start.21) | collective-permute-done | bytes 614432 | tf_op jit(solution)/shard_map/ppermute | solution.py:242
  112.3 10.4 %shard_map.69 = (bf16[480,640]{1,0:T(8,128)(2,1)S(1)}, bf16[480,640]{1,0:T(8,128)(2,1)S(1)}, bf16[480,384]{1,0:T(8,128)(2,1)S(1)}, bf16[480,384]{1,0:T(8,128)(2,1)S(1)}, bf16[480,640]{1,0:T(8,128)(2,1)}) custom-call(bf16[480,640]{1,0:T(8,128)(2,1)S(1)} %bitcast.310, bf16[480,640]{1,0:T(8,128)(2,1)S(1)} %get-tuple-element.46.own_ref, ...), custom_call_target="tpu_custom_call" | custom-call | flops 12386304000 | bytes 5898240 | tf_op jit(solution)/shard_map/pallas_call | solution.py:680
  122.8 4.4 %shard_map.70 = (bf16[5760,256]{1,0:T(8,128)(2,1)S(1)}, bf16[5760,128]{1,0:T(8,128)(2,1)S(1)}, bf16[960,640]{1,0:T(8,128)(2,1)S(1)}) custom-call(bf16[480,640]{1,0:T(8,128)(2,1)S(1)} %get-tuple-element.50.normed_ref, bf16[480,384]{1,0:T(8,128)(2,1)S(1)} %get-tuple-element.51.pre_grad_ref, bf16[480,384]{1,0:T(8,128)(2,1)S(1)} %get-tuple-element.52.activated_ref, ...), custom_call_target="tpu_custom_call" | custom-call | flops 7077888000 | bytes 5898240 | tf_op jit(solution)/shard_map/pallas_call | solution.py:707
  127.2 1.2 dynamic-slice_bitcast_fusion.5
  130.6 1.5 collective-permute-start.24
  132.1 1.1 slice.291
  133.3 1.5 pad_maximum_fusion
  136.0 10.7 %collective-permute-done.24.sent_ref = bf16[480,640]{1,0:T(8,128)(2,1)} collective-permute-done((bf16[480,640]{1,0:T(8,128)(2,1)}, bf16[480,640]{1,0:T(8,128)(2,1)}, u32[]{:S(2)}, u32[]{:S(2)}) %collective-permute-start.24) | collective-permute-done | bytes 614432 | tf_op jit(solution)/shard_map/ppermute | solution.py:242
  146.8 7.8 %shard_map.71 = (bf16[5760,256]{1,0:T(8,128)(2,1)S(1)}, bf16[5760,128]{1,0:T(8,128)(2,1)S(1)}, bf16[960,640]{1,0:T(8,128)(2,1)S(1)}) custom-call(bf16[480,640]{1,0:T(8,128)(2,1)S(1)} %copy-done.16, f32[5,640]{1,0:T(8,128)S(1)} %pad_maximum_fusion.7.embedding_ref, bf16[480,640]{1,0:T(8,128)(2,1)S(1)} %bitcast.313, ...), custom_call_target="tpu_custom_call" | custom-call | flops 8847360000 | bytes 7372800 | tf_op jit(solution)/shard_map/pallas_call | solution.py:717
  159.6 2.8 %collective-permute-start.35 = (bf16[360,256]{1,0:T(8,128)(2,1)S(1)}, bf16[360,256]{1,0:T(8,128)(2,1)S(1)}, u32[]{:S(2)}, u32[]{:S(2)}) collective-permute-start(bf16[360,256]{1,0:T(8,128)(2,1)S(1)} %get-tuple-element.101), channel_id=1, source_target_pairs={{0,4},{1,5},{2,6},{3,7},{4,8},{5,9},{6,10},{7,11},{8,12},{9,13},{1... | collective-permute-start | bytes 552968 | tf_op jit(solution)/shard_map/ppermute | solution.py:238
  162.4 1.3 collective-permute-start.36
  163.8 5.5 %collective-permute-done.32 = bf16[4,360,128]{2,1,0:T(8,128)(2,1)S(1)} collective-permute-done((bf16[4,360,128]{2,1,0:T(8,128)(2,1)S(1)}, bf16[4,360,128]{2,1,0:T(8,128)(2,1)S(1)}, u32[]{:S(2)}, u32[]{:S(2)}) %collective-permute-start.32) | collective-permute-done | bytes 368672 | tf_op jit(solution)/shard_map/ppermute | solution.py:238
  169.3 2.6 %collective-permute-start.37 = (bf16[360,256]{1,0:T(8,128)(2,1)S(1)}, bf16[360,256]{1,0:T(8,128)(2,1)S(1)}, u32[]{:S(2)}, u32[]{:S(2)}) collective-permute-start(bf16[360,256]{1,0:T(8,128)(2,1)S(1)} %get-tuple-element.99), channel_id=1, source_target_pairs={{0,12},{1,13},{2,14},{3,15},{4,0},{5,1},{6,2},{7,3},{8,4},{9,5},{1... | collective-permute-start | bytes 552968 | tf_op jit(solution)/shard_map/ppermute | solution.py:238
  172.8 1.5 collective-permute-start.33
  174.7 7.5 %collective-permute-done.33 = bf16[4,360,128]{2,1,0:T(8,128)(2,1)S(1)} collective-permute-done((bf16[4,360,128]{2,1,0:T(8,128)(2,1)S(1)}, bf16[4,360,128]{2,1,0:T(8,128)(2,1)S(1)}, u32[]{:S(2)}, u32[]{:S(2)}) %collective-permute-start.33) | collective-permute-done | bytes 368672 | tf_op jit(solution)/shard_map/ppermute | solution.py:238
  182.3 1.5 collective-permute-start.34
  184.9 1.9 collective-permute-start.38
  186.9 4.1 %collective-permute-done.34 = bf16[4,360,128]{2,1,0:T(8,128)(2,1)S(1)} collective-permute-done((bf16[4,360,128]{2,1,0:T(8,128)(2,1)S(1)}, bf16[4,360,128]{2,1,0:T(8,128)(2,1)S(1)}, u32[]{:S(2)}, u32[]{:S(2)}) %collective-permute-start.34) | collective-permute-done | bytes 368672 | tf_op jit(solution)/shard_map/ppermute | solution.py:238
  191.0 1.5 collective-permute-start.45
  192.9 1.4 collective-permute-start.43
  194.2 1.8 collective-permute-start.41
  196.0 8.8 %collective-permute-done.45 = bf16[4,128,640]{2,1,0:T(8,128)(2,1)S(1)} collective-permute-done((bf16[4,128,640]{2,1,0:T(8,128)(2,1)S(1)}, bf16[4,128,640]{2,1,0:T(8,128)(2,1)S(1)}, u32[]{:S(2)}, u32[]{:S(2)}) %collective-permute-start.45) | collective-permute-done | bytes 655392 | tf_op jit(solution)/shard_map/ppermute | solution.py:238
  205.0 4.6 %collective-permute-done.42 = bf16[360,256]{1,0:T(8,128)(2,1)S(1)} collective-permute-done((bf16[360,256]{1,0:T(8,128)(2,1)S(1)}, bf16[360,256]{1,0:T(8,128)(2,1)S(1)}, u32[]{:S(2)}, u32[]{:S(2)}) %collective-permute-start.42) | collective-permute-done | bytes 184352 | tf_op jit(solution)/shard_map/ppermute | solution.py:238
  209.7 1.4 collective-permute-start.48
  211.1 1.9 collective-permute-start.47
  213.3 1.6 collective-permute-start.46
  215.2 10.7 %collective-permute-done.48 = bf16[128,640]{1,0:T(8,128)(2,1)S(1)} collective-permute-done((bf16[128,640]{1,0:T(8,128)(2,1)S(1)}, bf16[128,640]{1,0:T(8,128)(2,1)S(1)}, u32[]{:S(2)}, u32[]{:S(2)}) %collective-permute-start.48) | collective-permute-done | bytes 163872 | tf_op jit(solution)/shard_map/ppermute | solution.py:238
  226.1 1.6 collective-permute-start.50
  227.8 2.1 fusion.3
  (195 shorter events, 26.2 us)
Async XLA Ops:
  0.6 4.9 %copy-start = (bf16[1,360,640]{2,1,0:T(8,128)(2,1)S(1)}, bf16[1,360,640]{2,1,0:T(8,128)(2,1)}, u32[]{:S(2)}) copy-start(bf16[1,360,640]{2,1,0:T(8,128)(2,1)} %param.8) | copy-start | bytes 1382404
  1.5 5.5 %copy-start.21 = (s32[5]{0:T(128)S(1)}, s32[5]{0:T(128)}, u32[]{:S(2)}) copy-start(s32[5]{0:T(128)} %param.6) | copy-start | bytes 64
  2.5 5.4 %collective-permute-start = (bf16[64,640]{1,0:T(8,128)(2,1)S(1)}, bf16[64,640]{1,0:T(8,128)(2,1)S(1)}, u32[]{:S(2)}, u32[]{:S(2)}) collective-permute-start(bf16[64,640]{1,0:T(8,128)(2,1)S(1)} %fusion.43), channel_id=1, source_target_pairs={{0,16},{16,0},{1,17},{17,1},{2,18},{18,2},{3,19},{19,3},{4,20},{20... | collective-permute-start | bytes 245768 | tf_op jit(solution)/shard_map/ppermute | solution.py:242
  7.0 17.4 %collective-permute-start.6 = (bf16[360,384]{1,0:T(8,128)(2,1)}, bf16[360,384]{1,0:T(8,128)(2,1)}, u32[]{:S(2)}, u32[]{:S(2)}) collective-permute-start(bf16[360,384]{1,0:T(8,128)(2,1)} %slice.274), channel_id=1, source_target_pairs={{0,16},{16,0},{1,17},{17,1},{2,18},{18,2},{3,19},{19,3},{4,20},{20... | collective-permute-start | bytes 829448 | tf_op jit(solution)/shard_map/ppermute | solution.py:242
  7.9 12.7 %collective-permute-start.2 = (bf16[128,640]{1,0:T(8,128)(2,1)S(1)}, bf16[128,640]{1,0:T(8,128)(2,1)S(1)}, u32[]{:S(2)}, u32[]{:S(2)}) collective-permute-start(bf16[128,640]{1,0:T(8,128)(2,1)S(1)} %maximum_select_fusion.15), channel_id=1, source_target_pairs={{0,8},{1,9},{2,10},{3,11},{4,12},{5,13},{6,14},{7,15},{8,0},{9,1},... | collective-permute-start | bytes 491528 | tf_op jit(solution)/shard_map/ppermute | solution.py:238
  11.1 9.6 %collective-permute-start.3 = (bf16[128,640]{1,0:T(8,128)(2,1)S(1)}, bf16[128,640]{1,0:T(8,128)(2,1)S(1)}, u32[]{:S(2)}, u32[]{:S(2)}) collective-permute-start(bf16[128,640]{1,0:T(8,128)(2,1)S(1)} %maximum_select_fusion.15), channel_id=1, source_target_pairs={{0,12},{1,13},{2,14},{3,15},{4,0},{5,1},{6,2},{7,3},{8,4},{9,5},{1... | collective-permute-start | bytes 491528 | tf_op jit(solution)/shard_map/ppermute | solution.py:238
  12.4 10.0 %collective-permute-start.1 = (bf16[128,640]{1,0:T(8,128)(2,1)S(1)}, bf16[128,640]{1,0:T(8,128)(2,1)S(1)}, u32[]{:S(2)}, u32[]{:S(2)}) collective-permute-start(bf16[128,640]{1,0:T(8,128)(2,1)S(1)} %maximum_select_fusion.15), channel_id=1, source_target_pairs={{0,4},{1,5},{2,6},{3,7},{4,8},{5,9},{6,10},{7,11},{8,12},{9,13},{1... | collective-permute-start | bytes 491528 | tf_op jit(solution)/shard_map/ppermute | solution.py:238
  22.7 18.0 %collective-permute-start.4 = (bf16[4,128,640]{2,1,0:T(8,128)(2,1)S(1)}, bf16[4,128,640]{2,1,0:T(8,128)(2,1)S(1)}, u32[]{:S(2)}, u32[]{:S(2)}) collective-permute-start(bf16[4,128,640]{2,1,0:T(8,128)(2,1)S(1)} %get-tuple-element.125), channel_id=1, source_target_pairs={{0,2},{1,3},{2,0},{3,1},{4,6},{5,7},{6,4},{7,5},{8,10},{9,11},{10,... | collective-permute-start | bytes 1966088 | tf_op jit(solution)/shard_map/ppermute | solution.py:238
  25.4 8.8 %collective-permute-start.7 = (bf16[360,256]{1,0:T(8,128)(2,1)S(1)}, bf16[360,256]{1,0:T(8,128)(2,1)S(1)}, u32[]{:S(2)}, u32[]{:S(2)}) collective-permute-start(bf16[360,256]{1,0:T(8,128)(2,1)S(1)} %get-tuple-element.37), channel_id=1, source_target_pairs={{0,4},{1,5},{2,6},{3,7},{4,8},{5,9},{6,10},{7,11},{8,12},{9,13},{1... | collective-permute-start | bytes 552968 | tf_op jit(solution)/shard_map/ppermute | solution.py:238
  28.4 12.4 %collective-permute-start.8 = (bf16[360,256]{1,0:T(8,128)(2,1)S(1)}, bf16[360,256]{1,0:T(8,128)(2,1)S(1)}, u32[]{:S(2)}, u32[]{:S(2)}) collective-permute-start(bf16[360,256]{1,0:T(8,128)(2,1)S(1)} %get-tuple-element.37), channel_id=1, source_target_pairs={{0,8},{1,9},{2,10},{3,11},{4,12},{5,13},{6,14},{7,15},{8,0},{9,1},... | collective-permute-start | bytes 552968 | tf_op jit(solution)/shard_map/ppermute | solution.py:238
  30.4 10.4 %collective-permute-start.9 = (bf16[360,256]{1,0:T(8,128)(2,1)S(1)}, bf16[360,256]{1,0:T(8,128)(2,1)S(1)}, u32[]{:S(2)}, u32[]{:S(2)}) collective-permute-start(bf16[360,256]{1,0:T(8,128)(2,1)S(1)} %get-tuple-element.37), channel_id=1, source_target_pairs={{0,12},{1,13},{2,14},{3,15},{4,0},{5,1},{6,2},{7,3},{8,4},{9,5},{1... | collective-permute-start | bytes 552968 | tf_op jit(solution)/shard_map/ppermute | solution.py:238
  40.9 12.4 %collective-permute-start.12 = (bf16[360,128]{1,0:T(8,128)(2,1)S(1)}, bf16[360,128]{1,0:T(8,128)(2,1)S(1)}, u32[]{:S(2)}, u32[]{:S(2)}) collective-permute-start(bf16[360,128]{1,0:T(8,128)(2,1)S(1)} %slice_select_fusion.2), channel_id=1, source_target_pairs={{0,4},{1,5},{2,6},{3,7},{4,8},{5,9},{6,10},{7,11},{8,12},{9,13},{1... | collective-permute-start | bytes 276488 | tf_op jit(solution)/shard_map/ppermute | solution.py:238
  47.2 8.7 %collective-permute-start.13 = (bf16[360,128]{1,0:T(8,128)(2,1)S(1)}, bf16[360,128]{1,0:T(8,128)(2,1)S(1)}, u32[]{:S(2)}, u32[]{:S(2)}) collective-permute-start(bf16[360,128]{1,0:T(8,128)(2,1)S(1)} %slice_select_fusion.2), channel_id=1, source_target_pairs={{0,8},{1,9},{2,10},{3,11},{4,12},{5,13},{6,14},{7,15},{8,0},{9,1},... | collective-permute-start | bytes 276488 | tf_op jit(solution)/shard_map/ppermute | solution.py:238
  50.6 5.6 %collective-permute-start.14 = (bf16[360,128]{1,0:T(8,128)(2,1)S(1)}, bf16[360,128]{1,0:T(8,128)(2,1)S(1)}, u32[]{:S(2)}, u32[]{:S(2)}) collective-permute-start(bf16[360,128]{1,0:T(8,128)(2,1)S(1)} %slice_select_fusion.2), channel_id=1, source_target_pairs={{0,12},{1,13},{2,14},{3,15},{4,0},{5,1},{6,2},{7,3},{8,4},{9,5},{1... | collective-permute-start | bytes 276488 | tf_op jit(solution)/shard_map/ppermute | solution.py:238
  50.9 10.1 %collective-permute-start.10 = (bf16[4,360,128]{2,1,0:T(8,128)(2,1)S(1)}, bf16[4,360,128]{2,1,0:T(8,128)(2,1)S(1)}, u32[]{:S(2)}, u32[]{:S(2)}) collective-permute-start(bf16[4,360,128]{2,1,0:T(8,128)(2,1)S(1)} %get-tuple-element.115), channel_id=1, source_target_pairs={{0,2},{1,3},{2,0},{3,1},{4,6},{5,7},{6,4},{7,5},{8,10},{9,11},{10,... | collective-permute-start | bytes 1105928 | tf_op jit(solution)/shard_map/ppermute | solution.py:238
  56.4 10.7 %collective-permute-start.19 = (bf16[4,360,128]{2,1,0:T(8,128)(2,1)S(1)}, bf16[4,360,128]{2,1,0:T(8,128)(2,1)S(1)}, u32[]{:S(2)}, u32[]{:S(2)}) collective-permute-start(bf16[4,360,128]{2,1,0:T(8,128)(2,1)S(1)} %get-tuple-element.135), channel_id=1, source_target_pairs={{0,2},{1,3},{2,0},{3,1},{4,6},{5,7},{6,4},{7,5},{8,10},{9,11},{10,... | collective-permute-start | bytes 1105928 | tf_op jit(solution)/shard_map/ppermute | solution.py:238
  61.0 7.7 %collective-permute-start.15 = (bf16[360,256]{1,0:T(8,128)(2,1)S(1)}, bf16[360,256]{1,0:T(8,128)(2,1)S(1)}, u32[]{:S(2)}, u32[]{:S(2)}) collective-permute-start(bf16[360,256]{1,0:T(8,128)(2,1)S(1)} %get-tuple-element.43), channel_id=1, source_target_pairs={{0,4},{1,5},{2,6},{3,7},{4,8},{5,9},{6,10},{7,11},{8,12},{9,13},{1... | collective-permute-start | bytes 552968 | tf_op jit(solution)/shard_map/ppermute | solution.py:238
  61.9 12.4 %collective-permute-start.16 = (bf16[360,256]{1,0:T(8,128)(2,1)S(1)}, bf16[360,256]{1,0:T(8,128)(2,1)S(1)}, u32[]{:S(2)}, u32[]{:S(2)}) collective-permute-start(bf16[360,256]{1,0:T(8,128)(2,1)S(1)} %get-tuple-element.43), channel_id=1, source_target_pairs={{0,8},{1,9},{2,10},{3,11},{4,12},{5,13},{6,14},{7,15},{8,0},{9,1},... | collective-permute-start | bytes 552968 | tf_op jit(solution)/shard_map/ppermute | solution.py:238
  63.5 10.8 %collective-permute-start.17 = (bf16[360,256]{1,0:T(8,128)(2,1)S(1)}, bf16[360,256]{1,0:T(8,128)(2,1)S(1)}, u32[]{:S(2)}, u32[]{:S(2)}) collective-permute-start(bf16[360,256]{1,0:T(8,128)(2,1)S(1)} %get-tuple-element.43), channel_id=1, source_target_pairs={{0,12},{1,13},{2,14},{3,15},{4,0},{5,1},{6,2},{7,3},{8,4},{9,5},{1... | collective-permute-start | bytes 552968 | tf_op jit(solution)/shard_map/ppermute | solution.py:238
  65.9 12.4 %collective-permute-start.5 = (bf16[4,2,128,640]{3,2,1,0:T(8,128)(2,1)S(1)}, bf16[4,2,128,640]{3,2,1,0:T(8,128)(2,1)S(1)}, u32[]{:S(2)}, u32[]{:S(2)}) collective-permute-start(bf16[4,2,128,640]{3,2,1,0:T(8,128)(2,1)S(1)} %maximum_select_fusion.7), channel_id=1, source_target_pairs={{0,1},{1,0},{2,3},{3,2},{4,5},{5,4},{6,7},{7,6},{8,9},{9,8},{10,11... | collective-permute-start | bytes 3932168 | tf_op jit(solution)/shard_map/ppermute | solution.py:238
  67.1 10.0 %collective-permute-start.11 = (bf16[4,360,128]{2,1,0:T(8,128)(2,1)S(1)}, bf16[4,360,128]{2,1,0:T(8,128)(2,1)S(1)}, u32[]{:S(2)}, u32[]{:S(2)}) collective-permute-start(bf16[4,360,128]{2,1,0:T(8,128)(2,1)S(1)} %get-tuple-element.41), channel_id=1, source_target_pairs={{0,2},{1,3},{2,0},{3,1},{4,6},{5,7},{6,4},{7,5},{8,10},{9,11},{10,... | collective-permute-start | bytes 1105928 | tf_op jit(solution)/shard_map/ppermute | solution.py:238
  74.4 3.5 %collective-permute-start.20 = (bf16[4,2,360,128]{3,2,0,1:T(8,128)(2,1)S(1)}, bf16[4,2,360,128]{3,2,0,1:T(8,128)(2,1)S(1)}, u32[]{:S(2)}, u32[]{:S(2)}) collective-permute-start(bf16[4,2,360,128]{3,2,0,1:T(8,128)(2,1)S(1)} %maximum_select_fusion.13), channel_id=1, source_target_pairs={{0,1},{1,0},{2,3},{3,2},{4,5},{5,4},{6,7},{7,6},{8,9},{9,8},{10,11... | collective-permute-start | bytes 2211848 | tf_op jit(solution)/shard_map/ppermute | solution.py:238
  75.6 18.9 %collective-permute-start.22 = (bf16[4,360,256]{2,1,0:T(8,128)(2,1)S(1)}, bf16[4,360,256]{2,1,0:T(8,128)(2,1)S(1)}, u32[]{:S(2)}, u32[]{:S(2)}) collective-permute-start(bf16[4,360,256]{2,1,0:T(8,128)(2,1)S(1)} %get-tuple-element.104), channel_id=1, source_target_pairs={{0,2},{1,3},{2,0},{3,1},{4,6},{5,7},{6,4},{7,5},{8,10},{9,11},{10,... | collective-permute-start | bytes 2211848 | tf_op jit(solution)/shard_map/ppermute | solution.py:238
  77.5 3.4 %collective-permute-start.18 = (bf16[4,2,360,256]{3,2,0,1:T(8,128)(2,1)S(1)}, bf16[4,2,360,256]{3,2,0,1:T(8,128)(2,1)S(1)}, u32[]{:S(2)}, u32[]{:S(2)}) collective-permute-start(bf16[4,2,360,256]{3,2,0,1:T(8,128)(2,1)S(1)} %maximum_select_fusion.3), channel_id=1, source_target_pairs={{0,1},{1,0},{2,3},{3,2},{4,5},{5,4},{6,7},{7,6},{8,9},{9,8},{10,11... | collective-permute-start | bytes 4423688 | tf_op jit(solution)/shard_map/ppermute | solution.py:238
  88.7 7.2 %copy-start.11 = (f32[480,384]{1,0:T(8,128)}, f32[480,384]{1,0:T(8,128)S(1)}, u32[]{:S(2)}) copy-start(f32[480,384]{1,0:T(8,128)S(1)} %get-tuple-element.56.preact_ref) | copy-start | bytes 2211844
  88.7 7.2 %copy-start.13 = (bf16[480,640]{1,0:T(8,128)(2,1)}, bf16[480,640]{1,0:T(8,128)(2,1)S(1)}, u32[]{:S(2)}) copy-start(bf16[480,640]{1,0:T(8,128)(2,1)S(1)} %get-tuple-element.55.normed_ref) | copy-start | bytes 1843204
  95.9 5.9 %collective-permute-start.23 = (bf16[4,2,360,256]{3,2,0,1:T(8,128)(2,1)}, bf16[4,2,360,256]{3,2,0,1:T(8,128)(2,1)}, u32[]{:S(2)}, u32[]{:S(2)}) collective-permute-start(bf16[4,2,360,256]{3,2,0,1:T(8,128)(2,1)} %maximum_select_fusion.6), channel_id=1, source_target_pairs={{0,1},{1,0},{2,3},{3,2},{4,5},{5,4},{6,7},{7,6},{8,9},{9,8},{10,11... | collective-permute-start | bytes 4423688 | tf_op jit(solution)/shard_map/ppermute | solution.py:238
  96.0 16.4 %collective-permute-start.21 = (bf16[480,640]{1,0:T(8,128)(2,1)S(1)}, bf16[480,640]{1,0:T(8,128)(2,1)}, u32[]{:S(2)}, u32[]{:S(2)}) collective-permute-start(bf16[480,640]{1,0:T(8,128)(2,1)S(1)} %get-tuple-element.46.own_ref), channel_id=1, source_target_pairs={{0,16},{16,0},{1,17},{17,1},{2,18},{18,2},{3,19},{19,3},{4,20},{20... | collective-permute-start | bytes 1843208 | tf_op jit(solution)/shard_map/ppermute | solution.py:242
  104.2 8.1 %copy-start.9 = (bf16[5,3,32,640]{3,2,1,0:T(8,128)(2,1)S(1)}, bf16[5,3,32,640]{3,2,1,0:T(8,128)(2,1)}, u32[]{:S(2)}) copy-start(bf16[5,3,32,640]{3,2,1,0:T(8,128)(2,1)} %param.7) | copy-start | bytes 1843204
  122.8 4.4 %copy-start.15 = (bf16[480,640]{1,0:T(8,128)(2,1)}, bf16[480,640]{1,0:T(8,128)(2,1)S(1)}, u32[]{:S(2)}) copy-start(bf16[480,640]{1,0:T(8,128)(2,1)S(1)} %get-tuple-element.48.hidden_ref) | copy-start | bytes 1843204
  129.5 3.8 %collective-permute-start.28 = (bf16[2,360,256]{2,1,0:T(8,128)(2,1)}, bf16[2,360,256]{2,1,0:T(8,128)(2,1)}, u32[]{:S(2)}, u32[]{:S(2)}) collective-permute-start(bf16[2,360,256]{2,1,0:T(8,128)(2,1)} %get-tuple-element.77), channel_id=1, source_target_pairs={{0,1},{1,0},{2,3},{3,2},{4,5},{5,4},{6,7},{7,6},{8,9},{9,8},{10,11... | collective-permute-start | bytes 1105928 | tf_op jit(solution)/shard_map/ppermute | solution.py:238
  129.6 3.7 %collective-permute-start.27 = (bf16[2,360,256]{2,1,0:T(8,128)(2,1)}, bf16[2,360,256]{2,1,0:T(8,128)(2,1)}, u32[]{:S(2)}, u32[]{:S(2)}) collective-permute-start(bf16[2,360,256]{2,1,0:T(8,128)(2,1)} %get-tuple-element.75), channel_id=1, source_target_pairs={{0,1},{1,0},{2,3},{3,2},{4,5},{5,4},{6,7},{7,6},{8,9},{9,8},{10,11... | collective-permute-start | bytes 1105928 | tf_op jit(solution)/shard_map/ppermute | solution.py:238
  130.1 3.2 %collective-permute-start.26 = (bf16[2,360,256]{2,1,0:T(8,128)(2,1)}, bf16[2,360,256]{2,1,0:T(8,128)(2,1)}, u32[]{:S(2)}, u32[]{:S(2)}) collective-permute-start(bf16[2,360,256]{2,1,0:T(8,128)(2,1)} %get-tuple-element.76), channel_id=1, source_target_pairs={{0,1},{1,0},{2,3},{3,2},{4,5},{5,4},{6,7},{7,6},{8,9},{9,8},{10,11... | collective-permute-start | bytes 1105928 | tf_op jit(solution)/shard_map/ppermute | solution.py:238
  130.2 3.1 %collective-permute-start.25 = (bf16[2,360,256]{2,1,0:T(8,128)(2,1)S(1)}, bf16[2,360,256]{2,1,0:T(8,128)(2,1)}, u32[]{:S(2)}, u32[]{:S(2)}) collective-permute-start(bf16[2,360,256]{2,1,0:T(8,128)(2,1)S(1)} %get-tuple-element.74), channel_id=1, source_target_pairs={{0,1},{1,0},{2,3},{3,2},{4,5},{5,4},{6,7},{7,6},{8,9},{9,8},{10,11... | collective-permute-start | bytes 1105928 | tf_op jit(solution)/shard_map/ppermute | solution.py:238
  130.6 16.2 %collective-permute-start.24 = (bf16[480,640]{1,0:T(8,128)(2,1)}, bf16[480,640]{1,0:T(8,128)(2,1)}, u32[]{:S(2)}, u32[]{:S(2)}) collective-permute-start(bf16[480,640]{1,0:T(8,128)(2,1)} %get-tuple-element.49.own_ref), channel_id=1, source_target_pairs={{0,16},{16,0},{1,17},{17,1},{2,18},{18,2},{3,19},{19,3},{4,20},{20... | collective-permute-start | bytes 1843208 | tf_op jit(solution)/shard_map/ppermute | solution.py:242
  134.8 11.9 %copy-start.10 = (bf16[5,3,32,640]{3,2,1,0:T(8,128)(2,1)S(1)}, bf16[5,3,32,640]{3,2,1,0:T(8,128)(2,1)}, u32[]{:S(2)}) copy-start(bf16[5,3,32,640]{3,2,1,0:T(8,128)(2,1)} %param.7) | copy-start | bytes 1843204
  134.8 11.9 %copy-start.12 = (f32[480,384]{1,0:T(8,128)S(1)}, f32[480,384]{1,0:T(8,128)}, u32[]{:S(2)}) copy-start(f32[480,384]{1,0:T(8,128)} %copy-done.11) | copy-start | bytes 2211844
  134.9 11.9 %copy-start.14 = (bf16[480,640]{1,0:T(8,128)(2,1)S(1)}, bf16[480,640]{1,0:T(8,128)(2,1)}, u32[]{:S(2)}) copy-start(bf16[480,640]{1,0:T(8,128)(2,1)} %copy-done.13) | copy-start | bytes 1843204
  134.9 11.9 %copy-start.16 = (bf16[480,640]{1,0:T(8,128)(2,1)S(1)}, bf16[480,640]{1,0:T(8,128)(2,1)}, u32[]{:S(2)}) copy-start(bf16[480,640]{1,0:T(8,128)(2,1)} %copy-done.15) | copy-start | bytes 1843204
  135.4 11.4 %copy-start.7 = (bf16[8,120,640]{2,1,0:T(8,128)(2,1)S(1)}, bf16[8,120,640]{2,1,0:T(8,128)(2,1)}, u32[]{:S(2)}) copy-start(bf16[8,120,640]{2,1,0:T(8,128)(2,1)} %copy-done.6) | copy-start | bytes 3686404
  135.4 19.9 %collective-permute-start.29 = (bf16[4,360,256]{2,1,0:T(8,128)(2,1)S(1)}, bf16[4,360,256]{2,1,0:T(8,128)(2,1)S(1)}, u32[]{:S(2)}, u32[]{:S(2)}) collective-permute-start(bf16[4,360,256]{2,1,0:T(8,128)(2,1)S(1)} %dynamic-slice_bitcast_fusion), channel_id=1, source_target_pairs={{0,2},{1,3},{2,0},{3,1},{4,6},{5,7},{6,4},{7,5},{8,10},{9,11},{10,... | collective-permute-start | bytes 2211848 | tf_op jit(solution)/shard_map/ppermute | solution.py:238
  146.8 7.8 %copy-start.5 = (bf16[5760,128]{1,0:T(8,128)(2,1)S(1)}, bf16[5760,128]{1,0:T(8,128)(2,1)}, u32[]{:S(2)}) copy-start(bf16[5760,128]{1,0:T(8,128)(2,1)} %copy-done.4) | copy-start | bytes 4423684
  155.2 3.2 %collective-permute-start.31 = (bf16[4,2,360,128]{3,2,0,1:T(8,128)(2,1)S(1)}, bf16[4,2,360,128]{3,2,0,1:T(8,128)(2,1)S(1)}, u32[]{:S(2)}, u32[]{:S(2)}) collective-permute-start(bf16[4,2,360,128]{3,2,0,1:T(8,128)(2,1)S(1)} %bitcast.337), channel_id=1, source_target_pairs={{0,1},{1,0},{2,3},{3,2},{4,5},{5,4},{6,7},{7,6},{8,9},{9,8},{10,11... | collective-permute-start | bytes 2211848 | tf_op jit(solution)/shard_map/ppermute | solution.py:238
  155.7 16.4 %collective-permute-start.30 = (bf16[4,2,360,256]{3,2,0,1:T(8,128)(2,1)S(1)}, bf16[4,2,360,256]{3,2,0,1:T(8,128)(2,1)S(1)}, u32[]{:S(2)}, u32[]{:S(2)}) collective-permute-start(bf16[4,2,360,256]{3,2,0,1:T(8,128)(2,1)S(1)} %bitcast.331), channel_id=1, source_target_pairs={{0,1},{1,0},{2,3},{3,2},{4,5},{5,4},{6,7},{7,6},{8,9},{9,8},{10,11... | collective-permute-start | bytes 4423688 | tf_op jit(solution)/shard_map/ppermute | solution.py:238
  157.9 16.4 %collective-permute-start.44 = (bf16[4,2,128,640]{3,2,1,0:T(8,128)(2,1)S(1)}, bf16[4,2,128,640]{3,2,1,0:T(8,128)(2,1)S(1)}, u32[]{:S(2)}, u32[]{:S(2)}) collective-permute-start(bf16[4,2,128,640]{3,2,1,0:T(8,128)(2,1)S(1)} %fusion.8), channel_id=1, source_target_pairs={{0,1},{1,0},{2,3},{3,2},{4,5},{5,4},{6,7},{7,6},{8,9},{9,8},{10,11... | collective-permute-start | bytes 3932168 | tf_op jit(solution)/shard_map/ppermute | solution.py:238
  158.7 10.6 %collective-permute-start.32 = (bf16[4,360,128]{2,1,0:T(8,128)(2,1)S(1)}, bf16[4,360,128]{2,1,0:T(8,128)(2,1)S(1)}, u32[]{:S(2)}, u32[]{:S(2)}) collective-permute-start(bf16[4,360,128]{2,1,0:T(8,128)(2,1)S(1)} %dynamic-slice_bitcast_fusion.7), channel_id=1, source_target_pairs={{0,2},{1,3},{2,0},{3,1},{4,6},{5,7},{6,4},{7,5},{8,10},{9,11},{10,... | collective-permute-start | bytes 1105928 | tf_op jit(solution)/shard_map/ppermute | solution.py:238
  159.6 24.2 %collective-permute-start.35 = (bf16[360,256]{1,0:T(8,128)(2,1)S(1)}, bf16[360,256]{1,0:T(8,128)(2,1)S(1)}, u32[]{:S(2)}, u32[]{:S(2)}) collective-permute-start(bf16[360,256]{1,0:T(8,128)(2,1)S(1)} %get-tuple-element.101), channel_id=1, source_target_pairs={{0,4},{1,5},{2,6},{3,7},{4,8},{5,9},{6,10},{7,11},{8,12},{9,13},{1... | collective-permute-start | bytes 552968 | tf_op jit(solution)/shard_map/ppermute | solution.py:238
  162.4 21.4 %collective-permute-start.36 = (bf16[360,256]{1,0:T(8,128)(2,1)S(1)}, bf16[360,256]{1,0:T(8,128)(2,1)S(1)}, u32[]{:S(2)}, u32[]{:S(2)}) collective-permute-start(bf16[360,256]{1,0:T(8,128)(2,1)S(1)} %get-tuple-element.100), channel_id=1, source_target_pairs={{0,8},{1,9},{2,10},{3,11},{4,12},{5,13},{6,14},{7,15},{8,0},{9,1},... | collective-permute-start | bytes 552968 | tf_op jit(solution)/shard_map/ppermute | solution.py:238
  169.3 14.5 %collective-permute-start.37 = (bf16[360,256]{1,0:T(8,128)(2,1)S(1)}, bf16[360,256]{1,0:T(8,128)(2,1)S(1)}, u32[]{:S(2)}, u32[]{:S(2)}) collective-permute-start(bf16[360,256]{1,0:T(8,128)(2,1)S(1)} %get-tuple-element.99), channel_id=1, source_target_pairs={{0,12},{1,13},{2,14},{3,15},{4,0},{5,1},{6,2},{7,3},{8,4},{9,5},{1... | collective-permute-start | bytes 552968 | tf_op jit(solution)/shard_map/ppermute | solution.py:238
  172.8 9.5 %collective-permute-start.33 = (bf16[4,360,128]{2,1,0:T(8,128)(2,1)S(1)}, bf16[4,360,128]{2,1,0:T(8,128)(2,1)S(1)}, u32[]{:S(2)}, u32[]{:S(2)}) collective-permute-start(bf16[4,360,128]{2,1,0:T(8,128)(2,1)S(1)} %dynamic-slice_bitcast_fusion.8), channel_id=1, source_target_pairs={{0,2},{1,3},{2,0},{3,1},{4,6},{5,7},{6,4},{7,5},{8,10},{9,11},{10,... | collective-permute-start | bytes 1105928 | tf_op jit(solution)/shard_map/ppermute | solution.py:238
  182.3 8.8 %collective-permute-start.34 = (bf16[4,360,128]{2,1,0:T(8,128)(2,1)S(1)}, bf16[4,360,128]{2,1,0:T(8,128)(2,1)S(1)}, u32[]{:S(2)}, u32[]{:S(2)}) collective-permute-start(bf16[4,360,128]{2,1,0:T(8,128)(2,1)S(1)} %dynamic-slice_bitcast_fusion.6), channel_id=1, source_target_pairs={{0,2},{1,3},{2,0},{3,1},{4,6},{5,7},{6,4},{7,5},{8,10},{9,11},{10,... | collective-permute-start | bytes 1105928 | tf_op jit(solution)/shard_map/ppermute | solution.py:238
  183.9 8.6 %collective-permute-start.40 = (bf16[360,128]{1,0:T(8,128)(2,1)S(1)}, bf16[360,128]{1,0:T(8,128)(2,1)S(1)}, u32[]{:S(2)}, u32[]{:S(2)}) collective-permute-start(bf16[360,128]{1,0:T(8,128)(2,1)S(1)} %get-tuple-element.131), channel_id=1, source_target_pairs={{0,12},{1,13},{2,14},{3,15},{4,0},{5,1},{6,2},{7,3},{8,4},{9,5},{1... | collective-permute-start | bytes 276488 | tf_op jit(solution)/shard_map/ppermute | solution.py:238
  184.2 8.3 %collective-permute-start.39 = (bf16[360,128]{1,0:T(8,128)(2,1)S(1)}, bf16[360,128]{1,0:T(8,128)(2,1)S(1)}, u32[]{:S(2)}, u32[]{:S(2)}) collective-permute-start(bf16[360,128]{1,0:T(8,128)(2,1)S(1)} %get-tuple-element.132), channel_id=1, source_target_pairs={{0,8},{1,9},{2,10},{3,11},{4,12},{5,13},{6,14},{7,15},{8,0},{9,1},... | collective-permute-start | bytes 276488 | tf_op jit(solution)/shard_map/ppermute | solution.py:238
  184.9 7.6 %collective-permute-start.38 = (bf16[360,128]{1,0:T(8,128)(2,1)S(1)}, bf16[360,128]{1,0:T(8,128)(2,1)S(1)}, u32[]{:S(2)}, u32[]{:S(2)}) collective-permute-start(bf16[360,128]{1,0:T(8,128)(2,1)S(1)} %get-tuple-element.130), channel_id=1, source_target_pairs={{0,4},{1,5},{2,6},{3,7},{4,8},{5,9},{6,10},{7,11},{8,12},{9,13},{1... | collective-permute-start | bytes 276488 | tf_op jit(solution)/shard_map/ppermute | solution.py:238
  191.0 13.8 %collective-permute-start.45 = (bf16[4,128,640]{2,1,0:T(8,128)(2,1)S(1)}, bf16[4,128,640]{2,1,0:T(8,128)(2,1)S(1)}, u32[]{:S(2)}, u32[]{:S(2)}) collective-permute-start(bf16[4,128,640]{2,1,0:T(8,128)(2,1)S(1)} %dynamic-slice_bitcast_fusion.1), channel_id=1, source_target_pairs={{0,2},{1,3},{2,0},{3,1},{4,6},{5,7},{6,4},{7,5},{8,10},{9,11},{10,... | collective-permute-start | bytes 1966088 | tf_op jit(solution)/shard_map/ppermute | solution.py:238
  192.9 12.1 %collective-permute-start.43 = (bf16[360,256]{1,0:T(8,128)(2,1)S(1)}, bf16[360,256]{1,0:T(8,128)(2,1)S(1)}, u32[]{:S(2)}, u32[]{:S(2)}) collective-permute-start(bf16[360,256]{1,0:T(8,128)(2,1)S(1)} %get-tuple-element.97), channel_id=1, source_target_pairs={{0,12},{1,13},{2,14},{3,15},{4,0},{5,1},{6,2},{7,3},{8,4},{9,5},{1... | collective-permute-start | bytes 552968 | tf_op jit(solution)/shard_map/ppermute | solution.py:238
  194.2 15.3 %collective-permute-start.42 = (bf16[360,256]{1,0:T(8,128)(2,1)S(1)}, bf16[360,256]{1,0:T(8,128)(2,1)S(1)}, u32[]{:S(2)}, u32[]{:S(2)}) collective-permute-start(bf16[360,256]{1,0:T(8,128)(2,1)S(1)} %get-tuple-element.98), channel_id=1, source_target_pairs={{0,8},{1,9},{2,10},{3,11},{4,12},{5,13},{6,14},{7,15},{8,0},{9,1},... | collective-permute-start | bytes 552968 | tf_op jit(solution)/shard_map/ppermute | solution.py:238
  194.2 15.3 %collective-permute-start.41 = (bf16[360,256]{1,0:T(8,128)(2,1)S(1)}, bf16[360,256]{1,0:T(8,128)(2,1)S(1)}, u32[]{:S(2)}, u32[]{:S(2)}) collective-permute-start(bf16[360,256]{1,0:T(8,128)(2,1)S(1)} %get-tuple-element.96), channel_id=1, source_target_pairs={{0,4},{1,5},{2,6},{3,7},{4,8},{5,9},{6,10},{7,11},{8,12},{9,13},{1... | collective-permute-start | bytes 552968 | tf_op jit(solution)/shard_map/ppermute | solution.py:238
  209.6 5.6 %collective-permute-start.49 = (bf16[128,640]{1,0:T(8,128)(2,1)S(1)}, bf16[128,640]{1,0:T(8,128)(2,1)S(1)}, u32[]{:S(2)}, u32[]{:S(2)}) collective-permute-start(bf16[128,640]{1,0:T(8,128)(2,1)S(1)} %get-tuple-element.121), channel_id=1, source_target_pairs={{0,12},{1,13},{2,14},{3,15},{4,0},{5,1},{6,2},{7,3},{8,4},{9,5},{1... | collective-permute-start | bytes 491528 | tf_op jit(solution)/shard_map/ppermute | solution.py:238
  209.7 16.2 %collective-permute-start.48 = (bf16[128,640]{1,0:T(8,128)(2,1)S(1)}, bf16[128,640]{1,0:T(8,128)(2,1)S(1)}, u32[]{:S(2)}, u32[]{:S(2)}) collective-permute-start(bf16[128,640]{1,0:T(8,128)(2,1)S(1)} %get-tuple-element.122), channel_id=1, source_target_pairs={{0,8},{1,9},{2,10},{3,11},{4,12},{5,13},{6,14},{7,15},{8,0},{9,1},... | collective-permute-start | bytes 491528 | tf_op jit(solution)/shard_map/ppermute | solution.py:238
  211.1 14.8 %collective-permute-start.47 = (bf16[128,640]{1,0:T(8,128)(2,1)S(1)}, bf16[128,640]{1,0:T(8,128)(2,1)S(1)}, u32[]{:S(2)}, u32[]{:S(2)}) collective-permute-start(bf16[128,640]{1,0:T(8,128)(2,1)S(1)} %get-tuple-element.120), channel_id=1, source_target_pairs={{0,4},{1,5},{2,6},{3,7},{4,8},{5,9},{6,10},{7,11},{8,12},{9,13},{1... | collective-permute-start | bytes 491528 | tf_op jit(solution)/shard_map/ppermute | solution.py:238
  213.3 14.3 %collective-permute-start.46 = (bf16[360,384]{1,0:T(8,128)(2,1)S(1)}, bf16[360,384]{1,0:T(8,128)(2,1)S(1)}, u32[]{:S(2)}, u32[]{:S(2)}) collective-permute-start(bf16[360,384]{1,0:T(8,128)(2,1)S(1)} %pad_maximum_fusion.6), channel_id=1, source_target_pairs={{0,16},{16,0},{1,17},{17,1},{2,18},{18,2},{3,19},{19,3},{4,20},{20... | collective-permute-start | bytes 829448 | tf_op jit(solution)/shard_map/ppermute | solution.py:242
  226.1 4.5 %collective-permute-start.50 = (bf16[64,640]{1,0:T(8,128)(2,1)S(1)}, bf16[64,640]{1,0:T(8,128)(2,1)S(1)}, u32[]{:S(2)}, u32[]{:S(2)}) collective-permute-start(bf16[64,640]{1,0:T(8,128)(2,1)S(1)} %select_convert_fusion.1), channel_id=1, source_target_pairs={{0,16},{16,0},{1,17},{17,1},{2,18},{18,2},{3,19},{19,3},{4,20},{20... | collective-permute-start | bytes 245768 | tf_op jit(solution)/shard_map/ppermute | solution.py:242
  227.8 3.7 %copy-start.1 = (bf16[1,360,640]{2,1,0:T(8,128)(2,1)S(1)}, bf16[1,360,640]{2,1,0:T(8,128)(2,1)}, u32[]{:S(2)}) copy-start(bf16[1,360,640]{2,1,0:T(8,128)(2,1)} %param.8) | copy-start | bytes 1382404
  (9 other events, 13.0 us)

commit v5 on v4

--- a/solution.py
+++ b/solution.py
@@ -379,10 +379,10 @@
     return in_order(y == 1, line[:, None], sent[:, None], 1)
 
 
-def gathered_on_chip(plane, earlier=None):
+def gathered_on_chip(plane, pieces=1, beside=None):
     _, _, c = coordinates()
-    plane = after(plane, earlier)
-    whole = in_order(c == 1, plane[:, :, None], sent_on_chip(plane)[:, :, None], 2)
+    sent = after(sent_on_chip(plane, pieces), beside)
+    whole = in_order(c == 1, plane[:, :, None], sent[:, :, None], 2)
     return whole.reshape(-1, plane.shape[3])
 
 
@@ -676,7 +676,7 @@
     )(hidden, embedding, keep_first, temporal_first, *spatial_first)
     mixed_given = swapped(mixed)
     plane_second = joined_over_y(line_second, after(side_second, mixed))
-    spatial_second = [gathered_on_chip(plane_second), tails]
+    spatial_second = [gathered_on_chip(plane_second, GRID[0], mixed_given), tails]
     hidden_second, normed_second, activated_second, pre_grad_second, back = vmem_call(
         functools.partial(second_forward, frames),
         (
@@ -742,7 +742,7 @@
         jnp.concatenate([line_low, line_high], 2), sent_tails
     )
     line, side = summed_over_y(chip_temporal, side)
-    share_temporal, _ = summed_over_z(line, sent_first)
+    share_temporal, _ = summed_over_z(line)
 
     kept = jnp.where(first, share_first, share_second)
     passed = jnp.where(first, share_second, share_first)

time: 236 us -> 228 us (0.966)
  waiting for transfers between devices: 100 us -> 93.9 us
  local copies, waits for them, and re-layouts: 13.4 us -> 16 us
    ppermute x6, waiting for transfers between devices: 20 us -> 15 us  [swapped(): return lax.ppermute(value, 'pipe', [(0, 1), (1, 0)])]
    select_n x13, other arithmetic: 6.5 us -> 3.65 us  [in_order(): jnp.where(swap, jnp.concatenate([other, own], axis), jnp.concatenate([own...]
    ppermute x45 -> x48, starting transfers between devices: 55.7 us -> 53.6 us  [shifted(): return lax.ppermute(value, 'dp', pairs)]
    ppermute x45 -> x48, waiting for transfers between devices: 80.5 us -> 78.9 us  [shifted(): return lax.ppermute(value, 'dp', pairs)]
  transfers between devices with their start and end apart: 51 -> 54, of which waited for: 23 -> 22; matrix products, arithmetic and copies ran while one was open for 12% -> 12% of each run, Pallas kernels for 6% -> 6%
where the time goes in v5:
time: 228 us; the launch traced here: 224 us
  waiting for transfers between devices  93.9 us (41%)
  starting transfers between devices  62.8 us (28%)
  Pallas kernels  28.8 us (13%)
  other arithmetic  17.6 us (8%)
  local copies, waits for them, and re-layouts  16 us (7%)
  matrix products  2.84 us (1%)
    ppermute x48, waiting for transfers between devices, shifted(): return lax.ppermute(value, 'dp', pairs)  78.9 us
    ppermute x48, starting transfers between devices, shifted(): return lax.ppermute(value, 'dp', pairs)  53.6 us
    ppermute x6, waiting for transfers between devices, swapped(): return lax.ppermute(value, 'pipe', [(0, 1), (1, 0)])  15 us
    pallas_call x1, Pallas kernels, paired_device(): vmem_call(functools.partial(second_forward, frames), (shape((rows, channe...  10.4 us
    ppermute x6, starting transfers between devices, swapped(): return lax.ppermute(value, 'pipe', [(0, 1), (1, 0)])  9.2 us
    pallas_call x1, Pallas kernels, paired_device(): vmem_call(functools.partial(first_terms, frames), terms_shape(), flops=sp...  7.77 us
    pallas_call x1, Pallas kernels, paired_device(): vmem_call(functools.partial(first_forward, frames), (shape((rows, channel...  6.24 us
  transfers between devices with their start and end apart: 54, of which 22 were waited for; matrix products, arithmetic and copies ran while one was open for 12% of the time, Pallas kernels for 6%

profile of v5, /device:TPU:0, one launch (start us, length us, event | category | flops | bytes accessed | tf_op | source)
XLA Modules:
  0.0 223.9 jit_solution(11754831818355538172)
XLA Ops:
  0.6 0.9 slice_bitcast_fusion.31
  1.5 0.9 slice_bitcast_fusion.26
  2.5 3.0 %collective-permute-start = (bf16[64,640]{1,0:T(8,128)(2,1)S(1)}, bf16[64,640]{1,0:T(8,128)(2,1)S(1)}, u32[]{:S(2)}, u32[]{:S(2)}) collective-permute-start(bf16[64,640]{1,0:T(8,128)(2,1)S(1)} %fusion.43), channel_id=1, source_target_pairs={{0,16},{16,0},{1,17},{17,1},{2,18},{18,2},{3,19},{19,3},{4,20},{20... | collective-permute-start | bytes 245768 | tf_op jit(solution)/shard_map/ppermute | solution.py:242
  7.9 3.2 %collective-permute-start.2 = (bf16[128,640]{1,0:T(8,128)(2,1)S(1)}, bf16[128,640]{1,0:T(8,128)(2,1)S(1)}, u32[]{:S(2)}, u32[]{:S(2)}) collective-permute-start(bf16[128,640]{1,0:T(8,128)(2,1)S(1)} %maximum_select_fusion.16), channel_id=1, source_target_pairs={{0,8},{1,9},{2,10},{3,11},{4,12},{5,13},{6,14},{7,15},{8,0},{9,1},... | collective-permute-start | bytes 491528 | tf_op jit(solution)/shard_map/ppermute | solution.py:238
  11.1 1.3 collective-permute-start.3
  13.1 7.5 %collective-permute-done.2 = bf16[128,640]{1,0:T(8,128)(2,1)S(1)} collective-permute-done((bf16[128,640]{1,0:T(8,128)(2,1)S(1)}, bf16[128,640]{1,0:T(8,128)(2,1)S(1)}, u32[]{:S(2)}, u32[]{:S(2)}) %collective-permute-start.2) | collective-permute-done | bytes 163872 | tf_op jit(solution)/shard_map/ppermute | solution.py:238
  20.7 1.8 collective-permute-done.1
  22.7 1.6 collective-permute-start.4
  24.4 1.0 broadcast_select_fusion.3
  25.4 3.0 %collective-permute-start.7 = (bf16[360,256]{1,0:T(8,128)(2,1)S(1)}, bf16[360,256]{1,0:T(8,128)(2,1)S(1)}, u32[]{:S(2)}, u32[]{:S(2)}) collective-permute-start(bf16[360,256]{1,0:T(8,128)(2,1)S(1)} %get-tuple-element.37), channel_id=1, source_target_pairs={{0,4},{1,5},{2,6},{3,7},{4,8},{5,9},{6,10},{7,11},{8,12},{9,13},{1... | collective-permute-start | bytes 552968 | tf_op jit(solution)/shard_map/ppermute | solution.py:238
  28.4 2.0 collective-permute-start.8
  30.4 2.8 %collective-permute-start.9 = (bf16[360,256]{1,0:T(8,128)(2,1)S(1)}, bf16[360,256]{1,0:T(8,128)(2,1)S(1)}, u32[]{:S(2)}, u32[]{:S(2)}) collective-permute-start(bf16[360,256]{1,0:T(8,128)(2,1)S(1)} %get-tuple-element.37), channel_id=1, source_target_pairs={{0,12},{1,13},{2,14},{3,15},{4,0},{5,1},{6,2},{7,3},{8,4},{9,5},{1... | collective-permute-start | bytes 552968 | tf_op jit(solution)/shard_map/ppermute | solution.py:238
  33.2 0.9 slice_select_fusion.2
  34.2 6.6 %collective-permute-done.8 = bf16[360,256]{1,0:T(8,128)(2,1)S(1)} collective-permute-done((bf16[360,256]{1,0:T(8,128)(2,1)S(1)}, bf16[360,256]{1,0:T(8,128)(2,1)S(1)}, u32[]{:S(2)}, u32[]{:S(2)}) %collective-permute-start.8) | collective-permute-done | bytes 184352 | tf_op jit(solution)/shard_map/ppermute | solution.py:238
  40.9 6.3 %collective-permute-start.12 = (bf16[360,128]{1,0:T(8,128)(2,1)S(1)}, bf16[360,128]{1,0:T(8,128)(2,1)S(1)}, u32[]{:S(2)}, u32[]{:S(2)}) collective-permute-start(bf16[360,128]{1,0:T(8,128)(2,1)S(1)} %slice_select_fusion.2), channel_id=1, source_target_pairs={{0,4},{1,5},{2,6},{3,7},{4,8},{5,9},{6,10},{7,11},{8,12},{9,13},{1... | collective-permute-start | bytes 276488 | tf_op jit(solution)/shard_map/ppermute | solution.py:238
  47.2 3.4 %collective-permute-start.13 = (bf16[360,128]{1,0:T(8,128)(2,1)S(1)}, bf16[360,128]{1,0:T(8,128)(2,1)S(1)}, u32[]{:S(2)}, u32[]{:S(2)}) collective-permute-start(bf16[360,128]{1,0:T(8,128)(2,1)S(1)} %slice_select_fusion.2), channel_id=1, source_target_pairs={{0,8},{1,9},{2,10},{3,11},{4,12},{5,13},{6,14},{7,15},{8,0},{9,1},... | collective-permute-start | bytes 276488 | tf_op jit(solution)/shard_map/ppermute | solution.py:238
  51.5 1.8 collective-permute-done.12
  53.2 2.7 %collective-permute-done.13 = bf16[360,128]{1,0:T(8,128)(2,1)S(1)} collective-permute-done((bf16[360,128]{1,0:T(8,128)(2,1)S(1)}, bf16[360,128]{1,0:T(8,128)(2,1)S(1)}, u32[]{:S(2)}, u32[]{:S(2)}) %collective-permute-start.13) | collective-permute-done | bytes 92192 | tf_op jit(solution)/shard_map/ppermute | solution.py:238
  57.2 3.8 %collective-permute-done.10 = bf16[4,360,128]{2,1,0:T(8,128)(2,1)S(1)} collective-permute-done((bf16[4,360,128]{2,1,0:T(8,128)(2,1)S(1)}, bf16[4,360,128]{2,1,0:T(8,128)(2,1)S(1)}, u32[]{:S(2)}, u32[]{:S(2)}) %collective-permute-start.10) | collective-permute-done | bytes 368672 | tf_op jit(solution)/shard_map/ppermute | solution.py:238
  61.0 1.0 collective-permute-start.15
  61.9 1.6 collective-permute-start.16
  63.5 2.0 collective-permute-start.17
  66.1 1.1 collective-permute-done.19
  67.6 1.0 collective-permute-done.15
  68.6 5.7 %collective-permute-done.16 = bf16[360,256]{1,0:T(8,128)(2,1)S(1)} collective-permute-done((bf16[360,256]{1,0:T(8,128)(2,1)S(1)}, bf16[360,256]{1,0:T(8,128)(2,1)S(1)}, u32[]{:S(2)}, u32[]{:S(2)}) %collective-permute-start.16) | collective-permute-done | bytes 184352 | tf_op jit(solution)/shard_map/ppermute | solution.py:238
  74.6 1.0 fusion.83
  76.2 0.9 collective-permute-done.11
  79.1 1.3 slice_bitcast_fusion.3
  82.4 6.2 %shard_map.68 = (bf16[480,640]{1,0:T(8,128)(2,1)S(1)}, f32[480,384]{1,0:T(8,128)S(1)}, bf16[480,640]{1,0:T(8,128)(2,1)S(1)}) custom-call(bf16[480,640]{1,0:T(8,128)(2,1)S(1)} %bitcast.324, f32[5,640]{1,0:T(8,128)S(1)} %pad_maximum_fusion.8.embedding_ref, f32[1,384]{1,0:T(1,128)S(1)} %select_n.855.keep_ref, bf16[960,640]{1,0:T(8,128)(2,1)S(1)} %bitcast.321, ...), custom_call_target="tpu_custom_call" | custom-call | flops 7077888000 | bytes 5898240 | tf_op jit(solution)/shard_map/pallas_call | solution.py:671
  88.7 1.6 collective-permute-start.21
  90.3 4.2 %collective-permute-done.22 = bf16[4,360,256]{2,1,0:T(8,128)(2,1)S(1)} collective-permute-done((bf16[4,360,256]{2,1,0:T(8,128)(2,1)S(1)}, bf16[4,360,256]{2,1,0:T(8,128)(2,1)S(1)}, u32[]{:S(2)}, u32[]{:S(2)}) %collective-permute-start.22) | collective-permute-done | bytes 737312 | tf_op jit(solution)/shard_map/ppermute | solution.py:238
  95.4 1.1 slice_bitcast_fusion.9
  97.5 1.1 slice.287
  98.6 1.1 slice.288
  99.7 1.7 maximum_select_fusion.13
  101.8 1.4 pad_maximum_fusion
  103.2 2.0 collective-permute-done.21.sent_ref
  106.2 0.9 copy-done.9
  107.0 10.4 %shard_map.69 = (bf16[480,640]{1,0:T(8,128)(2,1)S(1)}, bf16[480,640]{1,0:T(8,128)(2,1)S(1)}, bf16[480,384]{1,0:T(8,128)(2,1)S(1)}, bf16[480,384]{1,0:T(8,128)(2,1)S(1)}, bf16[480,640]{1,0:T(8,128)(2,1)}) custom-call(bf16[480,640]{1,0:T(8,128)(2,1)S(1)} %bitcast.325, bf16[480,640]{1,0:T(8,128)(2,1)S(1)} %get-tuple-element.46.own_ref, ...), custom_call_target="tpu_custom_call" | custom-call | flops 12386304000 | bytes 5898240 | tf_op jit(solution)/shard_map/pallas_call | solution.py:680
  117.5 4.4 %shard_map.70 = (bf16[5760,256]{1,0:T(8,128)(2,1)S(1)}, bf16[5760,128]{1,0:T(8,128)(2,1)S(1)}, bf16[960,640]{1,0:T(8,128)(2,1)S(1)}) custom-call(bf16[480,640]{1,0:T(8,128)(2,1)S(1)} %get-tuple-element.51.normed_ref, bf16[480,384]{1,0:T(8,128)(2,1)S(1)} %get-tuple-element.52.pre_grad_ref, bf16[480,384]{1,0:T(8,128)(2,1)S(1)} %get-tuple-element.53.activated_ref, ...), custom_call_target="tpu_custom_call" | custom-call | flops 7077888000 | bytes 5898240 | tf_op jit(solution)/shard_map/pallas_call | solution.py:707
  121.9 1.2 dynamic-slice_bitcast_fusion.5
  125.3 1.5 collective-permute-start.27
  126.8 1.1 slice.295
  128.0 1.5 pad_maximum_fusion.1
  130.8 10.7 %collective-permute-done.27.sent_ref = bf16[480,640]{1,0:T(8,128)(2,1)} collective-permute-done((bf16[480,640]{1,0:T(8,128)(2,1)}, bf16[480,640]{1,0:T(8,128)(2,1)}, u32[]{:S(2)}, u32[]{:S(2)}) %collective-permute-start.27) | collective-permute-done | bytes 614432 | tf_op jit(solution)/shard_map/ppermute | solution.py:242
  141.5 7.8 %shard_map.71 = (bf16[5760,256]{1,0:T(8,128)(2,1)S(1)}, bf16[5760,128]{1,0:T(8,128)(2,1)S(1)}, bf16[960,640]{1,0:T(8,128)(2,1)S(1)}) custom-call(bf16[480,640]{1,0:T(8,128)(2,1)S(1)} %copy-done.16, f32[5,640]{1,0:T(8,128)S(1)} %pad_maximum_fusion.8.embedding_ref, bf16[480,640]{1,0:T(8,128)(2,1)S(1)} %bitcast.328, ...), custom_call_target="tpu_custom_call" | custom-call | flops 8847360000 | bytes 7372800 | tf_op jit(solution)/shard_map/pallas_call | solution.py:717
  154.3 2.6 %collective-permute-start.38 = (bf16[360,256]{1,0:T(8,128)(2,1)S(1)}, bf16[360,256]{1,0:T(8,128)(2,1)S(1)}, u32[]{:S(2)}, u32[]{:S(2)}) collective-permute-start(bf16[360,256]{1,0:T(8,128)(2,1)S(1)} %get-tuple-element.105), channel_id=1, source_target_pairs={{0,4},{1,5},{2,6},{3,7},{4,8},{5,9},{6,10},{7,11},{8,12},{9,13},{1... | collective-permute-start | bytes 552968 | tf_op jit(solution)/shard_map/ppermute | solution.py:238
  157.6 6.4 %collective-permute-done.35 = bf16[4,360,128]{2,1,0:T(8,128)(2,1)S(1)} collective-permute-done((bf16[4,360,128]{2,1,0:T(8,128)(2,1)S(1)}, bf16[4,360,128]{2,1,0:T(8,128)(2,1)S(1)}, u32[]{:S(2)}, u32[]{:S(2)}) %collective-permute-start.35) | collective-permute-done | bytes 368672 | tf_op jit(solution)/shard_map/ppermute | solution.py:238
  164.0 2.6 %collective-permute-start.40 = (bf16[360,256]{1,0:T(8,128)(2,1)S(1)}, bf16[360,256]{1,0:T(8,128)(2,1)S(1)}, u32[]{:S(2)}, u32[]{:S(2)}) collective-permute-start(bf16[360,256]{1,0:T(8,128)(2,1)S(1)} %get-tuple-element.103), channel_id=1, source_target_pairs={{0,12},{1,13},{2,14},{3,15},{4,0},{5,1},{6,2},{7,3},{8,4},{9,5},{1... | collective-permute-start | bytes 552968 | tf_op jit(solution)/shard_map/ppermute | solution.py:238
  168.5 8.5 %collective-permute-done.36 = bf16[4,360,128]{2,1,0:T(8,128)(2,1)S(1)} collective-permute-done((bf16[4,360,128]{2,1,0:T(8,128)(2,1)S(1)}, bf16[4,360,128]{2,1,0:T(8,128)(2,1)S(1)}, u32[]{:S(2)}, u32[]{:S(2)}) %collective-permute-start.36) | collective-permute-done | bytes 368672 | tf_op jit(solution)/shard_map/ppermute | solution.py:238
  178.0 1.3 collective-permute-start.42
  179.4 1.9 collective-permute-start.41
  181.4 4.4 %collective-permute-done.37 = bf16[4,360,128]{2,1,0:T(8,128)(2,1)S(1)} collective-permute-done((bf16[4,360,128]{2,1,0:T(8,128)(2,1)S(1)}, bf16[4,360,128]{2,1,0:T(8,128)(2,1)S(1)}, u32[]{:S(2)}, u32[]{:S(2)}) %collective-permute-start.37) | collective-permute-done | bytes 368672 | tf_op jit(solution)/shard_map/ppermute | solution.py:238
  186.6 1.5 collective-permute-start.46
  188.3 1.7 collective-permute-start.44
  190.1 9.4 %collective-permute-done.48 = bf16[4,128,640]{2,1,0:T(8,128)(2,1)S(1)} collective-permute-done((bf16[4,128,640]{2,1,0:T(8,128)(2,1)S(1)}, bf16[4,128,640]{2,1,0:T(8,128)(2,1)S(1)}, u32[]{:S(2)}, u32[]{:S(2)}) %collective-permute-start.48) | collective-permute-done | bytes 655392 | tf_op jit(solution)/shard_map/ppermute | solution.py:238
  200.8 1.6 collective-permute-start.50
  202.5 10.3 %collective-permute-done.45 = bf16[360,256]{1,0:T(8,128)(2,1)S(1)} collective-permute-done((bf16[360,256]{1,0:T(8,128)(2,1)S(1)}, bf16[360,256]{1,0:T(8,128)(2,1)S(1)}, u32[]{:S(2)}, u32[]{:S(2)}) %collective-permute-start.45) | collective-permute-done | bytes 184352 | tf_op jit(solution)/shard_map/ppermute | solution.py:238
  213.0 1.6 collective-permute-start.49
  214.6 2.6 %collective-permute-done.51 = bf16[128,640]{1,0:T(8,128)(2,1)S(1)} collective-permute-done((bf16[128,640]{1,0:T(8,128)(2,1)S(1)}, bf16[128,640]{1,0:T(8,128)(2,1)S(1)}, u32[]{:S(2)}, u32[]{:S(2)}) %collective-permute-start.51) | collective-permute-done | bytes 163872 | tf_op jit(solution)/shard_map/ppermute | solution.py:238
  217.4 1.6 collective-permute-start.53
  218.9 1.6 collective-permute-done.49
  220.7 2.1 fusion.3
  222.9 0.8 broadcast_select_fusion.5
  (204 shorter events, 29.5 us)
Async XLA Ops:
  0.6 4.9 %copy-start = (bf16[1,360,640]{2,1,0:T(8,128)(2,1)S(1)}, bf16[1,360,640]{2,1,0:T(8,128)(2,1)}, u32[]{:S(2)}) copy-start(bf16[1,360,640]{2,1,0:T(8,128)(2,1)} %param.8) | copy-start | bytes 1382404
  1.5 5.5 %copy-start.21 = (s32[5]{0:T(128)S(1)}, s32[5]{0:T(128)}, u32[]{:S(2)}) copy-start(s32[5]{0:T(128)} %param.6) | copy-start | bytes 64
  2.5 5.4 %collective-permute-start = (bf16[64,640]{1,0:T(8,128)(2,1)S(1)}, bf16[64,640]{1,0:T(8,128)(2,1)S(1)}, u32[]{:S(2)}, u32[]{:S(2)}) collective-permute-start(bf16[64,640]{1,0:T(8,128)(2,1)S(1)} %fusion.43), channel_id=1, source_target_pairs={{0,16},{16,0},{1,17},{17,1},{2,18},{18,2},{3,19},{19,3},{4,20},{20... | collective-permute-start | bytes 245768 | tf_op jit(solution)/shard_map/ppermute | solution.py:242
  7.0 17.4 %collective-permute-start.6 = (bf16[360,384]{1,0:T(8,128)(2,1)}, bf16[360,384]{1,0:T(8,128)(2,1)}, u32[]{:S(2)}, u32[]{:S(2)}) collective-permute-start(bf16[360,384]{1,0:T(8,128)(2,1)} %slice.278), channel_id=1, source_target_pairs={{0,16},{16,0},{1,17},{17,1},{2,18},{18,2},{3,19},{19,3},{4,20},{20... | collective-permute-start | bytes 829448 | tf_op jit(solution)/shard_map/ppermute | solution.py:242
  7.9 12.7 %collective-permute-start.2 = (bf16[128,640]{1,0:T(8,128)(2,1)S(1)}, bf16[128,640]{1,0:T(8,128)(2,1)S(1)}, u32[]{:S(2)}, u32[]{:S(2)}) collective-permute-start(bf16[128,640]{1,0:T(8,128)(2,1)S(1)} %maximum_select_fusion.16), channel_id=1, source_target_pairs={{0,8},{1,9},{2,10},{3,11},{4,12},{5,13},{6,14},{7,15},{8,0},{9,1},... | collective-permute-start | bytes 491528 | tf_op jit(solution)/shard_map/ppermute | solution.py:238
  11.1 9.6 %collective-permute-start.3 = (bf16[128,640]{1,0:T(8,128)(2,1)S(1)}, bf16[128,640]{1,0:T(8,128)(2,1)S(1)}, u32[]{:S(2)}, u32[]{:S(2)}) collective-permute-start(bf16[128,640]{1,0:T(8,128)(2,1)S(1)} %maximum_select_fusion.16), channel_id=1, source_target_pairs={{0,12},{1,13},{2,14},{3,15},{4,0},{5,1},{6,2},{7,3},{8,4},{9,5},{1... | collective-permute-start | bytes 491528 | tf_op jit(solution)/shard_map/ppermute | solution.py:238
  12.4 10.0 %collective-permute-start.1 = (bf16[128,640]{1,0:T(8,128)(2,1)S(1)}, bf16[128,640]{1,0:T(8,128)(2,1)S(1)}, u32[]{:S(2)}, u32[]{:S(2)}) collective-permute-start(bf16[128,640]{1,0:T(8,128)(2,1)S(1)} %maximum_select_fusion.16), channel_id=1, source_target_pairs={{0,4},{1,5},{2,6},{3,7},{4,8},{5,9},{6,10},{7,11},{8,12},{9,13},{1... | collective-permute-start | bytes 491528 | tf_op jit(solution)/shard_map/ppermute | solution.py:238
  22.7 18.0 %collective-permute-start.4 = (bf16[4,128,640]{2,1,0:T(8,128)(2,1)S(1)}, bf16[4,128,640]{2,1,0:T(8,128)(2,1)S(1)}, u32[]{:S(2)}, u32[]{:S(2)}) collective-permute-start(bf16[4,128,640]{2,1,0:T(8,128)(2,1)S(1)} %get-tuple-element.129), channel_id=1, source_target_pairs={{0,2},{1,3},{2,0},{3,1},{4,6},{5,7},{6,4},{7,5},{8,10},{9,11},{10,... | collective-permute-start | bytes 1966088 | tf_op jit(solution)/shard_map/ppermute | solution.py:238
  25.4 8.8 %collective-permute-start.7 = (bf16[360,256]{1,0:T(8,128)(2,1)S(1)}, bf16[360,256]{1,0:T(8,128)(2,1)S(1)}, u32[]{:S(2)}, u32[]{:S(2)}) collective-permute-start(bf16[360,256]{1,0:T(8,128)(2,1)S(1)} %get-tuple-element.37), channel_id=1, source_target_pairs={{0,4},{1,5},{2,6},{3,7},{4,8},{5,9},{6,10},{7,11},{8,12},{9,13},{1... | collective-permute-start | bytes 552968 | tf_op jit(solution)/shard_map/ppermute | solution.py:238
  28.4 12.4 %collective-permute-start.8 = (bf16[360,256]{1,0:T(8,128)(2,1)S(1)}, bf16[360,256]{1,0:T(8,128)(2,1)S(1)}, u32[]{:S(2)}, u32[]{:S(2)}) collective-permute-start(bf16[360,256]{1,0:T(8,128)(2,1)S(1)} %get-tuple-element.37), channel_id=1, source_target_pairs={{0,8},{1,9},{2,10},{3,11},{4,12},{5,13},{6,14},{7,15},{8,0},{9,1},... | collective-permute-start | bytes 552968 | tf_op jit(solution)/shard_map/ppermute | solution.py:238
  30.4 10.4 %collective-permute-start.9 = (bf16[360,256]{1,0:T(8,128)(2,1)S(1)}, bf16[360,256]{1,0:T(8,128)(2,1)S(1)}, u32[]{:S(2)}, u32[]{:S(2)}) collective-permute-start(bf16[360,256]{1,0:T(8,128)(2,1)S(1)} %get-tuple-element.37), channel_id=1, source_target_pairs={{0,12},{1,13},{2,14},{3,15},{4,0},{5,1},{6,2},{7,3},{8,4},{9,5},{1... | collective-permute-start | bytes 552968 | tf_op jit(solution)/shard_map/ppermute | solution.py:238
  40.9 12.4 %collective-permute-start.12 = (bf16[360,128]{1,0:T(8,128)(2,1)S(1)}, bf16[360,128]{1,0:T(8,128)(2,1)S(1)}, u32[]{:S(2)}, u32[]{:S(2)}) collective-permute-start(bf16[360,128]{1,0:T(8,128)(2,1)S(1)} %slice_select_fusion.2), channel_id=1, source_target_pairs={{0,4},{1,5},{2,6},{3,7},{4,8},{5,9},{6,10},{7,11},{8,12},{9,13},{1... | collective-permute-start | bytes 276488 | tf_op jit(solution)/shard_map/ppermute | solution.py:238
  47.2 8.7 %collective-permute-start.13 = (bf16[360,128]{1,0:T(8,128)(2,1)S(1)}, bf16[360,128]{1,0:T(8,128)(2,1)S(1)}, u32[]{:S(2)}, u32[]{:S(2)}) collective-permute-start(bf16[360,128]{1,0:T(8,128)(2,1)S(1)} %slice_select_fusion.2), channel_id=1, source_target_pairs={{0,8},{1,9},{2,10},{3,11},{4,12},{5,13},{6,14},{7,15},{8,0},{9,1},... | collective-permute-start | bytes 276488 | tf_op jit(solution)/shard_map/ppermute | solution.py:238
  50.6 5.6 %collective-permute-start.14 = (bf16[360,128]{1,0:T(8,128)(2,1)S(1)}, bf16[360,128]{1,0:T(8,128)(2,1)S(1)}, u32[]{:S(2)}, u32[]{:S(2)}) collective-permute-start(bf16[360,128]{1,0:T(8,128)(2,1)S(1)} %slice_select_fusion.2), channel_id=1, source_target_pairs={{0,12},{1,13},{2,14},{3,15},{4,0},{5,1},{6,2},{7,3},{8,4},{9,5},{1... | collective-permute-start | bytes 276488 | tf_op jit(solution)/shard_map/ppermute | solution.py:238
  50.9 10.1 %collective-permute-start.10 = (bf16[4,360,128]{2,1,0:T(8,128)(2,1)S(1)}, bf16[4,360,128]{2,1,0:T(8,128)(2,1)S(1)}, u32[]{:S(2)}, u32[]{:S(2)}) collective-permute-start(bf16[4,360,128]{2,1,0:T(8,128)(2,1)S(1)} %get-tuple-element.119), channel_id=1, source_target_pairs={{0,2},{1,3},{2,0},{3,1},{4,6},{5,7},{6,4},{7,5},{8,10},{9,11},{10,... | collective-permute-start | bytes 1105928 | tf_op jit(solution)/shard_map/ppermute | solution.py:238
  56.4 10.7 %collective-permute-start.19 = (bf16[4,360,128]{2,1,0:T(8,128)(2,1)S(1)}, bf16[4,360,128]{2,1,0:T(8,128)(2,1)S(1)}, u32[]{:S(2)}, u32[]{:S(2)}) collective-permute-start(bf16[4,360,128]{2,1,0:T(8,128)(2,1)S(1)} %get-tuple-element.139), channel_id=1, source_target_pairs={{0,2},{1,3},{2,0},{3,1},{4,6},{5,7},{6,4},{7,5},{8,10},{9,11},{10,... | collective-permute-start | bytes 1105928 | tf_op jit(solution)/shard_map/ppermute | solution.py:238
  61.0 7.7 %collective-permute-start.15 = (bf16[360,256]{1,0:T(8,128)(2,1)S(1)}, bf16[360,256]{1,0:T(8,128)(2,1)S(1)}, u32[]{:S(2)}, u32[]{:S(2)}) collective-permute-start(bf16[360,256]{1,0:T(8,128)(2,1)S(1)} %get-tuple-element.43), channel_id=1, source_target_pairs={{0,4},{1,5},{2,6},{3,7},{4,8},{5,9},{6,10},{7,11},{8,12},{9,13},{1... | collective-permute-start | bytes 552968 | tf_op jit(solution)/shard_map/ppermute | solution.py:238
  61.9 12.4 %collective-permute-start.16 = (bf16[360,256]{1,0:T(8,128)(2,1)S(1)}, bf16[360,256]{1,0:T(8,128)(2,1)S(1)}, u32[]{:S(2)}, u32[]{:S(2)}) collective-permute-start(bf16[360,256]{1,0:T(8,128)(2,1)S(1)} %get-tuple-element.43), channel_id=1, source_target_pairs={{0,8},{1,9},{2,10},{3,11},{4,12},{5,13},{6,14},{7,15},{8,0},{9,1},... | collective-permute-start | bytes 552968 | tf_op jit(solution)/shard_map/ppermute | solution.py:238
  63.5 10.8 %collective-permute-start.17 = (bf16[360,256]{1,0:T(8,128)(2,1)S(1)}, bf16[360,256]{1,0:T(8,128)(2,1)S(1)}, u32[]{:S(2)}, u32[]{:S(2)}) collective-permute-start(bf16[360,256]{1,0:T(8,128)(2,1)S(1)} %get-tuple-element.43), channel_id=1, source_target_pairs={{0,12},{1,13},{2,14},{3,15},{4,0},{5,1},{6,2},{7,3},{8,4},{9,5},{1... | collective-permute-start | bytes 552968 | tf_op jit(solution)/shard_map/ppermute | solution.py:238
  65.9 12.4 %collective-permute-start.5 = (bf16[4,2,128,640]{3,2,1,0:T(8,128)(2,1)S(1)}, bf16[4,2,128,640]{3,2,1,0:T(8,128)(2,1)S(1)}, u32[]{:S(2)}, u32[]{:S(2)}) collective-permute-start(bf16[4,2,128,640]{3,2,1,0:T(8,128)(2,1)S(1)} %maximum_select_fusion.8), channel_id=1, source_target_pairs={{0,1},{1,0},{2,3},{3,2},{4,5},{5,4},{6,7},{7,6},{8,9},{9,8},{10,11... | collective-permute-start | bytes 3932168 | tf_op jit(solution)/shard_map/ppermute | solution.py:238
  67.1 10.0 %collective-permute-start.11 = (bf16[4,360,128]{2,1,0:T(8,128)(2,1)S(1)}, bf16[4,360,128]{2,1,0:T(8,128)(2,1)S(1)}, u32[]{:S(2)}, u32[]{:S(2)}) collective-permute-start(bf16[4,360,128]{2,1,0:T(8,128)(2,1)S(1)} %get-tuple-element.41), channel_id=1, source_target_pairs={{0,2},{1,3},{2,0},{3,1},{4,6},{5,7},{6,4},{7,5},{8,10},{9,11},{10,... | collective-permute-start | bytes 1105928 | tf_op jit(solution)/shard_map/ppermute | solution.py:238
  74.4 3.5 %collective-permute-start.20 = (bf16[4,2,360,128]{3,2,0,1:T(8,128)(2,1)S(1)}, bf16[4,2,360,128]{3,2,0,1:T(8,128)(2,1)S(1)}, u32[]{:S(2)}, u32[]{:S(2)}) collective-permute-start(bf16[4,2,360,128]{3,2,0,1:T(8,128)(2,1)S(1)} %maximum_select_fusion.14), channel_id=1, source_target_pairs={{0,1},{1,0},{2,3},{3,2},{4,5},{5,4},{6,7},{7,6},{8,9},{9,8},{10,11... | collective-permute-start | bytes 2211848 | tf_op jit(solution)/shard_map/ppermute | solution.py:238
  75.6 18.9 %collective-permute-start.22 = (bf16[4,360,256]{2,1,0:T(8,128)(2,1)S(1)}, bf16[4,360,256]{2,1,0:T(8,128)(2,1)S(1)}, u32[]{:S(2)}, u32[]{:S(2)}) collective-permute-start(bf16[4,360,256]{2,1,0:T(8,128)(2,1)S(1)} %get-tuple-element.108), channel_id=1, source_target_pairs={{0,2},{1,3},{2,0},{3,1},{4,6},{5,7},{6,4},{7,5},{8,10},{9,11},{10,... | collective-permute-start | bytes 2211848 | tf_op jit(solution)/shard_map/ppermute | solution.py:238
  77.5 3.4 %collective-permute-start.18 = (bf16[4,2,360,256]{3,2,0,1:T(8,128)(2,1)S(1)}, bf16[4,2,360,256]{3,2,0,1:T(8,128)(2,1)S(1)}, u32[]{:S(2)}, u32[]{:S(2)}) collective-permute-start(bf16[4,2,360,256]{3,2,0,1:T(8,128)(2,1)S(1)} %maximum_select_fusion.3), channel_id=1, source_target_pairs={{0,1},{1,0},{2,3},{3,2},{4,5},{5,4},{6,7},{7,6},{8,9},{9,8},{10,11... | collective-permute-start | bytes 4423688 | tf_op jit(solution)/shard_map/ppermute | solution.py:238
  88.7 6.1 %copy-start.11 = (f32[480,384]{1,0:T(8,128)}, f32[480,384]{1,0:T(8,128)S(1)}, u32[]{:S(2)}) copy-start(f32[480,384]{1,0:T(8,128)S(1)} %get-tuple-element.57.preact_ref) | copy-start | bytes 2211844
  88.7 6.1 %copy-start.13 = (bf16[480,640]{1,0:T(8,128)(2,1)}, bf16[480,640]{1,0:T(8,128)(2,1)S(1)}, u32[]{:S(2)}) copy-start(bf16[480,640]{1,0:T(8,128)(2,1)S(1)} %get-tuple-element.56.normed_ref) | copy-start | bytes 1843204
  88.7 16.4 %collective-permute-start.21 = (bf16[480,640]{1,0:T(8,128)(2,1)S(1)}, bf16[480,640]{1,0:T(8,128)(2,1)}, u32[]{:S(2)}, u32[]{:S(2)}) collective-permute-start(bf16[480,640]{1,0:T(8,128)(2,1)S(1)} %get-tuple-element.46.own_ref), channel_id=1, source_target_pairs={{0,16},{16,0},{1,17},{17,1},{2,18},{18,2},{3,19},{19,3},{4,20},{20... | collective-permute-start | bytes 1843208 | tf_op jit(solution)/shard_map/ppermute | solution.py:242
  96.5 5.3 %collective-permute-start.26 = (bf16[2,360,256]{2,1,0:T(8,128)(2,1)}, bf16[2,360,256]{2,1,0:T(8,128)(2,1)S(1)}, u32[]{:S(2)}, u32[]{:S(2)}) collective-permute-start(bf16[2,360,256]{2,1,0:T(8,128)(2,1)} %get-tuple-element.88), channel_id=1, source_target_pairs={{0,1},{1,0},{2,3},{3,2},{4,5},{5,4},{6,7},{7,6},{8,9},{9,8},{10,11... | collective-permute-start | bytes 1105928 | tf_op jit(solution)/shard_map/ppermute | solution.py:238
  96.5 5.3 %collective-permute-start.25 = (bf16[2,360,256]{2,1,0:T(8,128)(2,1)}, bf16[2,360,256]{2,1,0:T(8,128)(2,1)}, u32[]{:S(2)}, u32[]{:S(2)}) collective-permute-start(bf16[2,360,256]{2,1,0:T(8,128)(2,1)} %get-tuple-element.89), channel_id=1, source_target_pairs={{0,1},{1,0},{2,3},{3,2},{4,5},{5,4},{6,7},{7,6},{8,9},{9,8},{10,11... | collective-permute-start | bytes 1105928 | tf_op jit(solution)/shard_map/ppermute | solution.py:238
  97.0 4.8 %collective-permute-start.24 = (bf16[2,360,256]{2,1,0:T(8,128)(2,1)}, bf16[2,360,256]{2,1,0:T(8,128)(2,1)}, u32[]{:S(2)}, u32[]{:S(2)}) collective-permute-start(bf16[2,360,256]{2,1,0:T(8,128)(2,1)} %get-tuple-element.87), channel_id=1, source_target_pairs={{0,1},{1,0},{2,3},{3,2},{4,5},{5,4},{6,7},{7,6},{8,9},{9,8},{10,11... | collective-permute-start | bytes 1105928 | tf_op jit(solution)/shard_map/ppermute | solution.py:238
  97.0 4.8 %collective-permute-start.23 = (bf16[2,360,256]{2,1,0:T(8,128)(2,1)S(1)}, bf16[2,360,256]{2,1,0:T(8,128)(2,1)}, u32[]{:S(2)}, u32[]{:S(2)}) collective-permute-start(bf16[2,360,256]{2,1,0:T(8,128)(2,1)S(1)} %get-tuple-element.86), channel_id=1, source_target_pairs={{0,1},{1,0},{2,3},{3,2},{4,5},{5,4},{6,7},{7,6},{8,9},{9,8},{10,11... | collective-permute-start | bytes 1105928 | tf_op jit(solution)/shard_map/ppermute | solution.py:238
  123.9 4.1 %collective-permute-start.31 = (bf16[2,360,256]{2,1,0:T(8,128)(2,1)}, bf16[2,360,256]{2,1,0:T(8,128)(2,1)}, u32[]{:S(2)}, u32[]{:S(2)}) collective-permute-start(bf16[2,360,256]{2,1,0:T(8,128)(2,1)} %get-tuple-element.77), channel_id=1, source_target_pairs={{0,1},{1,0},{2,3},{3,2},{4,5},{5,4},{6,7},{7,6},{8,9},{9,8},{10,11... | collective-permute-start | bytes 1105928 | tf_op jit(solution)/shard_map/ppermute | solution.py:238
  124.3 3.7 %collective-permute-start.30 = (bf16[2,360,256]{2,1,0:T(8,128)(2,1)}, bf16[2,360,256]{2,1,0:T(8,128)(2,1)}, u32[]{:S(2)}, u32[]{:S(2)}) collective-permute-start(bf16[2,360,256]{2,1,0:T(8,128)(2,1)} %get-tuple-element.75), channel_id=1, source_target_pairs={{0,1},{1,0},{2,3},{3,2},{4,5},{5,4},{6,7},{7,6},{8,9},{9,8},{10,11... | collective-permute-start | bytes 1105928 | tf_op jit(solution)/shard_map/ppermute | solution.py:238
  124.8 3.2 %collective-permute-start.29 = (bf16[2,360,256]{2,1,0:T(8,128)(2,1)}, bf16[2,360,256]{2,1,0:T(8,128)(2,1)}, u32[]{:S(2)}, u32[]{:S(2)}) collective-permute-start(bf16[2,360,256]{2,1,0:T(8,128)(2,1)} %get-tuple-element.76), channel_id=1, source_target_pairs={{0,1},{1,0},{2,3},{3,2},{4,5},{5,4},{6,7},{7,6},{8,9},{9,8},{10,11... | collective-permute-start | bytes 1105928 | tf_op jit(solution)/shard_map/ppermute | solution.py:238
  124.9 3.1 %collective-permute-start.28 = (bf16[2,360,256]{2,1,0:T(8,128)(2,1)S(1)}, bf16[2,360,256]{2,1,0:T(8,128)(2,1)}, u32[]{:S(2)}, u32[]{:S(2)}) collective-permute-start(bf16[2,360,256]{2,1,0:T(8,128)(2,1)S(1)} %get-tuple-element.74), channel_id=1, source_target_pairs={{0,1},{1,0},{2,3},{3,2},{4,5},{5,4},{6,7},{7,6},{8,9},{9,8},{10,11... | collective-permute-start | bytes 1105928 | tf_op jit(solution)/shard_map/ppermute | solution.py:238
  125.3 16.2 %collective-permute-start.27 = (bf16[480,640]{1,0:T(8,128)(2,1)}, bf16[480,640]{1,0:T(8,128)(2,1)}, u32[]{:S(2)}, u32[]{:S(2)}) collective-permute-start(bf16[480,640]{1,0:T(8,128)(2,1)} %get-tuple-element.50.own_ref), channel_id=1, source_target_pairs={{0,16},{16,0},{1,17},{17,1},{2,18},{18,2},{3,19},{19,3},{4,20},{20... | collective-permute-start | bytes 1843208 | tf_op jit(solution)/shard_map/ppermute | solution.py:242
  129.5 11.9 %copy-start.10 = (bf16[5,3,32,640]{3,2,1,0:T(8,128)(2,1)S(1)}, bf16[5,3,32,640]{3,2,1,0:T(8,128)(2,1)}, u32[]{:S(2)}) copy-start(bf16[5,3,32,640]{3,2,1,0:T(8,128)(2,1)} %param.7) | copy-start | bytes 1843204
  129.6 11.9 %copy-start.12 = (f32[480,384]{1,0:T(8,128)S(1)}, f32[480,384]{1,0:T(8,128)}, u32[]{:S(2)}) copy-start(f32[480,384]{1,0:T(8,128)} %copy-done.11) | copy-start | bytes 2211844
  129.6 11.9 %copy-start.14 = (bf16[480,640]{1,0:T(8,128)(2,1)S(1)}, bf16[480,640]{1,0:T(8,128)(2,1)}, u32[]{:S(2)}) copy-start(bf16[480,640]{1,0:T(8,128)(2,1)} %copy-done.13) | copy-start | bytes 1843204
  129.6 11.9 %copy-start.16 = (bf16[480,640]{1,0:T(8,128)(2,1)S(1)}, bf16[480,640]{1,0:T(8,128)(2,1)}, u32[]{:S(2)}) copy-start(bf16[480,640]{1,0:T(8,128)(2,1)} %copy-done.15) | copy-start | bytes 1843204
  130.1 11.4 %copy-start.7 = (bf16[8,120,640]{2,1,0:T(8,128)(2,1)S(1)}, bf16[8,120,640]{2,1,0:T(8,128)(2,1)}, u32[]{:S(2)}) copy-start(bf16[8,120,640]{2,1,0:T(8,128)(2,1)} %copy-done.6) | copy-start | bytes 3686404
  130.1 19.9 %collective-permute-start.32 = (bf16[4,360,256]{2,1,0:T(8,128)(2,1)S(1)}, bf16[4,360,256]{2,1,0:T(8,128)(2,1)S(1)}, u32[]{:S(2)}, u32[]{:S(2)}) collective-permute-start(bf16[4,360,256]{2,1,0:T(8,128)(2,1)S(1)} %dynamic-slice_bitcast_fusion), channel_id=1, source_target_pairs={{0,2},{1,3},{2,0},{3,1},{4,6},{5,7},{6,4},{7,5},{8,10},{9,11},{10,... | collective-permute-start | bytes 2211848 | tf_op jit(solution)/shard_map/ppermute | solution.py:238
  141.5 7.8 %copy-start.5 = (bf16[5760,128]{1,0:T(8,128)(2,1)S(1)}, bf16[5760,128]{1,0:T(8,128)(2,1)}, u32[]{:S(2)}) copy-start(bf16[5760,128]{1,0:T(8,128)(2,1)} %copy-done.4) | copy-start | bytes 4423684
  150.0 3.2 %collective-permute-start.34 = (bf16[4,2,360,128]{3,2,0,1:T(8,128)(2,1)S(1)}, bf16[4,2,360,128]{3,2,0,1:T(8,128)(2,1)S(1)}, u32[]{:S(2)}, u32[]{:S(2)}) collective-permute-start(bf16[4,2,360,128]{3,2,0,1:T(8,128)(2,1)S(1)} %bitcast.354), channel_id=1, source_target_pairs={{0,1},{1,0},{2,3},{3,2},{4,5},{5,4},{6,7},{7,6},{8,9},{9,8},{10,11... | collective-permute-start | bytes 2211848 | tf_op jit(solution)/shard_map/ppermute | solution.py:238
  150.4 16.4 %collective-permute-start.33 = (bf16[4,2,360,256]{3,2,0,1:T(8,128)(2,1)S(1)}, bf16[4,2,360,256]{3,2,0,1:T(8,128)(2,1)S(1)}, u32[]{:S(2)}, u32[]{:S(2)}) collective-permute-start(bf16[4,2,360,256]{3,2,0,1:T(8,128)(2,1)S(1)} %bitcast.348), channel_id=1, source_target_pairs={{0,1},{1,0},{2,3},{3,2},{4,5},{5,4},{6,7},{7,6},{8,9},{9,8},{10,11... | collective-permute-start | bytes 4423688 | tf_op jit(solution)/shard_map/ppermute | solution.py:238
  152.6 15.5 %collective-permute-start.47 = (bf16[4,2,128,640]{3,2,1,0:T(8,128)(2,1)S(1)}, bf16[4,2,128,640]{3,2,1,0:T(8,128)(2,1)S(1)}, u32[]{:S(2)}, u32[]{:S(2)}) collective-permute-start(bf16[4,2,128,640]{3,2,1,0:T(8,128)(2,1)S(1)} %fusion.8), channel_id=1, source_target_pairs={{0,1},{1,0},{2,3},{3,2},{4,5},{5,4},{6,7},{7,6},{8,9},{9,8},{10,11... | collective-permute-start | bytes 3932168 | tf_op jit(solution)/shard_map/ppermute | solution.py:238
  153.4 10.6 %collective-permute-start.35 = (bf16[4,360,128]{2,1,0:T(8,128)(2,1)S(1)}, bf16[4,360,128]{2,1,0:T(8,128)(2,1)S(1)}, u32[]{:S(2)}, u32[]{:S(2)}) collective-permute-start(bf16[4,360,128]{2,1,0:T(8,128)(2,1)S(1)} %dynamic-slice_bitcast_fusion.7), channel_id=1, source_target_pairs={{0,2},{1,3},{2,0},{3,1},{4,6},{5,7},{6,4},{7,5},{8,10},{9,11},{10,... | collective-permute-start | bytes 1105928 | tf_op jit(solution)/shard_map/ppermute | solution.py:238
  154.3 23.2 %collective-permute-start.38 = (bf16[360,256]{1,0:T(8,128)(2,1)S(1)}, bf16[360,256]{1,0:T(8,128)(2,1)S(1)}, u32[]{:S(2)}, u32[]{:S(2)}) collective-permute-start(bf16[360,256]{1,0:T(8,128)(2,1)S(1)} %get-tuple-element.105), channel_id=1, source_target_pairs={{0,4},{1,5},{2,6},{3,7},{4,8},{5,9},{6,10},{7,11},{8,12},{9,13},{1... | collective-permute-start | bytes 552968 | tf_op jit(solution)/shard_map/ppermute | solution.py:238
  156.9 20.7 %collective-permute-start.39 = (bf16[360,256]{1,0:T(8,128)(2,1)S(1)}, bf16[360,256]{1,0:T(8,128)(2,1)S(1)}, u32[]{:S(2)}, u32[]{:S(2)}) collective-permute-start(bf16[360,256]{1,0:T(8,128)(2,1)S(1)} %get-tuple-element.104), channel_id=1, source_target_pairs={{0,8},{1,9},{2,10},{3,11},{4,12},{5,13},{6,14},{7,15},{8,0},{9,1},... | collective-permute-start | bytes 552968 | tf_op jit(solution)/shard_map/ppermute | solution.py:238
  164.0 13.6 %collective-permute-start.40 = (bf16[360,256]{1,0:T(8,128)(2,1)S(1)}, bf16[360,256]{1,0:T(8,128)(2,1)S(1)}, u32[]{:S(2)}, u32[]{:S(2)}) collective-permute-start(bf16[360,256]{1,0:T(8,128)(2,1)S(1)} %get-tuple-element.103), channel_id=1, source_target_pairs={{0,12},{1,13},{2,14},{3,15},{4,0},{5,1},{6,2},{7,3},{8,4},{9,5},{1... | collective-permute-start | bytes 552968 | tf_op jit(solution)/shard_map/ppermute | solution.py:238
  167.5 9.5 %collective-permute-start.36 = (bf16[4,360,128]{2,1,0:T(8,128)(2,1)S(1)}, bf16[4,360,128]{2,1,0:T(8,128)(2,1)S(1)}, u32[]{:S(2)}, u32[]{:S(2)}) collective-permute-start(bf16[4,360,128]{2,1,0:T(8,128)(2,1)S(1)} %dynamic-slice_bitcast_fusion.8), channel_id=1, source_target_pairs={{0,2},{1,3},{2,0},{3,1},{4,6},{5,7},{6,4},{7,5},{8,10},{9,11},{10,... | collective-permute-start | bytes 1105928 | tf_op jit(solution)/shard_map/ppermute | solution.py:238
  177.0 8.8 %collective-permute-start.37 = (bf16[4,360,128]{2,1,0:T(8,128)(2,1)S(1)}, bf16[4,360,128]{2,1,0:T(8,128)(2,1)S(1)}, u32[]{:S(2)}, u32[]{:S(2)}) collective-permute-start(bf16[4,360,128]{2,1,0:T(8,128)(2,1)S(1)} %dynamic-slice_bitcast_fusion.6), channel_id=1, source_target_pairs={{0,2},{1,3},{2,0},{3,1},{4,6},{5,7},{6,4},{7,5},{8,10},{9,11},{10,... | collective-permute-start | bytes 1105928 | tf_op jit(solution)/shard_map/ppermute | solution.py:238
  177.6 8.6 %collective-permute-start.43 = (bf16[360,128]{1,0:T(8,128)(2,1)S(1)}, bf16[360,128]{1,0:T(8,128)(2,1)S(1)}, u32[]{:S(2)}, u32[]{:S(2)}) collective-permute-start(bf16[360,128]{1,0:T(8,128)(2,1)S(1)} %get-tuple-element.135), channel_id=1, source_target_pairs={{0,12},{1,13},{2,14},{3,15},{4,0},{5,1},{6,2},{7,3},{8,4},{9,5},{1... | collective-permute-start | bytes 276488 | tf_op jit(solution)/shard_map/ppermute | solution.py:238
  178.0 8.2 %collective-permute-start.42 = (bf16[360,128]{1,0:T(8,128)(2,1)S(1)}, bf16[360,128]{1,0:T(8,128)(2,1)S(1)}, u32[]{:S(2)}, u32[]{:S(2)}) collective-permute-start(bf16[360,128]{1,0:T(8,128)(2,1)S(1)} %get-tuple-element.136), channel_id=1, source_target_pairs={{0,8},{1,9},{2,10},{3,11},{4,12},{5,13},{6,14},{7,15},{8,0},{9,1},... | collective-permute-start | bytes 276488 | tf_op jit(solution)/shard_map/ppermute | solution.py:238
  179.4 6.9 %collective-permute-start.41 = (bf16[360,128]{1,0:T(8,128)(2,1)S(1)}, bf16[360,128]{1,0:T(8,128)(2,1)S(1)}, u32[]{:S(2)}, u32[]{:S(2)}) collective-permute-start(bf16[360,128]{1,0:T(8,128)(2,1)S(1)} %get-tuple-element.134), channel_id=1, source_target_pairs={{0,4},{1,5},{2,6},{3,7},{4,8},{5,9},{6,10},{7,11},{8,12},{9,13},{1... | collective-permute-start | bytes 276488 | tf_op jit(solution)/shard_map/ppermute | solution.py:238
  185.7 13.8 %collective-permute-start.48 = (bf16[4,128,640]{2,1,0:T(8,128)(2,1)S(1)}, bf16[4,128,640]{2,1,0:T(8,128)(2,1)S(1)}, u32[]{:S(2)}, u32[]{:S(2)}) collective-permute-start(bf16[4,128,640]{2,1,0:T(8,128)(2,1)S(1)} %dynamic-slice_bitcast_fusion.1), channel_id=1, source_target_pairs={{0,2},{1,3},{2,0},{3,1},{4,6},{5,7},{6,4},{7,5},{8,10},{9,11},{10,... | collective-permute-start | bytes 1966088 | tf_op jit(solution)/shard_map/ppermute | solution.py:238
  186.6 14.2 %collective-permute-start.46 = (bf16[360,256]{1,0:T(8,128)(2,1)S(1)}, bf16[360,256]{1,0:T(8,128)(2,1)S(1)}, u32[]{:S(2)}, u32[]{:S(2)}) collective-permute-start(bf16[360,256]{1,0:T(8,128)(2,1)S(1)} %get-tuple-element.101), channel_id=1, source_target_pairs={{0,12},{1,13},{2,14},{3,15},{4,0},{5,1},{6,2},{7,3},{8,4},{9,5},{1... | collective-permute-start | bytes 552968 | tf_op jit(solution)/shard_map/ppermute | solution.py:238
  188.2 24.6 %collective-permute-start.45 = (bf16[360,256]{1,0:T(8,128)(2,1)S(1)}, bf16[360,256]{1,0:T(8,128)(2,1)S(1)}, u32[]{:S(2)}, u32[]{:S(2)}) collective-permute-start(bf16[360,256]{1,0:T(8,128)(2,1)S(1)} %get-tuple-element.102), channel_id=1, source_target_pairs={{0,8},{1,9},{2,10},{3,11},{4,12},{5,13},{6,14},{7,15},{8,0},{9,1},... | collective-permute-start | bytes 552968 | tf_op jit(solution)/shard_map/ppermute | solution.py:238
  188.3 24.4 %collective-permute-start.44 = (bf16[360,256]{1,0:T(8,128)(2,1)S(1)}, bf16[360,256]{1,0:T(8,128)(2,1)S(1)}, u32[]{:S(2)}, u32[]{:S(2)}) collective-permute-start(bf16[360,256]{1,0:T(8,128)(2,1)S(1)} %get-tuple-element.100), channel_id=1, source_target_pairs={{0,4},{1,5},{2,6},{3,7},{4,8},{5,9},{6,10},{7,11},{8,12},{9,13},{1... | collective-permute-start | bytes 552968 | tf_op jit(solution)/shard_map/ppermute | solution.py:238
  199.7 14.9 %collective-permute-start.52 = (bf16[128,640]{1,0:T(8,128)(2,1)S(1)}, bf16[128,640]{1,0:T(8,128)(2,1)S(1)}, u32[]{:S(2)}, u32[]{:S(2)}) collective-permute-start(bf16[128,640]{1,0:T(8,128)(2,1)S(1)} %get-tuple-element.125), channel_id=1, source_target_pairs={{0,12},{1,13},{2,14},{3,15},{4,0},{5,1},{6,2},{7,3},{8,4},{9,5},{1... | collective-permute-start | bytes 491528 | tf_op jit(solution)/shard_map/ppermute | solution.py:238
  200.2 17.0 %collective-permute-start.51 = (bf16[128,640]{1,0:T(8,128)(2,1)S(1)}, bf16[128,640]{1,0:T(8,128)(2,1)S(1)}, u32[]{:S(2)}, u32[]{:S(2)}) collective-permute-start(bf16[128,640]{1,0:T(8,128)(2,1)S(1)} %get-tuple-element.126), channel_id=1, source_target_pairs={{0,8},{1,9},{2,10},{3,11},{4,12},{5,13},{6,14},{7,15},{8,0},{9,1},... | collective-permute-start | bytes 491528 | tf_op jit(solution)/shard_map/ppermute | solution.py:238
  200.8 16.4 %collective-permute-start.50 = (bf16[128,640]{1,0:T(8,128)(2,1)S(1)}, bf16[128,640]{1,0:T(8,128)(2,1)S(1)}, u32[]{:S(2)}, u32[]{:S(2)}) collective-permute-start(bf16[128,640]{1,0:T(8,128)(2,1)S(1)} %get-tuple-element.124), channel_id=1, source_target_pairs={{0,4},{1,5},{2,6},{3,7},{4,8},{5,9},{6,10},{7,11},{8,12},{9,13},{1... | collective-permute-start | bytes 491528 | tf_op jit(solution)/shard_map/ppermute | solution.py:238
  213.0 7.5 %collective-permute-start.49 = (bf16[360,384]{1,0:T(8,128)(2,1)S(1)}, bf16[360,384]{1,0:T(8,128)(2,1)S(1)}, u32[]{:S(2)}, u32[]{:S(2)}) collective-permute-start(bf16[360,384]{1,0:T(8,128)(2,1)S(1)} %pad_maximum_fusion.7), channel_id=1, source_target_pairs={{0,16},{16,0},{1,17},{17,1},{2,18},{18,2},{3,19},{19,3},{4,20},{20... | collective-permute-start | bytes 829448 | tf_op jit(solution)/shard_map/ppermute | solution.py:242
  217.4 5.4 %collective-permute-start.53 = (bf16[64,640]{1,0:T(8,128)(2,1)S(1)}, bf16[64,640]{1,0:T(8,128)(2,1)S(1)}, u32[]{:S(2)}, u32[]{:S(2)}) collective-permute-start(bf16[64,640]{1,0:T(8,128)(2,1)S(1)} %select_convert_fusion.1), channel_id=1, source_target_pairs={{0,16},{16,0},{1,17},{17,1},{2,18},{18,2},{3,19},{19,3},{4,20},{20... | collective-permute-start | bytes 245768 | tf_op jit(solution)/shard_map/ppermute | solution.py:242
  (12 other events, 21.0 us)

commit v6 on v5

--- a/solution.py
+++ b/solution.py
@@ -641,8 +641,8 @@
     main_own, main_given = spatial_own[:, :main], given[:, :main]
     tails = jnp.where(tail, spatial_own[:, 2 * main :], given[:, main:])
     line, sent = gathered_over_z(jnp.where(first, main_own, main_given), sent, side_temporal)
-    line_tails, sent = gathered_over_z(tails, sent)
     side_low = sent_over_y(line[..., :LANES])
+    line_tails, sent = gathered_over_z(tails, (sent, side_low))
     side_high = sent_over_y(line[..., LANES:], side_low)
     side_tails = sent_over_y(line_tails)
     line_second, sent = gathered_over_z(

time: 228 us -> 240 us (1.053)
  starting transfers between devices: 62.8 us -> 80.1 us
  waiting for transfers between devices: 93.9 us -> 88.8 us
    ppermute x48, starting transfers between devices: 53.6 us -> 70.9 us  [shifted(): return lax.ppermute(value, 'dp', pairs)]
    ppermute x48, waiting for transfers between devices: 78.9 us -> 73.9 us  [shifted(): return lax.ppermute(value, 'dp', pairs)]
  transfers between devices with their start and end apart: 54 -> 54, of which waited for: 22 -> 23; matrix products, arithmetic and copies ran while one was open for 12% -> 11% of each run, Pallas kernels for 6% -> 6%
where the time goes in v6:
time: 240 us; the launch traced here: 236 us
  waiting for transfers between devices  88.8 us (37%)
  starting transfers between devices  80.1 us (33%)
  Pallas kernels  28.8 us (12%)
  other arithmetic  17.6 us (7%)
  local copies, waits for them, and re-layouts  16 us (7%)
  matrix products  2.84 us (1%)
    ppermute x48, waiting for transfers between devices, shifted(): return lax.ppermute(value, 'dp', pairs)  73.9 us
    ppermute x48, starting transfers between devices, shifted(): return lax.ppermute(value, 'dp', pairs)  70.9 us
    ppermute x6, waiting for transfers between devices, swapped(): return lax.ppermute(value, 'pipe', [(0, 1), (1, 0)])  14.9 us
    pallas_call x1, Pallas kernels, paired_device(): vmem_call(functools.partial(second_forward, frames), (shape((rows, channe...  10.4 us
    ppermute x6, starting transfers between devices, swapped(): return lax.ppermute(value, 'pipe', [(0, 1), (1, 0)])  9.23 us
    pallas_call x1, Pallas kernels, paired_device(): vmem_call(functools.partial(first_terms, frames), terms_shape(), flops=sp...  7.76 us
    pallas_call x1, Pallas kernels, paired_device(): vmem_call(functools.partial(first_forward, frames), (shape((rows, channel...  6.25 us
  transfers between devices with their start and end apart: 54, of which 23 were waited for; matrix products, arithmetic and copies ran while one was open for 11% of the time, Pallas kernels for 6%

profile of v6, /device:TPU:0, one launch (start us, length us, event | category | flops | bytes accessed | tf_op | source)
XLA Modules:
  0.0 236.0 jit_solution(3928125018693119047)
XLA Ops:
  2.4 3.0 %collective-permute-start = (bf16[64,640]{1,0:T(8,128)(2,1)S(1)}, bf16[64,640]{1,0:T(8,128)(2,1)S(1)}, u32[]{:S(2)}, u32[]{:S(2)}) collective-permute-start(bf16[64,640]{1,0:T(8,128)(2,1)S(1)} %fusion.43), channel_id=1, source_target_pairs={{0,16},{16,0},{1,17},{17,1},{2,18},{18,2},{3,19},{19,3},{4,20},{20... | collective-permute-start | bytes 245768 | tf_op jit(solution)/shard_map/ppermute | solution.py:242
  7.9 3.2 %collective-permute-start.2 = (bf16[128,640]{1,0:T(8,128)(2,1)S(1)}, bf16[128,640]{1,0:T(8,128)(2,1)S(1)}, u32[]{:S(2)}, u32[]{:S(2)}) collective-permute-start(bf16[128,640]{1,0:T(8,128)(2,1)S(1)} %maximum_select_fusion.16), channel_id=1, source_target_pairs={{0,8},{1,9},{2,10},{3,11},{4,12},{5,13},{6,14},{7,15},{8,0},{9,1},... | collective-permute-start | bytes 491528 | tf_op jit(solution)/shard_map/ppermute | solution.py:238
  11.1 1.3 collective-permute-start.3
  13.1 7.5 %collective-permute-done.2 = bf16[128,640]{1,0:T(8,128)(2,1)S(1)} collective-permute-done((bf16[128,640]{1,0:T(8,128)(2,1)S(1)}, bf16[128,640]{1,0:T(8,128)(2,1)S(1)}, u32[]{:S(2)}, u32[]{:S(2)}) %collective-permute-start.2) | collective-permute-done | bytes 163872 | tf_op jit(solution)/shard_map/ppermute | solution.py:238
  20.6 1.8 collective-permute-done.1
  22.5 1.0 fusion.81
  23.5 1.5 collective-permute-start.4
  25.2 3.0 %collective-permute-start.7 = (bf16[360,256]{1,0:T(8,128)(2,1)S(1)}, bf16[360,256]{1,0:T(8,128)(2,1)S(1)}, u32[]{:S(2)}, u32[]{:S(2)}) collective-permute-start(bf16[360,256]{1,0:T(8,128)(2,1)S(1)} %get-tuple-element.37), channel_id=1, source_target_pairs={{0,4},{1,5},{2,6},{3,7},{4,8},{5,9},{6,10},{7,11},{8,12},{9,13},{1... | collective-permute-start | bytes 552968 | tf_op jit(solution)/shard_map/ppermute | solution.py:238
  28.3 2.0 collective-permute-start.8
  30.3 2.8 %collective-permute-start.9 = (bf16[360,256]{1,0:T(8,128)(2,1)S(1)}, bf16[360,256]{1,0:T(8,128)(2,1)}, u32[]{:S(2)}, u32[]{:S(2)}) collective-permute-start(bf16[360,256]{1,0:T(8,128)(2,1)S(1)} %get-tuple-element.37), channel_id=1, source_target_pairs={{0,12},{1,13},{2,14},{3,15},{4,0},{5,1},{6,2},{7,3},{8,4},{9,5},{1... | collective-permute-start | bytes 552968 | tf_op jit(solution)/shard_map/ppermute | solution.py:238
  33.3 7.4 %collective-permute-done.8 = bf16[360,256]{1,0:T(8,128)(2,1)} collective-permute-done((bf16[360,256]{1,0:T(8,128)(2,1)S(1)}, bf16[360,256]{1,0:T(8,128)(2,1)}, u32[]{:S(2)}, u32[]{:S(2)}) %collective-permute-start.8) | collective-permute-done | bytes 184352 | tf_op jit(solution)/shard_map/ppermute | solution.py:238
  40.7 1.1 select_bitcast_fusion.7
  43.4 9.2 %collective-permute-done.10 = bf16[4,360,128]{2,1,0:T(8,128)(2,1)S(1)} collective-permute-done((bf16[4,360,128]{2,1,0:T(8,128)(2,1)S(1)}, bf16[4,360,128]{2,1,0:T(8,128)(2,1)S(1)}, u32[]{:S(2)}, u32[]{:S(2)}) %collective-permute-start.10) | collective-permute-done | bytes 368672 | tf_op jit(solution)/shard_map/ppermute | solution.py:238
  52.6 4.6 %collective-permute-start.12 = (bf16[360,128]{1,0:T(8,128)(2,1)S(1)}, bf16[360,128]{1,0:T(8,128)(2,1)S(1)}, u32[]{:S(2)}, u32[]{:S(2)}) collective-permute-start(bf16[360,128]{1,0:T(8,128)(2,1)S(1)} %slice_select_fusion.2), channel_id=1, source_target_pairs={{0,4},{1,5},{2,6},{3,7},{4,8},{5,9},{6,10},{7,11},{8,12},{9,13},{1... | collective-permute-start | bytes 276488 | tf_op jit(solution)/shard_map/ppermute | solution.py:238
  57.2 3.5 %collective-permute-start.13 = (bf16[360,128]{1,0:T(8,128)(2,1)S(1)}, bf16[360,128]{1,0:T(8,128)(2,1)S(1)}, u32[]{:S(2)}, u32[]{:S(2)}) collective-permute-start(bf16[360,128]{1,0:T(8,128)(2,1)S(1)} %slice_select_fusion.2), channel_id=1, source_target_pairs={{0,8},{1,9},{2,10},{3,11},{4,12},{5,13},{6,14},{7,15},{8,0},{9,1},... | collective-permute-start | bytes 276488 | tf_op jit(solution)/shard_map/ppermute | solution.py:238
  61.3 1.8 collective-permute-done.12
  63.0 2.9 %collective-permute-done.13 = bf16[360,128]{1,0:T(8,128)(2,1)S(1)} collective-permute-done((bf16[360,128]{1,0:T(8,128)(2,1)S(1)}, bf16[360,128]{1,0:T(8,128)(2,1)S(1)}, u32[]{:S(2)}, u32[]{:S(2)}) %collective-permute-start.13) | collective-permute-done | bytes 92192 | tf_op jit(solution)/shard_map/ppermute | solution.py:238
  66.1 1.3 collective-permute-start.15
  67.4 1.7 collective-permute-start.16
  70.3 5.2 %collective-permute-done.15 = bf16[360,256]{1,0:T(8,128)(2,1)S(1)} collective-permute-done((bf16[360,256]{1,0:T(8,128)(2,1)S(1)}, bf16[360,256]{1,0:T(8,128)(2,1)S(1)}, u32[]{:S(2)}, u32[]{:S(2)}) %collective-permute-start.15) | collective-permute-done | bytes 184352 | tf_op jit(solution)/shard_map/ppermute | solution.py:238
  76.1 3.7 %collective-permute-done.16 = bf16[360,256]{1,0:T(8,128)(2,1)S(1)} collective-permute-done((bf16[360,256]{1,0:T(8,128)(2,1)S(1)}, bf16[360,256]{1,0:T(8,128)(2,1)S(1)}, u32[]{:S(2)}, u32[]{:S(2)}) %collective-permute-start.16) | collective-permute-done | bytes 184352 | tf_op jit(solution)/shard_map/ppermute | solution.py:238
  79.8 1.0 fusion.83
  82.0 1.0 collective-permute-done.19
  84.2 1.3 slice_bitcast_fusion.3
  88.0 6.2 %shard_map.68 = (bf16[480,640]{1,0:T(8,128)(2,1)S(1)}, f32[480,384]{1,0:T(8,128)S(1)}, bf16[480,640]{1,0:T(8,128)(2,1)S(1)}) custom-call(bf16[480,640]{1,0:T(8,128)(2,1)S(1)} %bitcast.324, f32[5,640]{1,0:T(8,128)S(1)} %pad_maximum_fusion.8.embedding_ref, f32[1,384]{1,0:T(1,128)S(1)} %select_n.855.keep_ref, bf16[960,640]{1,0:T(8,128)(2,1)S(1)} %bitcast.321, ...), custom_call_target="tpu_custom_call" | custom-call | flops 7077888000 | bytes 5898240 | tf_op jit(solution)/shard_map/pallas_call | solution.py:671
  94.3 1.6 collective-permute-start.21
  95.9 3.3 %collective-permute-done.22 = bf16[4,360,256]{2,1,0:T(8,128)(2,1)S(1)} collective-permute-done((bf16[4,360,256]{2,1,0:T(8,128)(2,1)S(1)}, bf16[4,360,256]{2,1,0:T(8,128)(2,1)S(1)}, u32[]{:S(2)}, u32[]{:S(2)}) %collective-permute-start.22) | collective-permute-done | bytes 737312 | tf_op jit(solution)/shard_map/ppermute | solution.py:238
  100.0 1.1 slice_bitcast_fusion.9
  102.1 1.1 slice.287
  103.2 1.1 slice.288
  104.4 1.7 maximum_select_fusion.13
  106.4 1.4 pad_maximum_fusion
  107.8 2.8 %collective-permute-done.21.sent_ref = bf16[480,640]{1,0:T(8,128)(2,1)} collective-permute-done((bf16[480,640]{1,0:T(8,128)(2,1)S(1)}, bf16[480,640]{1,0:T(8,128)(2,1)}, u32[]{:S(2)}, u32[]{:S(2)}) %collective-permute-start.21) | collective-permute-done | bytes 614432 | tf_op jit(solution)/shard_map/ppermute | solution.py:242
  112.5 10.4 %shard_map.69 = (bf16[480,640]{1,0:T(8,128)(2,1)S(1)}, bf16[480,640]{1,0:T(8,128)(2,1)S(1)}, bf16[480,384]{1,0:T(8,128)(2,1)S(1)}, bf16[480,384]{1,0:T(8,128)(2,1)S(1)}, bf16[480,640]{1,0:T(8,128)(2,1)}) custom-call(bf16[480,640]{1,0:T(8,128)(2,1)S(1)} %bitcast.325, bf16[480,640]{1,0:T(8,128)(2,1)S(1)} %get-tuple-element.46.own_ref, ...), custom_call_target="tpu_custom_call" | custom-call | flops 12386304000 | bytes 5898240 | tf_op jit(solution)/shard_map/pallas_call | solution.py:680
  122.9 4.4 %shard_map.70 = (bf16[5760,256]{1,0:T(8,128)(2,1)S(1)}, bf16[5760,128]{1,0:T(8,128)(2,1)S(1)}, bf16[960,640]{1,0:T(8,128)(2,1)S(1)}) custom-call(bf16[480,640]{1,0:T(8,128)(2,1)S(1)} %get-tuple-element.51.normed_ref, bf16[480,384]{1,0:T(8,128)(2,1)S(1)} %get-tuple-element.52.pre_grad_ref, bf16[480,384]{1,0:T(8,128)(2,1)S(1)} %get-tuple-element.53.activated_ref, ...), custom_call_target="tpu_custom_call" | custom-call | flops 7077888000 | bytes 5898240 | tf_op jit(solution)/shard_map/pallas_call | solution.py:707
  127.3 1.2 dynamic-slice_bitcast_fusion.5
  130.8 1.5 collective-permute-start.27
  132.3 1.1 slice.295
  133.5 1.5 pad_maximum_fusion.1
  135.6 1.3 collective-permute-start.32
  136.9 10.0 %collective-permute-done.27.sent_ref = bf16[480,640]{1,0:T(8,128)(2,1)} collective-permute-done((bf16[480,640]{1,0:T(8,128)(2,1)}, bf16[480,640]{1,0:T(8,128)(2,1)}, u32[]{:S(2)}, u32[]{:S(2)}) %collective-permute-start.27) | collective-permute-done | bytes 614432 | tf_op jit(solution)/shard_map/ppermute | solution.py:242
  147.0 7.8 %shard_map.71 = (bf16[5760,256]{1,0:T(8,128)(2,1)S(1)}, bf16[5760,128]{1,0:T(8,128)(2,1)S(1)}, bf16[960,640]{1,0:T(8,128)(2,1)S(1)}) custom-call(bf16[480,640]{1,0:T(8,128)(2,1)S(1)} %copy-done.16, f32[5,640]{1,0:T(8,128)S(1)} %pad_maximum_fusion.8.embedding_ref, bf16[480,640]{1,0:T(8,128)(2,1)S(1)} %bitcast.328, ...), custom_call_target="tpu_custom_call" | custom-call | flops 8847360000 | bytes 7372800 | tf_op jit(solution)/shard_map/pallas_call | solution.py:717
  158.9 1.4 collective-permute-start.35
  160.5 4.5 %collective-permute-start.38 = (bf16[360,256]{1,0:T(8,128)(2,1)S(1)}, bf16[360,256]{1,0:T(8,128)(2,1)S(1)}, u32[]{:S(2)}, u32[]{:S(2)}) collective-permute-start(bf16[360,256]{1,0:T(8,128)(2,1)S(1)} %get-tuple-element.105), channel_id=1, source_target_pairs={{0,4},{1,5},{2,6},{3,7},{4,8},{5,9},{6,10},{7,11},{8,12},{9,13},{1... | collective-permute-start | bytes 552968 | tf_op jit(solution)/shard_map/ppermute | solution.py:238
  165.0 4.5 %collective-permute-start.39 = (bf16[360,256]{1,0:T(8,128)(2,1)S(1)}, bf16[360,256]{1,0:T(8,128)(2,1)S(1)}, u32[]{:S(2)}, u32[]{:S(2)}) collective-permute-start(bf16[360,256]{1,0:T(8,128)(2,1)S(1)} %get-tuple-element.104), channel_id=1, source_target_pairs={{0,8},{1,9},{2,10},{3,11},{4,12},{5,13},{6,14},{7,15},{8,0},{9,1},... | collective-permute-start | bytes 552968 | tf_op jit(solution)/shard_map/ppermute | solution.py:238
  169.5 5.2 %collective-permute-start.40 = (bf16[360,256]{1,0:T(8,128)(2,1)S(1)}, bf16[360,256]{1,0:T(8,128)(2,1)S(1)}, u32[]{:S(2)}, u32[]{:S(2)}) collective-permute-start(bf16[360,256]{1,0:T(8,128)(2,1)S(1)} %get-tuple-element.103), channel_id=1, source_target_pairs={{0,12},{1,13},{2,14},{3,15},{4,0},{5,1},{6,2},{7,3},{8,4},{9,5},{1... | collective-permute-start | bytes 552968 | tf_op jit(solution)/shard_map/ppermute | solution.py:238
  175.5 1.6 collective-permute-start.36
  177.5 7.5 %collective-permute-done.36 = bf16[4,360,128]{2,1,0:T(8,128)(2,1)S(1)} collective-permute-done((bf16[4,360,128]{2,1,0:T(8,128)(2,1)S(1)}, bf16[4,360,128]{2,1,0:T(8,128)(2,1)S(1)}, u32[]{:S(2)}, u32[]{:S(2)}) %collective-permute-start.36) | collective-permute-done | bytes 368672 | tf_op jit(solution)/shard_map/ppermute | solution.py:238
  185.0 1.5 collective-permute-start.37
  186.6 5.0 %collective-permute-start.43 = (bf16[360,128]{1,0:T(8,128)(2,1)S(1)}, bf16[360,128]{1,0:T(8,128)(2,1)S(1)}, u32[]{:S(2)}, u32[]{:S(2)}) collective-permute-start(bf16[360,128]{1,0:T(8,128)(2,1)S(1)} %get-tuple-element.135), channel_id=1, source_target_pairs={{0,12},{1,13},{2,14},{3,15},{4,0},{5,1},{6,2},{7,3},{8,4},{9,5},{1... | collective-permute-start | bytes 276488 | tf_op jit(solution)/shard_map/ppermute | solution.py:238
  192.7 1.0 collective-permute-done.37
  193.7 1.5 collective-permute-start.48
  195.2 3.1 %collective-permute-done.42 = bf16[360,128]{1,0:T(8,128)(2,1)S(1)} collective-permute-done((bf16[360,128]{1,0:T(8,128)(2,1)S(1)}, bf16[360,128]{1,0:T(8,128)(2,1)S(1)}, u32[]{:S(2)}, u32[]{:S(2)}) %collective-permute-start.42) | collective-permute-done | bytes 92192 | tf_op jit(solution)/shard_map/ppermute | solution.py:238
  198.7 1.9 collective-permute-start.46
  200.6 1.9 collective-permute-start.44
  202.5 5.0 %collective-permute-done.48 = bf16[4,128,640]{2,1,0:T(8,128)(2,1)S(1)} collective-permute-done((bf16[4,128,640]{2,1,0:T(8,128)(2,1)S(1)}, bf16[4,128,640]{2,1,0:T(8,128)(2,1)S(1)}, u32[]{:S(2)}, u32[]{:S(2)}) %collective-permute-start.48) | collective-permute-done | bytes 655392 | tf_op jit(solution)/shard_map/ppermute | solution.py:238
  207.7 6.0 %collective-permute-start.52 = (bf16[128,640]{1,0:T(8,128)(2,1)S(1)}, bf16[128,640]{1,0:T(8,128)(2,1)S(1)}, u32[]{:S(2)}, u32[]{:S(2)}) collective-permute-start(bf16[128,640]{1,0:T(8,128)(2,1)S(1)} %get-tuple-element.125), channel_id=1, source_target_pairs={{0,12},{1,13},{2,14},{3,15},{4,0},{5,1},{6,2},{7,3},{8,4},{9,5},{1... | collective-permute-start | bytes 491528 | tf_op jit(solution)/shard_map/ppermute | solution.py:238
  213.7 1.1 collective-permute-start.50
  214.8 10.1 %collective-permute-done.45 = bf16[360,256]{1,0:T(8,128)(2,1)S(1)} collective-permute-done((bf16[360,256]{1,0:T(8,128)(2,1)S(1)}, bf16[360,256]{1,0:T(8,128)(2,1)S(1)}, u32[]{:S(2)}, u32[]{:S(2)}) %collective-permute-start.45) | collective-permute-done | bytes 184352 | tf_op jit(solution)/shard_map/ppermute | solution.py:238
  225.1 1.6 collective-permute-start.49
  226.7 2.9 %collective-permute-done.51 = bf16[128,640]{1,0:T(8,128)(2,1)S(1)} collective-permute-done((bf16[128,640]{1,0:T(8,128)(2,1)S(1)}, bf16[128,640]{1,0:T(8,128)(2,1)S(1)}, u32[]{:S(2)}, u32[]{:S(2)}) %collective-permute-start.51) | collective-permute-done | bytes 163872 | tf_op jit(solution)/shard_map/ppermute | solution.py:238
  229.8 1.6 collective-permute-start.53
  231.4 1.2 collective-permute-done.49
  232.8 2.1 fusion.3
  (204 shorter events, 29.6 us)
Async XLA Ops:
  0.6 4.8 %copy-start = (bf16[1,360,640]{2,1,0:T(8,128)(2,1)S(1)}, bf16[1,360,640]{2,1,0:T(8,128)(2,1)}, u32[]{:S(2)}) copy-start(bf16[1,360,640]{2,1,0:T(8,128)(2,1)} %param.8) | copy-start | bytes 1382404
  2.4 5.4 %collective-permute-start = (bf16[64,640]{1,0:T(8,128)(2,1)S(1)}, bf16[64,640]{1,0:T(8,128)(2,1)S(1)}, u32[]{:S(2)}, u32[]{:S(2)}) collective-permute-start(bf16[64,640]{1,0:T(8,128)(2,1)S(1)} %fusion.43), channel_id=1, source_target_pairs={{0,16},{16,0},{1,17},{17,1},{2,18},{18,2},{3,19},{19,3},{4,20},{20... | collective-permute-start | bytes 245768 | tf_op jit(solution)/shard_map/ppermute | solution.py:242
  5.5 7.6 %copy-start.21 = (s32[5]{0:T(128)S(1)}, s32[5]{0:T(128)}, u32[]{:S(2)}) copy-start(s32[5]{0:T(128)} %param.6) | copy-start | bytes 64
  7.0 18.2 %collective-permute-start.6 = (bf16[360,384]{1,0:T(8,128)(2,1)}, bf16[360,384]{1,0:T(8,128)(2,1)S(1)}, u32[]{:S(2)}, u32[]{:S(2)}) collective-permute-start(bf16[360,384]{1,0:T(8,128)(2,1)} %slice.278), channel_id=1, source_target_pairs={{0,16},{16,0},{1,17},{17,1},{2,18},{18,2},{3,19},{19,3},{4,20},{20... | collective-permute-start | bytes 829448 | tf_op jit(solution)/shard_map/ppermute | solution.py:242
  7.9 12.7 %collective-permute-start.2 = (bf16[128,640]{1,0:T(8,128)(2,1)S(1)}, bf16[128,640]{1,0:T(8,128)(2,1)S(1)}, u32[]{:S(2)}, u32[]{:S(2)}) collective-permute-start(bf16[128,640]{1,0:T(8,128)(2,1)S(1)} %maximum_select_fusion.16), channel_id=1, source_target_pairs={{0,8},{1,9},{2,10},{3,11},{4,12},{5,13},{6,14},{7,15},{8,0},{9,1},... | collective-permute-start | bytes 491528 | tf_op jit(solution)/shard_map/ppermute | solution.py:238
  11.1 9.6 %collective-permute-start.3 = (bf16[128,640]{1,0:T(8,128)(2,1)S(1)}, bf16[128,640]{1,0:T(8,128)(2,1)S(1)}, u32[]{:S(2)}, u32[]{:S(2)}) collective-permute-start(bf16[128,640]{1,0:T(8,128)(2,1)S(1)} %maximum_select_fusion.16), channel_id=1, source_target_pairs={{0,12},{1,13},{2,14},{3,15},{4,0},{5,1},{6,2},{7,3},{8,4},{9,5},{1... | collective-permute-start | bytes 491528 | tf_op jit(solution)/shard_map/ppermute | solution.py:238
  12.4 10.0 %collective-permute-start.1 = (bf16[128,640]{1,0:T(8,128)(2,1)S(1)}, bf16[128,640]{1,0:T(8,128)(2,1)S(1)}, u32[]{:S(2)}, u32[]{:S(2)}) collective-permute-start(bf16[128,640]{1,0:T(8,128)(2,1)S(1)} %maximum_select_fusion.16), channel_id=1, source_target_pairs={{0,4},{1,5},{2,6},{3,7},{4,8},{5,9},{6,10},{7,11},{8,12},{9,13},{1... | collective-permute-start | bytes 491528 | tf_op jit(solution)/shard_map/ppermute | solution.py:238
  23.5 17.2 %collective-permute-start.4 = (bf16[4,128,640]{2,1,0:T(8,128)(2,1)}, bf16[4,128,640]{2,1,0:T(8,128)(2,1)S(1)}, u32[]{:S(2)}, u32[]{:S(2)}) collective-permute-start(bf16[4,128,640]{2,1,0:T(8,128)(2,1)} %get-tuple-element.129), channel_id=1, source_target_pairs={{0,2},{1,3},{2,0},{3,1},{4,6},{5,7},{6,4},{7,5},{8,10},{9,11},{10,... | collective-permute-start | bytes 1966088 | tf_op jit(solution)/shard_map/ppermute | solution.py:238
  25.2 8.1 %collective-permute-start.7 = (bf16[360,256]{1,0:T(8,128)(2,1)S(1)}, bf16[360,256]{1,0:T(8,128)(2,1)S(1)}, u32[]{:S(2)}, u32[]{:S(2)}) collective-permute-start(bf16[360,256]{1,0:T(8,128)(2,1)S(1)} %get-tuple-element.37), channel_id=1, source_target_pairs={{0,4},{1,5},{2,6},{3,7},{4,8},{5,9},{6,10},{7,11},{8,12},{9,13},{1... | collective-permute-start | bytes 552968 | tf_op jit(solution)/shard_map/ppermute | solution.py:238
  28.3 12.5 %collective-permute-start.8 = (bf16[360,256]{1,0:T(8,128)(2,1)S(1)}, bf16[360,256]{1,0:T(8,128)(2,1)}, u32[]{:S(2)}, u32[]{:S(2)}) collective-permute-start(bf16[360,256]{1,0:T(8,128)(2,1)S(1)} %get-tuple-element.37), channel_id=1, source_target_pairs={{0,8},{1,9},{2,10},{3,11},{4,12},{5,13},{6,14},{7,15},{8,0},{9,1},... | collective-permute-start | bytes 552968 | tf_op jit(solution)/shard_map/ppermute | solution.py:238
  30.3 10.5 %collective-permute-start.9 = (bf16[360,256]{1,0:T(8,128)(2,1)S(1)}, bf16[360,256]{1,0:T(8,128)(2,1)}, u32[]{:S(2)}, u32[]{:S(2)}) collective-permute-start(bf16[360,256]{1,0:T(8,128)(2,1)S(1)} %get-tuple-element.37), channel_id=1, source_target_pairs={{0,12},{1,13},{2,14},{3,15},{4,0},{5,1},{6,2},{7,3},{8,4},{9,5},{1... | collective-permute-start | bytes 552968 | tf_op jit(solution)/shard_map/ppermute | solution.py:238
  42.1 10.5 %collective-permute-start.10 = (bf16[4,360,128]{2,1,0:T(8,128)(2,1)S(1)}, bf16[4,360,128]{2,1,0:T(8,128)(2,1)S(1)}, u32[]{:S(2)}, u32[]{:S(2)}) collective-permute-start(bf16[4,360,128]{2,1,0:T(8,128)(2,1)S(1)} %get-tuple-element.119), channel_id=1, source_target_pairs={{0,2},{1,3},{2,0},{3,1},{4,6},{5,7},{6,4},{7,5},{8,10},{9,11},{10,... | collective-permute-start | bytes 1105928 | tf_op jit(solution)/shard_map/ppermute | solution.py:238
  43.3 40.1 %collective-permute-start.5 = (bf16[4,2,128,640]{3,2,1,0:T(8,128)(2,1)S(1)}, bf16[4,2,128,640]{3,2,1,0:T(8,128)(2,1)S(1)}, u32[]{:S(2)}, u32[]{:S(2)}) collective-permute-start(bf16[4,2,128,640]{3,2,1,0:T(8,128)(2,1)S(1)} %maximum_select_fusion.8), channel_id=1, source_target_pairs={{0,1},{1,0},{2,3},{3,2},{4,5},{5,4},{6,7},{7,6},{8,9},{9,8},{10,11... | collective-permute-start | bytes 3932168 | tf_op jit(solution)/shard_map/ppermute | solution.py:238
  52.6 10.4 %collective-permute-start.12 = (bf16[360,128]{1,0:T(8,128)(2,1)S(1)}, bf16[360,128]{1,0:T(8,128)(2,1)S(1)}, u32[]{:S(2)}, u32[]{:S(2)}) collective-permute-start(bf16[360,128]{1,0:T(8,128)(2,1)S(1)} %slice_select_fusion.2), channel_id=1, source_target_pairs={{0,4},{1,5},{2,6},{3,7},{4,8},{5,9},{6,10},{7,11},{8,12},{9,13},{1... | collective-permute-start | bytes 276488 | tf_op jit(solution)/shard_map/ppermute | solution.py:238
  57.2 8.8 %collective-permute-start.13 = (bf16[360,128]{1,0:T(8,128)(2,1)S(1)}, bf16[360,128]{1,0:T(8,128)(2,1)S(1)}, u32[]{:S(2)}, u32[]{:S(2)}) collective-permute-start(bf16[360,128]{1,0:T(8,128)(2,1)S(1)} %slice_select_fusion.2), channel_id=1, source_target_pairs={{0,8},{1,9},{2,10},{3,11},{4,12},{5,13},{6,14},{7,15},{8,0},{9,1},... | collective-permute-start | bytes 276488 | tf_op jit(solution)/shard_map/ppermute | solution.py:238
  60.7 5.4 %collective-permute-start.14 = (bf16[360,128]{1,0:T(8,128)(2,1)S(1)}, bf16[360,128]{1,0:T(8,128)(2,1)S(1)}, u32[]{:S(2)}, u32[]{:S(2)}) collective-permute-start(bf16[360,128]{1,0:T(8,128)(2,1)S(1)} %slice_select_fusion.2), channel_id=1, source_target_pairs={{0,12},{1,13},{2,14},{3,15},{4,0},{5,1},{6,2},{7,3},{8,4},{9,5},{1... | collective-permute-start | bytes 276488 | tf_op jit(solution)/shard_map/ppermute | solution.py:238
  60.7 20.6 %collective-permute-start.11 = (bf16[4,360,128]{2,1,0:T(8,128)(2,1)S(1)}, bf16[4,360,128]{2,1,0:T(8,128)(2,1)S(1)}, u32[]{:S(2)}, u32[]{:S(2)}) collective-permute-start(bf16[4,360,128]{2,1,0:T(8,128)(2,1)S(1)} %get-tuple-element.41), channel_id=1, source_target_pairs={{0,2},{1,3},{2,0},{3,1},{4,6},{5,7},{6,4},{7,5},{8,10},{9,11},{10,... | collective-permute-start | bytes 1105928 | tf_op jit(solution)/shard_map/ppermute | solution.py:238
  66.1 9.4 %collective-permute-start.15 = (bf16[360,256]{1,0:T(8,128)(2,1)S(1)}, bf16[360,256]{1,0:T(8,128)(2,1)S(1)}, u32[]{:S(2)}, u32[]{:S(2)}) collective-permute-start(bf16[360,256]{1,0:T(8,128)(2,1)S(1)} %get-tuple-element.43), channel_id=1, source_target_pairs={{0,4},{1,5},{2,6},{3,7},{4,8},{5,9},{6,10},{7,11},{8,12},{9,13},{1... | collective-permute-start | bytes 552968 | tf_op jit(solution)/shard_map/ppermute | solution.py:238
  67.4 12.3 %collective-permute-start.16 = (bf16[360,256]{1,0:T(8,128)(2,1)S(1)}, bf16[360,256]{1,0:T(8,128)(2,1)S(1)}, u32[]{:S(2)}, u32[]{:S(2)}) collective-permute-start(bf16[360,256]{1,0:T(8,128)(2,1)S(1)} %get-tuple-element.43), channel_id=1, source_target_pairs={{0,8},{1,9},{2,10},{3,11},{4,12},{5,13},{6,14},{7,15},{8,0},{9,1},... | collective-permute-start | bytes 552968 | tf_op jit(solution)/shard_map/ppermute | solution.py:238
  69.1 10.6 %collective-permute-start.17 = (bf16[360,256]{1,0:T(8,128)(2,1)S(1)}, bf16[360,256]{1,0:T(8,128)(2,1)S(1)}, u32[]{:S(2)}, u32[]{:S(2)}) collective-permute-start(bf16[360,256]{1,0:T(8,128)(2,1)S(1)} %get-tuple-element.43), channel_id=1, source_target_pairs={{0,12},{1,13},{2,14},{3,15},{4,0},{5,1},{6,2},{7,3},{8,4},{9,5},{1... | collective-permute-start | bytes 552968 | tf_op jit(solution)/shard_map/ppermute | solution.py:238
  75.5 7.5 %collective-permute-start.19 = (bf16[4,360,128]{2,1,0:T(8,128)(2,1)S(1)}, bf16[4,360,128]{2,1,0:T(8,128)(2,1)S(1)}, u32[]{:S(2)}, u32[]{:S(2)}) collective-permute-start(bf16[4,360,128]{2,1,0:T(8,128)(2,1)S(1)} %get-tuple-element.139), channel_id=1, source_target_pairs={{0,2},{1,3},{2,0},{3,1},{4,6},{5,7},{6,4},{7,5},{8,10},{9,11},{10,... | collective-permute-start | bytes 1105928 | tf_op jit(solution)/shard_map/ppermute | solution.py:238
  80.8 18.3 %collective-permute-start.22 = (bf16[4,360,256]{2,1,0:T(8,128)(2,1)S(1)}, bf16[4,360,256]{2,1,0:T(8,128)(2,1)S(1)}, u32[]{:S(2)}, u32[]{:S(2)}) collective-permute-start(bf16[4,360,256]{2,1,0:T(8,128)(2,1)S(1)} %get-tuple-element.108), channel_id=1, source_target_pairs={{0,2},{1,3},{2,0},{3,1},{4,6},{5,7},{6,4},{7,5},{8,10},{9,11},{10,... | collective-permute-start | bytes 2211848 | tf_op jit(solution)/shard_map/ppermute | solution.py:238
  81.7 4.7 %collective-permute-start.18 = (bf16[4,2,360,256]{3,2,0,1:T(8,128)(2,1)S(1)}, bf16[4,2,360,256]{3,2,0,1:T(8,128)(2,1)S(1)}, u32[]{:S(2)}, u32[]{:S(2)}) collective-permute-start(bf16[4,2,360,256]{3,2,0,1:T(8,128)(2,1)S(1)} %maximum_select_fusion.3), channel_id=1, source_target_pairs={{0,1},{1,0},{2,3},{3,2},{4,5},{5,4},{6,7},{7,6},{8,9},{9,8},{10,11... | collective-permute-start | bytes 4423688 | tf_op jit(solution)/shard_map/ppermute | solution.py:238
  83.2 2.9 %collective-permute-start.20 = (bf16[4,2,360,128]{3,2,0,1:T(8,128)(2,1)S(1)}, bf16[4,2,360,128]{3,2,0,1:T(8,128)(2,1)S(1)}, u32[]{:S(2)}, u32[]{:S(2)}) collective-permute-start(bf16[4,2,360,128]{3,2,0,1:T(8,128)(2,1)S(1)} %maximum_select_fusion.14), channel_id=1, source_target_pairs={{0,1},{1,0},{2,3},{3,2},{4,5},{5,4},{6,7},{7,6},{8,9},{9,8},{10,11... | collective-permute-start | bytes 2211848 | tf_op jit(solution)/shard_map/ppermute | solution.py:238
  94.3 5.1 %copy-start.11 = (f32[480,384]{1,0:T(8,128)}, f32[480,384]{1,0:T(8,128)S(1)}, u32[]{:S(2)}) copy-start(f32[480,384]{1,0:T(8,128)S(1)} %get-tuple-element.57.preact_ref) | copy-start | bytes 2211844
  94.3 5.1 %copy-start.13 = (bf16[480,640]{1,0:T(8,128)(2,1)}, bf16[480,640]{1,0:T(8,128)(2,1)S(1)}, u32[]{:S(2)}) copy-start(bf16[480,640]{1,0:T(8,128)(2,1)S(1)} %get-tuple-element.56.normed_ref) | copy-start | bytes 1843204
  94.3 16.3 %collective-permute-start.21 = (bf16[480,640]{1,0:T(8,128)(2,1)S(1)}, bf16[480,640]{1,0:T(8,128)(2,1)}, u32[]{:S(2)}, u32[]{:S(2)}) collective-permute-start(bf16[480,640]{1,0:T(8,128)(2,1)S(1)} %get-tuple-element.46.own_ref), channel_id=1, source_target_pairs={{0,16},{16,0},{1,17},{17,1},{2,18},{18,2},{3,19},{19,3},{4,20},{20... | collective-permute-start | bytes 1843208 | tf_op jit(solution)/shard_map/ppermute | solution.py:242
  101.1 5.3 %collective-permute-start.26 = (bf16[2,360,256]{2,1,0:T(8,128)(2,1)}, bf16[2,360,256]{2,1,0:T(8,128)(2,1)S(1)}, u32[]{:S(2)}, u32[]{:S(2)}) collective-permute-start(bf16[2,360,256]{2,1,0:T(8,128)(2,1)} %get-tuple-element.88), channel_id=1, source_target_pairs={{0,1},{1,0},{2,3},{3,2},{4,5},{5,4},{6,7},{7,6},{8,9},{9,8},{10,11... | collective-permute-start | bytes 1105928 | tf_op jit(solution)/shard_map/ppermute | solution.py:238
  101.1 5.3 %collective-permute-start.25 = (bf16[2,360,256]{2,1,0:T(8,128)(2,1)}, bf16[2,360,256]{2,1,0:T(8,128)(2,1)}, u32[]{:S(2)}, u32[]{:S(2)}) collective-permute-start(bf16[2,360,256]{2,1,0:T(8,128)(2,1)} %get-tuple-element.89), channel_id=1, source_target_pairs={{0,1},{1,0},{2,3},{3,2},{4,5},{5,4},{6,7},{7,6},{8,9},{9,8},{10,11... | collective-permute-start | bytes 1105928 | tf_op jit(solution)/shard_map/ppermute | solution.py:238
  101.6 4.8 %collective-permute-start.24 = (bf16[2,360,256]{2,1,0:T(8,128)(2,1)}, bf16[2,360,256]{2,1,0:T(8,128)(2,1)}, u32[]{:S(2)}, u32[]{:S(2)}) collective-permute-start(bf16[2,360,256]{2,1,0:T(8,128)(2,1)} %get-tuple-element.87), channel_id=1, source_target_pairs={{0,1},{1,0},{2,3},{3,2},{4,5},{5,4},{6,7},{7,6},{8,9},{9,8},{10,11... | collective-permute-start | bytes 1105928 | tf_op jit(solution)/shard_map/ppermute | solution.py:238
  101.6 4.8 %collective-permute-start.23 = (bf16[2,360,256]{2,1,0:T(8,128)(2,1)S(1)}, bf16[2,360,256]{2,1,0:T(8,128)(2,1)}, u32[]{:S(2)}, u32[]{:S(2)}) collective-permute-start(bf16[2,360,256]{2,1,0:T(8,128)(2,1)S(1)} %get-tuple-element.86), channel_id=1, source_target_pairs={{0,1},{1,0},{2,3},{3,2},{4,5},{5,4},{6,7},{7,6},{8,9},{9,8},{10,11... | collective-permute-start | bytes 1105928 | tf_op jit(solution)/shard_map/ppermute | solution.py:238
  129.3 4.1 %collective-permute-start.31 = (bf16[2,360,256]{2,1,0:T(8,128)(2,1)}, bf16[2,360,256]{2,1,0:T(8,128)(2,1)}, u32[]{:S(2)}, u32[]{:S(2)}) collective-permute-start(bf16[2,360,256]{2,1,0:T(8,128)(2,1)} %get-tuple-element.77), channel_id=1, source_target_pairs={{0,1},{1,0},{2,3},{3,2},{4,5},{5,4},{6,7},{7,6},{8,9},{9,8},{10,11... | collective-permute-start | bytes 1105928 | tf_op jit(solution)/shard_map/ppermute | solution.py:238
  129.8 3.7 %collective-permute-start.30 = (bf16[2,360,256]{2,1,0:T(8,128)(2,1)}, bf16[2,360,256]{2,1,0:T(8,128)(2,1)}, u32[]{:S(2)}, u32[]{:S(2)}) collective-permute-start(bf16[2,360,256]{2,1,0:T(8,128)(2,1)} %get-tuple-element.75), channel_id=1, source_target_pairs={{0,1},{1,0},{2,3},{3,2},{4,5},{5,4},{6,7},{7,6},{8,9},{9,8},{10,11... | collective-permute-start | bytes 1105928 | tf_op jit(solution)/shard_map/ppermute | solution.py:238
  130.3 3.2 %collective-permute-start.29 = (bf16[2,360,256]{2,1,0:T(8,128)(2,1)}, bf16[2,360,256]{2,1,0:T(8,128)(2,1)}, u32[]{:S(2)}, u32[]{:S(2)}) collective-permute-start(bf16[2,360,256]{2,1,0:T(8,128)(2,1)} %get-tuple-element.76), channel_id=1, source_target_pairs={{0,1},{1,0},{2,3},{3,2},{4,5},{5,4},{6,7},{7,6},{8,9},{9,8},{10,11... | collective-permute-start | bytes 1105928 | tf_op jit(solution)/shard_map/ppermute | solution.py:238
  130.3 3.1 %collective-permute-start.28 = (bf16[2,360,256]{2,1,0:T(8,128)(2,1)S(1)}, bf16[2,360,256]{2,1,0:T(8,128)(2,1)}, u32[]{:S(2)}, u32[]{:S(2)}) collective-permute-start(bf16[2,360,256]{2,1,0:T(8,128)(2,1)S(1)} %get-tuple-element.74), channel_id=1, source_target_pairs={{0,1},{1,0},{2,3},{3,2},{4,5},{5,4},{6,7},{7,6},{8,9},{9,8},{10,11... | collective-permute-start | bytes 1105928 | tf_op jit(solution)/shard_map/ppermute | solution.py:238
  130.8 16.2 %collective-permute-start.27 = (bf16[480,640]{1,0:T(8,128)(2,1)}, bf16[480,640]{1,0:T(8,128)(2,1)}, u32[]{:S(2)}, u32[]{:S(2)}) collective-permute-start(bf16[480,640]{1,0:T(8,128)(2,1)} %get-tuple-element.50.own_ref), channel_id=1, source_target_pairs={{0,16},{16,0},{1,17},{17,1},{2,18},{18,2},{3,19},{19,3},{4,20},{20... | collective-permute-start | bytes 1843208 | tf_op jit(solution)/shard_map/ppermute | solution.py:242
  135.0 11.9 %copy-start.10 = (bf16[5,3,32,640]{3,2,1,0:T(8,128)(2,1)S(1)}, bf16[5,3,32,640]{3,2,1,0:T(8,128)(2,1)}, u32[]{:S(2)}) copy-start(bf16[5,3,32,640]{3,2,1,0:T(8,128)(2,1)} %param.7) | copy-start | bytes 1843204
  135.0 11.9 %copy-start.12 = (f32[480,384]{1,0:T(8,128)S(1)}, f32[480,384]{1,0:T(8,128)}, u32[]{:S(2)}) copy-start(f32[480,384]{1,0:T(8,128)} %copy-done.11) | copy-start | bytes 2211844
  135.0 11.9 %copy-start.14 = (bf16[480,640]{1,0:T(8,128)(2,1)S(1)}, bf16[480,640]{1,0:T(8,128)(2,1)}, u32[]{:S(2)}) copy-start(bf16[480,640]{1,0:T(8,128)(2,1)} %copy-done.13) | copy-start | bytes 1843204
  135.0 11.9 %copy-start.16 = (bf16[480,640]{1,0:T(8,128)(2,1)S(1)}, bf16[480,640]{1,0:T(8,128)(2,1)}, u32[]{:S(2)}) copy-start(bf16[480,640]{1,0:T(8,128)(2,1)} %copy-done.15) | copy-start | bytes 1843204
  135.5 11.4 %copy-start.7 = (bf16[8,120,640]{2,1,0:T(8,128)(2,1)S(1)}, bf16[8,120,640]{2,1,0:T(8,128)(2,1)}, u32[]{:S(2)}) copy-start(bf16[8,120,640]{2,1,0:T(8,128)(2,1)} %copy-done.6) | copy-start | bytes 3686404
  135.6 19.9 %collective-permute-start.32 = (bf16[4,360,256]{2,1,0:T(8,128)(2,1)S(1)}, bf16[4,360,256]{2,1,0:T(8,128)(2,1)S(1)}, u32[]{:S(2)}, u32[]{:S(2)}) collective-permute-start(bf16[4,360,256]{2,1,0:T(8,128)(2,1)S(1)} %dynamic-slice_bitcast_fusion), channel_id=1, source_target_pairs={{0,2},{1,3},{2,0},{3,1},{4,6},{5,7},{6,4},{7,5},{8,10},{9,11},{10,... | collective-permute-start | bytes 2211848 | tf_op jit(solution)/shard_map/ppermute | solution.py:238
  146.9 7.8 %copy-start.5 = (bf16[5760,128]{1,0:T(8,128)(2,1)S(1)}, bf16[5760,128]{1,0:T(8,128)(2,1)}, u32[]{:S(2)}) copy-start(bf16[5760,128]{1,0:T(8,128)(2,1)} %copy-done.4) | copy-start | bytes 4423684
  155.4 3.2 %collective-permute-start.34 = (bf16[4,2,360,128]{3,2,0,1:T(8,128)(2,1)S(1)}, bf16[4,2,360,128]{3,2,0,1:T(8,128)(2,1)S(1)}, u32[]{:S(2)}, u32[]{:S(2)}) collective-permute-start(bf16[4,2,360,128]{3,2,0,1:T(8,128)(2,1)S(1)} %bitcast.353), channel_id=1, source_target_pairs={{0,1},{1,0},{2,3},{3,2},{4,5},{5,4},{6,7},{7,6},{8,9},{9,8},{10,11... | collective-permute-start | bytes 2211848 | tf_op jit(solution)/shard_map/ppermute | solution.py:238
  155.8 18.9 %collective-permute-start.33 = (bf16[4,2,360,256]{3,2,0,1:T(8,128)(2,1)S(1)}, bf16[4,2,360,256]{3,2,0,1:T(8,128)(2,1)S(1)}, u32[]{:S(2)}, u32[]{:S(2)}) collective-permute-start(bf16[4,2,360,256]{3,2,0,1:T(8,128)(2,1)S(1)} %bitcast.348), channel_id=1, source_target_pairs={{0,1},{1,0},{2,3},{3,2},{4,5},{5,4},{6,7},{7,6},{8,9},{9,8},{10,11... | collective-permute-start | bytes 4423688 | tf_op jit(solution)/shard_map/ppermute | solution.py:238
  158.1 19.0 %collective-permute-start.47 = (bf16[4,2,128,640]{3,2,1,0:T(8,128)(2,1)S(1)}, bf16[4,2,128,640]{3,2,1,0:T(8,128)(2,1)S(1)}, u32[]{:S(2)}, u32[]{:S(2)}) collective-permute-start(bf16[4,2,128,640]{3,2,1,0:T(8,128)(2,1)S(1)} %fusion.8), channel_id=1, source_target_pairs={{0,1},{1,0},{2,3},{3,2},{4,5},{5,4},{6,7},{7,6},{8,9},{9,8},{10,11... | collective-permute-start | bytes 3932168 | tf_op jit(solution)/shard_map/ppermute | solution.py:238
  158.9 10.6 %collective-permute-start.35 = (bf16[4,360,128]{2,1,0:T(8,128)(2,1)S(1)}, bf16[4,360,128]{2,1,0:T(8,128)(2,1)S(1)}, u32[]{:S(2)}, u32[]{:S(2)}) collective-permute-start(bf16[4,360,128]{2,1,0:T(8,128)(2,1)S(1)} %dynamic-slice_bitcast_fusion.7), channel_id=1, source_target_pairs={{0,2},{1,3},{2,0},{3,1},{4,6},{5,7},{6,4},{7,5},{8,10},{9,11},{10,... | collective-permute-start | bytes 1105928 | tf_op jit(solution)/shard_map/ppermute | solution.py:238
  160.5 26.0 %collective-permute-start.38 = (bf16[360,256]{1,0:T(8,128)(2,1)S(1)}, bf16[360,256]{1,0:T(8,128)(2,1)S(1)}, u32[]{:S(2)}, u32[]{:S(2)}) collective-permute-start(bf16[360,256]{1,0:T(8,128)(2,1)S(1)} %get-tuple-element.105), channel_id=1, source_target_pairs={{0,4},{1,5},{2,6},{3,7},{4,8},{5,9},{6,10},{7,11},{8,12},{9,13},{1... | collective-permute-start | bytes 552968 | tf_op jit(solution)/shard_map/ppermute | solution.py:238
  165.0 21.6 %collective-permute-start.39 = (bf16[360,256]{1,0:T(8,128)(2,1)S(1)}, bf16[360,256]{1,0:T(8,128)(2,1)S(1)}, u32[]{:S(2)}, u32[]{:S(2)}) collective-permute-start(bf16[360,256]{1,0:T(8,128)(2,1)S(1)} %get-tuple-element.104), channel_id=1, source_target_pairs={{0,8},{1,9},{2,10},{3,11},{4,12},{5,13},{6,14},{7,15},{8,0},{9,1},... | collective-permute-start | bytes 552968 | tf_op jit(solution)/shard_map/ppermute | solution.py:238
  169.5 17.1 %collective-permute-start.40 = (bf16[360,256]{1,0:T(8,128)(2,1)S(1)}, bf16[360,256]{1,0:T(8,128)(2,1)S(1)}, u32[]{:S(2)}, u32[]{:S(2)}) collective-permute-start(bf16[360,256]{1,0:T(8,128)(2,1)S(1)} %get-tuple-element.103), channel_id=1, source_target_pairs={{0,12},{1,13},{2,14},{3,15},{4,0},{5,1},{6,2},{7,3},{8,4},{9,5},{1... | collective-permute-start | bytes 552968 | tf_op jit(solution)/shard_map/ppermute | solution.py:238
  175.5 9.5 %collective-permute-start.36 = (bf16[4,360,128]{2,1,0:T(8,128)(2,1)S(1)}, bf16[4,360,128]{2,1,0:T(8,128)(2,1)S(1)}, u32[]{:S(2)}, u32[]{:S(2)}) collective-permute-start(bf16[4,360,128]{2,1,0:T(8,128)(2,1)S(1)} %dynamic-slice_bitcast_fusion.8), channel_id=1, source_target_pairs={{0,2},{1,3},{2,0},{3,1},{4,6},{5,7},{6,4},{7,5},{8,10},{9,11},{10,... | collective-permute-start | bytes 1105928 | tf_op jit(solution)/shard_map/ppermute | solution.py:238
  185.0 8.8 %collective-permute-start.37 = (bf16[4,360,128]{2,1,0:T(8,128)(2,1)S(1)}, bf16[4,360,128]{2,1,0:T(8,128)(2,1)S(1)}, u32[]{:S(2)}, u32[]{:S(2)}) collective-permute-start(bf16[4,360,128]{2,1,0:T(8,128)(2,1)S(1)} %dynamic-slice_bitcast_fusion.6), channel_id=1, source_target_pairs={{0,2},{1,3},{2,0},{3,1},{4,6},{5,7},{6,4},{7,5},{8,10},{9,11},{10,... | collective-permute-start | bytes 1105928 | tf_op jit(solution)/shard_map/ppermute | solution.py:238
  186.6 8.6 %collective-permute-start.43 = (bf16[360,128]{1,0:T(8,128)(2,1)S(1)}, bf16[360,128]{1,0:T(8,128)(2,1)S(1)}, u32[]{:S(2)}, u32[]{:S(2)}) collective-permute-start(bf16[360,128]{1,0:T(8,128)(2,1)S(1)} %get-tuple-element.135), channel_id=1, source_target_pairs={{0,12},{1,13},{2,14},{3,15},{4,0},{5,1},{6,2},{7,3},{8,4},{9,5},{1... | collective-permute-start | bytes 276488 | tf_op jit(solution)/shard_map/ppermute | solution.py:238
  191.6 6.8 %collective-permute-start.42 = (bf16[360,128]{1,0:T(8,128)(2,1)S(1)}, bf16[360,128]{1,0:T(8,128)(2,1)S(1)}, u32[]{:S(2)}, u32[]{:S(2)}) collective-permute-start(bf16[360,128]{1,0:T(8,128)(2,1)S(1)} %get-tuple-element.136), channel_id=1, source_target_pairs={{0,8},{1,9},{2,10},{3,11},{4,12},{5,13},{6,14},{7,15},{8,0},{9,1},... | collective-permute-start | bytes 276488 | tf_op jit(solution)/shard_map/ppermute | solution.py:238
  191.6 6.8 %collective-permute-start.41 = (bf16[360,128]{1,0:T(8,128)(2,1)S(1)}, bf16[360,128]{1,0:T(8,128)(2,1)S(1)}, u32[]{:S(2)}, u32[]{:S(2)}) collective-permute-start(bf16[360,128]{1,0:T(8,128)(2,1)S(1)} %get-tuple-element.134), channel_id=1, source_target_pairs={{0,4},{1,5},{2,6},{3,7},{4,8},{5,9},{6,10},{7,11},{8,12},{9,13},{1... | collective-permute-start | bytes 276488 | tf_op jit(solution)/shard_map/ppermute | solution.py:238
  193.7 13.8 %collective-permute-start.48 = (bf16[4,128,640]{2,1,0:T(8,128)(2,1)S(1)}, bf16[4,128,640]{2,1,0:T(8,128)(2,1)S(1)}, u32[]{:S(2)}, u32[]{:S(2)}) collective-permute-start(bf16[4,128,640]{2,1,0:T(8,128)(2,1)S(1)} %dynamic-slice_bitcast_fusion.1), channel_id=1, source_target_pairs={{0,2},{1,3},{2,0},{3,1},{4,6},{5,7},{6,4},{7,5},{8,10},{9,11},{10,... | collective-permute-start | bytes 1966088 | tf_op jit(solution)/shard_map/ppermute | solution.py:238
  198.7 15.0 %collective-permute-start.46 = (bf16[360,256]{1,0:T(8,128)(2,1)S(1)}, bf16[360,256]{1,0:T(8,128)(2,1)S(1)}, u32[]{:S(2)}, u32[]{:S(2)}) collective-permute-start(bf16[360,256]{1,0:T(8,128)(2,1)S(1)} %get-tuple-element.101), channel_id=1, source_target_pairs={{0,12},{1,13},{2,14},{3,15},{4,0},{5,1},{6,2},{7,3},{8,4},{9,5},{1... | collective-permute-start | bytes 552968 | tf_op jit(solution)/shard_map/ppermute | solution.py:238
  200.5 24.3 %collective-permute-start.45 = (bf16[360,256]{1,0:T(8,128)(2,1)S(1)}, bf16[360,256]{1,0:T(8,128)(2,1)S(1)}, u32[]{:S(2)}, u32[]{:S(2)}) collective-permute-start(bf16[360,256]{1,0:T(8,128)(2,1)S(1)} %get-tuple-element.102), channel_id=1, source_target_pairs={{0,8},{1,9},{2,10},{3,11},{4,12},{5,13},{6,14},{7,15},{8,0},{9,1},... | collective-permute-start | bytes 552968 | tf_op jit(solution)/shard_map/ppermute | solution.py:238
  200.6 24.3 %collective-permute-start.44 = (bf16[360,256]{1,0:T(8,128)(2,1)S(1)}, bf16[360,256]{1,0:T(8,128)(2,1)S(1)}, u32[]{:S(2)}, u32[]{:S(2)}) collective-permute-start(bf16[360,256]{1,0:T(8,128)(2,1)S(1)} %get-tuple-element.100), channel_id=1, source_target_pairs={{0,4},{1,5},{2,6},{3,7},{4,8},{5,9},{6,10},{7,11},{8,12},{9,13},{1... | collective-permute-start | bytes 552968 | tf_op jit(solution)/shard_map/ppermute | solution.py:238
  207.7 19.0 %collective-permute-start.52 = (bf16[128,640]{1,0:T(8,128)(2,1)S(1)}, bf16[128,640]{1,0:T(8,128)(2,1)S(1)}, u32[]{:S(2)}, u32[]{:S(2)}) collective-permute-start(bf16[128,640]{1,0:T(8,128)(2,1)S(1)} %get-tuple-element.125), channel_id=1, source_target_pairs={{0,12},{1,13},{2,14},{3,15},{4,0},{5,1},{6,2},{7,3},{8,4},{9,5},{1... | collective-permute-start | bytes 491528 | tf_op jit(solution)/shard_map/ppermute | solution.py:238
  213.7 16.0 %collective-permute-start.51 = (bf16[128,640]{1,0:T(8,128)(2,1)S(1)}, bf16[128,640]{1,0:T(8,128)(2,1)S(1)}, u32[]{:S(2)}, u32[]{:S(2)}) collective-permute-start(bf16[128,640]{1,0:T(8,128)(2,1)S(1)} %get-tuple-element.126), channel_id=1, source_target_pairs={{0,8},{1,9},{2,10},{3,11},{4,12},{5,13},{6,14},{7,15},{8,0},{9,1},... | collective-permute-start | bytes 491528 | tf_op jit(solution)/shard_map/ppermute | solution.py:238
  213.7 16.0 %collective-permute-start.50 = (bf16[128,640]{1,0:T(8,128)(2,1)S(1)}, bf16[128,640]{1,0:T(8,128)(2,1)S(1)}, u32[]{:S(2)}, u32[]{:S(2)}) collective-permute-start(bf16[128,640]{1,0:T(8,128)(2,1)S(1)} %get-tuple-element.124), channel_id=1, source_target_pairs={{0,4},{1,5},{2,6},{3,7},{4,8},{5,9},{6,10},{7,11},{8,12},{9,13},{1... | collective-permute-start | bytes 491528 | tf_op jit(solution)/shard_map/ppermute | solution.py:238
  225.1 7.5 %collective-permute-start.49 = (bf16[360,384]{1,0:T(8,128)(2,1)S(1)}, bf16[360,384]{1,0:T(8,128)(2,1)S(1)}, u32[]{:S(2)}, u32[]{:S(2)}) collective-permute-start(bf16[360,384]{1,0:T(8,128)(2,1)S(1)} %pad_maximum_fusion.7), channel_id=1, source_target_pairs={{0,16},{16,0},{1,17},{17,1},{2,18},{18,2},{3,19},{19,3},{4,20},{20... | collective-permute-start | bytes 829448 | tf_op jit(solution)/shard_map/ppermute | solution.py:242
  229.8 5.1 %collective-permute-start.53 = (bf16[64,640]{1,0:T(8,128)(2,1)S(1)}, bf16[64,640]{1,0:T(8,128)(2,1)S(1)}, u32[]{:S(2)}, u32[]{:S(2)}) collective-permute-start(bf16[64,640]{1,0:T(8,128)(2,1)S(1)} %select_convert_fusion.1), channel_id=1, source_target_pairs={{0,16},{16,0},{1,17},{17,1},{2,18},{18,2},{3,19},{19,3},{4,20},{20... | collective-permute-start | bytes 245768 | tf_op jit(solution)/shard_map/ppermute | solution.py:242
  (12 other events, 21.2 us)
